TPU v7x, 256 devices: a whole 4x4x8 slice. The times are simulated.
256 devices in a mesh: tile: 32 (over z, x_hi, core), src: 2 (over x_lo), elec: 4 (over y).
Axes of the slice: x: 4 (x_hi: 2, x_lo: 2; x = x_hi * 2 + x_lo), y: 4, z: 8, core: 2. Of those that a mesh axis runs over, the one named last changes fastest.
Arguments:
- potential: float32 [8, 256, 512, 256], P('src', 'tile', 'elec'), may hold values from -6 to 6
- source_term: float32 [8, 256, 512, 256], P('src', 'tile', 'elec'), may hold values from -6 to 6
- conductivity: float32 [256, 512, 256], P('tile', 'elec'), may hold values from 0.1 to 10
- contact_map: int32 [256, 512], P('tile', 'elec'), may hold values from 0 to 2048, as said below
- admittance: float32 [2048], replicated, may hold values from 0.5 to 5
- impedance: float32 [16, 128, 128], P('elec'), may hold values from -2 to 2
- source_pairs: int32 [8, 2], P('src'), may hold values from 0 to 2047, as said below
- amplitudes: float32 [8], P('src'), may hold values from 1 to 4
Outputs:
- relaxed_potential: float32 [8, 256, 512, 256], P('src', 'tile', 'elec')
- electrode_volts: float32 [8, 2048], P('src', 'elec')
Inputs may be any that keep to these rules, and one draw needn't show every extreme that they name: `contact_map`: values below 2048 name the touching electrode; 2048 marks an untouched row. `source_pairs`: the anode and cathode of a source differ.
All inputs are finite; a program needn't handle non-finite values.
Results may differ from a plain program's by a relative error of at most 0.0003.
Values sent between devices are 32-bit elements; how exact they have to be, the bound alone decides.
No kernel may reach another device: no remote copies, remote signals or barrier semaphores. Data moves between devices by JAX's collectives and lax.ppermute only.
A program may use at most 128 MiB of HBM per device.

v0:
```python
import jax
import jax.numpy as jnp
from jax import lax
from jax.sharding import PartitionSpec as P

SWEEPS = 2


OMEGA = 0.8
EXACT = lax.Precision.HIGHEST


def extended(cells, sides, width):
    for axis, dim in sides:
        count = lax.axis_size(axis)
        ends = count - 1
        head = lax.slice_in_dim(cells, 0, width, axis=dim)
        tail = lax.slice_in_dim(cells, cells.shape[dim] - width, cells.shape[dim], axis=dim)
        cells = jnp.concatenate(
            [
                lax.ppermute(tail, axis, [(i, (i + 1) % count) for i in range(ends)]),
                cells,
                lax.ppermute(head, axis, [((i + 1) % count, i) for i in range(ends)]),
            ],
            axis=dim,
        )
    return cells


def neighbours(padded):
    return [
        padded[..., :-2, 1:-1, 1:-1],
        padded[..., 2:, 1:-1, 1:-1],
        padded[..., 1:-1, :-2, 1:-1],
        padded[..., 1:-1, 2:, 1:-1],
        padded[..., 1:-1, 1:-1, :-2],
        padded[..., 1:-1, 1:-1, 2:],
    ]


def face_weights(middle, padded):
    return [2.0 * middle * neighbour / (middle + neighbour) for neighbour in neighbours(padded)]


def sum_weights(weights, zeta):
    return weights[0] + weights[1] + weights[2] + weights[3] + weights[4] + weights[5] + zeta


def relax_once(current, padded, weights, diagonal, source_term):
    others = neighbours(padded)
    pulled = weights[0] * others[0]
    for number in range(1, 6):
        pulled = pulled + weights[number] * others[number]
    return current + OMEGA * (source_term - diagonal * current + pulled) / diagonal


def apply_blocks(impedance, summed, amplitudes, source_pairs, first_electrode):
    sources = summed.shape[0]
    count = summed.shape[1]
    electrode_ids = first_electrode + lax.broadcasted_iota(jnp.int32, (1, count), 1)
    anodes = source_pairs[:, 0:1]
    cathode = source_pairs[:, 1:2]
    scale = amplitudes[:, None]
    injected = scale * (electrode_ids == anodes).astype(jnp.float32) - scale * (
        electrode_ids == cathode
    ).astype(jnp.float32)
    charges = (summed + injected).reshape(sources, impedance.shape[0], impedance.shape[1])
    voltages = jnp.einsum("bij,sbj->sbi", impedance, charges, precision=EXACT)
    return voltages.reshape(sources, count)


def per_device(
    potential,
    source_term,
    conductivity,
    contact_map,
    admittance,
    impedance,
    source_pairs,
    amplitudes,
):
    sources = potential.shape[0]
    cells_x = conductivity.shape[0]
    cells_y = conductivity.shape[1]
    electrodes = admittance.shape[0]
    owned_count = impedance.shape[0] * impedance.shape[1]
    row_ids = contact_map.reshape(-1)
    row_count = row_ids.shape[0]
    electrode_cols = lax.broadcasted_iota(jnp.int32, (1, electrodes), 1)
    onehot = (row_ids[:, None] == electrode_cols).astype(jnp.float32)
    zeta = jnp.dot(onehot, admittance, precision=EXACT).reshape(cells_x, cells_y, 1)
    cond_padded = extended(conductivity, (("tile", 0), ("elec", 1)), 1)
    cond_padded = jnp.pad(cond_padded, ((0, 0), (0, 0), (1, 1)))
    weights = face_weights(conductivity, cond_padded)
    diagonal = sum_weights(weights, zeta)
    current = potential
    for sweep in range(SWEEPS):
        padded = extended(current, (("tile", 1), ("elec", 2)), 1)
        padded = jnp.pad(padded, ((0, 0), (0, 0), (0, 0), (1, 1)))
        current = relax_once(current, padded, weights, diagonal, source_term)
    row_means = jnp.mean(current, axis=-1).reshape(sources, row_count)
    partial_value = jnp.dot(row_means, onehot, precision=EXACT)
    summed = lax.psum(partial_value, "tile")
    owned = lax.psum_scatter(summed, "elec", scatter_dimension=1, tiled=True)
    electrode_volts = apply_blocks(
        impedance, owned, amplitudes, source_pairs, lax.axis_index("elec") * owned_count
    )
    full_volts = lax.all_gather(electrode_volts, "elec", axis=1, tiled=True)
    row_volts = lax.dot_general(full_volts, onehot, (((1,), (1,)), ((), ())), precision=EXACT)
    row_volts = row_volts.reshape(sources, cells_x, cells_y, 1)
    relaxed_potential = current + zeta * (row_volts - current) / diagonal
    return (relaxed_potential, electrode_volts)


def solution(mesh):
    placed = (
        P("src", "tile", "elec", None),
        P("src", "tile", "elec", None),
        P("tile", "elec", None),
        P("tile", "elec"),
        P(),
        P("elec", None, None),
        P("src", None),
        P("src"),
    )
    return jax.shard_map(
        per_device,
        mesh=mesh,
        in_specs=placed,
        out_specs=(P("src", "tile", "elec", None), P("src", "elec")),
        check_vma=False,
    )
```

profile of v0, /device:TPU:1, one launch (start us, length us, event | category | flops | bytes accessed | tf_op | source)
XLA Modules:
  0.0 260.4 jit_solution(8068780766682605968)
XLA Ops:
  7.2 0.0 copy-start
  7.2 0.0 copy-start.12
  7.2 0.0 copy-start.11
  7.2 0.0 reduce-scatter.4.cloned.1.call-start
  7.2 1.0 fusion.65
  8.3 6.0 %collective-permute-start = (f32[1,128,256]{2,1,0:T(8,128)S(1)}, f32[1,128,256]{2,1,0:T(8,128)S(1)}, u32[]{:S(2)}, u32[]{:S(2)}) collective-permute-start(f32[1,128,256]{2,1,0:T(8,128)S(1)} %get-tuple-element.22), channel_id=1, source_target_pairs={{0,8},{8,16},{16,24},{24,32},{32,40},{40,48},{48,56},{56,64},{64,7... | collective-permute-start | bytes 393224 | tf_op jit(solution)/shard_map/ppermute | solution.py:21
  14.3 1.9 collective-permute-start.1
  16.2 1.3 fusion.63
  17.6 5.1 %collective-permute-start.4 = (f32[4,1,128,256]{3,2,1,0:T(8,128)S(1)}, f32[4,1,128,256]{3,2,1,0:T(8,128)S(1)}, u32[]{:S(2)}, u32[]{:S(2)}) collective-permute-start(f32[4,1,128,256]{3,2,1,0:T(8,128)S(1)} %get-tuple-element.18), channel_id=1, source_target_pairs={{0,8},{8,16},{16,24},{24,32},{32,40},{40,48},{48,56},{56,64},{64,7... | collective-permute-start | bytes 1572872 | tf_op jit(solution)/shard_map/ppermute | solution.py:21
  22.7 1.9 collective-permute-start.5
  24.6 0.0 collective-permute-done
  24.7 1.3 constant_dynamic-update-slice_fusion.1
  26.0 0.0 copy-start.2
  26.0 0.0 collective-permute-done.1
  26.1 3.5 %collective-permute-start.2 = (f32[10,1,256]{2,1,0:T(1,128)S(1)}, f32[10,1,256]{2,1,0:T(1,128)S(1)}, u32[]{:S(2)}, u32[]{:S(2)}) collective-permute-start(f32[10,1,256]{2,1,0:T(1,128)S(1)} %get-tuple-element.20), channel_id=1, source_target_pairs={{0,1},{1,2},{2,3},{4,5},{5,6},{6,7},{8,9},{9,10},{10,11},{12,13},{... | collective-permute-start | bytes 30728 | tf_op jit(solution)/shard_map/ppermute | solution.py:21
  29.5 1.3 collective-permute-start.3
  30.8 0.0 copy-done.12
  30.8 0.0 copy-done.11
  30.9 3.8 %fusion.2 = f32[1,1024]{1,0:T(1,128)S(1)} fusion(f32[2048,1]{0,1:T(1,128)S(1)} %bitcast.36, s32[1024]{0:T(1024)S(1)} %bitcast.37), kind=kOutput, calls=%fused_computation.5 | convolution fusion | flops 27262976 | bytes 16384 | tf_op jit(solution)/shard_map/dot_general | solution.py:91
  34.7 0.0 collective-permute-done.2
  34.7 0.0 collective-permute-done.3
  34.7 0.7 select_maximum_fusion.6
  35.5 0.0 collective-permute-done.4
  35.5 0.0 copy-start.6
  35.5 0.8 copy-done.6
  36.3 0.0 copy-done.2
  36.3 0.0 copy-start.3
  36.3 0.6 constant_dynamic-update-slice_fusion.4
  37.0 0.0 collective-permute-done.5
  37.0 0.0 copy-start.7
  37.0 0.0 copy-start.1
  37.0 0.1 fusion.61
  37.1 4.0 %collective-permute-start.6 = (f32[4,10,1,256]{3,2,1,0:T(1,128)S(1)}, f32[4,10,1,256]{3,2,1,0:T(1,128)S(1)}, u32[]{:S(2)}, u32[]{:S(2)}) collective-permute-start(f32[4,10,1,256]{3,2,1,0:T(1,128)S(1)} %get-tuple-element.13), channel_id=1, source_target_pairs={{0,1},{1,2},{2,3},{4,5},{5,6},{6,7},{8,9},{9,10},{10,11},{12,13},{... | collective-permute-start | bytes 122888 | tf_op jit(solution)/shard_map/ppermute | solution.py:21
  41.1 1.3 collective-permute-start.7
  42.4 3.5 %add_add_fusion = (f32[8,128,256]{2,1,0:T(8,128)S(1)}, f32[8,128,256]{2,1,0:T(8,128)S(1)}, f32[8,128,256]{2,1,0:T(8,128)S(1)}, f32[8,128,256]{2,1,0:T(8,128)}, f...) fusion(f32[8,128]{1,0:T(8,128)S(1)} %bitcast.34, f32[8,128,256]{2,1,0:T(8,128)S(1)} %copy-done.3, ...), kind=kLoop, calls=%fused_computation.77 | loop fusion | flops 7602176 | bytes 12083200 | tf_op jit(solution)/shard_map/add | solution.py:46
  46.0 0.0 collective-permute-done.6
  46.0 0.0 collective-permute-done.7
  46.0 0.0 copy-done.1
  46.0 5.9 %select_maximum_fusion.4 = f32[4,10,130,258]{3,2,1,0:T(8,128)} fusion(f32[4,10,1,256]{3,2,1,0:T(1,128)S(1)} %collective-permute-done.7, f32[4,10,128,256]{3,2,1,0:T(8,128)S(1)} %constant_dynamic-update-slice_fusion.3, f32[4,10,1,256]{3,2,1,0:T(1,128)S(1)} %collective-permute-done.6), kind=kLoop, calls=%fused_computation.10 | loop fusion | flops 10732800 | bytes 10691200 | tf_op jit(solution)/shard_map/concatenate | solution.py:19
  51.9 18.1 %fusion.21 = f32[4,8,128,256]{3,2,1,0:T(8,128)} fusion(f32[4,8,128,256]{3,2,1,0:T(8,128)} %param.8, f32[4,10,130,258]{3,2,1,0:T(8,128)} %select_maximum_fusion.4, f32[4,10,1,256]{3,2,1,0:T(1,128)S(1)} %collective-permute-done.7, f32[4,10,128,256]{3,2,1,0:T(8,128)} %copy-done.1, f32[4,10,1,256]{3,2,1,0:T(1,128)S(1)} %collective-permute-done.6, ...), kind=kLoop, calls=%fused_computation.41 | loop fusion | flops 22020096 | bytes 34684928 | tf_op jit(solution)/shard_map/add | solution.py:54
  70.0 0.0 copy-start.9
  70.0 1.3 fusion.62
  71.3 7.2 %collective-permute-start.8 = (f32[4,1,128,256]{3,2,1,0:T(8,128)S(1)}, f32[4,1,128,256]{3,2,1,0:T(8,128)S(1)}, u32[]{:S(2)}, u32[]{:S(2)}) collective-permute-start(f32[4,1,128,256]{3,2,1,0:T(8,128)S(1)} %get-tuple-element.15), channel_id=1, source_target_pairs={{0,8},{8,16},{16,24},{24,32},{32,40},{40,48},{48,56},{56,64},{64,7... | collective-permute-start | bytes 1572872 | tf_op jit(solution)/shard_map/ppermute | solution.py:21
  78.5 1.9 collective-permute-start.9
  80.4 4.0 %collective-permute-done.8 = f32[4,1,128,256]{3,2,1,0:T(8,128)S(1)} collective-permute-done((f32[4,1,128,256]{3,2,1,0:T(8,128)S(1)}, f32[4,1,128,256]{3,2,1,0:T(8,128)S(1)}, u32[]{:S(2)}, u32[]{:S(2)}) %collective-permute-start.8) | collective-permute-done | bytes 524320 | tf_op jit(solution)/shard_map/ppermute | solution.py:21
  84.4 6.1 %collective-permute-done.9 = f32[4,1,128,256]{3,2,1,0:T(8,128)S(1)} collective-permute-done((f32[4,1,128,256]{3,2,1,0:T(8,128)S(1)}, f32[4,1,128,256]{3,2,1,0:T(8,128)S(1)}, u32[]{:S(2)}, u32[]{:S(2)}) %collective-permute-start.9) | collective-permute-done | bytes 524320 | tf_op jit(solution)/shard_map/ppermute | solution.py:23
  90.5 1.9 pad_maximum_fusion.18
  92.4 0.0 copy-done.5
  92.4 3.3 %collective-permute-start.10 = (f32[4,10,1,256]{3,2,1,0:T(1,128)}, f32[4,10,1,256]{3,2,1,0:T(1,128)S(1)}, u32[]{:S(2)}, u32[]{:S(2)}) collective-permute-start(f32[4,10,1,256]{3,2,1,0:T(1,128)} %get-tuple-element.11), channel_id=1, source_target_pairs={{0,1},{1,2},{2,3},{4,5},{5,6},{6,7},{8,9},{9,10},{10,11},{12,13},{... | collective-permute-start | bytes 122888 | tf_op jit(solution)/shard_map/ppermute | solution.py:21
  95.7 1.3 collective-permute-start.11
  97.0 0.1 collective-permute-done.10
  97.1 3.3 %collective-permute-done.11 = f32[4,10,1,256]{3,2,1,0:T(1,128)S(1)} collective-permute-done((f32[4,10,1,256]{3,2,1,0:T(1,128)S(1)}, f32[4,10,1,256]{3,2,1,0:T(1,128)S(1)}, u32[]{:S(2)}, u32[]{:S(2)}) %collective-permute-start.11) | collective-permute-done | bytes 40992 | tf_op jit(solution)/shard_map/ppermute | solution.py:23
  100.4 8.6 %select_maximum_fusion = f32[4,10,130,258]{3,2,1,0:T(8,128)} fusion(f32[4,10,1,256]{3,2,1,0:T(1,128)S(1)} %collective-permute-done.11, f32[4,10,1,256]{3,2,1,0:T(1,128)S(1)} %collective-permute-done.10, f32[4,1,128,256]{3,2,1,0:T(8,128)} %copy-done.5, f32[4,8,128,256]{3,2,1,0:T(8,128)} %fusion.21, f32[4,1,128,256]{3,2,1,0:T(8,128)} %copy-done.4), kind=kLoop, calls=%fused_computation.6 | loop fusion | flops 16099200 | bytes 10691200 | tf_op jit(solution)/shard_map/concatenate | solution.py:19
  109.1 18.6 %fusion.57 = (f32[4,8,128]{2,1,0:T(8,128)S(1)}, f32[4,8,128,256]{3,2,1,0:T(8,128)}) fusion(f32[4,8,128,256]{3,2,1,0:T(8,128)} %fusion.21, f32[4,10,130,258]{3,2,1,0:T(8,128)} %select_maximum_fusion, f32[8,128,256]{2,1,0:T(8,128)} %get-tuple-element.10, f32[8,128,256]{2,1,0:T(8,128)} %get-tuple-element.9, f32[4,10,1,256]{3,2,1,0:T(1,128)S(1)} %collective-permute-done.11, ...), kind=kLoop, calls=%fused_computation.111 | loop fusion | flops 27258880 | bytes 29458432 | tf_op jit(solution)/shard_map/reduce_sum | solution.py:101
  127.7 0.0 copy-start.10
  127.7 7.8 %fusion.33 = f32[2048,4]{1,0:T(8,128)} fusion(s32[1024]{0:T(1024)S(1)} %bitcast.38, f32[1,4,8,128]{3,2,1,0:T(8,128)S(1)} %multiply_bitcast_fusion), kind=kOutput, calls=%fused_computation.61 | convolution fusion | flops 102760448 | bytes 53248
  135.5 0.0 reduce-scatter.4.cloned.1.call-update
  135.6 31.4 %reduce-scatter.4.cloned.1.call-done = f32[512,4]{1,0:T(8,128)} async-done(((f32[2048,4]{1,0:T(8,128)}), f32[512,4]{1,0:T(8,128)}) %reduce-scatter.4.cloned.1.call-update) | async-done | bytes 8208
  167.0 1.1 copy.13
  168.0 68.0 %psum.8 = f32[4,512]{1,0:T(4,128)S(1)} all-reduce(f32[4,512]{1,0:T(4,128)S(1)} %copy.13), channel_id=1, replica_groups=mesh['tile'=32,'src'=2,'elec'=4] {'tile'}, use_global_device_ids=true, to_apply=%region_1.2 | all-reduce | flops 2048 | bytes 16384 | tf_op jit(solution)/shard_map/psum | solution.py:103
  236.1 0.5 convolution_bitcast_fusion
  236.6 9.1 %all_gather.3 = f32[4,2048]{1,0:T(4,128)S(1)} all-gather(f32[4,512]{1,0:T(4,128)S(1)} %convolution_bitcast_fusion), channel_id=1, replica_groups=mesh['tile'=32,'src'=2,'elec'=4] {'elec'}, dimensions={1}, use_global_device_ids=true | all-gather | bytes 40960 | tf_op jit(solution)/shard_map/all_gather | solution.py:108
  245.7 3.8 %fusion.35 = f32[1,4,8,128]{3,1,2,0:T(4,128)S(1)} fusion(f32[4,2048]{1,0:T(4,128)S(1)} %all_gather.3, s32[1024]{0:T(1024)S(1)} %bitcast.39), kind=kOutput, calls=%fused_computation.65 | convolution fusion | flops 102760448 | bytes 53248 | tf_op jit(solution)/shard_map/dot_general | solution.py:109
  249.5 4.1 %divide_add_fusion = f32[4,8,128,256]{3,2,1,0:T(8,128)} fusion(f32[4,8,128,256]{3,2,1,0:T(8,128)} %get-tuple-element.3, f32[4,8,128]{2,1,0:T(8,128)S(1)} %bitcast.33, f32[8,128]{1,0:T(8,128)S(1)} %bitcast.35, f32[8,128,256]{2,1,0:T(8,128)S(1)} %get-tuple-element.4), kind=kLoop, calls=%fused_computation.55 | loop fusion | flops 4194304 | bytes 9457664 | tf_op jit(solution)/shard_map/add | solution.py:111
  (19 shorter events, 0.2 us)
Async XLA Ops:
  7.2 228.9 %copy-start = (f32[4,128,128]{2,1,0:T(8,128)S(1)}, f32[4,128,128]{2,1,0:T(8,128)}, u32[]{:S(2)}) copy-start(f32[4,128,128]{2,1,0:T(8,128)} %param.13) | copy-start | bytes 786436
  7.2 23.7 %copy-start.12 = (s32[8,128]{1,0:T(8,128)S(1)}, s32[8,128]{1,0:T(8,128)}, u32[]{:S(2)}) copy-start(s32[8,128]{1,0:T(8,128)} %param.11) | copy-start | bytes 12292
  7.2 23.7 %copy-start.11 = (f32[2048]{0:T(1024)S(1)}, f32[2048]{0:T(1024)}, u32[]{:S(2)}) copy-start(f32[2048]{0:T(1024)} %param.12) | copy-start | bytes 24580
  7.2 159.8 %reduce-scatter.4.cloned.1.call-start = ((), (), s32[]{:S(2)}) async-start(), calls=%async_computation.1 | async-start | bytes 1310720
  8.3 16.4 %collective-permute-start = (f32[1,128,256]{2,1,0:T(8,128)S(1)}, f32[1,128,256]{2,1,0:T(8,128)S(1)}, u32[]{:S(2)}, u32[]{:S(2)}) collective-permute-start(f32[1,128,256]{2,1,0:T(8,128)S(1)} %get-tuple-element.22), channel_id=1, source_target_pairs={{0,8},{8,16},{16,24},{24,32},{32,40},{40,48},{48,56},{56,64},{64,7... | collective-permute-start | bytes 393224 | tf_op jit(solution)/shard_map/ppermute | solution.py:21
  14.3 11.7 %collective-permute-start.1 = (f32[1,128,256]{2,1,0:T(8,128)S(1)}, f32[1,128,256]{2,1,0:T(8,128)S(1)}, u32[]{:S(2)}, u32[]{:S(2)}) collective-permute-start(f32[1,128,256]{2,1,0:T(8,128)S(1)} %get-tuple-element.21), channel_id=1, source_target_pairs={{8,0},{16,8},{24,16},{32,24},{40,32},{48,40},{56,48},{64,56},{72,6... | collective-permute-start | bytes 393224 | tf_op jit(solution)/shard_map/ppermute | solution.py:23
  17.6 17.9 %collective-permute-start.4 = (f32[4,1,128,256]{3,2,1,0:T(8,128)S(1)}, f32[4,1,128,256]{3,2,1,0:T(8,128)S(1)}, u32[]{:S(2)}, u32[]{:S(2)}) collective-permute-start(f32[4,1,128,256]{3,2,1,0:T(8,128)S(1)} %get-tuple-element.18), channel_id=1, source_target_pairs={{0,8},{8,16},{16,24},{24,32},{32,40},{40,48},{48,56},{56,64},{64,7... | collective-permute-start | bytes 1572872 | tf_op jit(solution)/shard_map/ppermute | solution.py:21
  22.7 14.3 %collective-permute-start.5 = (f32[4,1,128,256]{3,2,1,0:T(8,128)S(1)}, f32[4,1,128,256]{3,2,1,0:T(8,128)S(1)}, u32[]{:S(2)}, u32[]{:S(2)}) collective-permute-start(f32[4,1,128,256]{3,2,1,0:T(8,128)S(1)} %get-tuple-element.17), channel_id=1, source_target_pairs={{8,0},{16,8},{24,16},{32,24},{40,32},{48,40},{56,48},{64,56},{72,6... | collective-permute-start | bytes 1572872 | tf_op jit(solution)/shard_map/ppermute | solution.py:23
  26.0 10.3 %copy-start.2 = (f32[4,8,128,256]{3,2,1,0:T(8,128)S(1)}, f32[4,8,128,256]{3,2,1,0:T(8,128)}, u32[]{:S(2)}) copy-start(f32[4,8,128,256]{3,2,1,0:T(8,128)} %param.8) | copy-start | bytes 12582916
  26.1 8.6 %collective-permute-start.2 = (f32[10,1,256]{2,1,0:T(1,128)S(1)}, f32[10,1,256]{2,1,0:T(1,128)S(1)}, u32[]{:S(2)}, u32[]{:S(2)}) collective-permute-start(f32[10,1,256]{2,1,0:T(1,128)S(1)} %get-tuple-element.20), channel_id=1, source_target_pairs={{0,1},{1,2},{2,3},{4,5},{5,6},{6,7},{8,9},{9,10},{10,11},{12,13},{... | collective-permute-start | bytes 30728 | tf_op jit(solution)/shard_map/ppermute | solution.py:21
  29.5 5.2 %collective-permute-start.3 = (f32[10,1,256]{2,1,0:T(1,128)S(1)}, f32[10,1,256]{2,1,0:T(1,128)S(1)}, u32[]{:S(2)}, u32[]{:S(2)}) collective-permute-start(f32[10,1,256]{2,1,0:T(1,128)S(1)} %get-tuple-element.19), channel_id=1, source_target_pairs={{1,0},{2,1},{3,2},{5,4},{6,5},{7,6},{9,8},{10,9},{11,10},{13,12},{... | collective-permute-start | bytes 30728 | tf_op jit(solution)/shard_map/ppermute | solution.py:23
  35.5 0.8 copy-start.6
  36.3 6.1 %copy-start.3 = (f32[8,128,256]{2,1,0:T(8,128)S(1)}, f32[8,128,256]{2,1,0:T(8,128)}, u32[]{:S(2)}) copy-start(f32[8,128,256]{2,1,0:T(8,128)} %param.10) | copy-start | bytes 3145732
  37.0 9.0 %copy-start.7 = (f32[4,1,128,256]{3,2,1,0:T(8,128)}, f32[4,1,128,256]{3,2,1,0:T(8,128)S(1)}, u32[]{:S(2)}) copy-start(f32[4,1,128,256]{3,2,1,0:T(8,128)S(1)} %collective-permute-done.5) | copy-start | bytes 1572868
  37.0 9.0 %copy-start.1 = (f32[4,10,128,256]{3,2,1,0:T(8,128)}, f32[4,10,128,256]{3,2,1,0:T(8,128)S(1)}, u32[]{:S(2)}) copy-start(f32[4,10,128,256]{3,2,1,0:T(8,128)S(1)} %constant_dynamic-update-slice_fusion.3) | copy-start | bytes 15728644
  37.1 8.9 %collective-permute-start.6 = (f32[4,10,1,256]{3,2,1,0:T(1,128)S(1)}, f32[4,10,1,256]{3,2,1,0:T(1,128)S(1)}, u32[]{:S(2)}, u32[]{:S(2)}) collective-permute-start(f32[4,10,1,256]{3,2,1,0:T(1,128)S(1)} %get-tuple-element.13), channel_id=1, source_target_pairs={{0,1},{1,2},{2,3},{4,5},{5,6},{6,7},{8,9},{9,10},{10,11},{12,13},{... | collective-permute-start | bytes 122888 | tf_op jit(solution)/shard_map/ppermute | solution.py:21
  41.1 4.9 %collective-permute-start.7 = (f32[4,10,1,256]{3,2,1,0:T(1,128)S(1)}, f32[4,10,1,256]{3,2,1,0:T(1,128)S(1)}, u32[]{:S(2)}, u32[]{:S(2)}) collective-permute-start(f32[4,10,1,256]{3,2,1,0:T(1,128)S(1)} %get-tuple-element.14), channel_id=1, source_target_pairs={{1,0},{2,1},{3,2},{5,4},{6,5},{7,6},{9,8},{10,9},{11,10},{13,12},{... | collective-permute-start | bytes 122888 | tf_op jit(solution)/shard_map/ppermute | solution.py:23
  70.0 26.9 %copy-start.9 = (s32[4,2]{0,1:T(2,128)S(1)}, s32[4,2]{0,1:T(2,128)}, u32[]{:S(2)}) copy-start(s32[4,2]{0,1:T(2,128)} %param.14) | copy-start | bytes 100
  71.3 13.1 %collective-permute-start.8 = (f32[4,1,128,256]{3,2,1,0:T(8,128)S(1)}, f32[4,1,128,256]{3,2,1,0:T(8,128)S(1)}, u32[]{:S(2)}, u32[]{:S(2)}) collective-permute-start(f32[4,1,128,256]{3,2,1,0:T(8,128)S(1)} %get-tuple-element.15), channel_id=1, source_target_pairs={{0,8},{8,16},{16,24},{24,32},{32,40},{40,48},{48,56},{56,64},{64,7... | collective-permute-start | bytes 1572872 | tf_op jit(solution)/shard_map/ppermute | solution.py:21
  78.5 12.0 %collective-permute-start.9 = (f32[4,1,128,256]{3,2,1,0:T(8,128)S(1)}, f32[4,1,128,256]{3,2,1,0:T(8,128)S(1)}, u32[]{:S(2)}, u32[]{:S(2)}) collective-permute-start(f32[4,1,128,256]{3,2,1,0:T(8,128)S(1)} %get-tuple-element.16), channel_id=1, source_target_pairs={{8,0},{16,8},{24,16},{32,24},{40,32},{48,40},{56,48},{64,56},{72,6... | collective-permute-start | bytes 1572872 | tf_op jit(solution)/shard_map/ppermute | solution.py:23
  84.4 6.1 %copy-start.4 = (f32[4,1,128,256]{3,2,1,0:T(8,128)}, f32[4,1,128,256]{3,2,1,0:T(8,128)S(1)}, u32[]{:S(2)}) copy-start(f32[4,1,128,256]{3,2,1,0:T(8,128)S(1)} %collective-permute-done.8) | copy-start | bytes 1572868
  90.5 1.9 copy-start.5
  92.4 4.7 %collective-permute-start.10 = (f32[4,10,1,256]{3,2,1,0:T(1,128)}, f32[4,10,1,256]{3,2,1,0:T(1,128)S(1)}, u32[]{:S(2)}, u32[]{:S(2)}) collective-permute-start(f32[4,10,1,256]{3,2,1,0:T(1,128)} %get-tuple-element.11), channel_id=1, source_target_pairs={{0,1},{1,2},{2,3},{4,5},{5,6},{6,7},{8,9},{9,10},{10,11},{12,13},{... | collective-permute-start | bytes 122888 | tf_op jit(solution)/shard_map/ppermute | solution.py:21
  95.7 4.7 %collective-permute-start.11 = (f32[4,10,1,256]{3,2,1,0:T(1,128)S(1)}, f32[4,10,1,256]{3,2,1,0:T(1,128)S(1)}, u32[]{:S(2)}, u32[]{:S(2)}) collective-permute-start(f32[4,10,1,256]{3,2,1,0:T(1,128)S(1)} %get-tuple-element.12), channel_id=1, source_target_pairs={{1,0},{2,1},{3,2},{5,4},{6,5},{7,6},{9,8},{10,9},{11,10},{13,12},{... | collective-permute-start | bytes 122888 | tf_op jit(solution)/shard_map/ppermute | solution.py:23
  127.7 108.4 %copy-start.10 = (f32[4]{0:T(128)S(1)}, f32[4]{0:T(128)}, u32[]{:S(2)}) copy-start(f32[4]{0:T(128)} %param.15) | copy-start | bytes 52
  236.6 17.0 %copy-start.8 = (f32[4,512]{1,0:T(4,128)}, f32[4,512]{1,0:T(4,128)S(1)}, u32[]{:S(2)}) copy-start(f32[4,512]{1,0:T(4,128)S(1)} %convolution_bitcast_fusion) | copy-start | bytes 24580
Sparse Core Ops, SparseCore 0:
  135.7 31.2 reduce-scatter.3
where the time goes:
time: 265 us; the launch traced here: 260 us
  blocking collectives  77.1 us (29%)
  other arithmetic  61.5 us (23%)
  waiting for transfers between devices  45 us (17%)
  starting transfers between devices  38.7 us (15%)
  matrix products  16 us (6%)
  between operations  14.4 us (5%)
  local copies, waits for them, and re-layouts  7.65 us (3%)
    psum x1, blocking collectives, per_device(): summed = lax.psum(partial_value, 'tile')  68 us
    unnamed x2, waiting for transfers between devices  31.4 us
    ppermute x6, starting transfers between devices, extended(): lax.ppermute(tail, axis, [(i, (i + 1) % count) for i in range(ends)])  29.1 us
    reduce_sum x1, other arithmetic, per_device(): row_means = jnp.mean(current, axis=-1).reshape(sources, row_count)  18.6 us
    add x1, other arithmetic, relax_once(): current + OMEGA * (source_term - diagonal * current + pulled) / diagonal  18.1 us
    concatenate x3, other arithmetic, extended(): jnp.concatenate([lax.ppermute(tail, axis, [(i, (i + 1) % count) for i in...  15.3 us
    ppermute x6, starting transfers between devices, extended(): lax.ppermute(head, axis, [((i + 1) % count, i) for i in range(ends)])  9.64 us
    ppermute x6, waiting for transfers between devices, extended(): lax.ppermute(head, axis, [((i + 1) % count, i) for i in range(ends)])  9.45 us
  transfers between devices with their start and end apart: 13, of which 5 were waited for; matrix products, arithmetic and copies ran while one was open for 4% of the time, Pallas kernels for 0%

commit v1 on v0

v1 whole, which is shorter than its diff:
```python
import jax
import jax.numpy as jnp
from jax import lax
from jax.experimental import pallas as pl
from jax.experimental.pallas import tpu as pltpu
from jax.sharding import Mesh
from jax.sharding import PartitionSpec as P

OMEGA = 0.8
KEEP = 1.0 - OMEGA
TINY = 1e-30
F32 = jnp.float32
EXACT = lax.Precision.HIGHEST
VMEM_LIMIT = 24 * 1024 * 1024
TILE = ("zx", "core")

NT = (((1,), (1,)), ((), ()))


def params():
    return pltpu.CompilerParams(vmem_limit_bytes=VMEM_LIMIT)


def vmem():
    return pl.BlockSpec(memory_space=pltpu.VMEM)


def smem():
    return pl.BlockSpec(memory_space=pltpu.SMEM)


def hbm():
    return pl.BlockSpec(memory_space=pl.ANY)


def f32(*shape):
    return jax.ShapeDtypeStruct(shape, F32)


def kept(*shape):
    return pltpu.VMEM(shape, F32)


def face(a, b):
    return 2.0 * a * b / jnp.maximum(a + b, TINY)


def iota(shape, dim):
    return lax.broadcasted_iota(jnp.int32, shape, dim)


def shift_up(a, axis):
    return pltpu.roll(a, a.shape[axis] - 1, axis)


def shift_down(a, axis):
    return pltpu.roll(a, 1, axis)


def in_line(flux_weight, u, axis):
    return flux_weight * shift_up(u, axis) + shift_down(flux_weight * u, axis)


def line_weight(c, axis):
    w = face(c, shift_up(c, axis))
    return jnp.where(iota(c.shape, axis) < c.shape[axis] - 1, w, 0.0)


def both_sides(w, axis):
    return w + shift_down(w, axis)


def row_sums(slabs):
    folded = jnp.concatenate([p[:, :128] + p[:, 128:] for p in slabs], axis=0)
    head = folded.astype(jnp.bfloat16)
    rest = (folded - head.astype(F32)).astype(jnp.bfloat16)
    ones = jnp.ones((8, 128), jnp.bfloat16)
    total = lax.dot_general(ones, head, NT, preferred_element_type=F32)
    total = total + lax.dot_general(ones, rest, NT, preferred_element_type=F32)
    return jnp.concatenate([total[0:1, 128 * s : 128 * s + 128] for s in range(4)], axis=0)


def to_lanes(column):
    mask = iota((8, 128), 0) == iota((8, 128), 1)
    return jnp.sum(jnp.where(mask, column, jnp.zeros_like(column)), axis=0, keepdims=True)


def gather_rows(ids, table):
    block = lax.shift_right_logical(ids, 7)
    lane = lax.bitwise_and(ids, 127)
    found = jnp.zeros(ids.shape, F32)
    for b in range(16):
        row = jnp.broadcast_to(table[b : b + 1], ids.shape)
        got = jnp.take_along_axis(row, lane, axis=1)
        found = jnp.where(block == b, got, found)
    return found


def edges_kernel(u_lo, u_hi, c_lo, c_hi, cmap, out_lo, out_hi):
    for out, u, c, near, far, lane in (
        (out_lo, u_lo, c_lo, 0, 1, 0),
        (out_hi, u_hi, c_hi, 7, 6, 127),
    ):
        for x in range(8):
            for s in range(4):
                out[8 * s + x : 8 * s + x + 1, :] = u[s, x, near : near + 1, :]
            out[32 + x : 33 + x, :] = c[x, near : near + 1, :]
            out[40 + x : 41 + x, :] = c[x, far : far + 1, :]
        out[48:56, :] = jnp.zeros((8, 256), F32)
        out[48:49, 0:128] = to_lanes(cmap[:, lane : lane + 1].astype(F32))


def edges(u, c, cmap):
    return pl.pallas_call(
        edges_kernel,
        grid=(1,),
        in_specs=[
            pl.BlockSpec((4, 8, 8, 256), lambda i: (0, 0, 0, 0)),
            pl.BlockSpec((4, 8, 8, 256), lambda i: (0, 0, 15, 0)),
            pl.BlockSpec((8, 8, 256), lambda i: (0, 0, 0)),
            pl.BlockSpec((8, 8, 256), lambda i: (0, 15, 0)),
            pl.BlockSpec((8, 128), lambda i: (0, 0)),
        ],
        out_specs=[pl.BlockSpec((56, 256), lambda i: (0, 0))] * 2,
        out_shape=[f32(56, 256)] * 2,
        compiler_params=params(),
        name="edges",
    )(u, u, c, c, cmap)


def faces_kernel(c0, c1, c6, c7, cmap, y_lo, y_hi, down, up):
    for out, near, far, x in ((down, c0, c1, 0), (up, c7, c6, 7)):
        out[0:128, :] = near[0]
        out[128:256, :] = far[0]
        out[256:272, :] = jnp.zeros((16, 256), F32)
        out[256:257, :] = y_lo[32 + x : 33 + x, :]
        out[257:258, :] = y_hi[32 + x : 33 + x, :]
        out[258:259, 0:128] = cmap[x : x + 1, :].astype(F32)


def faces(c, cmap, y_lo, y_hi):
    def row(x):
        return pl.BlockSpec((1, 128, 256), lambda i: (x, 0, 0))

    edge = pl.BlockSpec((56, 256), lambda i: (0, 0))
    return pl.pallas_call(
        faces_kernel,
        grid=(1,),
        in_specs=[row(0), row(1), row(6), row(7), pl.BlockSpec((8, 128), lambda i: (0, 0)), edge, edge],
        out_specs=[pl.BlockSpec((272, 256), lambda i: (0, 0))] * 2,
        out_shape=[f32(272, 256)] * 2,
        compiler_params=params(),
        name="faces",
    )(c, c, c, c, cmap, y_lo, y_hi)


def local_sweep(u, below, above, f, w_below, w_above, wy, wz, gain):
    pulled = f + in_line(wy, u, 0)
    pulled = pulled + in_line(wz, u, 1)
    if below is not None:
        pulled = pulled + w_below * below
    if above is not None:
        pulled = pulled + w_above * above
    return KEEP * u + gain * pulled


def inner_kernel(
    u_hbm, f_hbm, c_hbm, cmap, admittance, y_lo, y_hi,
    u1, u2, wx, wy, wz, gain, wyl, wyh, zeta_t, sums,
    u, f, c, sems,
):
    copy_c = pltpu.make_async_copy(c_hbm, c, sems.at[0])
    copy_u = pltpu.make_async_copy(u_hbm, u, sems.at[1])
    copy_f = pltpu.make_async_copy(f_hbm, f, sems.at[2])
    copy_c.start()
    copy_u.start()
    copy_f.start()
    zeta = gather_rows(cmap[...], admittance[...])
    padded = jnp.concatenate([zeta, jnp.zeros((120, 128), F32)], axis=0)
    zeta_t[...] = jnp.transpose(padded)
    copy_c.wait()
    for x in range(8):
        here = c[x]
        if x < 7:
            wx[x] = face(here, c[x + 1])
        along_y = line_weight(here, 0)
        along_z = line_weight(here, 1)
        wy[x] = along_y
        wz[x] = along_z
        low = face(here[0:1], y_lo[32 + x : 33 + x, :])
        high = face(here[127:128], y_hi[32 + x : 33 + x, :])
        wyl[x : x + 1, :] = low
        wyh[x : x + 1, :] = high
        diag = both_sides(along_y, 0) + both_sides(along_z, 1) + zeta_t[:, x : x + 1]
        row = iota((128, 256), 0)
        diag = diag + jnp.where(row == 0, low, 0.0) + jnp.where(row == 127, high, 0.0)
        if x > 0:
            diag = diag + wx[x - 1]
        if x < 7:
            diag = diag + wx[x]
        gain[x] = diag if x in (0, 7) else OMEGA / diag
    copy_u.wait()
    copy_f.wait()

    def first(x, carry):
        for s in range(4):
            new = local_sweep(
                u[s, x], u[s, x - 1], u[s, x + 1], f[s, x], wx[x - 1], wx[x], wy[x], wz[x], gain[x]
            )
            u1[s, x] = new
            u1[s, x, 0:1, :] = (
                u1[s, x, 0:1, :] + gain[x, 0:1, :] * wyl[pl.ds(x, 1), :] * y_lo[pl.ds(8 * s + x, 1), :]
            )
            u1[s, x, 127:128, :] = (
                u1[s, x, 127:128, :] + gain[x, 127:128, :] * wyh[pl.ds(x, 1), :] * y_hi[pl.ds(8 * s + x, 1), :]
            )
        return carry

    lax.fori_loop(1, 7, first, 0)

    def second(x, carry):
        slabs = []
        for s in range(4):
            new = local_sweep(
                u1[s, x], u1[s, x - 1], u1[s, x + 1], f[s, x], wx[x - 1], wx[x], wy[x], wz[x], gain[x]
            )
            u2[s, x - 2] = new
            slabs.append(new)
        sums[x - 2] = row_sums(slabs)
        return carry

    lax.fori_loop(2, 6, second, 0)


def inner(u, f, c, cmap, admittance, y_lo, y_hi):
    outs = [
        kept(4, 8, 128, 256), kept(4, 4, 128, 256), kept(7, 128, 256), kept(8, 128, 256), kept(8, 128, 256),
        kept(8, 128, 256), kept(8, 256), kept(8, 256), kept(128, 128), kept(4, 4, 128),
    ]
    return pl.pallas_call(
        inner_kernel,
        in_specs=[hbm()] * 3 + [vmem()] * 4,
        out_specs=[vmem()] * len(outs),
        out_shape=outs,
        scratch_shapes=[
            pltpu.VMEM((4, 8, 128, 256), F32),
            pltpu.VMEM((4, 8, 128, 256), F32),
            pltpu.VMEM((8, 128, 256), F32),
            pltpu.SemaphoreType.DMA((3,)),
        ],
        compiler_params=params(),
        cost_estimate=pl.CostEstimate(flops=100_000_000, bytes_accessed=30_000_000, transcendentals=0),
        name="inner",
    )(u, f, c, cmap, admittance, y_lo, y_hi)


def outer_kernel(
    core, u_hbm, f_hbm, c_hbm, cmap, admittance, y_lo, y_hi, x_lo, x_hi, uh_lo, uh_hi,
    u1, wx, wy, wz, gain, wyl, wyh, sums,
    face_lo, face_hi, edge_lo, edge_hi, u2, gain_out, wxf, mine, other,
    u, f, c, ids, sems,
):
    copies = []
    for n, x in enumerate((0, 1, 6, 7)):
        copies.append(pltpu.make_async_copy(u_hbm.at[:, x], u.at[n], sems.at[0, n]))
        copies.append(pltpu.make_async_copy(f_hbm.at[:, x], f.at[n], sems.at[1, n]))
    for n, x in enumerate((0, 7)):
        copies.append(pltpu.make_async_copy(c_hbm.at[x], c.at[n], sems.at[2, n]))
    for copy in copies:
        copy.start()
    ids[0:8, :] = cmap[...]
    ids[8:16, :] = jnp.full((8, 128), 2048, jnp.int32)
    ids[8:9, :] = x_lo[258:259, 0:128].astype(jnp.int32)
    ids[9:10, :] = x_hi[258:259, 0:128].astype(jnp.int32)
    lanes = iota((1, 128), 1)
    low_ids = y_lo[48:49, 0:128].astype(jnp.int32)
    high_ids = pltpu.roll(y_hi[48:49, 0:128], 8, 1).astype(jnp.int32)
    ids[10:11, :] = jnp.where(lanes < 8, low_ids, jnp.where(lanes < 16, high_ids, 2048))
    table = admittance[...]
    zeta = gather_rows(ids[8:16, :], table)
    zeta_t = jnp.transpose(jnp.concatenate([zeta, jnp.zeros((120, 128), F32)], axis=0))
    for copy in copies:
        copy.wait()
    row = iota((128, 256), 0)

    pushed = []
    for n, (x, msg, halo, inside, out) in enumerate(
        ((0, x_lo, uh_lo, 1, face_lo), (7, x_hi, uh_hi, 2, face_hi))
    ):
        here = c[n]
        there = msg[0:128, :]
        outside = face(here, there)
        wxf[n] = outside
        g = OMEGA / (gain[x] + outside)
        gain_out[n] = g
        for s in range(4):
            new = local_sweep(
                u[3 * n, s], halo[s], u[inside, s], f[3 * n, s], outside, wx[0 if n == 0 else 6], wy[x], wz[x], g
            )
            out[s] = new
            out[s, 0:1, :] = out[s, 0:1, :] + g[0:1] * wyl[x : x + 1, :] * y_lo[8 * s + x : 8 * s + x + 1, :]
            out[s, 127:128, :] = (
                out[s, 127:128, :] + g[127:128] * wyh[x : x + 1, :] * y_hi[8 * s + x : 8 * s + x + 1, :]
            )
        beyond = face(there, msg[128:256, :])
        along_y = line_weight(there, 0)
        diag = both_sides(along_y, 0) + both_sides(line_weight(there, 1), 1) + zeta_t[:, n : n + 1]
        diag = diag + outside + beyond
        diag = diag + jnp.where(row == 0, face(there[0:1], msg[256:257, :]), 0.0)
        diag = diag + jnp.where(row == 127, face(there[127:128], msg[257:258, :]), 0.0)
        factor = OMEGA * outside / jnp.maximum(diag, TINY)
        pushed.append(row_sums([factor * out[s] for s in range(4)]))

    edge_sums = jnp.zeros((4, 128), F32)
    for n, (msg, own, ext, edge, y) in enumerate(
        ((y_lo, wyl, 256, edge_lo, 0), (y_hi, wyh, 257, edge_hi, 127))
    ):
        for s in range(4):
            edge[8 * s : 8 * s + 1, :] = face_lo[s, y : y + 1, :]
            for x in range(1, 7):
                edge[8 * s + x : 8 * s + x + 1, :] = u1[s, x, y : y + 1, :]
            edge[8 * s + 7 : 8 * s + 8, :] = face_hi[s, y : y + 1, :]
        there = msg[32:40, :]
        beyond = face(there, msg[40:48, :])
        along_x = line_weight(there, 0)
        x_rows = iota((8, 256), 0)
        diag = both_sides(along_x, 0) + both_sides(line_weight(there, 1), 1) + own[...] + beyond
        diag = diag + jnp.where(x_rows == 0, face(there[0:1], x_lo[ext : ext + 1, :]), 0.0)
        diag = diag + jnp.where(x_rows == 7, face(there[7:8], x_hi[ext : ext + 1, :]), 0.0)
        diag = diag + zeta_t[8 * n : 8 * n + 8, 2:3]
        factor = OMEGA * own[...] / jnp.maximum(diag, TINY)
        lined = []
        for s in range(4):
            line = to_lanes(jnp.sum(factor * edge[8 * s : 8 * s + 8, :], axis=1, keepdims=True))
            lined.append(pltpu.roll(line, 8 * n, 1) if n else line)
        edge_sums = edge_sums + jnp.concatenate(lined, axis=0)

    own_sums = {}
    for n, (x, below, at, above, w_below, w_above, g) in enumerate(
        (
            (0, None, lambda s: face_lo[s], lambda s: u1[s, 1], None, 0, gain_out[0]),
            (1, lambda s: face_lo[s], lambda s: u1[s, 1], lambda s: u1[s, 2], 0, 1, gain[1]),
            (6, lambda s: u1[s, 5], lambda s: u1[s, 6], lambda s: face_hi[s], 5, 6, gain[6]),
            (7, lambda s: u1[s, 6], lambda s: face_hi[s], None, 6, None, gain_out[1]),
        )
    ):
        slabs = []
        for s in range(4):
            new = local_sweep(
                at(s),
                None if below is None else below(s),
                None if above is None else above(s),
                f[n, s],
                None if below is None else wx[w_below],
                None if above is None else wx[w_above],
                wy[x],
                wz[x],
                g,
            )
            u2[s, n] = new
            slabs.append(new)
        own_sums[x] = row_sums(slabs)
    for x in range(2, 6):
        own_sums[x] = sums[x - 2]
    rows = [own_sums[x] for x in range(8)] + pushed + [edge_sums]

    place = iota((64, 128), 0)
    block_of = 4 * ((place // 8) % 4) + 2 * (place // 32) + (place // 4) % 2
    total = jnp.zeros((192, 128), F32)
    for k, values in enumerate(rows):
        id_row = ids[k : k + 1, :]
        hit = lax.shift_right_logical(id_row, 7) == block_of
        spread = jnp.where(hit, jnp.concatenate([values] * 16, axis=0), 0.0)
        lane_hit = lax.bitwise_and(id_row, 127) == iota((128, 128), 0)
        onehot = jnp.where(lane_hit, 1.0, 0.0).astype(jnp.bfloat16)
        a = spread.astype(jnp.bfloat16)
        spread = spread - a.astype(F32)
        b = spread.astype(jnp.bfloat16)
        spread = spread - b.astype(F32)
        parts = jnp.concatenate([a, b, spread.astype(jnp.bfloat16)], axis=0)
        total = total + lax.dot_general(parts, onehot, NT, preferred_element_type=F32)
    contact = (total[0:64] + total[64:128] + total[128:192]) * (1.0 / 256.0)
    first_half = core[0] == 0
    mine[...] = jnp.where(first_half, contact[0:32], contact[32:64])
    other[...] = jnp.where(first_half, contact[32:64], contact[0:32])


def outer(core, u, f, c, cmap, admittance, y_lo, y_hi, x_lo, x_hi, uh_lo, uh_hi, u1, wx, wy, wz, gain, wyl, wyh, sums):
    outs = [
        kept(4, 128, 256), kept(4, 128, 256), kept(32, 256), kept(32, 256),
        kept(4, 4, 128, 256), kept(2, 128, 256), kept(2, 128, 256), f32(32, 128), f32(32, 128),
    ]
    return pl.pallas_call(
        outer_kernel,
        in_specs=[smem()] + [hbm()] * 3 + [vmem()] * 16,
        out_specs=[vmem()] * len(outs),
        out_shape=outs,
        scratch_shapes=[
            pltpu.VMEM((4, 4, 128, 256), F32),
            pltpu.VMEM((4, 4, 128, 256), F32),
            pltpu.VMEM((2, 128, 256), F32),
            pltpu.VMEM((16, 128), jnp.int32),
            pltpu.SemaphoreType.DMA((3, 4)),
        ],
        compiler_params=params(),
        cost_estimate=pl.CostEstimate(flops=50_000_000, bytes_accessed=15_000_000, transcendentals=0),
        name="outer",
    )(core, u, f, c, cmap, admittance, y_lo, y_hi, x_lo, x_hi, uh_lo, uh_hi, u1, wx, wy, wz, gain, wyl, wyh, sums)


def spread_kernel(mine, got, out):
    both = mine[...] + got[...]
    for n in range(out.shape[0]):
        out[n] = both


def spread(mine, got, count):
    return pl.pallas_call(
        spread_kernel,
        in_specs=[vmem()] * 2,
        out_specs=vmem(),
        out_shape=f32(count, 32, 128),
        compiler_params=params(),
        name="spread",
    )(mine, got)


def gathered_kernel(parts, out):
    out[...] = jnp.sum(parts[...], axis=0)


def gathered(parts):
    return pl.pallas_call(
        gathered_kernel,
        in_specs=[vmem()],
        out_specs=vmem(),
        out_shape=f32(32, 128),
        compiler_params=params(),
        name="gathered",
    )(parts)


def blocks_kernel(place, pairs, amplitudes, a0, a1, a2, a3, i0, i1, i2, i3, out, charges):
    core, elec = place[0], place[1]
    row = iota((32, 128), 0)
    electrode = (4 * (row // 8) + 2 * core + (row // 4) % 2) * 128 + iota((32, 128), 1)
    total = a0[...] + a1[...] + a2[...] + a3[...]
    for s in range(4):
        at = row % 4 == s
        amount = amplitudes[s]
        total = total + jnp.where(at & (electrode == pairs[s, 0]), amount, 0.0)
        total = total - jnp.where(at & (electrode == pairs[s, 1]), amount, 0.0)
    for e in range(4):
        charges[e] = total[8 * e : 8 * e + 8]
    upper = iota((8, 128), 0) < 4
    for turn, blocks in ((0, i0), (3, i1), (1, i2), (2, i3)):
        e = lax.rem(elec + turn, 4)
        charge = charges[e]
        first = lax.dot_general(charge, blocks[0], NT, precision=EXACT, preferred_element_type=F32)
        second = lax.dot_general(charge, blocks[1], NT, precision=EXACT, preferred_element_type=F32)
        out[e] = jnp.where(upper, first, second)


def blocks(place, pairs, amplitudes, parts, impedances):
    return pl.pallas_call(
        blocks_kernel,
        in_specs=[smem()] * 3 + [vmem()] * 8,
        out_specs=vmem(),
        out_shape=f32(4, 8, 128),
        scratch_shapes=[pltpu.VMEM((4, 8, 128), F32)],
        compiler_params=params(),
        name="blocks",
    )(place, pairs, amplitudes, *parts, *impedances)


def correct_kernel(
    place, cmap, own, got, u2a, u2b, gain, gain_b, wxf, wyl, wyh, zeta_t, uh_lo, uh_hi, e_lo, e_hi,
    out_hbm, volts, table, buf, sems,
):
    core, elec = place[0], place[1]
    table[core] = own[...]
    table[1 - core] = got[...]
    for h in range(2):
        for j in range(2):
            volts[:, 128 * (2 * h + j) : 128 * (2 * h + j) + 128] = table[h, elec, 4 * j : 4 * j + 4, :]
    ids = cmap[...]
    block = lax.shift_right_logical(ids, 7)
    lane = lax.bitwise_and(ids, 127)
    touched = []
    for s in range(4):
        found = jnp.zeros((8, 128), F32)
        for b in range(16):
            e, h, j = b // 4, (b // 2) % 2, b % 2
            row = jnp.broadcast_to(table[h, e, 4 * j + s : 4 * j + s + 1, :], (8, 128))
            found = jnp.where(block == b, jnp.take_along_axis(row, lane, axis=1), found)
        touched.append(found)
    stacked = jnp.concatenate(touched + [jnp.zeros((96, 128), F32)], axis=0)
    volts_t = jnp.transpose(stacked)
    copies = []
    for x in (2, 3, 4, 5, 1, 6, 0, 7):
        if x in (0, 7):
            g = gain_b[x // 7]
        else:
            g = gain[x]
        pull = (1.0 / OMEGA) * zeta_t[:, x : x + 1] * g
        for s in range(4):
            if 2 <= x <= 5:
                u = u2a[s, x - 2]
            else:
                u = u2b[s, {0: 0, 1: 1, 6: 2, 7: 3}[x]]
            if x == 0:
                u = u + g * wxf[0] * uh_lo[s]
            if x == 7:
                u = u + g * wxf[1] * uh_hi[s]
            buf[s, x] = u
            buf[s, x, 0:1, :] = u[0:1] + g[0:1] * wyl[x : x + 1, :] * e_lo[8 * s + x : 8 * s + x + 1, :]
            buf[s, x, 127:128, :] = u[127:128] + g[127:128] * wyh[x : x + 1, :] * e_hi[8 * s + x : 8 * s + x + 1, :]
            u = buf[s, x]
            buf[s, x] = u + pull * (volts_t[:, 8 * s + x : 8 * s + x + 1] - u)
        copy = pltpu.make_async_copy(buf.at[:, x], out_hbm.at[:, x], sems.at[x])
        copy.start()
        copies.append(copy)
    for copy in copies:
        copy.wait()


def correct(place, cmap, own, got, u2a, u2b, gain, gain_b, wxf, wyl, wyh, zeta_t, uh_lo, uh_hi, e_lo, e_hi):
    return pl.pallas_call(
        correct_kernel,
        in_specs=[smem()] + [vmem()] * 15,
        out_specs=[hbm(), vmem()],
        out_shape=[f32(4, 8, 128, 256), f32(4, 512)],
        scratch_shapes=[
            pltpu.VMEM((2, 4, 8, 128), F32),
            pltpu.VMEM((4, 8, 128, 256), F32),
            pltpu.SemaphoreType.DMA((8,)),
        ],
        compiler_params=params(),
        name="correct",
    )(place, cmap, own, got, u2a, u2b, gain, gain_b, wxf, wyl, wyh, zeta_t, uh_lo, uh_hi, e_lo, e_hi)


def per_device(u, f, c, cmap, admittance, impedance, pairs, amplitudes):
    tiles = lax.axis_size(TILE)
    groups = lax.axis_size("zx")
    elecs = lax.axis_size("elec")
    core = lax.axis_index("core")
    elec = lax.axis_index("elec")
    place = jnp.stack([core, elec]).astype(jnp.int32)
    admittance = admittance.reshape(16, 128)

    def from_below(a, axis, count):
        return lax.ppermute(a, axis, [(i, i + 1) for i in range(count - 1)])

    def from_above(a, axis, count):
        return lax.ppermute(a, axis, [(i + 1, i) for i in range(count - 1)])

    def rotated(a, turn):
        return lax.ppermute(a, "elec", [(i, (i + turn) % elecs) for i in range(elecs)])

    def swapped(a):
        return lax.ppermute(a, "core", [(0, 1), (1, 0)])

    def around(a):
        return [a, rotated(a, 1), rotated(a, elecs - 1), rotated(a, 2)]

    own_lo, own_hi = edges(u, c, cmap)
    y_lo = from_below(own_hi, "elec", elecs)
    y_hi = from_above(own_lo, "elec", elecs)
    uh_lo = from_below(u[:, 7], TILE, tiles)
    uh_hi = from_above(u[:, 0], TILE, tiles)
    down, up = faces(c, cmap, y_lo, y_hi)
    x_lo = from_below(up, TILE, tiles)
    x_hi = from_above(down, TILE, tiles)
    impedances = around(lax.dynamic_slice_in_dim(impedance, 2 * core, 2, axis=0))

    u1, u2a, wx, wy, wz, gain, wyl, wyh, zeta_t, sums = inner(u, f, c, cmap, admittance, y_lo, y_hi)
    face_lo, face_hi, edge_lo, edge_hi, u2b, gain_b, wxf, mine, other = outer(
        place, u, f, c, cmap, admittance, y_lo, y_hi, x_lo, x_hi, uh_lo, uh_hi,
        u1, wx, wy, wz, gain, wyl, wyh, sums,
    )
    parts = spread(mine, swapped(other), groups)
    parts = lax.all_to_all(parts, "zx", 0, 0, tiled=True)
    summed = gathered(parts)
    h_lo = from_below(face_hi, TILE, tiles)
    h_hi = from_above(face_lo, TILE, tiles)
    e_lo = from_below(edge_hi, "elec", elecs)
    e_hi = from_above(edge_lo, "elec", elecs)
    own = blocks(place, pairs, amplitudes, around(summed), impedances)
    got = swapped(own)
    out, volts = correct(
        place, cmap, own, got, u2a, u2b, gain, gain_b, wxf, wyl, wyh, zeta_t, h_lo, h_hi, e_lo, e_hi
    )
    return out, volts


def solution(mesh):
    tile, src, elec = mesh.devices.shape
    cut = Mesh(mesh.devices.reshape(tile // 2, 2, src, elec), ("zx", "core", "src", "elec"))
    placed = (
        P("src", TILE, "elec", None),
        P("src", TILE, "elec", None),
        P(TILE, "elec", None),
        P(TILE, "elec"),
        P(),
        P("elec", None, None),
        P("src", None),
        P("src"),
    )
    return jax.shard_map(
        per_device,
        mesh=cut,
        in_specs=placed,
        out_specs=(P("src", TILE, "elec", None), P("src", "elec")),
        check_vma=False,
    )
```

time: 265 us -> 118 us (0.45); the launches traced: 260 us -> 117 us
  blocking collectives: 77.1 us -> 0 us
  other arithmetic: 61.5 us -> 0.08 us
  waiting for transfers between devices: 45 us -> 8.33 us
  Pallas kernels: 0 us -> 23.1 us
  starting transfers between devices: 38.7 us -> 58.4 us
  local copies, waits for them, and re-layouts: 7.65 us -> 25.7 us
  matrix products: 16 us -> 0 us
  between operations: 14.4 us -> 1.07 us
    psum x1 -> x0, blocking collectives: 68 us -> none  [per_device(): summed = lax.psum(partial_value, 'tile')]
    unnamed x2 -> x0, waiting for transfers between devices: 31.4 us -> none
    add x4 -> x0, other arithmetic: 25.7 us -> none  [the longest x1 18.1 us: relax_once(): current + OMEGA * (source_term - diagonal * current + pulled) / diagonal]
    pallas_call x0 -> x8, Pallas kernels: none -> 23.1 us  [the longest x1 9.02 us: inner(): pl.pallas_call(inner_kernel, in_specs=[hbm()] * 3 + [vmem()] * 4, out_spe...]
    unnamed x32 -> x49, local copies, waits for them, and re-layouts: 3.92 us -> 23.3 us
    reduce_sum x1 -> x0, other arithmetic: 18.6 us -> none  [per_device(): row_means = jnp.mean(current, axis=-1).reshape(sources, row_count)]
    concatenate x3 -> x0, other arithmetic: 15.3 us -> none  [extended(): jnp.concatenate([lax.ppermute(tail, axis, [(i, (i + 1) % count) for i in...]
    all_to_all x0 -> x1, starting transfers between devices: none -> 12.8 us  [per_device(): parts = lax.all_to_all(parts, 'zx', 0, 0, tiled=True)]
  transfers between devices with their start and end apart: 13 -> 19, of which waited for: 5 -> 6; matrix products, arithmetic and copies ran while one was open for 4% -> 1% of each run, Pallas kernels for 0% -> 10%
where the time goes in v1:
time: 118 us; the launch traced here: 117 us
  starting transfers between devices  58.4 us (49%)
  local copies, waits for them, and re-layouts  25.7 us (22%)
  Pallas kernels  23.1 us (20%)
  waiting for transfers between devices  8.33 us (7%)
    unnamed x49, local copies, waits for them, and re-layouts  23.3 us
    ppermute x5, starting transfers between devices, from_below(): return lax.ppermute(a, axis, [(i, i + 1) for i in range(count - 1)])  22.9 us
    all_to_all x1, starting transfers between devices, per_device(): parts = lax.all_to_all(parts, 'zx', 0, 0, tiled=True)  12.8 us
    ppermute x6, starting transfers between devices, rotated(): lax.ppermute(a, 'elec', [(i, (i + turn) % elecs) for i in range(elecs)])  10.8 us
    pallas_call x1, Pallas kernels, inner(): pl.pallas_call(inner_kernel, in_specs=[hbm()] * 3 + [vmem()] * 4, out_spe...  9.02 us
    ppermute x5, starting transfers between devices, from_above(): return lax.ppermute(a, axis, [(i + 1, i) for i in range(count - 1)])  8.35 us
    pallas_call x1, Pallas kernels, outer(): pl.pallas_call(outer_kernel, in_specs=[smem()] + [hbm()] * 3 + [vmem()] *...  7.33 us
    ppermute x5, waiting for transfers between devices, from_above(): return lax.ppermute(a, axis, [(i + 1, i) for i in range(count - 1)])  3.62 us
  transfers between devices with their start and end apart: 19, of which 6 were waited for; matrix products, arithmetic and copies ran while one was open for 1% of the time, Pallas kernels for 10%

profile of v1, /device:TPU:1, one launch (start us, length us, event | category | flops | bytes accessed | tf_op | source)
XLA Modules:
  0.0 116.6 jit_solution(4725314945185711842)
XLA Ops:
  0.6 0.0 copy-start
  0.6 2.3 %slice_bitcast_fusion = (f32[4,128,256]{2,1,0:T(8,128)}, f32[4,128,256]{2,1,0:T(8,128)}) fusion(f32[4,8,128,256]{3,2,1,0:T(8,128)} %u_hbm.3), kind=kLoop, calls=%fused_computation | loop fusion | bytes 2097152 | tf_op jit(solution)/shard_map/squeeze | solution.py:571
  3.0 6.0 %collective-permute-start.4 = (f32[4,128,256]{2,1,0:T(8,128)}, f32[4,128,256]{2,1,0:T(8,128)S(1)}, u32[]{:S(2)}, u32[]{:S(2)}) collective-permute-start(f32[4,128,256]{2,1,0:T(8,128)} %get-tuple-element.49), channel_id=1, source_target_pairs={{0,8},{8,16},{16,24},{24,32},{32,40},{40,48},{48,56},{56,64},{64,7... | collective-permute-start | bytes 1572872 | tf_op jit(solution)/shard_map/ppermute | solution.py:553
  9.0 1.9 %collective-permute-start.5 = (f32[4,128,256]{2,1,0:T(8,128)}, f32[4,128,256]{2,1,0:T(8,128)S(1)}, u32[]{:S(2)}, u32[]{:S(2)}) collective-permute-start(f32[4,128,256]{2,1,0:T(8,128)} %get-tuple-element.48), channel_id=1, source_target_pairs={{8,0},{16,8},{24,16},{32,24},{40,32},{48,40},{56,48},{64,56},{72,6... | collective-permute-start | bytes 1572872 | tf_op jit(solution)/shard_map/ppermute | solution.py:556
  10.9 0.0 copy-start.1
  10.9 2.2 %copy-done.1 = f32[4,8,128,256]{3,2,1,0:T(8,128)S(1)} copy-done((f32[4,8,128,256]{3,2,1,0:T(8,128)S(1)}, f32[4,8,128,256]{3,2,1,0:T(8,128)}, u32[]{:S(2)}) %copy-start.1) | copy-done | bytes 4194328
  13.1 1.2 %copy-done.3 = f32[8,128,256]{2,1,0:T(8,128)S(1)} copy-done((f32[8,128,256]{2,1,0:T(8,128)S(1)}, f32[8,128,256]{2,1,0:T(8,128)}, u32[]{:S(2)}) %copy-start.3) | copy-done | bytes 1048600
  14.4 0.7 copy-done.14
  15.0 0.1 edges.1
  15.1 0.0 copy-start.4
  15.2 0.0 copy-start.15
  15.2 0.0 copy-start.18
  15.2 3.3 %collective-permute-start = (f32[56,256]{1,0:T(8,128)S(1)}, f32[56,256]{1,0:T(8,128)S(1)}, u32[]{:S(2)}, u32[]{:S(2)}) collective-permute-start(f32[56,256]{1,0:T(8,128)S(1)} %get-tuple-element.25), channel_id=1, source_target_pairs={{0,1},{1,2},{2,3},{4,5},{5,6},{6,7},{8,9},{9,10},{10,11},{12,13},{... | collective-permute-start | bytes 172040 | tf_op jit(solution)/shard_map/ppermute | solution.py:553
  18.5 1.3 %collective-permute-start.1 = (f32[56,256]{1,0:T(8,128)S(1)}, f32[56,256]{1,0:T(8,128)S(1)}, u32[]{:S(2)}, u32[]{:S(2)}) collective-permute-start(f32[56,256]{1,0:T(8,128)S(1)} %get-tuple-element.26), channel_id=1, source_target_pairs={{1,0},{2,1},{3,2},{5,4},{6,5},{7,6},{9,8},{10,9},{11,10},{13,12},{... | collective-permute-start | bytes 172040 | tf_op jit(solution)/shard_map/ppermute | solution.py:556
  19.8 0.0 collective-permute-done.y_lo
  19.8 3.6 %collective-permute-done.1.y_hi = f32[56,256]{1,0:T(8,128)S(1)} collective-permute-done((f32[56,256]{1,0:T(8,128)S(1)}, f32[56,256]{1,0:T(8,128)S(1)}, u32[]{:S(2)}, u32[]{:S(2)}) %collective-permute-start.1) | collective-permute-done | bytes 57376 | tf_op jit(solution)/shard_map/ppermute | solution.py:556
  23.4 0.8 faces.1
  24.3 6.6 %collective-permute-start.2 = (f32[272,256]{1,0:T(8,128)}, f32[272,256]{1,0:T(8,128)}, u32[]{:S(2)}, u32[]{:S(2)}) collective-permute-start(f32[272,256]{1,0:T(8,128)} %get-tuple-element.27), channel_id=1, source_target_pairs={{0,8},{8,16},{16,24},{24,32},{32,40},{40,48},{48,56},{56,64},{64,7... | collective-permute-start | bytes 835592 | tf_op jit(solution)/shard_map/ppermute | solution.py:553
  30.9 1.9 %collective-permute-start.3 = (f32[272,256]{1,0:T(8,128)}, f32[272,256]{1,0:T(8,128)}, u32[]{:S(2)}, u32[]{:S(2)}) collective-permute-start(f32[272,256]{1,0:T(8,128)} %get-tuple-element.28), channel_id=1, source_target_pairs={{8,0},{16,8},{24,16},{32,24},{40,32},{48,40},{56,48},{64,56},{72,6... | collective-permute-start | bytes 835592 | tf_op jit(solution)/shard_map/ppermute | solution.py:556
  32.8 0.1 pad_add_fusion.core.place
  32.9 2.2 %copy-done.2 = f32[4,8,128,256]{3,2,1,0:T(8,128)S(1)} copy-done((f32[4,8,128,256]{3,2,1,0:T(8,128)S(1)}, f32[4,8,128,256]{3,2,1,0:T(8,128)}, u32[]{:S(2)}) %copy-start.2) | copy-done | bytes 4194328
  35.1 2.2 %copy-done.5 = f32[4,8,128,256]{3,2,1,0:T(8,128)S(1)} copy-done((f32[4,8,128,256]{3,2,1,0:T(8,128)S(1)}, f32[4,8,128,256]{3,2,1,0:T(8,128)}, u32[]{:S(2)}) %copy-start.5) | copy-done | bytes 4194328
  37.3 9.0 %inner.1 = (f32[4,8,128,256]{3,2,1,0:T(8,128)S(1)}, f32[4,4,128,256]{3,2,1,0:T(8,128)S(1)}, f32[7,128,256]{2,1,0:T(8,128)S(1)}, f32[8,128,256]{2,1,0:T(8,128)S(1...) custom-call(f32[4,8,128,256]{3,2,1,0:T(8,128)S(1)} %copy-done.2, ...), custom_call_target="tpu_custom_call" | custom-call | flops 100000000 | bytes 30000000 | tf_op jit(solution)/shard_map/inner/pallas_call | solution.py:240
  46.3 0.0 copy-start.6
  46.3 1.3 %copy-done.6 = f32[4,4,128,256]{3,2,1,0:T(8,128)} copy-done((f32[4,4,128,256]{3,2,1,0:T(8,128)}, f32[4,4,128,256]{3,2,1,0:T(8,128)S(1)}, u32[]{:S(2)}) %copy-start.6) | copy-done | bytes 2097176
  47.6 0.6 copy-done.16
  48.2 0.0 collective-permute-done.2.x_lo
  48.2 0.0 collective-permute-done.3.x_hi
  48.2 0.0 collective-permute-done.4.uh_lo
  48.3 7.3 %outer.1 = (f32[4,128,256]{2,1,0:T(8,128)S(1)}, f32[4,128,256]{2,1,0:T(8,128)S(1)}, f32[32,256]{1,0:T(8,128)S(1)}, f32[32,256]{1,0:T(8,128)S(1)}, f32[4,4,128,25...) custom-call(s32[2]{0:T(128)S(1)} %pad_add_fusion.core.place, ...), custom_call_target="tpu_custom_call" | custom-call | flops 50000000 | bytes 15000000 | tf_op jit(solution)/shard_map/outer/pallas_call | solution.py:393
  55.6 1.3 %copy-done.8 = f32[4,4,128,256]{3,2,1,0:T(8,128)} copy-done((f32[4,4,128,256]{3,2,1,0:T(8,128)}, f32[4,4,128,256]{3,2,1,0:T(8,128)S(1)}, u32[]{:S(2)}) %copy-start.8) | copy-done | bytes 2097176
  56.9 0.7 copy-done.10
  57.6 0.7 copy-done.12
  58.3 0.8 copy-done.20
  59.1 0.8 copy-done.21
  59.9 0.6 copy-done.22
  60.5 0.6 copy-done.23
  61.2 1.2 %collective-permute-done.6.got = f32[32,128]{1,0:T(8,128)S(1)} collective-permute-done((f32[32,128]{1,0:T(8,128)S(1)}, f32[32,128]{1,0:T(8,128)S(1)}, u32[]{:S(2)}, u32[]{:S(2)}) %collective-permute-start.6) | collective-permute-done | bytes 16416 | tf_op jit(solution)/shard_map/ppermute | solution.py:562
  62.3 0.7 spread.1
  63.1 12.8 %all-to-all-start = ((f32[16,32,128]{2,1,0:T(8,128)}), f32[16,32,128]{2,1,0:T(8,128)S(1)}, u32[]{:S(2)}, u32[]{:S(2)}) async-start(f32[16,32,128]{2,1,0:T(8,128)} %spread.1), calls=%async_computation | async-start | bytes 524288 | tf_op jit(solution)/shard_map/all_to_all | solution.py:583
  75.9 5.6 %collective-permute-start.14 = (f32[4,128,256]{2,1,0:T(8,128)}, f32[4,128,256]{2,1,0:T(8,128)S(1)}, u32[]{:S(2)}, u32[]{:S(2)}) collective-permute-start(f32[4,128,256]{2,1,0:T(8,128)} %copy-done.21), channel_id=1, source_target_pairs={{0,8},{8,16},{16,24},{24,32},{32,40},{40,48},{48,56},{56,64},{64,7... | collective-permute-start | bytes 1572872 | tf_op jit(solution)/shard_map/ppermute | solution.py:553
  81.4 1.9 %collective-permute-start.15 = (f32[4,128,256]{2,1,0:T(8,128)}, f32[4,128,256]{2,1,0:T(8,128)S(1)}, u32[]{:S(2)}, u32[]{:S(2)}) collective-permute-start(f32[4,128,256]{2,1,0:T(8,128)} %copy-done.20), channel_id=1, source_target_pairs={{8,0},{16,8},{24,16},{32,24},{40,32},{48,40},{56,48},{64,56},{72,6... | collective-permute-start | bytes 1572872 | tf_op jit(solution)/shard_map/ppermute | solution.py:556
  83.4 1.4 %collective-permute-start.10 = (f32[2,128,128]{2,1,0:T(8,128)S(1)}, f32[2,128,128]{2,1,0:T(8,128)S(1)}, u32[]{:S(2)}, u32[]{:S(2)}) collective-permute-start(f32[2,128,128]{2,1,0:T(8,128)S(1)} %constant_dynamic-slice_fusion.i0), channel_id=1, source_target_pairs={{0,1},{1,2},{2,3},{3,0},{4,5},{5,6},{6,7},{7,4},{8,9},{9,10},{10,1... | collective-permute-start | bytes 393224 | tf_op jit(solution)/shard_map/ppermute | solution.py:559
  84.8 1.4 %collective-permute-start.11 = (f32[2,128,128]{2,1,0:T(8,128)S(1)}, f32[2,128,128]{2,1,0:T(8,128)S(1)}, u32[]{:S(2)}, u32[]{:S(2)}) collective-permute-start(f32[2,128,128]{2,1,0:T(8,128)S(1)} %constant_dynamic-slice_fusion.i0), channel_id=1, source_target_pairs={{0,3},{1,0},{2,1},{3,2},{4,7},{5,4},{6,5},{7,6},{8,11},{9,8},{10,9... | collective-permute-start | bytes 393224 | tf_op jit(solution)/shard_map/ppermute | solution.py:559
  86.1 1.4 %collective-permute-start.12 = (f32[2,128,128]{2,1,0:T(8,128)S(1)}, f32[2,128,128]{2,1,0:T(8,128)S(1)}, u32[]{:S(2)}, u32[]{:S(2)}) collective-permute-start(f32[2,128,128]{2,1,0:T(8,128)S(1)} %constant_dynamic-slice_fusion.i0), channel_id=1, source_target_pairs={{0,2},{1,3},{2,0},{3,1},{4,6},{5,7},{6,4},{7,5},{8,10},{9,11},{10,... | collective-permute-start | bytes 393224 | tf_op jit(solution)/shard_map/ppermute | solution.py:559
  87.5 0.8 all-to-all-done.parts
  88.4 1.5 %collective-permute-done.10.i1 = f32[2,128,128]{2,1,0:T(8,128)S(1)} collective-permute-done((f32[2,128,128]{2,1,0:T(8,128)S(1)}, f32[2,128,128]{2,1,0:T(8,128)S(1)}, u32[]{:S(2)}, u32[]{:S(2)}) %collective-permute-start.10) | collective-permute-done | bytes 131104 | tf_op jit(solution)/shard_map/ppermute | solution.py:559
  89.9 0.3 collective-permute-start.7
  90.2 2.4 %collective-permute-start.8 = (f32[32,128]{1,0:T(8,128)S(1)}, f32[32,128]{1,0:T(8,128)S(1)}, u32[]{:S(2)}, u32[]{:S(2)}) collective-permute-start(f32[32,128]{1,0:T(8,128)S(1)} %gathered.1.a0), channel_id=1, source_target_pairs={{0,3},{1,0},{2,1},{3,2},{4,7},{5,4},{6,5},{7,6},{8,11},{9,8},{10,9... | collective-permute-start | bytes 49160 | tf_op jit(solution)/shard_map/ppermute | solution.py:559
  92.6 1.4 %collective-permute-start.16 = (f32[32,256]{1,0:T(8,128)}, f32[32,256]{1,0:T(8,128)S(1)}, u32[]{:S(2)}, u32[]{:S(2)}) collective-permute-start(f32[32,256]{1,0:T(8,128)} %copy-done.23), channel_id=1, source_target_pairs={{0,1},{1,2},{2,3},{4,5},{5,6},{6,7},{8,9},{9,10},{10,11},{12,13},{... | collective-permute-start | bytes 98312 | tf_op jit(solution)/shard_map/ppermute | solution.py:553
  94.0 1.3 %collective-permute-start.17 = (f32[32,256]{1,0:T(8,128)}, f32[32,256]{1,0:T(8,128)S(1)}, u32[]{:S(2)}, u32[]{:S(2)}) collective-permute-start(f32[32,256]{1,0:T(8,128)} %copy-done.22), channel_id=1, source_target_pairs={{1,0},{2,1},{3,2},{5,4},{6,5},{7,6},{9,8},{10,9},{11,10},{13,12},{... | collective-permute-start | bytes 98312 | tf_op jit(solution)/shard_map/ppermute | solution.py:556
  95.3 4.0 %collective-permute-start.9 = (f32[32,128]{1,0:T(8,128)S(1)}, f32[32,128]{1,0:T(8,128)S(1)}, u32[]{:S(2)}, u32[]{:S(2)}) collective-permute-start(f32[32,128]{1,0:T(8,128)S(1)} %gathered.1.a0), channel_id=1, source_target_pairs={{0,2},{1,3},{2,0},{3,1},{4,6},{5,7},{6,4},{7,5},{8,10},{9,11},{10,... | collective-permute-start | bytes 49160 | tf_op jit(solution)/shard_map/ppermute | solution.py:559
  99.2 0.8 copy.12.pairs
  100.0 0.4 collective-permute-done.9.a3
  100.4 0.7 copy-done.19
  101.0 1.5 %blocks.1.own = f32[4,8,128]{2,1,0:T(8,128)S(1)} custom-call(s32[2]{0:T(128)S(1)} %pad_add_fusion.core.place, s32[4,2]{1,0:T(4,128)S(1)} %copy.12.pairs, f32[4]{0:T(128)S(1)} %copy-done.19, f32[32,128]{1,0:T(8,128)S(1)} %gathered.1.a0, f32[32,128]{1,0:T(8,128)S(1)} %collective-permute-done.7.a1, f32[32,128]{1,0:T(8,128)S(1)} %collective-permute-done.8.a2, ...), custom_call_target="tpu_custom_call" | custom-call | tf_op jit(solution)/shard_map/blocks/pallas_call | solution.py:465
  102.5 3.6 %collective-permute-start.13 = (f32[4,8,128]{2,1,0:T(8,128)S(1)}, f32[4,8,128]{2,1,0:T(8,128)S(1)}, u32[]{:S(2)}, u32[]{:S(2)}) collective-permute-start(f32[4,8,128]{2,1,0:T(8,128)S(1)} %blocks.1.own), channel_id=1, source_target_pairs={{0,8},{8,0},{1,9},{9,1},{2,10},{10,2},{3,11},{11,3},{4,12},{12,4},... | collective-permute-start | bytes 49160 | tf_op jit(solution)/shard_map/ppermute | solution.py:562
  106.1 0.8 collective-permute-done.13.got
  106.9 1.6 %copy-done.7 = f32[4,4,128,256]{3,2,1,0:T(8,128)S(1)} copy-done((f32[4,4,128,256]{3,2,1,0:T(8,128)S(1)}, f32[4,4,128,256]{3,2,1,0:T(8,128)}, u32[]{:S(2)}) %copy-start.7) | copy-done | bytes 2097176
  108.5 1.6 %copy-done.9 = f32[4,4,128,256]{3,2,1,0:T(8,128)S(1)} copy-done((f32[4,4,128,256]{3,2,1,0:T(8,128)S(1)}, f32[4,4,128,256]{3,2,1,0:T(8,128)}, u32[]{:S(2)}) %copy-start.9) | copy-done | bytes 2097176
  110.1 0.9 copy-done.11
  111.1 0.9 copy-done.13
  112.0 0.8 copy-done.17
  112.9 3.6 %correct.1 = (f32[4,8,128,256]{3,2,1,0:T(8,128)}, f32[4,512]{1,0:T(4,128)}) custom-call(s32[2]{0:T(128)S(1)} %pad_add_fusion.core.place, s32[8,128]{1,0:T(8,128)S(1)} %copy-done.15, f32[4,8,128]{2,1,0:T(8,128)S(1)} %blocks.1.own, f32[4,8,128]{2,1,0:T(8,128)S(1)} %collective-permute-done.13.got, f32[4,4,128,256]{3,2,1,0:T(8,128)S(1)} %copy-done.7, ...), custom_call_target="tpu_custom_call" | custom-call | tf_op jit(solution)/shard_map/correct/pallas_call | solution.py:528
  (34 shorter events, 0.1 us)
Async XLA Ops:
  0.6 82.7 %copy-start = (f32[4,128,128]{2,1,0:T(8,128)S(1)}, f32[4,128,128]{2,1,0:T(8,128)}, u32[]{:S(2)}) copy-start(f32[4,128,128]{2,1,0:T(8,128)} %param.13) | copy-start | bytes 786436
  3.0 45.3 %collective-permute-start.4 = (f32[4,128,256]{2,1,0:T(8,128)}, f32[4,128,256]{2,1,0:T(8,128)S(1)}, u32[]{:S(2)}, u32[]{:S(2)}) collective-permute-start(f32[4,128,256]{2,1,0:T(8,128)} %get-tuple-element.49), channel_id=1, source_target_pairs={{0,8},{8,16},{16,24},{24,32},{32,40},{40,48},{48,56},{56,64},{64,7... | collective-permute-start | bytes 1572872 | tf_op jit(solution)/shard_map/ppermute | solution.py:553
  9.0 39.2 %collective-permute-start.5 = (f32[4,128,256]{2,1,0:T(8,128)}, f32[4,128,256]{2,1,0:T(8,128)S(1)}, u32[]{:S(2)}, u32[]{:S(2)}) collective-permute-start(f32[4,128,256]{2,1,0:T(8,128)} %get-tuple-element.48), channel_id=1, source_target_pairs={{8,0},{16,8},{24,16},{32,24},{40,32},{48,40},{56,48},{64,56},{72,6... | collective-permute-start | bytes 1572872 | tf_op jit(solution)/shard_map/ppermute | solution.py:556
  10.9 2.2 %copy-start.1 = (f32[4,8,128,256]{3,2,1,0:T(8,128)S(1)}, f32[4,8,128,256]{3,2,1,0:T(8,128)}, u32[]{:S(2)}) copy-start(f32[4,8,128,256]{3,2,1,0:T(8,128)} %u_hbm.3) | copy-start | bytes 12582916
  13.1 1.2 %copy-start.3 = (f32[8,128,256]{2,1,0:T(8,128)S(1)}, f32[8,128,256]{2,1,0:T(8,128)}, u32[]{:S(2)}) copy-start(f32[8,128,256]{2,1,0:T(8,128)} %c_hbm.3) | copy-start | bytes 3145732
  14.4 0.7 copy-start.14
  15.1 17.7 %copy-start.4 = (f32[8,128,256]{2,1,0:T(8,128)S(1)}, f32[8,128,256]{2,1,0:T(8,128)}, u32[]{:S(2)}) copy-start(f32[8,128,256]{2,1,0:T(8,128)} %c_hbm.3) | copy-start | bytes 3145732
  15.2 17.7 %copy-start.15 = (s32[8,128]{1,0:T(8,128)S(1)}, s32[8,128]{1,0:T(8,128)}, u32[]{:S(2)}) copy-start(s32[8,128]{1,0:T(8,128)} %cmap.9) | copy-start | bytes 12292
  15.2 17.7 %copy-start.18 = (f32[2048]{0:T(1024)S(1)}, f32[2048]{0:T(1024)}, u32[]{:S(2)}) copy-start(f32[2048]{0:T(1024)} %param.12) | copy-start | bytes 24580
  15.2 4.6 %collective-permute-start = (f32[56,256]{1,0:T(8,128)S(1)}, f32[56,256]{1,0:T(8,128)S(1)}, u32[]{:S(2)}, u32[]{:S(2)}) collective-permute-start(f32[56,256]{1,0:T(8,128)S(1)} %get-tuple-element.25), channel_id=1, source_target_pairs={{0,1},{1,2},{2,3},{4,5},{5,6},{6,7},{8,9},{9,10},{10,11},{12,13},{... | collective-permute-start | bytes 172040 | tf_op jit(solution)/shard_map/ppermute | solution.py:553
  18.5 4.9 %collective-permute-start.1 = (f32[56,256]{1,0:T(8,128)S(1)}, f32[56,256]{1,0:T(8,128)S(1)}, u32[]{:S(2)}, u32[]{:S(2)}) collective-permute-start(f32[56,256]{1,0:T(8,128)S(1)} %get-tuple-element.26), channel_id=1, source_target_pairs={{1,0},{2,1},{3,2},{5,4},{6,5},{7,6},{9,8},{10,9},{11,10},{13,12},{... | collective-permute-start | bytes 172040 | tf_op jit(solution)/shard_map/ppermute | solution.py:556
  24.3 24.0 %collective-permute-start.2 = (f32[272,256]{1,0:T(8,128)}, f32[272,256]{1,0:T(8,128)}, u32[]{:S(2)}, u32[]{:S(2)}) collective-permute-start(f32[272,256]{1,0:T(8,128)} %get-tuple-element.27), channel_id=1, source_target_pairs={{0,8},{8,16},{16,24},{24,32},{32,40},{40,48},{48,56},{56,64},{64,7... | collective-permute-start | bytes 835592 | tf_op jit(solution)/shard_map/ppermute | solution.py:553
  30.9 17.4 %collective-permute-start.3 = (f32[272,256]{1,0:T(8,128)}, f32[272,256]{1,0:T(8,128)}, u32[]{:S(2)}, u32[]{:S(2)}) collective-permute-start(f32[272,256]{1,0:T(8,128)} %get-tuple-element.28), channel_id=1, source_target_pairs={{8,0},{16,8},{24,16},{32,24},{40,32},{48,40},{56,48},{64,56},{72,6... | collective-permute-start | bytes 835592 | tf_op jit(solution)/shard_map/ppermute | solution.py:556
  32.9 2.2 %copy-start.2 = (f32[4,8,128,256]{3,2,1,0:T(8,128)S(1)}, f32[4,8,128,256]{3,2,1,0:T(8,128)}, u32[]{:S(2)}) copy-start(f32[4,8,128,256]{3,2,1,0:T(8,128)} %u_hbm.3) | copy-start | bytes 12582916
  35.1 2.2 %copy-start.5 = (f32[4,8,128,256]{3,2,1,0:T(8,128)S(1)}, f32[4,8,128,256]{3,2,1,0:T(8,128)}, u32[]{:S(2)}) copy-start(f32[4,8,128,256]{3,2,1,0:T(8,128)} %f_hbm.3) | copy-start | bytes 12582916
  46.3 1.3 %copy-start.6 = (f32[4,4,128,256]{3,2,1,0:T(8,128)}, f32[4,4,128,256]{3,2,1,0:T(8,128)S(1)}, u32[]{:S(2)}) copy-start(f32[4,4,128,256]{3,2,1,0:T(8,128)S(1)} %get-tuple-element.39.u2a) | copy-start | bytes 6291460
  47.6 0.6 copy-start.16
  55.6 1.3 %copy-start.8 = (f32[4,4,128,256]{3,2,1,0:T(8,128)}, f32[4,4,128,256]{3,2,1,0:T(8,128)S(1)}, u32[]{:S(2)}) copy-start(f32[4,4,128,256]{3,2,1,0:T(8,128)S(1)} %get-tuple-element.40.u2b) | copy-start | bytes 6291460
  56.9 0.7 copy-start.10
  57.6 0.7 copy-start.12
  58.3 0.8 copy-start.20
  59.1 0.8 copy-start.21
  59.9 0.6 copy-start.22
  60.5 0.6 copy-start.23
  61.2 1.2 %collective-permute-start.6 = (f32[32,128]{1,0:T(8,128)S(1)}, f32[32,128]{1,0:T(8,128)S(1)}, u32[]{:S(2)}, u32[]{:S(2)}) collective-permute-start(f32[32,128]{1,0:T(8,128)S(1)} %get-tuple-element.38), channel_id=1, source_target_pairs={{0,8},{8,0},{1,9},{9,1},{2,10},{10,2},{3,11},{11,3},{4,12},{12,4},... | collective-permute-start | bytes 49160 | tf_op jit(solution)/shard_map/ppermute | solution.py:562
  63.1 25.3 %all-to-all-start = ((f32[16,32,128]{2,1,0:T(8,128)}), f32[16,32,128]{2,1,0:T(8,128)S(1)}, u32[]{:S(2)}, u32[]{:S(2)}) async-start(f32[16,32,128]{2,1,0:T(8,128)} %spread.1), calls=%async_computation | async-start | bytes 524288 | tf_op jit(solution)/shard_map/all_to_all | solution.py:583
  75.9 30.3 %collective-permute-start.14 = (f32[4,128,256]{2,1,0:T(8,128)}, f32[4,128,256]{2,1,0:T(8,128)S(1)}, u32[]{:S(2)}, u32[]{:S(2)}) collective-permute-start(f32[4,128,256]{2,1,0:T(8,128)} %copy-done.21), channel_id=1, source_target_pairs={{0,8},{8,16},{16,24},{24,32},{32,40},{40,48},{48,56},{56,64},{64,7... | collective-permute-start | bytes 1572872 | tf_op jit(solution)/shard_map/ppermute | solution.py:553
  81.4 24.7 %collective-permute-start.15 = (f32[4,128,256]{2,1,0:T(8,128)}, f32[4,128,256]{2,1,0:T(8,128)S(1)}, u32[]{:S(2)}, u32[]{:S(2)}) collective-permute-start(f32[4,128,256]{2,1,0:T(8,128)} %copy-done.20), channel_id=1, source_target_pairs={{8,0},{16,8},{24,16},{32,24},{40,32},{48,40},{56,48},{64,56},{72,6... | collective-permute-start | bytes 1572872 | tf_op jit(solution)/shard_map/ppermute | solution.py:556
  83.4 6.5 %collective-permute-start.10 = (f32[2,128,128]{2,1,0:T(8,128)S(1)}, f32[2,128,128]{2,1,0:T(8,128)S(1)}, u32[]{:S(2)}, u32[]{:S(2)}) collective-permute-start(f32[2,128,128]{2,1,0:T(8,128)S(1)} %constant_dynamic-slice_fusion.i0), channel_id=1, source_target_pairs={{0,1},{1,2},{2,3},{3,0},{4,5},{5,6},{6,7},{7,4},{8,9},{9,10},{10,1... | collective-permute-start | bytes 393224 | tf_op jit(solution)/shard_map/ppermute | solution.py:559
  84.8 5.4 %collective-permute-start.11 = (f32[2,128,128]{2,1,0:T(8,128)S(1)}, f32[2,128,128]{2,1,0:T(8,128)S(1)}, u32[]{:S(2)}, u32[]{:S(2)}) collective-permute-start(f32[2,128,128]{2,1,0:T(8,128)S(1)} %constant_dynamic-slice_fusion.i0), channel_id=1, source_target_pairs={{0,3},{1,0},{2,1},{3,2},{4,7},{5,4},{6,5},{7,6},{8,11},{9,8},{10,9... | collective-permute-start | bytes 393224 | tf_op jit(solution)/shard_map/ppermute | solution.py:559
  86.1 6.4 %collective-permute-start.12 = (f32[2,128,128]{2,1,0:T(8,128)S(1)}, f32[2,128,128]{2,1,0:T(8,128)S(1)}, u32[]{:S(2)}, u32[]{:S(2)}) collective-permute-start(f32[2,128,128]{2,1,0:T(8,128)S(1)} %constant_dynamic-slice_fusion.i0), channel_id=1, source_target_pairs={{0,2},{1,3},{2,0},{3,1},{4,6},{5,7},{6,4},{7,5},{8,10},{9,11},{10,... | collective-permute-start | bytes 393224 | tf_op jit(solution)/shard_map/ppermute | solution.py:559
  89.9 4.1 %collective-permute-start.7 = (f32[32,128]{1,0:T(8,128)S(1)}, f32[32,128]{1,0:T(8,128)S(1)}, u32[]{:S(2)}, u32[]{:S(2)}) collective-permute-start(f32[32,128]{1,0:T(8,128)S(1)} %gathered.1.a0), channel_id=1, source_target_pairs={{0,1},{1,2},{2,3},{3,0},{4,5},{5,6},{6,7},{7,4},{8,9},{9,10},{10,1... | collective-permute-start | bytes 49160 | tf_op jit(solution)/shard_map/ppermute | solution.py:559
  90.2 5.1 %collective-permute-start.8 = (f32[32,128]{1,0:T(8,128)S(1)}, f32[32,128]{1,0:T(8,128)S(1)}, u32[]{:S(2)}, u32[]{:S(2)}) collective-permute-start(f32[32,128]{1,0:T(8,128)S(1)} %gathered.1.a0), channel_id=1, source_target_pairs={{0,3},{1,0},{2,1},{3,2},{4,7},{5,4},{6,5},{7,6},{8,11},{9,8},{10,9... | collective-permute-start | bytes 49160 | tf_op jit(solution)/shard_map/ppermute | solution.py:559
  92.6 13.5 %collective-permute-start.16 = (f32[32,256]{1,0:T(8,128)}, f32[32,256]{1,0:T(8,128)S(1)}, u32[]{:S(2)}, u32[]{:S(2)}) collective-permute-start(f32[32,256]{1,0:T(8,128)} %copy-done.23), channel_id=1, source_target_pairs={{0,1},{1,2},{2,3},{4,5},{5,6},{6,7},{8,9},{9,10},{10,11},{12,13},{... | collective-permute-start | bytes 98312 | tf_op jit(solution)/shard_map/ppermute | solution.py:553
  94.0 12.1 %collective-permute-start.17 = (f32[32,256]{1,0:T(8,128)}, f32[32,256]{1,0:T(8,128)S(1)}, u32[]{:S(2)}, u32[]{:S(2)}) collective-permute-start(f32[32,256]{1,0:T(8,128)} %copy-done.22), channel_id=1, source_target_pairs={{1,0},{2,1},{3,2},{5,4},{6,5},{7,6},{9,8},{10,9},{11,10},{13,12},{... | collective-permute-start | bytes 98312 | tf_op jit(solution)/shard_map/ppermute | solution.py:556
  95.3 5.1 %collective-permute-start.9 = (f32[32,128]{1,0:T(8,128)S(1)}, f32[32,128]{1,0:T(8,128)S(1)}, u32[]{:S(2)}, u32[]{:S(2)}) collective-permute-start(f32[32,128]{1,0:T(8,128)S(1)} %gathered.1.a0), channel_id=1, source_target_pairs={{0,2},{1,3},{2,0},{3,1},{4,6},{5,7},{6,4},{7,5},{8,10},{9,11},{10,... | collective-permute-start | bytes 49160 | tf_op jit(solution)/shard_map/ppermute | solution.py:559
  100.4 0.7 copy-start.19
  102.5 4.4 %collective-permute-start.13 = (f32[4,8,128]{2,1,0:T(8,128)S(1)}, f32[4,8,128]{2,1,0:T(8,128)S(1)}, u32[]{:S(2)}, u32[]{:S(2)}) collective-permute-start(f32[4,8,128]{2,1,0:T(8,128)S(1)} %blocks.1.own), channel_id=1, source_target_pairs={{0,8},{8,0},{1,9},{9,1},{2,10},{10,2},{3,11},{11,3},{4,12},{12,4},... | collective-permute-start | bytes 49160 | tf_op jit(solution)/shard_map/ppermute | solution.py:562
  106.9 1.6 %copy-start.7 = (f32[4,4,128,256]{3,2,1,0:T(8,128)S(1)}, f32[4,4,128,256]{3,2,1,0:T(8,128)}, u32[]{:S(2)}) copy-start(f32[4,4,128,256]{3,2,1,0:T(8,128)} %copy-done.6) | copy-start | bytes 6291460
  108.5 1.6 %copy-start.9 = (f32[4,4,128,256]{3,2,1,0:T(8,128)S(1)}, f32[4,4,128,256]{3,2,1,0:T(8,128)}, u32[]{:S(2)}) copy-start(f32[4,4,128,256]{3,2,1,0:T(8,128)} %copy-done.8) | copy-start | bytes 6291460
  110.1 0.9 copy-start.11
  111.1 0.9 copy-start.13
  112.0 0.8 copy-start.17

commit v2 on v0

v2 whole, which is shorter than its diff:
```python
import jax
import jax.numpy as jnp
from jax import lax
from jax.experimental import pallas as pl
from jax.experimental.pallas import tpu as pltpu
from jax.sharding import Mesh
from jax.sharding import PartitionSpec as P

OMEGA = 0.8
KEEP = 1.0 - OMEGA
TINY = 1e-30
F32 = jnp.float32
EXACT = lax.Precision.HIGHEST
MIB = 1024 * 1024
TILE = ("zx", "core")

NT = (((1,), (1,)), ((), ()))


def params(mib):
    return pltpu.CompilerParams(vmem_limit_bytes=mib * MIB)


def vmem():
    return pl.BlockSpec(memory_space=pltpu.VMEM)


def hbm():
    return pl.BlockSpec(memory_space=pltpu.HBM)


def f32(*shape):
    return jax.ShapeDtypeStruct(shape, F32)


def kept(*shape):
    return pltpu.VMEM(shape, F32)


def stored(*shape):
    return pltpu.HBM(shape, F32)


def in_hbm(a):
    return pltpu.with_memory_space_constraint(a, pltpu.HBM)


def inverse(a):
    r = pl.reciprocal(a, approx=True)
    return r * (2.0 - a * r)


def face(a, b):
    return (2.0 * a * b) * inverse(a + b)


def outer_face(a, b):
    return (2.0 * a * b) * inverse(jnp.maximum(a + b, TINY))


def iota(shape, dim):
    return lax.broadcasted_iota(jnp.int32, shape, dim)


def shift_up(a, axis):
    return pltpu.roll(a, a.shape[axis] - 1, axis)


def shift_down(a, axis):
    return pltpu.roll(a, 1, axis)


def in_line(flux_weight, u, axis):
    return flux_weight * shift_up(u, axis) + shift_down(flux_weight * u, axis)


def line_weight(c, axis):
    w = face(c, shift_up(c, axis))
    return jnp.where(iota(c.shape, axis) < c.shape[axis] - 1, w, 0.0)


def both_sides(w, axis):
    return w + shift_down(w, axis)


def row_sums(slabs):
    folded = jnp.concatenate([p[:, :128] + p[:, 128:] for p in slabs], axis=0)
    head = folded.astype(jnp.bfloat16)
    rest = (folded - head.astype(F32)).astype(jnp.bfloat16)
    ones = jnp.ones((8, 128), jnp.bfloat16)
    total = lax.dot_general(ones, head, NT, preferred_element_type=F32)
    total = total + lax.dot_general(ones, rest, NT, preferred_element_type=F32)
    return jnp.concatenate([total[0:1, 128 * s : 128 * s + 128] for s in range(4)], axis=0)


def to_lanes(column):
    mask = iota((8, 128), 0) == iota((8, 128), 1)
    return jnp.sum(jnp.where(mask, column, jnp.zeros_like(column)), axis=0, keepdims=True)


def gather_rows(ids, table):
    block = lax.shift_right_logical(ids, 7)
    lane = lax.bitwise_and(ids, 127)
    found = jnp.zeros(ids.shape, F32)
    for b in range(16):
        row = jnp.broadcast_to(table[b : b + 1], ids.shape)
        got = jnp.take_along_axis(row, lane, axis=1)
        found = jnp.where(block == b, got, found)
    return found


def scatter(id_rows, values):
    place = iota((64, 128), 0)
    block_of = 4 * ((place // 8) % 4) + 2 * (place // 32) + (place // 4) % 2
    total = jnp.zeros((192, 128), F32)
    for id_row, value in zip(id_rows, values):
        hit = lax.shift_right_logical(id_row, 7) == block_of
        spread = jnp.where(hit, jnp.concatenate([value] * 16, axis=0), 0.0)
        lane_hit = lax.bitwise_and(id_row, 127) == iota((128, 128), 0)
        onehot = jnp.where(lane_hit, 1.0, 0.0).astype(jnp.bfloat16)
        a = spread.astype(jnp.bfloat16)
        spread = spread - a.astype(F32)
        b = spread.astype(jnp.bfloat16)
        spread = spread - b.astype(F32)
        parts = jnp.concatenate([a, b, spread.astype(jnp.bfloat16)], axis=0)
        total = total + lax.dot_general(parts, onehot, NT, preferred_element_type=F32)
    return total[0:64] + total[64:128] + total[128:192]


ROW_C = 512
ROW_C2 = 640
ROW_MAP = 768
ROWS = 776


def sides():
    core = lax.axis_index("core")
    return 1 - core, core


def edges_kernel(
    u_hbm, c_hbm, imp_hbm, cmap_hbm, out_lo, out_hi, near_out, far_out, blocks, u, c, cmap, imp, sems, whole_sems
):
    core = lax.axis_index("core")
    copies = [pltpu.make_async_copy(cmap_hbm, cmap, sems.at[4])]
    for n, y in enumerate((0, 120)):
        copies.append(pltpu.make_async_copy(u_hbm.at[:, :, pl.ds(y, 8)], u.at[n], sems.at[2 * n]))
        copies.append(pltpu.make_async_copy(c_hbm.at[:, pl.ds(y, 8)], c.at[n], sems.at[2 * n + 1]))
    whole = []
    for n, (out, side) in enumerate(zip((near_out, far_out), sides())):
        for s in range(4):
            whole.append((u_hbm.at[s, 7 * side], out.at[pl.ds(128 * s, 128)], whole_sems.at[n, s]))
        whole.append((c_hbm.at[7 * side], out.at[pl.ds(ROW_C, 128)], whole_sems.at[n, 4]))
        whole.append((c_hbm.at[1 + 5 * side], out.at[pl.ds(ROW_C2, 128)], whole_sems.at[n, 5]))
    whole.append((imp_hbm.at[2 * core], imp.at[0], whole_sems.at[0, 7]))
    whole.append((imp_hbm.at[2 * core + 1], imp.at[1], whole_sems.at[1, 7]))
    whole = [pltpu.make_async_copy(*copy) for copy in whole]
    for copy in copies + whole:
        copy.start()
    for copy in copies:
        copy.wait()
    for n, out, near, far, lane in ((0, out_lo, 0, 1, 0), (1, out_hi, 7, 6, 127)):
        for x in range(8):
            for s in range(4):
                out[8 * s + x : 8 * s + x + 1, :] = u[n, s, x, near : near + 1, :]
            out[32 + x : 33 + x, :] = c[n, x, near : near + 1, :]
            out[40 + x : 41 + x, :] = c[n, x, far : far + 1, :]
        out[48:56, :] = jnp.zeros((8, 256), F32)
        out[48:49, 0:128] = to_lanes(cmap[:, lane : lane + 1].astype(F32))
    for out, side in zip((near_out, far_out), sides()):
        out[ROW_MAP:ROWS, :] = jnp.zeros((8, 256), F32)
        out[ROW_MAP : ROW_MAP + 1, 0:128] = cmap[pl.ds(7 * side, 1), :].astype(F32)
    for copy in whole:
        copy.wait()
    blocks[:, 0:128] = imp[0]
    blocks[:, 128:256] = imp[1]


def edges(u, c, impedance, cmap):
    return pl.pallas_call(
        edges_kernel,
        in_specs=[hbm()] * 4,
        out_specs=[vmem()] * 5,
        out_shape=[f32(56, 256), f32(56, 256), f32(ROWS, 256), f32(ROWS, 256), f32(128, 256)],
        scratch_shapes=[
            pltpu.VMEM((2, 4, 8, 8, 256), F32),
            pltpu.VMEM((2, 8, 8, 256), F32),
            pltpu.VMEM((8, 128), jnp.int32),
            pltpu.VMEM((2, 128, 128), F32),
            pltpu.SemaphoreType.DMA((5,)),
            pltpu.SemaphoreType.DMA((2, 8)),
        ],
        compiler_params=params(4),
        name="edges",
    )(u, c, impedance, cmap)


def corners_kernel(y_lo, y_hi, near_out, far_out):
    for out, side in zip((near_out, far_out), sides()):
        out[...] = jnp.zeros((8, 256), F32)
        out[0:1, :] = y_lo[pl.ds(32 + 7 * side, 1), :]
        out[1:2, :] = y_hi[pl.ds(32 + 7 * side, 1), :]


def corners(y_lo, y_hi):
    return pl.pallas_call(
        corners_kernel,
        in_specs=[vmem()] * 2,
        out_specs=[vmem()] * 2,
        out_shape=[f32(8, 256)] * 2,
        compiler_params=params(2),
        name="corners",
    )(y_lo, y_hi)


def weights_kernel(u_hbm, f_hbm, c_hbm, cmap, admittance, u, f, wx, wy, wz, diag, zeta_t, c, sems):
    copy = pltpu.make_async_copy(c_hbm, c, sems.at[0])
    later = [pltpu.make_async_copy(u_hbm, u, sems.at[1]), pltpu.make_async_copy(f_hbm, f, sems.at[2])]
    copy.start()
    for other in later:
        other.start()
    zeta = gather_rows(cmap[...], admittance[...])
    zeta_t[...] = jnp.transpose(jnp.concatenate([zeta, jnp.zeros((120, 128), F32)], axis=0))
    copy.wait()
    for x in range(8):
        here = c[x]
        if x < 7:
            wx[x] = face(here, c[x + 1])
        along_y = line_weight(here, 0)
        along_z = line_weight(here, 1)
        wy[x] = along_y
        wz[x] = along_z
        total = both_sides(along_y, 0) + both_sides(along_z, 1) + zeta_t[:, x : x + 1]
        if x > 0:
            total = total + wx[x - 1]
        if x < 7:
            total = total + wx[x]
        diag[x] = total
    for other in later:
        other.wait()


def weights(u, f, c, cmap, admittance):
    outs = [
        kept(4, 8, 128, 256), kept(4, 8, 128, 256),
        kept(7, 128, 256), kept(8, 128, 256), kept(8, 128, 256), kept(8, 128, 256), kept(128, 128),
    ]
    return pl.pallas_call(
        weights_kernel,
        in_specs=[hbm()] * 3 + [vmem()] * 2,
        out_specs=[vmem()] * len(outs),
        out_shape=outs,
        scratch_shapes=[pltpu.VMEM((8, 128, 256), F32), pltpu.SemaphoreType.DMA((3,))],
        compiler_params=params(8),
        cost_estimate=pl.CostEstimate(flops=20_000_000, bytes_accessed=6_000_000, transcendentals=0),
        name="weights",
    )(u, f, c, cmap, admittance)


def inner_kernel(
    u, f, cmap, own_lo, own_hi, y_lo, y_hi, wx, wy, wz, diag,
    u2, gain, wyl, wyh, pulled1, keep1, pulled2, edge_lo, edge_hi, contact,
    u1, sums,
):
    wyl[...] = outer_face(own_lo[32:40, :], y_lo[32:40, :])
    wyh[...] = outer_face(own_hi[32:40, :], y_hi[32:40, :])
    for x in range(8):
        gain[x] = diag[x]
        gain[x, 0:1, :] = gain[x, 0:1, :] + wyl[x : x + 1, :]
        gain[x, 127:128, :] = gain[x, 127:128, :] + wyh[x : x + 1, :]
        if x not in (0, 7):
            gain[x] = OMEGA * inverse(gain[x])

    for n, x in enumerate((0, 7)):
        for s in range(4):
            pulled = f[s, x] + in_line(wy[x], u[s, x], 0)
            pulled = pulled + in_line(wz[x], u[s, x], 1)
            pulled = pulled + (wx[0] * u[s, 1] if x == 0 else wx[6] * u[s, 6])
            pulled1[n, s] = pulled
            pulled1[n, s, 0:1, :] = pulled1[n, s, 0:1, :] + wyl[x : x + 1, :] * y_lo[8 * s + x : 8 * s + x + 1, :]
            pulled1[n, s, 127:128, :] = (
                pulled1[n, s, 127:128, :] + wyh[x : x + 1, :] * y_hi[8 * s + x : 8 * s + x + 1, :]
            )
            keep1[n, s] = KEEP * u[s, x]

    def first(x, carry):
        for s in range(4):
            pulled = f[s, x] + in_line(wy[x], u[s, x], 0)
            pulled = pulled + in_line(wz[x], u[s, x], 1)
            pulled = pulled + wx[x - 1] * u[s, x - 1] + wx[x] * u[s, x + 1]
            u1[s, x] = KEEP * u[s, x] + gain[x] * pulled
            low = u1[s, x, 0:1, :] + gain[x, 0:1, :] * wyl[pl.ds(x, 1), :] * y_lo[pl.ds(8 * s + x, 1), :]
            high = u1[s, x, 127:128, :] + gain[x, 127:128, :] * wyh[pl.ds(x, 1), :] * y_hi[pl.ds(8 * s + x, 1), :]
            u1[s, x, 0:1, :] = low
            u1[s, x, 127:128, :] = high
            edge_lo[pl.ds(8 * s + x, 1), :] = low
            edge_hi[pl.ds(8 * s + x, 1), :] = high
        return carry

    lax.fori_loop(1, 7, first, 0)

    for s in range(4):
        pulled2[0, s] = f[s, 0] + wx[0] * u1[s, 1]
        pulled2[1, s] = f[s, 7] + wx[6] * u1[s, 6]
        u1[s, 0] = jnp.zeros((128, 256), F32)
        u1[s, 7] = jnp.zeros((128, 256), F32)

    def second(x, carry):
        slabs = []
        for s in range(4):
            pulled = f[s, x] + in_line(wy[x], u1[s, x], 0)
            pulled = pulled + in_line(wz[x], u1[s, x], 1)
            pulled = pulled + wx[x - 1] * u1[s, x - 1] + wx[x] * u1[s, x + 1]
            new = KEEP * u1[s, x] + gain[x] * pulled
            u2[s, x - 1] = new
            slabs.append(new)
        sums[x] = row_sums(slabs)
        return carry

    lax.fori_loop(1, 7, second, 0)
    contact[...] = scatter([cmap[x : x + 1, :] for x in range(1, 7)], [sums[x] for x in range(1, 7)])


def inner(u, f, cmap, own_lo, own_hi, y_lo, y_hi, wx, wy, wz, diag):
    outs = [
        kept(4, 6, 128, 256), kept(8, 128, 256), kept(8, 256), kept(8, 256),
        kept(2, 4, 128, 256), kept(2, 4, 128, 256), kept(2, 4, 128, 256),
        kept(32, 256), kept(32, 256), kept(64, 128),
    ]
    return pl.pallas_call(
        inner_kernel,
        in_specs=[vmem()] * 11,
        out_specs=[vmem()] * len(outs),
        out_shape=outs,
        scratch_shapes=[
            pltpu.VMEM((4, 8, 128, 256), F32),
            pltpu.VMEM((8, 4, 128), F32),
        ],
        compiler_params=params(12),
        cost_estimate=pl.CostEstimate(flops=100_000_000, bytes_accessed=25_000_000, transcendentals=0),
        name="inner",
    )(u, f, cmap, own_lo, own_hi, y_lo, y_hi, wx, wy, wz, diag)


def outer_kernel(
    pairs, amplitudes, cmap, admittance, blocks, near, far, y_lo, y_hi, x_near, x_far, ends_near, ends_far,
    wx, wy, wz, gain, wyl, wyh, u2, pulled1, keep1, pulled2, e_lo, e_hi, contact, zeta_in,
    face_near_out, face_far_out, edge_lo_out, edge_hi_out, u2_out, gain_out, wxf_out, misc_out, zeta_out, mine, other,
    ids, face_near, face_far, edge_lo, edge_hi, u2b, gain_b, wxf, misc, c_own, sems, u2_sems,
):
    copies = []
    rows_in = [
        pltpu.make_async_copy(source.at[pl.ds(ROW_C, 128)], c_own.at[n], sems.at[11 + n])
        for n, source in enumerate((near, far))
    ]
    for copy in rows_in:
        copy.start()

    def send(source, target, sem):
        copy = pltpu.make_async_copy(source, target, sem)
        copy.start()
        copies.append(copy)

    send(gain.at[pl.ds(1, 6)], gain_out.at[pl.ds(1, 6)], sems.at[0])
    send(zeta_in, zeta_out, sems.at[1])
    send(u2.at[:, pl.ds(1, 4)], u2_out.at[:, pl.ds(2, 4)], sems.at[2])
    misc[0:8, :] = wyl[...]
    misc[8:16, :] = wyh[...]
    send(misc, misc_out, sems.at[3])
    ids[0:8, :] = jnp.full((8, 128), 2048, jnp.int32)
    ids[0:1, :] = x_near[ROW_MAP : ROW_MAP + 1, 0:128].astype(jnp.int32)
    ids[1:2, :] = x_far[ROW_MAP : ROW_MAP + 1, 0:128].astype(jnp.int32)
    lanes = iota((1, 128), 1)
    low_ids = y_lo[48:49, 0:128].astype(jnp.int32)
    high_ids = pltpu.roll(y_hi[48:49, 0:128], 8, 1).astype(jnp.int32)
    ids[2:3, :] = jnp.where(lanes < 8, low_ids, jnp.where(lanes < 16, high_ids, 2048))
    zeta = gather_rows(ids[...], admittance[...])
    zeta_t = jnp.transpose(jnp.concatenate([zeta, jnp.zeros((120, 128), F32)], axis=0))
    row = iota((128, 256), 0)

    id_rows = []
    values = []
    for copy in rows_in:
        copy.wait()
    for n, (side, msg, ends, out, sent) in enumerate(
        zip(sides(), (x_near, x_far), (ends_near, ends_far), (face_near, face_far), (face_near_out, face_far_out))
    ):
        x = 7 * side
        there = msg[ROW_C : ROW_C + 128, :]
        outside = outer_face(c_own[n], there)
        wxf[n] = outside
        g = OMEGA * inverse(gain[x] + outside)
        gain_b[n] = g
        for s in range(4):
            out[s] = keep1[side, s] + g * (pulled1[side, s] + outside * msg[128 * s : 128 * s + 128, :])
        send(out, sent, sems.at[4 + n])
        send(gain_b.at[n], gain_out.at[x], sems.at[6 + n])
        spare = jnp.maximum(there, TINY)
        diag = both_sides(line_weight(spare, 0), 0) + both_sides(line_weight(spare, 1), 1) + zeta_t[:, n : n + 1]
        diag = diag + outside + outer_face(there, msg[ROW_C2 : ROW_C2 + 128, :])
        diag = diag + jnp.where(row == 0, outer_face(there[0:1], ends[0:1, :]), 0.0)
        diag = diag + jnp.where(row == 127, outer_face(there[127:128], ends[1:2, :]), 0.0)
        factor = OMEGA * outside * inverse(jnp.maximum(diag, TINY))
        id_rows.append(ids[n : n + 1, :])
        values.append(row_sums([factor * out[s] for s in range(4)]))
        inside = 1 + 5 * side
        factor = gain[inside] * wx[6 * side]
        slabs = []
        for s in range(4):
            new = factor * out[s]
            u2b[2 * n + 1, s] = u2[s, 5 * side] + new
            slabs.append(new)
        send(u2b.at[2 * n + 1], u2_out.at[:, inside], u2_sems.at[2 * n + 1])
        id_rows.append(cmap[pl.ds(inside, 1), :])
        values.append(row_sums(slabs))
        slabs = []
        for s in range(4):
            pulled = pulled2[side, s] + in_line(wy[x], out[s], 0)
            pulled = pulled + in_line(wz[x], out[s], 1)
            new = KEEP * out[s] + g * pulled
            u2b[2 * n, s] = new
            slabs.append(new)
        send(u2b.at[2 * n], u2_out.at[:, x], u2_sems.at[2 * n])
        id_rows.append(cmap[pl.ds(x, 1), :])
        values.append(row_sums(slabs))

    send(wxf, wxf_out, sems.at[8])

    edge_sums = jnp.zeros((4, 128), F32)
    for n, (msg, own, inside, edge, y, sent) in enumerate(
        ((y_lo, wyl, e_lo, edge_lo, 0, edge_lo_out), (y_hi, wyh, e_hi, edge_hi, 127, edge_hi_out))
    ):
        edge[0:32, :] = inside[...]
        for s in range(4):
            for side, out in zip(sides(), (face_near, face_far)):
                edge[pl.ds(8 * s + 7 * side, 1), :] = out[s, y : y + 1, :]
        edge[32:160, :] = blocks[...]
        send(edge, sent, sems.at[9 + n])
        there = msg[32:40, :]
        x_rows = iota((8, 256), 0)
        spare = jnp.maximum(there, TINY)
        diag = both_sides(line_weight(spare, 0), 0) + both_sides(line_weight(spare, 1), 1) + own[...]
        diag = diag + outer_face(there, msg[40:48, :])
        for side, ends in zip(sides(), (ends_near, ends_far)):
            diag = diag + jnp.where(x_rows == 7 * side, outer_face(there, ends[n : n + 1, :]), 0.0)
        diag = diag + zeta_t[8 * n : 8 * n + 8, 2:3]
        factor = OMEGA * own[...] * inverse(jnp.maximum(diag, TINY))
        lined = []
        for s in range(4):
            line = to_lanes(jnp.sum(factor * edge[8 * s : 8 * s + 8, :], axis=1, keepdims=True))
            lined.append(pltpu.roll(line, 8 * n, 1) if n else line)
        edge_sums = edge_sums + jnp.concatenate(lined, axis=0)
    id_rows.append(ids[2:3, :])
    values.append(edge_sums)

    total = (contact[...] + scatter(id_rows, values)) * (1.0 / 256.0)
    place = iota((64, 128), 0)
    electrode = (4 * ((place // 8) % 4) + 2 * (place // 32) + (place // 4) % 2) * 128 + iota((64, 128), 1)
    adds = jnp.logical_and(lax.axis_index("zx") == 0, lax.axis_index("elec") == 0)
    adds = jnp.logical_and(adds, lax.axis_index("core") == 0)
    for s in range(4):
        at = place % 4 == s
        amount = jnp.where(adds, amplitudes[s], 0.0)
        total = total + jnp.where(at & (electrode == pairs[2 * s]), amount, 0.0)
        total = total - jnp.where(at & (electrode == pairs[2 * s + 1]), amount, 0.0)
    first_half = lax.axis_index("core") == 0
    mine[...] = jnp.where(first_half, total[0:32], total[32:64])
    other[...] = jnp.where(first_half, total[32:64], total[0:32])
    for copy in copies:
        copy.wait()


def outer(pairs, amplitudes, *args):
    outs = [
        stored(4, 128, 256), stored(4, 128, 256), stored(160, 256), stored(160, 256),
        stored(4, 8, 128, 256), stored(8, 128, 256), stored(2, 128, 256), stored(16, 256), stored(128, 128),
        f32(32, 128), f32(32, 128),
    ]
    specs = [vmem()] * len(args)
    specs[3] = specs[4] = hbm()
    return pl.pallas_call(
        outer_kernel,
        in_specs=[pl.BlockSpec(memory_space=pltpu.SMEM)] * 2 + specs,
        out_specs=[hbm()] * 9 + [vmem()] * 2,
        out_shape=outs,
        scratch_shapes=[
            pltpu.VMEM((8, 128), jnp.int32),
            pltpu.VMEM((4, 128, 256), F32),
            pltpu.VMEM((4, 128, 256), F32),
            pltpu.VMEM((160, 256), F32),
            pltpu.VMEM((160, 256), F32),
            pltpu.VMEM((4, 4, 128, 256), F32),
            pltpu.VMEM((2, 128, 256), F32),
            pltpu.VMEM((2, 128, 256), F32),
            pltpu.VMEM((16, 256), F32),
            pltpu.VMEM((2, 128, 256), F32),
            pltpu.SemaphoreType.DMA((13,)),
            pltpu.SemaphoreType.DMA((4,)),
        ],
        compiler_params=params(32),
        cost_estimate=pl.CostEstimate(flops=50_000_000, bytes_accessed=15_000_000, transcendentals=0),
        name="outer",
    )(pairs, amplitudes, *args)


def spread_kernel(mine, got, out, both, sems):
    both[...] = mine[...] + got[...]
    copies = [pltpu.make_async_copy(both, out.at[n], sems.at[n]) for n in range(out.shape[0])]
    for copy in copies:
        copy.start()
    for copy in copies:
        copy.wait()


def spread(mine, got, count):
    return pl.pallas_call(
        spread_kernel,
        in_specs=[vmem()] * 2,
        out_specs=hbm(),
        out_shape=stored(count, 32, 128),
        scratch_shapes=[pltpu.VMEM((32, 128), F32), pltpu.SemaphoreType.DMA((count,))],
        compiler_params=params(2),
        name="spread",
    )(mine, got)


def blocks_kernel(a0, a1, a2, a3, i0, i1, i2, i3, pull, out, charges):
    elec = lax.axis_index("elec")
    total = a0[...] + a1[...] + a2[...] + a3[...]
    for e in range(4):
        charges[e] = total[8 * e : 8 * e + 8]
    upper = iota((8, 128), 0) < 4
    for turn, blocks in ((0, i0), (3, i1), (1, i2), (2, i3)):
        e = lax.rem(elec + turn, 4)
        charge = charges[e]
        start = blocks.shape[0] - 128
        both = blocks[start : start + 128, :]
        first = lax.dot_general(charge, both[:, 0:128], NT, precision=EXACT, preferred_element_type=F32)
        second = lax.dot_general(charge, both[:, 128:256], NT, precision=EXACT, preferred_element_type=F32)
        out[e] = jnp.where(upper, first, second)


def blocks(parts, impedances, pull):
    return pl.pallas_call(
        blocks_kernel,
        in_specs=[vmem()] * 8 + [pl.BlockSpec(memory_space=pl.ANY)],
        out_specs=vmem(),
        out_shape=f32(4, 8, 128),
        scratch_shapes=[pltpu.VMEM((4, 8, 128), F32)],
        compiler_params=params(4),
        name="blocks",
    )(*parts, *impedances, pull)


def ready_kernel(
    u2_hbm, gain_hbm, wxf_hbm, misc_hbm, zeta_hbm, h_near, h_far, e_lo, e_hi, base, pull,
    gain, wxf, misc, zeta_t, sems, small_sems,
):
    order = (2, 3, 4, 5, 1, 6, 0, 7)
    copies = {x: pltpu.make_async_copy(u2_hbm.at[:, x], base.at[:, x], sems.at[x]) for x in order}
    small = [
        pltpu.make_async_copy(source, target, small_sems.at[n])
        for n, (source, target) in enumerate(
            ((zeta_hbm, zeta_t), (misc_hbm, misc), (gain_hbm, gain), (wxf_hbm, wxf))
        )
    ]
    for copy in small:
        copy.start()
    for x in order:
        copies[x].start()
    for copy in small:
        copy.wait()
    for x in order:
        g = gain[x]
        part = (1.0 / OMEGA) * zeta_t[:, x : x + 1] * g
        pull[x] = part
        low = g[0:1] * misc[x : x + 1, :]
        high = g[127:128] * misc[8 + x : 9 + x, :]
        copies[x].wait()
        for s in range(4):
            at = 8 * s + x
            if x in (0, 7):
                from_near = sides()[0] == x // 7
                halo = jnp.where(from_near, wxf[0] * h_near[s], wxf[1] * h_far[s])
                base[s, x] = base[s, x] + g * halo
            base[s, x, 0:1, :] = base[s, x, 0:1, :] + low * e_lo[at : at + 1, :]
            base[s, x, 127:128, :] = base[s, x, 127:128, :] + high * e_hi[at : at + 1, :]
            u = base[s, x]
            base[s, x] = u - part * u


def ready(*args):
    return pl.pallas_call(
        ready_kernel,
        in_specs=[hbm()] * 5 + [vmem()] * 4,
        out_specs=[vmem()] * 2,
        out_shape=[kept(4, 8, 128, 256), kept(8, 128, 256)],
        scratch_shapes=[
            pltpu.VMEM((8, 128, 256), F32),
            pltpu.VMEM((2, 128, 256), F32),
            pltpu.VMEM((16, 256), F32),
            pltpu.VMEM((128, 128), F32),
            pltpu.SemaphoreType.DMA((8,)),
            pltpu.SemaphoreType.DMA((4,)),
        ],
        compiler_params=params(8),
        cost_estimate=pl.CostEstimate(flops=10_000_000, bytes_accessed=8_000_000, transcendentals=0),
        name="ready",
    )(*args)


def correct_kernel(cmap, own, got, base, pull, out_hbm, volts, table, buf, sems):
    core = lax.axis_index("core")
    elec = lax.axis_index("elec")
    table[core] = own[...]
    table[1 - core] = got[...]
    for h in range(2):
        for j in range(2):
            volts[:, 128 * (2 * h + j) : 128 * (2 * h + j) + 128] = table[h, elec, 4 * j : 4 * j + 4, :]
    ids = cmap[...]
    block = lax.shift_right_logical(ids, 7)
    lane = lax.bitwise_and(ids, 127)
    touched = []
    for s in range(4):
        found = jnp.zeros((8, 128), F32)
        for b in range(16):
            e, h, j = b // 4, (b // 2) % 2, b % 2
            row = jnp.broadcast_to(table[h, e, 4 * j + s : 4 * j + s + 1, :], (8, 128))
            found = jnp.where(block == b, jnp.take_along_axis(row, lane, axis=1), found)
        touched.append(found)
    stacked = jnp.concatenate(touched + [jnp.zeros((96, 128), F32)], axis=0)
    volts_t = jnp.transpose(stacked)
    copies = []
    for x in range(8):
        for s in range(4):
            buf[s, x] = base[s, x] + pull[x] * volts_t[:, 8 * s + x : 8 * s + x + 1]
        copy = pltpu.make_async_copy(buf.at[:, x], out_hbm.at[:, x], sems.at[x])
        copy.start()
        copies.append(copy)
    for copy in copies:
        copy.wait()


def correct(*args):
    return pl.pallas_call(
        correct_kernel,
        in_specs=[vmem()] * 5,
        out_specs=[hbm(), vmem()],
        out_shape=[f32(4, 8, 128, 256), f32(4, 512)],
        scratch_shapes=[
            pltpu.VMEM((2, 4, 8, 128), F32),
            pltpu.VMEM((4, 8, 128, 256), F32),
            pltpu.SemaphoreType.DMA((8,)),
        ],
        compiler_params=params(8),
        name="correct",
    )(*args)


def per_device(u, f, c, cmap, admittance, impedance, pairs, amplitudes):
    tiles = lax.axis_size(TILE)
    groups = lax.axis_size("zx")
    elecs = lax.axis_size("elec")
    admittance = admittance.reshape(16, 128)
    u, f, c, impedance = in_hbm(u), in_hbm(f), in_hbm(c), in_hbm(impedance)

    def from_below(a):
        return lax.ppermute(a, "elec", [(i, i + 1) for i in range(elecs - 1)])

    def from_above(a):
        return lax.ppermute(a, "elec", [(i + 1, i) for i in range(elecs - 1)])

    def rotated(a, turn):
        return lax.ppermute(a, "elec", [(i, (i + turn) % elecs) for i in range(elecs)])

    def near(a):
        return lax.ppermute(a, "core", [(0, 1), (1, 0)])

    def far(a):
        pairs = [(i, i + 1) for i in range(1, tiles - 1, 2)]
        return lax.ppermute(a, TILE, pairs + [(j, i) for i, j in pairs])

    own_lo, own_hi, row_near, row_far, side = edges(u, c, impedance, in_hbm(cmap))
    y_lo = from_below(own_hi)
    y_hi = from_above(own_lo)
    x_far = far(row_far)
    x_near = near(row_near)
    opposite = rotated(side, 2)
    ends_near, ends_far = corners(y_lo, y_hi)
    ends_far = far(ends_far)
    ends_near = near(ends_near)

    u, f, wx, wy, wz, diag, zeta_t = weights(u, f, c, cmap, admittance)
    u2, gain, wyl, wyh, pulled1, keep1, pulled2, e_lo, e_hi, contact = inner(
        u, f, cmap, own_lo, own_hi, y_lo, y_hi, wx, wy, wz, diag
    )
    face_near, face_far, edge_lo, edge_hi, u2, gain, wxf, misc, zeta_t, mine, other = outer(
        pairs.reshape(-1), amplitudes, cmap, admittance, side, in_hbm(row_near), in_hbm(row_far),
        y_lo, y_hi, x_near, x_far, ends_near, ends_far,
        wx, wy, wz, gain, wyl, wyh, u2, pulled1, keep1, pulled2, e_lo, e_hi, contact, zeta_t,
    )
    parts = spread(mine, near(other), groups)
    parts = lax.all_to_all(parts, "zx", 0, 0, tiled=True)
    summed = jnp.sum(parts, axis=0)
    h_far = far(face_far)
    h_near = near(face_near)
    e_lo = rotated(edge_hi, 1)
    e_hi = rotated(edge_lo, elecs - 1)
    base, pull = ready(
        in_hbm(u2), in_hbm(gain), in_hbm(wxf), in_hbm(misc), in_hbm(zeta_t), h_near, h_far, e_lo, e_hi
    )
    around = (summed, rotated(summed, 1), rotated(summed, elecs - 1), rotated(summed, 2))
    own = blocks(around, (side, e_lo, e_hi, opposite), pull)
    got = near(own)
    out, volts = correct(cmap, own, got, base, pull)
    return out, volts


def solution(mesh):
    tile, src, elec = mesh.devices.shape
    cut = Mesh(mesh.devices.reshape(tile // 2, 2, src, elec), ("zx", "core", "src", "elec"))
    placed = (
        P("src", TILE, "elec", None),
        P("src", TILE, "elec", None),
        P(TILE, "elec", None),
        P(TILE, "elec"),
        P(),
        P("elec", None, None),
        P("src", None),
        P("src"),
    )
    return jax.shard_map(
        per_device,
        mesh=cut,
        in_specs=placed,
        out_specs=(P("src", TILE, "elec", None), P("src", "elec")),
        check_vma=False,
    )
```

time: 265 us -> 85 us (0.32); the launches traced: 260 us -> 84.6 us
  blocking collectives: 77.1 us -> 0 us
  other arithmetic: 61.5 us -> 0.02 us
  waiting for transfers between devices: 45 us -> 9.23 us
  Pallas kernels: 0 us -> 30.6 us
  matrix products: 16 us -> 0 us
  between operations: 14.4 us -> 1.1 us
  local copies, waits for them, and re-layouts: 7.65 us -> 1.45 us
  starting transfers between devices: 38.7 us -> 42.2 us
    psum x1 -> x0, blocking collectives: 68 us -> none  [per_device(): summed = lax.psum(partial_value, 'tile')]
    unnamed x2 -> x0, waiting for transfers between devices: 31.4 us -> none
    pallas_call x0 -> x9, Pallas kernels: none -> 30.6 us  [the longest x1 10.2 us: inner(): pl.pallas_call(inner_kernel, in_specs=[vmem()] * 11, out_specs=[vmem()] *...]
    add x4 -> x0, other arithmetic: 25.7 us -> none  [the longest x1 18.1 us: relax_once(): current + OMEGA * (source_term - diagonal * current + pulled) / diagonal]
    reduce_sum x1, other arithmetic: 18.6 us -> 0.02 us  [per_device(): summed = jnp.sum(parts, axis=0)]
    concatenate x3 -> x0, other arithmetic: 15.3 us -> none  [extended(): jnp.concatenate([lax.ppermute(tail, axis, [(i, (i + 1) % count) for i in...]
    ppermute x12 -> x16, waiting for transfers between devices: 13.5 us -> 2.05 us  [the longest x5 2.02 us: near(): return lax.ppermute(a, 'core', [(0, 1), (1, 0)])]
    all_gather x1 -> x0, blocking collectives: 9.08 us -> none  [per_device(): full_volts = lax.all_gather(electrode_volts, 'elec', axis=1, tiled=True)]
  transfers between devices with their start and end apart: 13 -> 17, of which waited for: 5 -> 3; matrix products, arithmetic and copies ran while one was open for 4% -> 2% of each run, Pallas kernels for 0% -> 23%
where the time goes in v2:
time: 85 us; the launch traced here: 84.6 us
  starting transfers between devices  42.2 us (50%)
  Pallas kernels  30.6 us (36%)
  waiting for transfers between devices  9.23 us (11%)
  local copies, waits for them, and re-layouts  1.45 us (2%)
  between operations  1.1 us (1%)
    ppermute x3, starting transfers between devices, far(): return lax.ppermute(a, TILE, pairs + [(j, i) for i, j in pairs])  11.7 us
    ppermute x6, starting transfers between devices, rotated(): lax.ppermute(a, 'elec', [(i, (i + turn) % elecs) for i in range(elecs)])  10.9 us
    pallas_call x1, Pallas kernels, inner(): pl.pallas_call(inner_kernel, in_specs=[vmem()] * 11, out_specs=[vmem()] *...  10.2 us
    all_to_all x1, starting transfers between devices, per_device(): parts = lax.all_to_all(parts, 'zx', 0, 0, tiled=True)  8.74 us
    all_to_all x1, waiting for transfers between devices, per_device(): parts = lax.all_to_all(parts, 'zx', 0, 0, tiled=True)  7.18 us
    ppermute x5, starting transfers between devices, near(): return lax.ppermute(a, 'core', [(0, 1), (1, 0)])  6.38 us
    pallas_call x1, Pallas kernels, outer(): pl.pallas_call(outer_kernel, in_specs=[pl.BlockSpec(memory_space=pltpu.SM...  5.53 us
    pallas_call x1, Pallas kernels, ready(): pl.pallas_call(ready_kernel, in_specs=[hbm()] * 5 + [vmem()] * 4, out_spe...  4.2 us
  transfers between devices with their start and end apart: 17, of which 3 were waited for; matrix products, arithmetic and copies ran while one was open for 2% of the time, Pallas kernels for 23%

profile of v2, /device:TPU:1, one launch (start us, length us, event | category | flops | bytes accessed | tf_op | source)
XLA Modules:
  0.0 84.6 jit_solution(17983781418572709181)
XLA Ops:
  0.6 0.0 copy-start.2
  0.6 0.0 copy-start.5
  0.7 0.0 copy-start.3
  0.7 1.9 %edges.1 = (f32[56,256]{1,0:T(8,128)S(1)}, f32[56,256]{1,0:T(8,128)S(1)}, f32[776,256]{1,0:T(8,128)S(1)}, f32[776,256]{1,0:T(8,128)S(1)}, f32[128,256]{1,0:T(8,128)S(1)}) custom-call(f32[4,8,128,256]{3,2,1,0:T(8,128)} %u_hbm.3, f32[8,128,256]{2,1,0:T(8,128)} %c_hbm.3, f32[4,128,128]{2,1,0:T(8,128)} %imp_hbm.1, s32[8,128]{1,0:T(8,128)} %cmap.7), custom_call_target="tpu_custom_call" | custom-call | tf_op jit(solution)/shard_map/edges/pallas_call | solution.py:180
  2.6 0.0 copy-start
  2.6 0.0 copy-start.1
  2.6 3.3 %collective-permute-start.2 = (f32[776,256]{1,0:T(8,128)S(1)}, f32[776,256]{1,0:T(8,128)S(1)}, u32[]{:S(2)}, u32[]{:S(2)}) collective-permute-start(f32[776,256]{1,0:T(8,128)S(1)} %get-tuple-element.40.near), channel_id=1, source_target_pairs={{0,8},{8,0},{1,9},{9,1},{2,10},{10,2},{3,11},{11,3},{4,12},{12,4},... | collective-permute-start | bytes 2383880 | tf_op jit(solution)/shard_map/ppermute | solution.py:677
  6.0 2.8 %collective-permute-start.3 = (f32[776,256]{1,0:T(8,128)S(1)}, f32[776,256]{1,0:T(8,128)S(1)}, u32[]{:S(2)}, u32[]{:S(2)}) collective-permute-start(f32[776,256]{1,0:T(8,128)S(1)} %get-tuple-element.41.far), channel_id=1, source_target_pairs={{8,16},{24,32},{40,48},{56,64},{72,80},{88,96},{104,112},{120,128}... | collective-permute-start | bytes 2383880 | tf_op jit(solution)/shard_map/ppermute | solution.py:681
  8.8 3.2 %collective-permute-start = (f32[56,256]{1,0:T(8,128)S(1)}, f32[56,256]{1,0:T(8,128)S(1)}, u32[]{:S(2)}, u32[]{:S(2)}) collective-permute-start(f32[56,256]{1,0:T(8,128)S(1)} %get-tuple-element.42.own_hi), channel_id=1, source_target_pairs={{0,1},{1,2},{2,3},{4,5},{5,6},{6,7},{8,9},{9,10},{10,11},{12,13},{... | collective-permute-start | bytes 172040 | tf_op jit(solution)/shard_map/ppermute | solution.py:668
  12.0 1.3 %collective-permute-start.1 = (f32[56,256]{1,0:T(8,128)S(1)}, f32[56,256]{1,0:T(8,128)S(1)}, u32[]{:S(2)}, u32[]{:S(2)}) collective-permute-start(f32[56,256]{1,0:T(8,128)S(1)} %get-tuple-element.43.own_lo), channel_id=1, source_target_pairs={{1,0},{2,1},{3,2},{5,4},{6,5},{7,6},{9,8},{10,9},{11,10},{13,12},{... | collective-permute-start | bytes 172040 | tf_op jit(solution)/shard_map/ppermute | solution.py:671
  13.3 0.0 copy-done.5
  13.3 0.7 copy.11
  14.0 0.8 reshape.10.pairs
  14.7 0.0 copy-done.2
  14.7 0.0 copy-done.3
  14.7 3.8 %weights.1 = (f32[4,8,128,256]{3,2,1,0:T(8,128)S(1)}, f32[4,8,128,256]{3,2,1,0:T(8,128)S(1)}, f32[7,128,256]{2,1,0:T(8,128)S(1)}, f32[8,128,256]{2,1,0:T(8,128)S...) custom-call(f32[4,8,128,256]{3,2,1,0:T(8,128)} %u_hbm.3, ...), custom_call_target="tpu_custom_call" | custom-call | flops 20000000 | bytes 6000000 | tf_op jit(solution)/shard_map/weights/pallas_call | solution.py:248
  18.5 0.0 copy-done
  18.6 0.0 copy-done.1
  18.6 0.0 collective-permute-done.y_lo
  18.6 0.0 collective-permute-done.1.y_hi
  18.6 0.1 collective-permute-start.4
  18.7 3.9 %collective-permute-start.5 = (f32[8,256]{1,0:T(8,128)S(1)}, f32[8,256]{1,0:T(8,128)S(1)}, u32[]{:S(2)}, u32[]{:S(2)}) collective-permute-start(f32[8,256]{1,0:T(8,128)S(1)} %get-tuple-element.45), channel_id=1, source_target_pairs={{8,16},{24,32},{40,48},{56,64},{72,80},{88,96},{104,112},{120,128}... | collective-permute-start | bytes 24584 | tf_op jit(solution)/shard_map/ppermute | solution.py:681
  22.6 0.0 copy-start.4
  22.6 10.2 %inner.1 = (f32[4,6,128,256]{3,2,1,0:T(8,128)S(1)}, f32[8,128,256]{2,1,0:T(8,128)S(1)}, f32[8,256]{1,0:T(8,128)S(1)}, f32[8,256]{1,0:T(8,128)S(1)}, f32[2,4,128,...) custom-call(f32[4,8,128,256]{3,2,1,0:T(8,128)S(1)} %get-tuple-elemen, ...), custom_call_target="tpu_custom_call" | custom-call | flops 100000000 | bytes 25000000 | tf_op jit(solution)/shard_map/inner/pallas_call | solution.py:330
  32.9 0.0 collective-permute-done.4.ends_near
  32.9 0.0 collective-permute-done.5.ends_far
  32.9 0.0 collective-permute-done.2.x_near
  32.9 0.0 collective-permute-done.3.x_far
  32.9 0.0 copy-done.4
  32.9 5.5 %outer.1 = (f32[4,128,256]{2,1,0:T(8,128)}, f32[4,128,256]{2,1,0:T(8,128)}, f32[160,256]{1,0:T(8,128)}, f32[160,256]{1,0:T(8,128)}, f32[4,8,128,256]{3,2,1,0:T(8...) custom-call(s32[8]{0:T(128)S(1)} %reshape.10.pairs, ...), custom_call_target="tpu_custom_call" | custom-call | flops 50000000 | bytes 15000000 | tf_op jit(solution)/shard_map/outer/pallas_call | solution.py:481
  38.4 0.1 collective-permute-start.13
  38.5 5.0 %collective-permute-start.14 = (f32[4,128,256]{2,1,0:T(8,128)}, f32[4,128,256]{2,1,0:T(8,128)S(1)}, u32[]{:S(2)}, u32[]{:S(2)}) collective-permute-start(f32[4,128,256]{2,1,0:T(8,128)} %get-tuple-element.73), channel_id=1, source_target_pairs={{8,16},{24,32},{40,48},{56,64},{72,80},{88,96},{104,112},{120,128}... | collective-permute-start | bytes 1572872 | tf_op jit(solution)/shard_map/ppermute | solution.py:681
  43.6 0.1 collective-permute-start.6
  43.7 1.2 %collective-permute-done.6.got = f32[32,128]{1,0:T(8,128)S(1)} collective-permute-done((f32[32,128]{1,0:T(8,128)S(1)}, f32[32,128]{1,0:T(8,128)S(1)}, u32[]{:S(2)}, u32[]{:S(2)}) %collective-permute-start.6) | collective-permute-done | bytes 16416 | tf_op jit(solution)/shard_map/ppermute | solution.py:677
  44.9 0.8 %spread.1 = f32[16,32,128]{2,1,0:T(8,128)} custom-call(f32[32,128]{1,0:T(8,128)S(1)} %get-tuple-element.63.mine, f32[32,128]{1,0:T(8,128)S(1)} %collective-permute-done.6.got), custom_call_target="tpu_custom_call" | custom-call | tf_op jit(solution)/shard_map/spread/pallas_call | solution.py:516
  45.7 8.7 %all-to-all-start = ((f32[16,32,128]{2,1,0:T(8,128)}), f32[16,32,128]{2,1,0:T(8,128)S(1)}, u32[]{:S(2)}, u32[]{:S(2)}) async-start(f32[16,32,128]{2,1,0:T(8,128)} %spread.1), calls=%async_computation | async-start | bytes 524288 | tf_op jit(solution)/shard_map/all_to_all | solution.py:703
  54.5 2.3 %collective-permute-start.10 = (f32[160,256]{1,0:T(8,128)}, f32[160,256]{1,0:T(8,128)S(1)}, u32[]{:S(2)}, u32[]{:S(2)}) collective-permute-start(f32[160,256]{1,0:T(8,128)} %get-tuple-element.65), channel_id=1, source_target_pairs={{0,1},{1,2},{2,3},{3,0},{4,5},{5,6},{6,7},{7,4},{8,9},{9,10},{10,1... | collective-permute-start | bytes 491528 | tf_op jit(solution)/shard_map/ppermute | solution.py:674
  56.7 1.5 %collective-permute-start.11 = (f32[160,256]{1,0:T(8,128)}, f32[160,256]{1,0:T(8,128)S(1)}, u32[]{:S(2)}, u32[]{:S(2)}) collective-permute-start(f32[160,256]{1,0:T(8,128)} %get-tuple-element.66), channel_id=1, source_target_pairs={{0,3},{1,0},{2,1},{3,2},{4,7},{5,4},{6,5},{7,6},{8,11},{9,8},{10,9... | collective-permute-start | bytes 491528 | tf_op jit(solution)/shard_map/ppermute | solution.py:674
  58.2 1.6 %collective-permute-start.12 = (f32[128,256]{1,0:T(8,128)S(1)}, f32[128,256]{1,0:T(8,128)S(1)}, u32[]{:S(2)}, u32[]{:S(2)}) collective-permute-start(f32[128,256]{1,0:T(8,128)S(1)} %get-tuple-element.39.blocks.i0), channel_id=1, source_target_pairs={{0,2},{1,3},{2,0},{3,1},{4,6},{5,7},{6,4},{7,5},{8,10},{9,11},{10,... | collective-permute-start | bytes 393224 | tf_op jit(solution)/shard_map/ppermute | solution.py:674
  59.8 7.2 %all-to-all-done = f32[16,32,128]{2,1,0:T(8,128)S(1)} async-done(((f32[16,32,128]{2,1,0:T(8,128)}), f32[16,32,128]{2,1,0:T(8,128)S(1)}, u32[]{:S(2)}, u32[]{:S(2)}) %all-to-all-start) | async-done | bytes 262176 | tf_op jit(solution)/shard_map/all_to_all | solution.py:703
  67.0 0.0 collective-permute-done.10.e_lo.i1
  67.0 2.4 %collective-permute-start.7 = (f32[32,128]{1,0:T(8,128)S(1)}, f32[32,128]{1,0:T(8,128)S(1)}, u32[]{:S(2)}, u32[]{:S(2)}) collective-permute-start(f32[32,128]{1,0:T(8,128)S(1)} %reduce_sum.9.a0), channel_id=1, source_target_pairs={{0,1},{1,2},{2,3},{3,0},{4,5},{5,6},{6,7},{7,4},{8,9},{9,10},{10,1... | collective-permute-start | bytes 49160 | tf_op jit(solution)/shard_map/ppermute | solution.py:674
  69.5 0.0 collective-permute-done.11.e_hi.i2
  69.5 1.5 %collective-permute-start.8 = (f32[32,128]{1,0:T(8,128)S(1)}, f32[32,128]{1,0:T(8,128)S(1)}, u32[]{:S(2)}, u32[]{:S(2)}) collective-permute-start(f32[32,128]{1,0:T(8,128)S(1)} %reduce_sum.9.a0), channel_id=1, source_target_pairs={{0,3},{1,0},{2,1},{3,2},{4,7},{5,4},{6,5},{7,6},{8,11},{9,8},{10,9... | collective-permute-start | bytes 49160 | tf_op jit(solution)/shard_map/ppermute | solution.py:674
  71.0 0.0 collective-permute-done.13.h_near
  71.0 1.6 %collective-permute-start.9 = (f32[32,128]{1,0:T(8,128)S(1)}, f32[32,128]{1,0:T(8,128)S(1)}, u32[]{:S(2)}, u32[]{:S(2)}) collective-permute-start(f32[32,128]{1,0:T(8,128)S(1)} %reduce_sum.9.a0), channel_id=1, source_target_pairs={{0,2},{1,3},{2,0},{3,1},{4,6},{5,7},{6,4},{7,5},{8,10},{9,11},{10,... | collective-permute-start | bytes 49160 | tf_op jit(solution)/shard_map/ppermute | solution.py:674
  72.6 0.0 collective-permute-done.14.h_far
  72.6 4.2 %ready.1 = (f32[4,8,128,256]{3,2,1,0:T(8,128)S(1)}, f32[8,128,256]{2,1,0:T(8,128)S(1)}) custom-call(f32[4,8,128,256]{3,2,1,0:T(8,128)} %get-tuple-element.67.u2_hbm, f32[8,128,256]{2,1,0:T(8,128)} %get-tuple-element.68.gain_hbm, f32[2,128,256]{2,1,0:T(8,128)} %get-tuple-element.69.wxf_hbm, f32[16,256]{1,0:T(8,128)} %get-tuple-element.70.misc_hbm, ...), custom_call_target="tpu_custom_call" | custom-call | flops 10000000 | bytes 8000000 | tf_op jit(solution)/shard_map/ready/pallas_call | solution.py:593
  76.8 0.0 collective-permute-done.12.i3
  76.8 0.0 collective-permute-done.7.a1
  76.8 0.0 collective-permute-done.8.a2
  76.8 0.0 collective-permute-done.9.a3
  76.8 0.9 %blocks.1.own = f32[4,8,128]{2,1,0:T(8,128)S(1)} custom-call(f32[32,128]{1,0:T(8,128)S(1)} %reduce_sum.9.a0, f32[32,128]{1,0:T(8,128)S(1)} %collective-permute-done.7.a1, f32[32,128]{1,0:T(8,128)S(1)} %collective-permute-done.8.a2, f32[32,128]{1,0:T(8,128)S(1)} %collective-permute-done.9.a3, f32[128,256]{1,0:T(8,128)S(1)} %get-tuple-element.39.blocks.i0, ...), custom_call_target="tpu_custom_call" | custom-call | tf_op jit(solution)/shard_map/blocks/pallas_call | solution.py:544
  77.7 2.8 %collective-permute-start.15 = (f32[4,8,128]{2,1,0:T(8,128)S(1)}, f32[4,8,128]{2,1,0:T(8,128)S(1)}, u32[]{:S(2)}, u32[]{:S(2)}) collective-permute-start(f32[4,8,128]{2,1,0:T(8,128)S(1)} %blocks.1.own), channel_id=1, source_target_pairs={{0,8},{8,0},{1,9},{9,1},{2,10},{10,2},{3,11},{11,3},{4,12},{12,4},... | collective-permute-start | bytes 49160 | tf_op jit(solution)/shard_map/ppermute | solution.py:677
  80.5 0.8 collective-permute-done.15.got
  81.3 3.1 %correct.1 = (f32[4,8,128,256]{3,2,1,0:T(8,128)}, f32[4,512]{1,0:T(4,128)}) custom-call(s32[8,128]{1,0:T(8,128)S(1)} %copy-done.2, f32[4,8,128]{2,1,0:T(8,128)S(1)} %blocks.1.own, f32[4,8,128]{2,1,0:T(8,128)S(1)} %collective-permute-done.15.got, f32[4,8,128,256]{3,2,1,0:T(8,128)S(1)} %get-tuple-element.75.base, f32[8,128,256]{2,1,0:T(8,128)S(1)} %get-tuple-element.74.pull), custom_call_target="tpu_custom_call" | custom-call | tf_op jit(solution)/shard_map/correct/pallas_call | solution.py:645
  (2 shorter events, 0.0 us)
Async XLA Ops:
  0.6 14.1 %copy-start.2 = (s32[8,128]{1,0:T(8,128)S(1)}, s32[8,128]{1,0:T(8,128)}, u32[]{:S(2)}) copy-start(s32[8,128]{1,0:T(8,128)} %cmap.7) | copy-start | bytes 12292
  0.6 12.7 %copy-start.5 = (s32[4,2]{0,1:T(2,128)S(1)}, s32[4,2]{0,1:T(2,128)}, u32[]{:S(2)}) copy-start(s32[4,2]{0,1:T(2,128)} %param.14) | copy-start | bytes 100
  0.7 14.1 %copy-start.3 = (f32[2048]{0:T(1024)S(1)}, f32[2048]{0:T(1024)}, u32[]{:S(2)}) copy-start(f32[2048]{0:T(1024)} %param.12) | copy-start | bytes 24580
  2.6 15.9 %copy-start = (f32[776,256]{1,0:T(8,128)}, f32[776,256]{1,0:T(8,128)S(1)}, u32[]{:S(2)}) copy-start(f32[776,256]{1,0:T(8,128)S(1)} %get-tuple-element.40.near) | copy-start | bytes 2383876
  2.6 15.9 %copy-start.1 = (f32[776,256]{1,0:T(8,128)}, f32[776,256]{1,0:T(8,128)S(1)}, u32[]{:S(2)}) copy-start(f32[776,256]{1,0:T(8,128)S(1)} %get-tuple-element.41.far) | copy-start | bytes 2383876
  2.6 30.2 %collective-permute-start.2 = (f32[776,256]{1,0:T(8,128)S(1)}, f32[776,256]{1,0:T(8,128)S(1)}, u32[]{:S(2)}, u32[]{:S(2)}) collective-permute-start(f32[776,256]{1,0:T(8,128)S(1)} %get-tuple-element.40.near), channel_id=1, source_target_pairs={{0,8},{8,0},{1,9},{9,1},{2,10},{10,2},{3,11},{11,3},{4,12},{12,4},... | collective-permute-start | bytes 2383880 | tf_op jit(solution)/shard_map/ppermute | solution.py:677
  6.0 26.9 %collective-permute-start.3 = (f32[776,256]{1,0:T(8,128)S(1)}, f32[776,256]{1,0:T(8,128)S(1)}, u32[]{:S(2)}, u32[]{:S(2)}) collective-permute-start(f32[776,256]{1,0:T(8,128)S(1)} %get-tuple-element.41.far), channel_id=1, source_target_pairs={{8,16},{24,32},{40,48},{56,64},{72,80},{88,96},{104,112},{120,128}... | collective-permute-start | bytes 2383880 | tf_op jit(solution)/shard_map/ppermute | solution.py:681
  8.8 9.8 %collective-permute-start = (f32[56,256]{1,0:T(8,128)S(1)}, f32[56,256]{1,0:T(8,128)S(1)}, u32[]{:S(2)}, u32[]{:S(2)}) collective-permute-start(f32[56,256]{1,0:T(8,128)S(1)} %get-tuple-element.42.own_hi), channel_id=1, source_target_pairs={{0,1},{1,2},{2,3},{4,5},{5,6},{6,7},{8,9},{9,10},{10,11},{12,13},{... | collective-permute-start | bytes 172040 | tf_op jit(solution)/shard_map/ppermute | solution.py:668
  12.0 6.6 %collective-permute-start.1 = (f32[56,256]{1,0:T(8,128)S(1)}, f32[56,256]{1,0:T(8,128)S(1)}, u32[]{:S(2)}, u32[]{:S(2)}) collective-permute-start(f32[56,256]{1,0:T(8,128)S(1)} %get-tuple-element.43.own_lo), channel_id=1, source_target_pairs={{1,0},{2,1},{3,2},{5,4},{6,5},{7,6},{9,8},{10,9},{11,10},{13,12},{... | collective-permute-start | bytes 172040 | tf_op jit(solution)/shard_map/ppermute | solution.py:671
  18.6 14.2 %collective-permute-start.4 = (f32[8,256]{1,0:T(8,128)S(1)}, f32[8,256]{1,0:T(8,128)S(1)}, u32[]{:S(2)}, u32[]{:S(2)}) collective-permute-start(f32[8,256]{1,0:T(8,128)S(1)} %get-tuple-element.44), channel_id=1, source_target_pairs={{0,8},{8,0},{1,9},{9,1},{2,10},{10,2},{3,11},{11,3},{4,12},{12,4},... | collective-permute-start | bytes 24584 | tf_op jit(solution)/shard_map/ppermute | solution.py:677
  18.7 14.2 %collective-permute-start.5 = (f32[8,256]{1,0:T(8,128)S(1)}, f32[8,256]{1,0:T(8,128)S(1)}, u32[]{:S(2)}, u32[]{:S(2)}) collective-permute-start(f32[8,256]{1,0:T(8,128)S(1)} %get-tuple-element.45), channel_id=1, source_target_pairs={{8,16},{24,32},{40,48},{56,64},{72,80},{88,96},{104,112},{120,128}... | collective-permute-start | bytes 24584 | tf_op jit(solution)/shard_map/ppermute | solution.py:681
  22.6 10.3 %copy-start.4 = (f32[4]{0:T(128)S(1)}, f32[4]{0:T(128)}, u32[]{:S(2)}) copy-start(f32[4]{0:T(128)} %amplitudes.1) | copy-start | bytes 52
  38.4 32.6 %collective-permute-start.13 = (f32[4,128,256]{2,1,0:T(8,128)}, f32[4,128,256]{2,1,0:T(8,128)S(1)}, u32[]{:S(2)}, u32[]{:S(2)}) collective-permute-start(f32[4,128,256]{2,1,0:T(8,128)} %get-tuple-element.72), channel_id=1, source_target_pairs={{0,8},{8,0},{1,9},{9,1},{2,10},{10,2},{3,11},{11,3},{4,12},{12,4},... | collective-permute-start | bytes 1572872 | tf_op jit(solution)/shard_map/ppermute | solution.py:677
  38.5 34.0 %collective-permute-start.14 = (f32[4,128,256]{2,1,0:T(8,128)}, f32[4,128,256]{2,1,0:T(8,128)S(1)}, u32[]{:S(2)}, u32[]{:S(2)}) collective-permute-start(f32[4,128,256]{2,1,0:T(8,128)} %get-tuple-element.73), channel_id=1, source_target_pairs={{8,16},{24,32},{40,48},{56,64},{72,80},{88,96},{104,112},{120,128}... | collective-permute-start | bytes 1572872 | tf_op jit(solution)/shard_map/ppermute | solution.py:681
  43.6 1.3 %collective-permute-start.6 = (f32[32,128]{1,0:T(8,128)S(1)}, f32[32,128]{1,0:T(8,128)S(1)}, u32[]{:S(2)}, u32[]{:S(2)}) collective-permute-start(f32[32,128]{1,0:T(8,128)S(1)} %get-tuple-element.64), channel_id=1, source_target_pairs={{0,8},{8,0},{1,9},{9,1},{2,10},{10,2},{3,11},{11,3},{4,12},{12,4},... | collective-permute-start | bytes 49160 | tf_op jit(solution)/shard_map/ppermute | solution.py:677
  45.7 21.3 %all-to-all-start = ((f32[16,32,128]{2,1,0:T(8,128)}), f32[16,32,128]{2,1,0:T(8,128)S(1)}, u32[]{:S(2)}, u32[]{:S(2)}) async-start(f32[16,32,128]{2,1,0:T(8,128)} %spread.1), calls=%async_computation | async-start | bytes 524288 | tf_op jit(solution)/shard_map/all_to_all | solution.py:703
  54.5 12.6 %collective-permute-start.10 = (f32[160,256]{1,0:T(8,128)}, f32[160,256]{1,0:T(8,128)S(1)}, u32[]{:S(2)}, u32[]{:S(2)}) collective-permute-start(f32[160,256]{1,0:T(8,128)} %get-tuple-element.65), channel_id=1, source_target_pairs={{0,1},{1,2},{2,3},{3,0},{4,5},{5,6},{6,7},{7,4},{8,9},{9,10},{10,1... | collective-permute-start | bytes 491528 | tf_op jit(solution)/shard_map/ppermute | solution.py:674
  56.7 12.7 %collective-permute-start.11 = (f32[160,256]{1,0:T(8,128)}, f32[160,256]{1,0:T(8,128)S(1)}, u32[]{:S(2)}, u32[]{:S(2)}) collective-permute-start(f32[160,256]{1,0:T(8,128)} %get-tuple-element.66), channel_id=1, source_target_pairs={{0,3},{1,0},{2,1},{3,2},{4,7},{5,4},{6,5},{7,6},{8,11},{9,8},{10,9... | collective-permute-start | bytes 491528 | tf_op jit(solution)/shard_map/ppermute | solution.py:674
  58.2 18.5 %collective-permute-start.12 = (f32[128,256]{1,0:T(8,128)S(1)}, f32[128,256]{1,0:T(8,128)S(1)}, u32[]{:S(2)}, u32[]{:S(2)}) collective-permute-start(f32[128,256]{1,0:T(8,128)S(1)} %get-tuple-element.39.blocks.i0), channel_id=1, source_target_pairs={{0,2},{1,3},{2,0},{3,1},{4,6},{5,7},{6,4},{7,5},{8,10},{9,11},{10,... | collective-permute-start | bytes 393224 | tf_op jit(solution)/shard_map/ppermute | solution.py:674
  67.0 9.8 %collective-permute-start.7 = (f32[32,128]{1,0:T(8,128)S(1)}, f32[32,128]{1,0:T(8,128)S(1)}, u32[]{:S(2)}, u32[]{:S(2)}) collective-permute-start(f32[32,128]{1,0:T(8,128)S(1)} %reduce_sum.9.a0), channel_id=1, source_target_pairs={{0,1},{1,2},{2,3},{3,0},{4,5},{5,6},{6,7},{7,4},{8,9},{9,10},{10,1... | collective-permute-start | bytes 49160 | tf_op jit(solution)/shard_map/ppermute | solution.py:674
  69.5 7.3 %collective-permute-start.8 = (f32[32,128]{1,0:T(8,128)S(1)}, f32[32,128]{1,0:T(8,128)S(1)}, u32[]{:S(2)}, u32[]{:S(2)}) collective-permute-start(f32[32,128]{1,0:T(8,128)S(1)} %reduce_sum.9.a0), channel_id=1, source_target_pairs={{0,3},{1,0},{2,1},{3,2},{4,7},{5,4},{6,5},{7,6},{8,11},{9,8},{10,9... | collective-permute-start | bytes 49160 | tf_op jit(solution)/shard_map/ppermute | solution.py:674
  71.0 5.8 %collective-permute-start.9 = (f32[32,128]{1,0:T(8,128)S(1)}, f32[32,128]{1,0:T(8,128)S(1)}, u32[]{:S(2)}, u32[]{:S(2)}) collective-permute-start(f32[32,128]{1,0:T(8,128)S(1)} %reduce_sum.9.a0), channel_id=1, source_target_pairs={{0,2},{1,3},{2,0},{3,1},{4,6},{5,7},{6,4},{7,5},{8,10},{9,11},{10,... | collective-permute-start | bytes 49160 | tf_op jit(solution)/shard_map/ppermute | solution.py:674
  77.7 3.6 %collective-permute-start.15 = (f32[4,8,128]{2,1,0:T(8,128)S(1)}, f32[4,8,128]{2,1,0:T(8,128)S(1)}, u32[]{:S(2)}, u32[]{:S(2)}) collective-permute-start(f32[4,8,128]{2,1,0:T(8,128)S(1)} %blocks.1.own), channel_id=1, source_target_pairs={{0,8},{8,0},{1,9},{9,1},{2,10},{10,2},{3,11},{11,3},{4,12},{12,4},... | collective-permute-start | bytes 49160 | tf_op jit(solution)/shard_map/ppermute | solution.py:677

commit v3 on v2

--- a/solution.py
+++ b/solution.py
@@ -138,11 +138,17 @@
     return 1 - core, core
 
 
+def has_elecs():
+    elec = lax.axis_index("elec")
+    last = lax.axis_size("elec") - 1
+    return jnp.where(elec > 0, 1.0, 0.0), jnp.where(elec < last, 1.0, 0.0)
+
+
 def edges_kernel(
-    u_hbm, c_hbm, imp_hbm, cmap_hbm, out_lo, out_hi, near_out, far_out, blocks, u, c, cmap, imp, sems, whole_sems
+    u_hbm, c_hbm, imp_hbm, cmap_hbm, out_lo, out_hi, near_out, far_out, blocks, u, c, cmap, imp, side_by_side, sems, whole_sems
 ):
     core = lax.axis_index("core")
-    copies = [pltpu.make_async_copy(cmap_hbm, cmap, sems.at[4])]
+    copies = []
     for n, y in enumerate((0, 120)):
         copies.append(pltpu.make_async_copy(u_hbm.at[:, :, pl.ds(y, 8)], u.at[n], sems.at[2 * n]))
         copies.append(pltpu.make_async_copy(c_hbm.at[:, pl.ds(y, 8)], c.at[n], sems.at[2 * n + 1]))
@@ -152,14 +158,22 @@
             whole.append((u_hbm.at[s, 7 * side], out.at[pl.ds(128 * s, 128)], whole_sems.at[n, s]))
         whole.append((c_hbm.at[7 * side], out.at[pl.ds(ROW_C, 128)], whole_sems.at[n, 4]))
         whole.append((c_hbm.at[1 + 5 * side], out.at[pl.ds(ROW_C2, 128)], whole_sems.at[n, 5]))
-    whole.append((imp_hbm.at[2 * core], imp.at[0], whole_sems.at[0, 7]))
-    whole.append((imp_hbm.at[2 * core + 1], imp.at[1], whole_sems.at[1, 7]))
+    rows_of_blocks = [
+        pltpu.make_async_copy(imp_hbm.at[2 * core + n], imp.at[n], whole_sems.at[n, 7]) for n in range(2)
+    ]
     whole = [pltpu.make_async_copy(*copy) for copy in whole]
-    for copy in copies + whole:
+    copies.append(pltpu.make_async_copy(cmap_hbm, cmap, sems.at[4]))
+    for copy in copies + rows_of_blocks + whole:
         copy.start()
-    for copy in copies:
+    for copy in copies + rows_of_blocks:
         copy.wait()
+    side_by_side[:, 0:128] = imp[0]
+    side_by_side[:, 128:256] = imp[1]
+    copy_blocks = pltpu.make_async_copy(side_by_side, blocks, sems.at[5])
+    copy_blocks.start()
     for n, out, near, far, lane in ((0, out_lo, 0, 1, 0), (1, out_hi, 7, 6, 127)):
+        out[56:184, 0:128] = imp[0]
+        out[56:184, 128:256] = imp[1]
         for x in range(8):
             for s in range(4):
                 out[8 * s + x : 8 * s + x + 1, :] = u[n, s, x, near : near + 1, :]
@@ -172,22 +186,22 @@
         out[ROW_MAP : ROW_MAP + 1, 0:128] = cmap[pl.ds(7 * side, 1), :].astype(F32)
     for copy in whole:
         copy.wait()
-    blocks[:, 0:128] = imp[0]
-    blocks[:, 128:256] = imp[1]
+    copy_blocks.wait()
 
 
 def edges(u, c, impedance, cmap):
     return pl.pallas_call(
         edges_kernel,
         in_specs=[hbm()] * 4,
-        out_specs=[vmem()] * 5,
-        out_shape=[f32(56, 256), f32(56, 256), f32(ROWS, 256), f32(ROWS, 256), f32(128, 256)],
+        out_specs=[vmem()] * 4 + [hbm()],
+        out_shape=[f32(184, 256), f32(184, 256), f32(ROWS, 256), f32(ROWS, 256), stored(128, 256)],
         scratch_shapes=[
             pltpu.VMEM((2, 4, 8, 8, 256), F32),
             pltpu.VMEM((2, 8, 8, 256), F32),
             pltpu.VMEM((8, 128), jnp.int32),
             pltpu.VMEM((2, 128, 128), F32),
-            pltpu.SemaphoreType.DMA((5,)),
+            pltpu.VMEM((128, 256), F32),
+            pltpu.SemaphoreType.DMA((6,)),
             pltpu.SemaphoreType.DMA((2, 8)),
         ],
         compiler_params=params(4),
@@ -196,10 +210,11 @@
 
 
 def corners_kernel(y_lo, y_hi, near_out, far_out):
+    below, above = has_elecs()
     for out, side in zip((near_out, far_out), sides()):
         out[...] = jnp.zeros((8, 256), F32)
-        out[0:1, :] = y_lo[pl.ds(32 + 7 * side, 1), :]
-        out[1:2, :] = y_hi[pl.ds(32 + 7 * side, 1), :]
+        out[0:1, :] = below * y_lo[pl.ds(32 + 7 * side, 1), :]
+        out[1:2, :] = above * y_hi[pl.ds(32 + 7 * side, 1), :]
 
 
 def corners(y_lo, y_hi):
@@ -213,12 +228,22 @@
     )(y_lo, y_hi)
 
 
-def weights_kernel(u_hbm, f_hbm, c_hbm, cmap, admittance, u, f, wx, wy, wz, diag, zeta_t, c, sems):
+def weights_kernel(
+    u_hbm, f_hbm, c_hbm, cmap_hbm, admittance_hbm, u, f, wx, wy, wz, diag, zeta_t, c, cmap, admittance, sems
+):
+    small = [
+        pltpu.make_async_copy(cmap_hbm, cmap, sems.at[3]),
+        pltpu.make_async_copy(admittance_hbm, admittance, sems.at[4]),
+    ]
     copy = pltpu.make_async_copy(c_hbm, c, sems.at[0])
     later = [pltpu.make_async_copy(u_hbm, u, sems.at[1]), pltpu.make_async_copy(f_hbm, f, sems.at[2])]
+    for other in small:
+        other.start()
     copy.start()
     for other in later:
         other.start()
+    for other in small:
+        other.wait()
     zeta = gather_rows(cmap[...], admittance[...])
     zeta_t[...] = jnp.transpose(jnp.concatenate([zeta, jnp.zeros((120, 128), F32)], axis=0))
     copy.wait()
@@ -247,10 +272,15 @@
     ]
     return pl.pallas_call(
         weights_kernel,
-        in_specs=[hbm()] * 3 + [vmem()] * 2,
+        in_specs=[hbm()] * 5,
         out_specs=[vmem()] * len(outs),
         out_shape=outs,
-        scratch_shapes=[pltpu.VMEM((8, 128, 256), F32), pltpu.SemaphoreType.DMA((3,))],
+        scratch_shapes=[
+            pltpu.VMEM((8, 128, 256), F32),
+            pltpu.VMEM((8, 128), jnp.int32),
+            pltpu.VMEM((16, 128), F32),
+            pltpu.SemaphoreType.DMA((5,)),
+        ],
         compiler_params=params(8),
         cost_estimate=pl.CostEstimate(flops=20_000_000, bytes_accessed=6_000_000, transcendentals=0),
         name="weights",
@@ -259,11 +289,12 @@
 
 def inner_kernel(
     u, f, cmap, own_lo, own_hi, y_lo, y_hi, wx, wy, wz, diag,
-    u2, gain, wyl, wyh, pulled1, keep1, pulled2, edge_lo, edge_hi, contact,
-    u1, sums,
+    u2, u2_out, gain, wyl, wyh, pulled1, keep1, pulled2, edge_lo, edge_hi, contact,
+    u1, sums, middle, sems,
 ):
-    wyl[...] = outer_face(own_lo[32:40, :], y_lo[32:40, :])
-    wyh[...] = outer_face(own_hi[32:40, :], y_hi[32:40, :])
+    below, above = has_elecs()
+    wyl[...] = outer_face(own_lo[32:40, :], below * y_lo[32:40, :])
+    wyh[...] = outer_face(own_hi[32:40, :], above * y_hi[32:40, :])
     for x in range(8):
         gain[x] = diag[x]
         gain[x, 0:1, :] = gain[x, 0:1, :] + wyl[x : x + 1, :]
@@ -305,48 +336,58 @@
         u1[s, 0] = jnp.zeros((128, 256), F32)
         u1[s, 7] = jnp.zeros((128, 256), F32)
 
-    def second(x, carry):
+    def second(x, target):
         slabs = []
         for s in range(4):
             pulled = f[s, x] + in_line(wy[x], u1[s, x], 0)
             pulled = pulled + in_line(wz[x], u1[s, x], 1)
             pulled = pulled + wx[x - 1] * u1[s, x - 1] + wx[x] * u1[s, x + 1]
             new = KEEP * u1[s, x] + gain[x] * pulled
-            u2[s, x - 1] = new
+            target[s] = new
             slabs.append(new)
         sums[x] = row_sums(slabs)
+
+    def second_middle(x, carry):
+        second(x, middle.at[x - 2])
+        pltpu.make_async_copy(middle.at[x - 2], u2_out.at[:, x - 2], sems.at[x - 2]).start()
         return carry
 
-    lax.fori_loop(1, 7, second, 0)
+    lax.fori_loop(2, 6, second_middle, 0)
+    second(1, u2.at[0])
+    second(6, u2.at[1])
     contact[...] = scatter([cmap[x : x + 1, :] for x in range(1, 7)], [sums[x] for x in range(1, 7)])
+    for n in range(4):
+        pltpu.make_async_copy(middle.at[n], u2_out.at[:, n], sems.at[n]).wait()
 
 
 def inner(u, f, cmap, own_lo, own_hi, y_lo, y_hi, wx, wy, wz, diag):
     outs = [
-        kept(4, 6, 128, 256), kept(8, 128, 256), kept(8, 256), kept(8, 256),
+        kept(2, 4, 128, 256), stored(4, 4, 128, 256), kept(8, 128, 256), kept(8, 256), kept(8, 256),
         kept(2, 4, 128, 256), kept(2, 4, 128, 256), kept(2, 4, 128, 256),
         kept(32, 256), kept(32, 256), kept(64, 128),
     ]
     return pl.pallas_call(
         inner_kernel,
         in_specs=[vmem()] * 11,
-        out_specs=[vmem()] * len(outs),
+        out_specs=[vmem(), hbm()] + [vmem()] * (len(outs) - 2),
         out_shape=outs,
         scratch_shapes=[
             pltpu.VMEM((4, 8, 128, 256), F32),
             pltpu.VMEM((8, 4, 128), F32),
+            pltpu.VMEM((4, 4, 128, 256), F32),
+            pltpu.SemaphoreType.DMA((4,)),
         ],
-        compiler_params=params(12),
+        compiler_params=params(16),
         cost_estimate=pl.CostEstimate(flops=100_000_000, bytes_accessed=25_000_000, transcendentals=0),
         name="inner",
     )(u, f, cmap, own_lo, own_hi, y_lo, y_hi, wx, wy, wz, diag)
 
 
 def outer_kernel(
-    pairs, amplitudes, cmap, admittance, blocks, near, far, y_lo, y_hi, x_near, x_far, ends_near, ends_far,
+    pairs, amplitudes, cmap, admittance, near, far, y_lo, y_hi, x_near, x_far, ends_near, ends_far,
     wx, wy, wz, gain, wyl, wyh, u2, pulled1, keep1, pulled2, e_lo, e_hi, contact, zeta_in,
-    face_near_out, face_far_out, edge_lo_out, edge_hi_out, u2_out, gain_out, wxf_out, misc_out, zeta_out, mine, other,
-    ids, face_near, face_far, edge_lo, edge_hi, u2b, gain_b, wxf, misc, c_own, sems, u2_sems,
+    face_near_out, face_far_out, edge_lo_out, edge_hi_out, u2_out, gain_out, wxf_out, misc_out, zeta_out, mine,
+    ids, face_near, face_far, edge_lo, edge_hi, u2b, gain_b, wxf, misc, c_own, passed, sems, u2_sems, near_sems, edge_sems,
 ):
     copies = []
     rows_in = [
@@ -363,7 +404,6 @@
 
     send(gain.at[pl.ds(1, 6)], gain_out.at[pl.ds(1, 6)], sems.at[0])
     send(zeta_in, zeta_out, sems.at[1])
-    send(u2.at[:, pl.ds(1, 4)], u2_out.at[:, pl.ds(2, 4)], sems.at[2])
     misc[0:8, :] = wyl[...]
     misc[8:16, :] = wyh[...]
     send(misc, misc_out, sems.at[3])
@@ -393,7 +433,11 @@
         gain_b[n] = g
         for s in range(4):
             out[s] = keep1[side, s] + g * (pulled1[side, s] + outside * msg[128 * s : 128 * s + 128, :])
-        send(out, sent, sems.at[4 + n])
+        if n:
+            send(out, sent, sems.at[4])
+        else:
+            for s in range(4):
+                send(out.at[s], sent.at[pl.ds(128 * s, 128)], near_sems.at[s])
         send(gain_b.at[n], gain_out.at[x], sems.at[6 + n])
         spare = jnp.maximum(there, TINY)
         diag = both_sides(line_weight(spare, 0), 0) + both_sides(line_weight(spare, 1), 1) + zeta_t[:, n : n + 1]
@@ -408,9 +452,9 @@
         slabs = []
         for s in range(4):
             new = factor * out[s]
-            u2b[2 * n + 1, s] = u2[s, 5 * side] + new
+            u2b[2 * n + 1, s] = u2[side, s] + new
             slabs.append(new)
-        send(u2b.at[2 * n + 1], u2_out.at[:, inside], u2_sems.at[2 * n + 1])
+        send(u2b.at[2 * n + 1], u2_out.at[2 * side + 1], u2_sems.at[2 * n + 1])
         id_rows.append(cmap[pl.ds(inside, 1), :])
         values.append(row_sums(slabs))
         slabs = []
@@ -420,7 +464,7 @@
             new = KEEP * out[s] + g * pulled
             u2b[2 * n, s] = new
             slabs.append(new)
-        send(u2b.at[2 * n], u2_out.at[:, x], u2_sems.at[2 * n])
+        send(u2b.at[2 * n], u2_out.at[2 * side], u2_sems.at[2 * n])
         id_rows.append(cmap[pl.ds(x, 1), :])
         values.append(row_sums(slabs))
 
@@ -434,8 +478,7 @@
         for s in range(4):
             for side, out in zip(sides(), (face_near, face_far)):
                 edge[pl.ds(8 * s + 7 * side, 1), :] = out[s, y : y + 1, :]
-        edge[32:160, :] = blocks[...]
-        send(edge, sent, sems.at[9 + n])
+        send(edge, sent, edge_sems.at[n])
         there = msg[32:40, :]
         x_rows = iota((8, 256), 0)
         spare = jnp.maximum(there, TINY)
@@ -460,42 +503,47 @@
     adds = jnp.logical_and(adds, lax.axis_index("core") == 0)
     for s in range(4):
         at = place % 4 == s
-        amount = jnp.where(adds, amplitudes[s], 0.0)
-        total = total + jnp.where(at & (electrode == pairs[2 * s]), amount, 0.0)
-        total = total - jnp.where(at & (electrode == pairs[2 * s + 1]), amount, 0.0)
+        amount = jnp.where(adds, amplitudes[0:1, s : s + 1], 0.0)
+        total = total + jnp.where(at & (electrode == pairs[0:1, s : s + 1]), amount, 0.0)
+        total = total - jnp.where(at & (electrode == pairs[1:2, s : s + 1]), amount, 0.0)
     first_half = lax.axis_index("core") == 0
     mine[...] = jnp.where(first_half, total[0:32], total[32:64])
-    other[...] = jnp.where(first_half, total[32:64], total[0:32])
+    passed[:, 0:128] = jnp.where(first_half, total[32:48], total[0:16])
+    passed[:, 128:256] = jnp.where(first_half, total[48:64], total[16:32])
+    send(passed, face_near_out.at[pl.ds(512, 16)], sems.at[10])
     for copy in copies:
         copy.wait()
 
 
 def outer(pairs, amplitudes, *args):
     outs = [
-        stored(4, 128, 256), stored(4, 128, 256), stored(160, 256), stored(160, 256),
-        stored(4, 8, 128, 256), stored(8, 128, 256), stored(2, 128, 256), stored(16, 256), stored(128, 128),
-        f32(32, 128), f32(32, 128),
+        stored(528, 256), stored(4, 128, 256), stored(32, 256), stored(32, 256),
+        stored(4, 4, 128, 256), stored(8, 128, 256), stored(2, 128, 256), stored(16, 256), stored(128, 128),
+        f32(32, 128),
     ]
     specs = [vmem()] * len(args)
-    specs[3] = specs[4] = hbm()
+    specs[2] = specs[3] = hbm()
     return pl.pallas_call(
         outer_kernel,
-        in_specs=[pl.BlockSpec(memory_space=pltpu.SMEM)] * 2 + specs,
-        out_specs=[hbm()] * 9 + [vmem()] * 2,
+        in_specs=[vmem()] * 2 + specs,
+        out_specs=[hbm()] * 9 + [vmem()],
         out_shape=outs,
         scratch_shapes=[
             pltpu.VMEM((8, 128), jnp.int32),
             pltpu.VMEM((4, 128, 256), F32),
             pltpu.VMEM((4, 128, 256), F32),
-            pltpu.VMEM((160, 256), F32),
-            pltpu.VMEM((160, 256), F32),
+            pltpu.VMEM((32, 256), F32),
+            pltpu.VMEM((32, 256), F32),
             pltpu.VMEM((4, 4, 128, 256), F32),
             pltpu.VMEM((2, 128, 256), F32),
             pltpu.VMEM((2, 128, 256), F32),
             pltpu.VMEM((16, 256), F32),
             pltpu.VMEM((2, 128, 256), F32),
+            pltpu.VMEM((16, 256), F32),
             pltpu.SemaphoreType.DMA((13,)),
             pltpu.SemaphoreType.DMA((4,)),
+            pltpu.SemaphoreType.DMA((4,)),
+            pltpu.SemaphoreType.DMA((2,)),
         ],
         compiler_params=params(32),
         cost_estimate=pl.CostEstimate(flops=50_000_000, bytes_accessed=15_000_000, transcendentals=0),
@@ -503,8 +551,12 @@
     )(pairs, amplitudes, *args)
 
 
-def spread_kernel(mine, got, out, both, sems):
-    both[...] = mine[...] + got[...]
+def spread_kernel(mine, got_hbm, out, both, got, got_sem, sems):
+    copy = pltpu.make_async_copy(got_hbm.at[pl.ds(512, 16)], got, got_sem)
+    copy.start()
+    copy.wait()
+    both[0:16, :] = mine[0:16, :] + got[:, 0:128]
+    both[16:32, :] = mine[16:32, :] + got[:, 128:256]
     copies = [pltpu.make_async_copy(both, out.at[n], sems.at[n]) for n in range(out.shape[0])]
     for copy in copies:
         copy.start()
@@ -515,22 +567,57 @@
 def spread(mine, got, count):
     return pl.pallas_call(
         spread_kernel,
-        in_specs=[vmem()] * 2,
+        in_specs=[vmem(), pl.BlockSpec(memory_space=pl.ANY)],
         out_specs=hbm(),
         out_shape=stored(count, 32, 128),
-        scratch_shapes=[pltpu.VMEM((32, 128), F32), pltpu.SemaphoreType.DMA((count,))],
+        scratch_shapes=[
+            pltpu.VMEM((32, 128), F32),
+            pltpu.VMEM((16, 256), F32),
+            pltpu.SemaphoreType.DMA,
+            pltpu.SemaphoreType.DMA((count,)),
+        ],
         compiler_params=params(2),
         name="spread",
     )(mine, got)
 
 
+def gathered_kernel(parts_hbm, edge_lo, edge_hi, to_above, to_below, out, parts, sems, edge_sems):
+    copies = [pltpu.make_async_copy(parts_hbm.at[n], parts.at[n], sems.at[n]) for n in range(parts.shape[0])]
+    for n, (source, target) in enumerate(((edge_hi, to_above), (edge_lo, to_below))):
+        copies.append(pltpu.make_async_copy(source, target.at[pl.ds(16, 32)], edge_sems.at[n]))
+    for copy in copies:
+        copy.start()
+    for copy in copies:
+        copy.wait()
+    total = jnp.sum(parts[...], axis=0)
+    for target in (out, to_above, to_below):
+        target[0:16, 0:128] = total[0:16]
+        target[0:16, 128:256] = total[16:32]
+
+
+def gathered(parts, edge_lo, edge_hi):
+    return pl.pallas_call(
+        gathered_kernel,
+        in_specs=[hbm()] * 3,
+        out_specs=[vmem()] * 3,
+        out_shape=[f32(48, 256), f32(48, 256), f32(16, 256)],
+        scratch_shapes=[
+            pltpu.VMEM(parts.shape, F32),
+            pltpu.SemaphoreType.DMA((parts.shape[0],)),
+            pltpu.SemaphoreType.DMA((2,)),
+        ],
+        compiler_params=params(4),
+        name="gathered",
+    )(parts, edge_lo, edge_hi)
+
+
 def blocks_kernel(a0, a1, a2, a3, i0, i1, i2, i3, pull, out, charges):
     elec = lax.axis_index("elec")
-    total = a0[...] + a1[...] + a2[...] + a3[...]
+    total = a0[0:16, :] + a1[0:16, :] + a2[...] + a3[0:16, :]
     for e in range(4):
-        charges[e] = total[8 * e : 8 * e + 8]
+        charges[e] = total[8 * (e % 2) : 8 * (e % 2) + 8, 128 * (e // 2) : 128 * (e // 2) + 128]
     upper = iota((8, 128), 0) < 4
-    for turn, blocks in ((0, i0), (3, i1), (1, i2), (2, i3)):
+    for turn, blocks in ((3, i0), (1, i1), (0, i2), (2, i3)):
         e = lax.rem(elec + turn, 4)
         charge = charges[e]
         start = blocks.shape[0] - 128
@@ -553,11 +640,13 @@
 
 
 def ready_kernel(
-    u2_hbm, gain_hbm, wxf_hbm, misc_hbm, zeta_hbm, h_near, h_far, e_lo, e_hi, base, pull,
+    after, inner_hbm, outer_hbm, gain_hbm, wxf_hbm, misc_hbm, zeta_hbm, base, pull, sides_out, rows_out,
     gain, wxf, misc, zeta_t, sems, small_sems,
 ):
     order = (2, 3, 4, 5, 1, 6, 0, 7)
-    copies = {x: pltpu.make_async_copy(u2_hbm.at[:, x], base.at[:, x], sems.at[x]) for x in order}
+    rows = {x: inner_hbm.at[:, x - 2] for x in range(2, 6)}
+    rows.update({x: outer_hbm.at[n] for n, x in enumerate((0, 1, 7, 6))})
+    copies = {x: pltpu.make_async_copy(rows[x], base.at[:, x], sems.at[x]) for x in order}
     small = [
         pltpu.make_async_copy(source, target, small_sems.at[n])
         for n, (source, target) in enumerate(
@@ -574,17 +663,13 @@
         g = gain[x]
         part = (1.0 / OMEGA) * zeta_t[:, x : x + 1] * g
         pull[x] = part
-        low = g[0:1] * misc[x : x + 1, :]
-        high = g[127:128] * misc[8 + x : 9 + x, :]
+        sides_out[x : x + 1, :] = (1.0 - part[0:1]) * g[0:1] * misc[x : x + 1, :]
+        sides_out[8 + x : 9 + x, :] = (1.0 - part[127:128]) * g[127:128] * misc[8 + x : 9 + x, :]
         copies[x].wait()
-        for s in range(4):
-            at = 8 * s + x
-            if x in (0, 7):
-                from_near = sides()[0] == x // 7
-                halo = jnp.where(from_near, wxf[0] * h_near[s], wxf[1] * h_far[s])
-                base[s, x] = base[s, x] + g * halo
-            base[s, x, 0:1, :] = base[s, x, 0:1, :] + low * e_lo[at : at + 1, :]
-            base[s, x, 127:128, :] = base[s, x, 127:128, :] + high * e_hi[at : at + 1, :]
+        if x in (0, 7):
+            n = jnp.where(sides()[0] == x // 7, 0, 1)
+            rows_out[x // 7] = (1.0 - part) * g * wxf[n]
+        for s in range(4):
             u = base[s, x]
             base[s, x] = u - part * u
 
@@ -592,9 +677,9 @@
 def ready(*args):
     return pl.pallas_call(
         ready_kernel,
-        in_specs=[hbm()] * 5 + [vmem()] * 4,
-        out_specs=[vmem()] * 2,
-        out_shape=[kept(4, 8, 128, 256), kept(8, 128, 256)],
+        in_specs=[pl.BlockSpec(memory_space=pl.ANY)] + [hbm()] * 6,
+        out_specs=[vmem()] * 4,
+        out_shape=[kept(4, 8, 128, 256), kept(8, 128, 256), kept(16, 256), kept(2, 128, 256)],
         scratch_shapes=[
             pltpu.VMEM((8, 128, 256), F32),
             pltpu.VMEM((2, 128, 256), F32),
@@ -609,7 +694,9 @@
     )(*args)
 
 
-def correct_kernel(cmap, own, got, base, pull, out_hbm, volts, table, buf, sems):
+def correct_kernel(
+    cmap, own, got, base, pull, weight, row_weight, e_lo, e_hi, h_near, h_far, out_hbm, volts, table, buf, sems
+):
     core = lax.axis_index("core")
     elec = lax.axis_index("elec")
     table[core] = own[...]
@@ -631,9 +718,19 @@
     stacked = jnp.concatenate(touched + [jnp.zeros((96, 128), F32)], axis=0)
     volts_t = jnp.transpose(stacked)
     copies = []
-    for x in range(8):
-        for s in range(4):
-            buf[s, x] = base[s, x] + pull[x] * volts_t[:, 8 * s + x : 8 * s + x + 1]
+    near_side = sides()[0]
+    for x in (1, 2, 3, 4, 5, 6, 0, 7):
+        for s in range(4):
+            at = 8 * s + x
+            new = base[s, x] + pull[x] * volts_t[:, at : at + 1]
+            if x in (0, 7):
+                halo = jnp.where(near_side == x // 7, h_near[128 * s : 128 * s + 128, :], h_far[s])
+                new = new + row_weight[x // 7] * halo
+            buf[s, x] = new
+            low = weight[x : x + 1, :] * e_lo[16 + at : 17 + at, :]
+            high = weight[8 + x : 9 + x, :] * e_hi[16 + at : 17 + at, :]
+            buf[s, x, 0:1, :] = buf[s, x, 0:1, :] + low
+            buf[s, x, 127:128, :] = buf[s, x, 127:128, :] + high
         copy = pltpu.make_async_copy(buf.at[:, x], out_hbm.at[:, x], sems.at[x])
         copy.start()
         copies.append(copy)
@@ -644,7 +741,7 @@
 def correct(*args):
     return pl.pallas_call(
         correct_kernel,
-        in_specs=[vmem()] * 5,
+        in_specs=[vmem()] * 11,
         out_specs=[hbm(), vmem()],
         out_shape=[f32(4, 8, 128, 256), f32(4, 512)],
         scratch_shapes=[
@@ -664,12 +761,6 @@
     admittance = admittance.reshape(16, 128)
     u, f, c, impedance = in_hbm(u), in_hbm(f), in_hbm(c), in_hbm(impedance)
 
-    def from_below(a):
-        return lax.ppermute(a, "elec", [(i, i + 1) for i in range(elecs - 1)])
-
-    def from_above(a):
-        return lax.ppermute(a, "elec", [(i + 1, i) for i in range(elecs - 1)])
-
     def rotated(a, turn):
         return lax.ppermute(a, "elec", [(i, (i + turn) % elecs) for i in range(elecs)])
 
@@ -681,8 +772,8 @@
         return lax.ppermute(a, TILE, pairs + [(j, i) for i, j in pairs])
 
     own_lo, own_hi, row_near, row_far, side = edges(u, c, impedance, in_hbm(cmap))
-    y_lo = from_below(own_hi)
-    y_hi = from_above(own_lo)
+    y_lo = rotated(own_hi, 1)
+    y_hi = rotated(own_lo, elecs - 1)
     x_far = far(row_far)
     x_near = near(row_near)
     opposite = rotated(side, 2)
@@ -690,29 +781,28 @@
     ends_far = far(ends_far)
     ends_near = near(ends_near)
 
-    u, f, wx, wy, wz, diag, zeta_t = weights(u, f, c, cmap, admittance)
-    u2, gain, wyl, wyh, pulled1, keep1, pulled2, e_lo, e_hi, contact = inner(
+    u, f, wx, wy, wz, diag, zeta_t = weights(u, f, c, in_hbm(cmap), in_hbm(admittance))
+    u2, u2_inner, gain, wyl, wyh, pulled1, keep1, pulled2, e_lo, e_hi, contact = inner(
         u, f, cmap, own_lo, own_hi, y_lo, y_hi, wx, wy, wz, diag
     )
-    face_near, face_far, edge_lo, edge_hi, u2, gain, wxf, misc, zeta_t, mine, other = outer(
-        pairs.reshape(-1), amplitudes, cmap, admittance, side, in_hbm(row_near), in_hbm(row_far),
+    face_near, face_far, edge_lo, edge_hi, u2_outer, gain, wxf, misc, zeta_t, mine = outer(
+        pairs.T, amplitudes.reshape(1, -1), cmap, admittance, in_hbm(row_near), in_hbm(row_far),
         y_lo, y_hi, x_near, x_far, ends_near, ends_far,
         wx, wy, wz, gain, wyl, wyh, u2, pulled1, keep1, pulled2, e_lo, e_hi, contact, zeta_t,
     )
-    parts = spread(mine, near(other), groups)
-    parts = lax.all_to_all(parts, "zx", 0, 0, tiled=True)
-    summed = jnp.sum(parts, axis=0)
     h_far = far(face_far)
     h_near = near(face_near)
-    e_lo = rotated(edge_hi, 1)
-    e_hi = rotated(edge_lo, elecs - 1)
-    base, pull = ready(
-        in_hbm(u2), in_hbm(gain), in_hbm(wxf), in_hbm(misc), in_hbm(zeta_t), h_near, h_far, e_lo, e_hi
+    parts = spread(mine, h_near, groups)
+    parts = lax.all_to_all(parts, "zx", 0, 0, tiled=True)
+    to_above, to_below, summed = gathered(in_hbm(parts), in_hbm(edge_lo), in_hbm(edge_hi))
+    base, pull, weight, row_weight = ready(
+        summed, in_hbm(u2_inner), in_hbm(u2_outer), in_hbm(gain), in_hbm(wxf), in_hbm(misc), in_hbm(zeta_t)
     )
-    around = (summed, rotated(summed, 1), rotated(summed, elecs - 1), rotated(summed, 2))
-    own = blocks(around, (side, e_lo, e_hi, opposite), pull)
+    e_lo = rotated(to_above, 1)
+    e_hi = rotated(to_below, elecs - 1)
+    own = blocks((e_lo, e_hi, summed, rotated(summed, 2)), (y_lo, y_hi, side, opposite), pull)
     got = near(own)
-    out, volts = correct(cmap, own, got, base, pull)
+    out, volts = correct(cmap, own, got, base, pull, weight, row_weight, e_lo, e_hi, h_near, h_far)
     return out, volts
 
 

time: 85 us -> 80.4 us (0.946)
  starting transfers between devices: 42.2 us -> 39.7 us
  waiting for transfers between devices: 9.23 us -> 7.6 us
    ppermute x2 -> x0, starting transfers between devices: 4.5 us -> none  [the longest x1 3.2 us: from_below(): return lax.ppermute(a, 'elec', [(i, i + 1) for i in range(elecs - 1)])]
    all_to_all x1, waiting for transfers between devices: 7.18 us -> 4.6 us  [per_device(): parts = lax.all_to_all(parts, 'zx', 0, 0, tiled=True)]
    ppermute x3, starting transfers between devices: 11.7 us -> 13.2 us  [far(): return lax.ppermute(a, TILE, pairs + [(j, i) for i, j in pairs])]
    all_to_all x1, starting transfers between devices: 8.74 us -> 9.86 us  [per_device(): parts = lax.all_to_all(parts, 'zx', 0, 0, tiled=True)]
    ppermute x5 -> x4, waiting for transfers between devices: 2.02 us -> 2.97 us  [near(): return lax.ppermute(a, 'core', [(0, 1), (1, 0)])]
    ppermute x6, starting transfers between devices: 10.9 us -> 9.95 us  [rotated(): lax.ppermute(a, 'elec', [(i, (i + turn) % elecs) for i in range(elecs)])]
    pallas_call x7 -> x8, Pallas kernels: 29.6 us -> 29.9 us  [the longest x1 9.77 us: inner(): pl.pallas_call(inner_kernel, in_specs=[vmem()] * 11, out_specs=[vmem(), h...]
    ppermute x5 -> x4, starting transfers between devices: 6.38 us -> 6.64 us  [near(): return lax.ppermute(a, 'core', [(0, 1), (1, 0)])]
  transfers between devices with their start and end apart: 17 -> 14, of which waited for: 3 -> 3; matrix products, arithmetic and copies ran while one was open for 2% -> 0% of each run, Pallas kernels for 23% -> 24%
where the time goes in v3:
time: 80.4 us; the launch traced here: 80 us
  starting transfers between devices  39.7 us (49%)
  Pallas kernels  30.9 us (38%)
  waiting for transfers between devices  7.6 us (9%)
  between operations  1.09 us (1%)
    ppermute x3, starting transfers between devices, far(): return lax.ppermute(a, TILE, pairs + [(j, i) for i, j in pairs])  13.2 us
    ppermute x6, starting transfers between devices, rotated(): lax.ppermute(a, 'elec', [(i, (i + turn) % elecs) for i in range(elecs)])  9.95 us
    all_to_all x1, starting transfers between devices, per_device(): parts = lax.all_to_all(parts, 'zx', 0, 0, tiled=True)  9.86 us
    pallas_call x1, Pallas kernels, inner(): pl.pallas_call(inner_kernel, in_specs=[vmem()] * 11, out_specs=[vmem(), h...  9.77 us
    ppermute x4, starting transfers between devices, near(): return lax.ppermute(a, 'core', [(0, 1), (1, 0)])  6.64 us
    pallas_call x1, Pallas kernels, outer(): pl.pallas_call(outer_kernel, in_specs=[vmem()] * 2 + specs, out_specs=[hb...  5.04 us
    all_to_all x1, waiting for transfers between devices, per_device(): parts = lax.all_to_all(parts, 'zx', 0, 0, tiled=True)  4.6 us
    pallas_call x1, Pallas kernels, weights(): pl.pallas_call(weights_kernel, in_specs=[hbm()] * 5, out_specs=[vmem()] *...  3.85 us
  transfers between devices with their start and end apart: 14, of which 3 were waited for; matrix products, arithmetic and copies ran while one was open for 0% of the time, Pallas kernels for 24%

profile of v3, /device:TPU:1, one launch (start us, length us, event | category | flops | bytes accessed | tf_op | source)
XLA Modules:
  0.0 80.0 jit_solution(10383091481089033626)
XLA Ops:
  0.6 2.5 %edges.1 = (f32[184,256]{1,0:T(8,128)S(1)}, f32[184,256]{1,0:T(8,128)S(1)}, f32[776,256]{1,0:T(8,128)S(1)}, f32[776,256]{1,0:T(8,128)S(1)}, f32[128,256]{1,0:T(8,128)}) custom-call(f32[4,8,128,256]{3,2,1,0:T(8,128)} %u_hbm.3, f32[8,128,256]{2,1,0:T(8,128)} %c_hbm.3, f32[4,128,128]{2,1,0:T(8,128)} %imp_hbm.1, s32[8,128]{1,0:T(8,128)} %cmap.5), custom_call_target="tpu_custom_call" | custom-call | tf_op jit(solution)/shard_map/edges/pallas_call | solution.py:193
  3.1 0.0 copy-start
  3.1 0.0 copy-start.1
  3.1 3.3 %collective-permute-start.2 = (f32[776,256]{1,0:T(8,128)S(1)}, f32[776,256]{1,0:T(8,128)S(1)}, u32[]{:S(2)}, u32[]{:S(2)}) collective-permute-start(f32[776,256]{1,0:T(8,128)S(1)} %get-tuple-element.44.near), channel_id=1, source_target_pairs={{0,8},{8,0},{1,9},{9,1},{2,10},{10,2},{3,11},{11,3},{4,12},{12,4},... | collective-permute-start | bytes 2383880 | tf_op jit(solution)/shard_map/ppermute | solution.py:768
  6.5 2.8 %collective-permute-start.3 = (f32[776,256]{1,0:T(8,128)S(1)}, f32[776,256]{1,0:T(8,128)S(1)}, u32[]{:S(2)}, u32[]{:S(2)}) collective-permute-start(f32[776,256]{1,0:T(8,128)S(1)} %get-tuple-element.45.far), channel_id=1, source_target_pairs={{8,16},{24,32},{40,48},{56,64},{72,80},{88,96},{104,112},{120,128}... | collective-permute-start | bytes 2383880 | tf_op jit(solution)/shard_map/ppermute | solution.py:772
  9.3 1.4 %collective-permute-start = (f32[184,256]{1,0:T(8,128)S(1)}, f32[184,256]{1,0:T(8,128)S(1)}, u32[]{:S(2)}, u32[]{:S(2)}) collective-permute-start(f32[184,256]{1,0:T(8,128)S(1)} %get-tuple-element.46.own_hi), channel_id=1, source_target_pairs={{0,1},{1,2},{2,3},{3,0},{4,5},{5,6},{6,7},{7,4},{8,9},{9,10},{10,1... | collective-permute-start | bytes 565256 | tf_op jit(solution)/shard_map/ppermute | solution.py:765
  10.7 1.5 %collective-permute-start.1 = (f32[184,256]{1,0:T(8,128)S(1)}, f32[184,256]{1,0:T(8,128)S(1)}, u32[]{:S(2)}, u32[]{:S(2)}) collective-permute-start(f32[184,256]{1,0:T(8,128)S(1)} %get-tuple-element.47.own_lo), channel_id=1, source_target_pairs={{0,3},{1,0},{2,1},{3,2},{4,7},{5,4},{6,5},{7,6},{8,11},{9,8},{10,9... | collective-permute-start | bytes 565256 | tf_op jit(solution)/shard_map/ppermute | solution.py:765
  12.2 0.0 copy-start.3
  12.2 3.8 %weights.1 = (f32[4,8,128,256]{3,2,1,0:T(8,128)S(1)}, f32[4,8,128,256]{3,2,1,0:T(8,128)S(1)}, f32[7,128,256]{2,1,0:T(8,128)S(1)}, f32[8,128,256]{2,1,0:T(8,128)S...) custom-call(f32[4,8,128,256]{3,2,1,0:T(8,128)} %u_hbm.3, ...), custom_call_target="tpu_custom_call" | custom-call | flops 20000000 | bytes 6000000 | tf_op jit(solution)/shard_map/weights/pallas_call | solution.py:273
  16.0 0.0 copy-done
  16.1 0.0 copy-done.1
  16.1 0.0 collective-permute-done.y_lo.i0
  16.1 0.0 collective-permute-done.1.y_hi.i1
  16.1 0.1 collective-permute-start.4
  16.2 5.1 %collective-permute-start.5 = (f32[8,256]{1,0:T(8,128)S(1)}, f32[8,256]{1,0:T(8,128)S(1)}, u32[]{:S(2)}, u32[]{:S(2)}) collective-permute-start(f32[8,256]{1,0:T(8,128)S(1)} %get-tuple-element.49), channel_id=1, source_target_pairs={{8,16},{24,32},{40,48},{56,64},{72,80},{88,96},{104,112},{120,128}... | collective-permute-start | bytes 24584 | tf_op jit(solution)/shard_map/ppermute | solution.py:772
  21.3 0.0 copy-done.3
  21.3 0.0 copy-start.4
  21.3 0.0 copy-start.5
  21.3 0.0 copy-start.6
  21.3 9.8 %inner.1 = (f32[2,4,128,256]{3,2,1,0:T(8,128)S(1)}, f32[4,4,128,256]{3,2,1,0:T(8,128)}, f32[8,128,256]{2,1,0:T(8,128)S(1)}, f32[8,256]{1,0:T(8,128)S(1)}, f32[8,...) custom-call(f32[4,8,128,256]{3,2,1,0:T(8,128)S(1)} %get-tuple-elemen, ...), custom_call_target="tpu_custom_call" | custom-call | flops 100000000 | bytes 25000000 | tf_op jit(solution)/shard_map/inner/pallas_call | solution.py:369
  31.1 0.0 collective-permute-done.4.ends_near
  31.1 0.0 collective-permute-done.5.ends_far
  31.1 0.0 collective-permute-done.2.x_near
  31.1 0.0 collective-permute-done.3.x_far
  31.2 0.0 copy-done.4
  31.2 0.0 copy-done.5
  31.2 0.0 copy-done.6
  31.2 0.0 copy-start.2
  31.2 5.0 %outer.1 = (f32[528,256]{1,0:T(8,128)}, f32[4,128,256]{2,1,0:T(8,128)}, f32[32,256]{1,0:T(8,128)}, f32[32,256]{1,0:T(8,128)}, f32[4,4,128,256]{3,2,1,0:T(8,128)}...) custom-call(s32[2,4]{1,0:T(2,128)S(1)} %bitcast.5, ...), custom_call_target="tpu_custom_call" | custom-call | flops 50000000 | bytes 15000000 | tf_op jit(solution)/shard_map/outer/pallas_call | solution.py:526
  36.2 0.1 collective-permute-start.6
  36.3 2.1 %collective-permute-done.6.got_hbm.h_near = f32[528,256]{1,0:T(8,128)S(1)} collective-permute-done((f32[528,256]{1,0:T(8,128)}, f32[528,256]{1,0:T(8,128)S(1)}, u32[]{:S(2)}, u32[]{:S(2)}) %collective-permute-start.6) | collective-permute-done | bytes 540704 | tf_op jit(solution)/shard_map/ppermute | solution.py:768
  38.5 0.9 %spread.1 = f32[16,32,128]{2,1,0:T(8,128)} custom-call(f32[32,128]{1,0:T(8,128)S(1)} %get-tuple-element.67.mine, f32[528,256]{1,0:T(8,128)S(1)} %collective-permute-done.6.got_hbm.h_near), custom_call_target="tpu_custom_call" | custom-call | tf_op jit(solution)/shard_map/spread/pallas_call | solution.py:568
  39.4 9.9 %all-to-all-start = ((f32[16,32,128]{2,1,0:T(8,128)}), f32[16,32,128]{2,1,0:T(8,128)S(1)}, u32[]{:S(2)}, u32[]{:S(2)}) async-start(f32[16,32,128]{2,1,0:T(8,128)} %spread.1), calls=%async_computation | async-start | bytes 524288 | tf_op jit(solution)/shard_map/all_to_all | solution.py:796
  49.2 5.4 %collective-permute-start.12 = (f32[4,128,256]{2,1,0:T(8,128)}, f32[4,128,256]{2,1,0:T(8,128)S(1)}, u32[]{:S(2)}, u32[]{:S(2)}) collective-permute-start(f32[4,128,256]{2,1,0:T(8,128)} %get-tuple-element.85), channel_id=1, source_target_pairs={{8,16},{24,32},{40,48},{56,64},{72,80},{88,96},{104,112},{120,128}... | collective-permute-start | bytes 1572872 | tf_op jit(solution)/shard_map/ppermute | solution.py:772
  54.6 0.0 copy-done.2
  54.6 2.9 %collective-permute-start.10 = (f32[128,256]{1,0:T(8,128)S(1)}, f32[128,256]{1,0:T(8,128)S(1)}, u32[]{:S(2)}, u32[]{:S(2)}) collective-permute-start(f32[128,256]{1,0:T(8,128)S(1)} %copy-done.2), channel_id=1, source_target_pairs={{0,2},{1,3},{2,0},{3,1},{4,6},{5,7},{6,4},{7,5},{8,10},{9,11},{10,... | collective-permute-start | bytes 393224 | tf_op jit(solution)/shard_map/ppermute | solution.py:765
  57.5 4.6 %all-to-all-done.parts_hbm = f32[16,32,128]{2,1,0:T(8,128)S(1)} async-done(((f32[16,32,128]{2,1,0:T(8,128)}), f32[16,32,128]{2,1,0:T(8,128)S(1)}, u32[]{:S(2)}, u32[]{:S(2)}) %all-to-all-start) | async-done | bytes 262176 | tf_op jit(solution)/shard_map/all_to_all | solution.py:796
  62.1 0.0 copy-start.7
  62.1 0.7 copy-done.7
  62.8 1.1 %gathered.1 = (f32[48,256]{1,0:T(8,128)S(1)}, f32[48,256]{1,0:T(8,128)S(1)}, f32[16,256]{1,0:T(8,128)S(1)}) custom-call(f32[16,32,128]{2,1,0:T(8,128)} %copy-done.7, f32[32,256]{1,0:T(8,128)} %get-tuple-element.69.edge_lo, f32[32,256]{1,0:T(8,128)} %get-tuple-element.70.edge_hi), custom_call_target="tpu_custom_call" | custom-call | tf_op jit(solution)/shard_map/gathered/pallas_call | solution.py:599
  63.9 1.4 %collective-permute-start.7 = (f32[48,256]{1,0:T(8,128)S(1)}, f32[48,256]{1,0:T(8,128)S(1)}, u32[]{:S(2)}, u32[]{:S(2)}) collective-permute-start(f32[48,256]{1,0:T(8,128)S(1)} %get-tuple-element.71), channel_id=1, source_target_pairs={{0,1},{1,2},{2,3},{3,0},{4,5},{5,6},{6,7},{7,4},{8,9},{9,10},{10,1... | collective-permute-start | bytes 147464 | tf_op jit(solution)/shard_map/ppermute | solution.py:765
  65.3 1.5 %collective-permute-start.8 = (f32[48,256]{1,0:T(8,128)S(1)}, f32[48,256]{1,0:T(8,128)S(1)}, u32[]{:S(2)}, u32[]{:S(2)}) collective-permute-start(f32[48,256]{1,0:T(8,128)S(1)} %get-tuple-element.72), channel_id=1, source_target_pairs={{0,3},{1,0},{2,1},{3,2},{4,7},{5,4},{6,5},{7,6},{8,11},{9,8},{10,9... | collective-permute-start | bytes 147464 | tf_op jit(solution)/shard_map/ppermute | solution.py:765
  66.8 1.3 %collective-permute-start.9 = (f32[16,256]{1,0:T(8,128)S(1)}, f32[16,256]{1,0:T(8,128)S(1)}, u32[]{:S(2)}, u32[]{:S(2)}) collective-permute-start(f32[16,256]{1,0:T(8,128)S(1)} %get-tuple-element.73.after.a2), channel_id=1, source_target_pairs={{0,2},{1,3},{2,0},{3,1},{4,6},{5,7},{6,4},{7,5},{8,10},{9,11},{10,... | collective-permute-start | bytes 49160 | tf_op jit(solution)/shard_map/ppermute | solution.py:765
  68.1 3.7 %ready.1 = (f32[4,8,128,256]{3,2,1,0:T(8,128)S(1)}, f32[8,128,256]{2,1,0:T(8,128)S(1)}, f32[16,256]{1,0:T(8,128)S(1)}, f32[2,128,256]{2,1,0:T(8,128)S(1)}) custom-call(f32[16,256]{1,0:T(8,128)S(1)} %get-tuple-element.73.after.a2, f32[4,4,128,256]{3,2,1,0:T(8,128)} %get-tuple-element.75.inner_hbm, f32[4,4,128,256]{3,2,1,0:T(8,128)} %get-tuple-element.76.outer_hbm, ...), custom_call_target="tpu_custom_call" | custom-call | flops 10000000 | bytes 8000000 | tf_op jit(solution)/shard_map/ready/pallas_call | solution.py:678
  71.8 0.0 collective-permute-done.10.i3
  71.8 0.0 collective-permute-done.9.a3
  71.8 0.0 collective-permute-done.7.a0.e_lo
  71.9 0.0 collective-permute-done.8.a1.e_hi
  71.9 0.9 %blocks.1.own = f32[4,8,128]{2,1,0:T(8,128)S(1)} custom-call(f32[48,256]{1,0:T(8,128)S(1)} %collective-permute-done.7.a0.e_lo, f32[48,256]{1,0:T(8,128)S(1)} %collective-permute-done.8.a1.e_hi, f32[16,256]{1,0:T(8,128)S(1)} %get-tuple-element.73.after.a2, f32[16,256]{1,0:T(8,128)S(1)} %collective-permute-done.9.a3, ...), custom_call_target="tpu_custom_call" | custom-call | tf_op jit(solution)/shard_map/blocks/pallas_call | solution.py:631
  72.8 3.1 %collective-permute-start.11 = (f32[4,8,128]{2,1,0:T(8,128)S(1)}, f32[4,8,128]{2,1,0:T(8,128)S(1)}, u32[]{:S(2)}, u32[]{:S(2)}) collective-permute-start(f32[4,8,128]{2,1,0:T(8,128)S(1)} %blocks.1.own), channel_id=1, source_target_pairs={{0,8},{8,0},{1,9},{9,1},{2,10},{10,2},{3,11},{11,3},{4,12},{12,4},... | collective-permute-start | bytes 49160 | tf_op jit(solution)/shard_map/ppermute | solution.py:768
  75.9 0.0 collective-permute-done.12.h_far
  75.9 0.8 %collective-permute-done.11.got = f32[4,8,128]{2,1,0:T(8,128)S(1)} collective-permute-done((f32[4,8,128]{2,1,0:T(8,128)S(1)}, f32[4,8,128]{2,1,0:T(8,128)S(1)}, u32[]{:S(2)}, u32[]{:S(2)}) %collective-permute-start.11) | collective-permute-done | bytes 16416 | tf_op jit(solution)/shard_map/ppermute | solution.py:768
  76.8 3.1 %correct.1 = (f32[4,8,128,256]{3,2,1,0:T(8,128)}, f32[4,512]{1,0:T(4,128)}) custom-call(s32[8,128]{1,0:T(8,128)S(1)} %copy-done.3, f32[4,8,128]{2,1,0:T(8,128)S(1)} %blocks.1.own, f32[4,8,128]{2,1,0:T(8,128)S(1)} %collective-permute-done.11.got, f32[4,8,128,256]{3,2,1,0:T(8,128)S(1)} %get-tuple-element.82.base, f32[8,128,256]{2,1,0:T(8,128)S(1)} %get-tuple-element.81.pull, ...), custom_call_target="tpu_custom_call" | custom-call | tf_op jit(solution)/shard_map/correct/pallas_call | solution.py:742
  (1 shorter events, 0.0 us)
Async XLA Ops:
  3.1 12.9 %copy-start = (f32[776,256]{1,0:T(8,128)}, f32[776,256]{1,0:T(8,128)S(1)}, u32[]{:S(2)}) copy-start(f32[776,256]{1,0:T(8,128)S(1)} %get-tuple-element.44.near) | copy-start | bytes 2383876
  3.1 12.9 %copy-start.1 = (f32[776,256]{1,0:T(8,128)}, f32[776,256]{1,0:T(8,128)S(1)}, u32[]{:S(2)}) copy-start(f32[776,256]{1,0:T(8,128)S(1)} %get-tuple-element.45.far) | copy-start | bytes 2383876
  3.1 28.0 %collective-permute-start.2 = (f32[776,256]{1,0:T(8,128)S(1)}, f32[776,256]{1,0:T(8,128)S(1)}, u32[]{:S(2)}, u32[]{:S(2)}) collective-permute-start(f32[776,256]{1,0:T(8,128)S(1)} %get-tuple-element.44.near), channel_id=1, source_target_pairs={{0,8},{8,0},{1,9},{9,1},{2,10},{10,2},{3,11},{11,3},{4,12},{12,4},... | collective-permute-start | bytes 2383880 | tf_op jit(solution)/shard_map/ppermute | solution.py:768
  6.5 24.7 %collective-permute-start.3 = (f32[776,256]{1,0:T(8,128)S(1)}, f32[776,256]{1,0:T(8,128)S(1)}, u32[]{:S(2)}, u32[]{:S(2)}) collective-permute-start(f32[776,256]{1,0:T(8,128)S(1)} %get-tuple-element.45.far), channel_id=1, source_target_pairs={{8,16},{24,32},{40,48},{56,64},{72,80},{88,96},{104,112},{120,128}... | collective-permute-start | bytes 2383880 | tf_op jit(solution)/shard_map/ppermute | solution.py:772
  9.3 6.8 %collective-permute-start = (f32[184,256]{1,0:T(8,128)S(1)}, f32[184,256]{1,0:T(8,128)S(1)}, u32[]{:S(2)}, u32[]{:S(2)}) collective-permute-start(f32[184,256]{1,0:T(8,128)S(1)} %get-tuple-element.46.own_hi), channel_id=1, source_target_pairs={{0,1},{1,2},{2,3},{3,0},{4,5},{5,6},{6,7},{7,4},{8,9},{9,10},{10,1... | collective-permute-start | bytes 565256 | tf_op jit(solution)/shard_map/ppermute | solution.py:765
  10.7 5.4 %collective-permute-start.1 = (f32[184,256]{1,0:T(8,128)S(1)}, f32[184,256]{1,0:T(8,128)S(1)}, u32[]{:S(2)}, u32[]{:S(2)}) collective-permute-start(f32[184,256]{1,0:T(8,128)S(1)} %get-tuple-element.47.own_lo), channel_id=1, source_target_pairs={{0,3},{1,0},{2,1},{3,2},{4,7},{5,4},{6,5},{7,6},{8,11},{9,8},{10,9... | collective-permute-start | bytes 565256 | tf_op jit(solution)/shard_map/ppermute | solution.py:765
  12.2 9.1 %copy-start.3 = (s32[8,128]{1,0:T(8,128)S(1)}, s32[8,128]{1,0:T(8,128)}, u32[]{:S(2)}) copy-start(s32[8,128]{1,0:T(8,128)} %cmap.5) | copy-start | bytes 12292
  16.1 15.0 %collective-permute-start.4 = (f32[8,256]{1,0:T(8,128)S(1)}, f32[8,256]{1,0:T(8,128)S(1)}, u32[]{:S(2)}, u32[]{:S(2)}) collective-permute-start(f32[8,256]{1,0:T(8,128)S(1)} %get-tuple-element.48), channel_id=1, source_target_pairs={{0,8},{8,0},{1,9},{9,1},{2,10},{10,2},{3,11},{11,3},{4,12},{12,4},... | collective-permute-start | bytes 24584 | tf_op jit(solution)/shard_map/ppermute | solution.py:768
  16.2 14.9 %collective-permute-start.5 = (f32[8,256]{1,0:T(8,128)S(1)}, f32[8,256]{1,0:T(8,128)S(1)}, u32[]{:S(2)}, u32[]{:S(2)}) collective-permute-start(f32[8,256]{1,0:T(8,128)S(1)} %get-tuple-element.49), channel_id=1, source_target_pairs={{8,16},{24,32},{40,48},{56,64},{72,80},{88,96},{104,112},{120,128}... | collective-permute-start | bytes 24584 | tf_op jit(solution)/shard_map/ppermute | solution.py:772
  21.3 9.9 %copy-start.4 = (f32[2048]{0:T(1024)S(1)}, f32[2048]{0:T(1024)}, u32[]{:S(2)}) copy-start(f32[2048]{0:T(1024)} %param.12) | copy-start | bytes 24580
  21.3 9.9 %copy-start.5 = (s32[4,2]{0,1:T(2,128)S(1)}, s32[4,2]{0,1:T(2,128)}, u32[]{:S(2)}) copy-start(s32[4,2]{0,1:T(2,128)} %param.14) | copy-start | bytes 100
  21.3 9.9 %copy-start.6 = (f32[4]{0:T(128)S(1)}, f32[4]{0:T(128)}, u32[]{:S(2)}) copy-start(f32[4]{0:T(128)} %param.15) | copy-start | bytes 52
  31.2 23.4 %copy-start.2 = (f32[128,256]{1,0:T(8,128)S(1)}, f32[128,256]{1,0:T(8,128)}, u32[]{:S(2)}) copy-start(f32[128,256]{1,0:T(8,128)} %get-tuple-element.74.i2) | copy-start | bytes 393220
  36.2 2.2 %collective-permute-start.6 = (f32[528,256]{1,0:T(8,128)}, f32[528,256]{1,0:T(8,128)S(1)}, u32[]{:S(2)}, u32[]{:S(2)}) collective-permute-start(f32[528,256]{1,0:T(8,128)} %get-tuple-element.68), channel_id=1, source_target_pairs={{0,8},{8,0},{1,9},{9,1},{2,10},{10,2},{3,11},{11,3},{4,12},{12,4},... | collective-permute-start | bytes 1622024 | tf_op jit(solution)/shard_map/ppermute | solution.py:768
  39.4 22.7 %all-to-all-start = ((f32[16,32,128]{2,1,0:T(8,128)}), f32[16,32,128]{2,1,0:T(8,128)S(1)}, u32[]{:S(2)}, u32[]{:S(2)}) async-start(f32[16,32,128]{2,1,0:T(8,128)} %spread.1), calls=%async_computation | async-start | bytes 524288 | tf_op jit(solution)/shard_map/all_to_all | solution.py:796
  49.2 26.7 %collective-permute-start.12 = (f32[4,128,256]{2,1,0:T(8,128)}, f32[4,128,256]{2,1,0:T(8,128)S(1)}, u32[]{:S(2)}, u32[]{:S(2)}) collective-permute-start(f32[4,128,256]{2,1,0:T(8,128)} %get-tuple-element.85), channel_id=1, source_target_pairs={{8,16},{24,32},{40,48},{56,64},{72,80},{88,96},{104,112},{120,128}... | collective-permute-start | bytes 1572872 | tf_op jit(solution)/shard_map/ppermute | solution.py:772
  54.6 17.2 %collective-permute-start.10 = (f32[128,256]{1,0:T(8,128)S(1)}, f32[128,256]{1,0:T(8,128)S(1)}, u32[]{:S(2)}, u32[]{:S(2)}) collective-permute-start(f32[128,256]{1,0:T(8,128)S(1)} %copy-done.2), channel_id=1, source_target_pairs={{0,2},{1,3},{2,0},{3,1},{4,6},{5,7},{6,4},{7,5},{8,10},{9,11},{10,... | collective-permute-start | bytes 393224 | tf_op jit(solution)/shard_map/ppermute | solution.py:765
  62.1 0.7 copy-start.7
  63.9 7.9 %collective-permute-start.7 = (f32[48,256]{1,0:T(8,128)S(1)}, f32[48,256]{1,0:T(8,128)S(1)}, u32[]{:S(2)}, u32[]{:S(2)}) collective-permute-start(f32[48,256]{1,0:T(8,128)S(1)} %get-tuple-element.71), channel_id=1, source_target_pairs={{0,1},{1,2},{2,3},{3,0},{4,5},{5,6},{6,7},{7,4},{8,9},{9,10},{10,1... | collective-permute-start | bytes 147464 | tf_op jit(solution)/shard_map/ppermute | solution.py:765
  65.3 6.6 %collective-permute-start.8 = (f32[48,256]{1,0:T(8,128)S(1)}, f32[48,256]{1,0:T(8,128)S(1)}, u32[]{:S(2)}, u32[]{:S(2)}) collective-permute-start(f32[48,256]{1,0:T(8,128)S(1)} %get-tuple-element.72), channel_id=1, source_target_pairs={{0,3},{1,0},{2,1},{3,2},{4,7},{5,4},{6,5},{7,6},{8,11},{9,8},{10,9... | collective-permute-start | bytes 147464 | tf_op jit(solution)/shard_map/ppermute | solution.py:765
  66.8 5.0 %collective-permute-start.9 = (f32[16,256]{1,0:T(8,128)S(1)}, f32[16,256]{1,0:T(8,128)S(1)}, u32[]{:S(2)}, u32[]{:S(2)}) collective-permute-start(f32[16,256]{1,0:T(8,128)S(1)} %get-tuple-element.73.after.a2), channel_id=1, source_target_pairs={{0,2},{1,3},{2,0},{3,1},{4,6},{5,7},{6,4},{7,5},{8,10},{9,11},{10,... | collective-permute-start | bytes 49160 | tf_op jit(solution)/shard_map/ppermute | solution.py:765
  72.8 4.0 %collective-permute-start.11 = (f32[4,8,128]{2,1,0:T(8,128)S(1)}, f32[4,8,128]{2,1,0:T(8,128)S(1)}, u32[]{:S(2)}, u32[]{:S(2)}) collective-permute-start(f32[4,8,128]{2,1,0:T(8,128)S(1)} %blocks.1.own), channel_id=1, source_target_pairs={{0,8},{8,0},{1,9},{9,1},{2,10},{10,2},{3,11},{11,3},{4,12},{12,4},... | collective-permute-start | bytes 49160 | tf_op jit(solution)/shard_map/ppermute | solution.py:768

commit v4 on v3

--- a/solution.py
+++ b/solution.py
@@ -83,8 +83,46 @@
     return w + shift_down(w, axis)
 
 
+def tile(k):
+    return pl.ds(8 * k, 8)
+
+
+def sweep(u_at, f_at, wy_at, wz_at, sides_at, emit):
+    row = iota((8, 256), 0)
+    here = [u_at(s, 0) for s in range(4)]
+    rolled = [pltpu.roll(here[s], 7, 0) for s in range(4)]
+    before = [None] * 4
+    for k in range(16):
+        wy = wy_at(k)
+        wz = wz_at(k)
+        weights_here = [weight(k) for weight, _ in sides_at]
+        for s in range(4):
+            u = here[s]
+            up = rolled[s]
+            if k < 15:
+                here[s] = u_at(s, k + 1)
+                rolled[s] = pltpu.roll(here[s], 7, 0)
+                up = jnp.where(row == 7, rolled[s], up)
+            down = pltpu.roll(wy * u, 1, 0)
+            pulled = f_at(s, k) + wy * up
+            pulled = pulled + jnp.where(row == 0, 0.0 if k == 0 else before[s], down)
+            before[s] = down
+            pulled = pulled + wz * shift_up(u, 1)
+            pulled = pulled + shift_down(wz * u, 1)
+            for weight, (_, neighbour) in zip(weights_here, sides_at):
+                pulled = pulled + weight * neighbour(s, k)
+            emit(s, k, u, pulled)
+
+
+def fold(p):
+    return p[:, :128] + p[:, 128:]
+
+
 def row_sums(slabs):
-    folded = jnp.concatenate([p[:, :128] + p[:, 128:] for p in slabs], axis=0)
+    return folded_sums(jnp.concatenate([fold(p) for p in slabs], axis=0))
+
+
+def folded_sums(folded):
     head = folded.astype(jnp.bfloat16)
     rest = (folded - head.astype(F32)).astype(jnp.bfloat16)
     ones = jnp.ones((8, 128), jnp.bfloat16)
@@ -229,132 +267,197 @@
 
 
 def weights_kernel(
-    u_hbm, f_hbm, c_hbm, cmap_hbm, admittance_hbm, u, f, wx, wy, wz, diag, zeta_t, c, cmap, admittance, sems
+    u_hbm, c_hbm, cmap_hbm, admittance_hbm, u, wx, wy, wz, diag, zeta_t, rim, c, cmap, admittance, sems, u_sems
 ):
     small = [
-        pltpu.make_async_copy(cmap_hbm, cmap, sems.at[3]),
-        pltpu.make_async_copy(admittance_hbm, admittance, sems.at[4]),
+        pltpu.make_async_copy(cmap_hbm, cmap, sems.at[8]),
+        pltpu.make_async_copy(admittance_hbm, admittance, sems.at[9]),
     ]
-    copy = pltpu.make_async_copy(c_hbm, c, sems.at[0])
-    later = [pltpu.make_async_copy(u_hbm, u, sems.at[1]), pltpu.make_async_copy(f_hbm, f, sems.at[2])]
-    for other in small:
-        other.start()
-    copy.start()
-    for other in later:
-        other.start()
-    for other in small:
-        other.wait()
+    rows = [pltpu.make_async_copy(c_hbm.at[x], c.at[x], sems.at[x]) for x in range(8)]
+    later = [pltpu.make_async_copy(u_hbm.at[s], u.at[s], u_sems.at[s]) for s in range(4)]
+    for copy in small + rows + later:
+        copy.start()
+    for copy in small:
+        copy.wait()
     zeta = gather_rows(cmap[...], admittance[...])
     zeta_t[...] = jnp.transpose(jnp.concatenate([zeta, jnp.zeros((120, 128), F32)], axis=0))
-    copy.wait()
+    row = iota((8, 256), 0)
+    last_lane = iota((8, 256), 1) == 255
+    rows[0].wait()
     for x in range(8):
-        here = c[x]
         if x < 7:
-            wx[x] = face(here, c[x + 1])
-        along_y = line_weight(here, 0)
-        along_z = line_weight(here, 1)
-        wy[x] = along_y
-        wz[x] = along_z
-        total = both_sides(along_y, 0) + both_sides(along_z, 1) + zeta_t[:, x : x + 1]
-        if x > 0:
-            total = total + wx[x - 1]
-        if x < 7:
-            total = total + wx[x]
-        diag[x] = total
-    for other in later:
-        other.wait()
-
-
-def weights(u, f, c, cmap, admittance):
+            rows[x + 1].wait()
+        here = c[x, tile(0), :]
+        rolled = pltpu.roll(here, 7, 0)
+        before = None
+        for k in range(16):
+            up = rolled
+            now = here
+            if k < 15:
+                here = c[x, tile(k + 1), :]
+                rolled = pltpu.roll(here, 7, 0)
+                up = jnp.where(row == 7, rolled, up)
+            along_y = face(now, up)
+            if k == 15:
+                along_y = jnp.where(row == 7, 0.0, along_y)
+            down = pltpu.roll(along_y, 1, 0)
+            along_z = jnp.where(last_lane, 0.0, face(now, shift_up(now, 1)))
+            total = along_y + jnp.where(row == 0, 0.0 if k == 0 else before, down)
+            before = down
+            total = total + along_z + shift_down(along_z, 1)
+            total = total + zeta_t[tile(k), x : x + 1]
+            if x < 7:
+                along_x = face(now, c[x + 1, tile(k), :])
+                wx[x, tile(k), :] = along_x
+                total = total + along_x
+            if x > 0:
+                total = total + wx[x - 1, tile(k), :]
+            wy[x, tile(k), :] = along_y
+            wz[x, tile(k), :] = along_z
+            diag[x, tile(k), :] = total
+    rim[0] = c[0]
+    rim[1] = c[7]
+    for copy in later:
+        copy.wait()
+
+
+def weights(u, c, cmap, admittance):
     outs = [
-        kept(4, 8, 128, 256), kept(4, 8, 128, 256),
+        kept(4, 8, 128, 256),
         kept(7, 128, 256), kept(8, 128, 256), kept(8, 128, 256), kept(8, 128, 256), kept(128, 128),
+        kept(2, 128, 256),
     ]
     return pl.pallas_call(
         weights_kernel,
-        in_specs=[hbm()] * 5,
+        in_specs=[hbm()] * 4,
         out_specs=[vmem()] * len(outs),
         out_shape=outs,
         scratch_shapes=[
             pltpu.VMEM((8, 128, 256), F32),
             pltpu.VMEM((8, 128), jnp.int32),
             pltpu.VMEM((16, 128), F32),
-            pltpu.SemaphoreType.DMA((5,)),
+            pltpu.SemaphoreType.DMA((10,)),
+            pltpu.SemaphoreType.DMA((4,)),
         ],
-        compiler_params=params(8),
+        compiler_params=params(4),
         cost_estimate=pl.CostEstimate(flops=20_000_000, bytes_accessed=6_000_000, transcendentals=0),
         name="weights",
-    )(u, f, c, cmap, admittance)
+    )(u, c, cmap, admittance)
 
 
 def inner_kernel(
-    u, f, cmap, own_lo, own_hi, y_lo, y_hi, wx, wy, wz, diag,
+    u, f_hbm, cmap, own_lo, own_hi, y_lo, y_hi, wx, wy, wz, diag,
     u2, u2_out, gain, wyl, wyh, pulled1, keep1, pulled2, edge_lo, edge_hi, contact,
-    u1, sums, middle, sems,
+    f, u1, sums, folded, middle, sems, f_sems,
 ):
+    def row_of_f(x):
+        return pltpu.make_async_copy(f_hbm.at[:, x], f.at[:, x], f_sems.at[x])
+
+    for x in (1, 2, 3, 4, 5, 6, 0, 7):
+        row_of_f(x).start()
+
     below, above = has_elecs()
     wyl[...] = outer_face(own_lo[32:40, :], below * y_lo[32:40, :])
     wyh[...] = outer_face(own_hi[32:40, :], above * y_hi[32:40, :])
+    row = iota((8, 256), 0)
     for x in range(8):
-        gain[x] = diag[x]
-        gain[x, 0:1, :] = gain[x, 0:1, :] + wyl[x : x + 1, :]
-        gain[x, 127:128, :] = gain[x, 127:128, :] + wyh[x : x + 1, :]
-        if x not in (0, 7):
-            gain[x] = OMEGA * inverse(gain[x])
-
-    for n, x in enumerate((0, 7)):
-        for s in range(4):
-            pulled = f[s, x] + in_line(wy[x], u[s, x], 0)
-            pulled = pulled + in_line(wz[x], u[s, x], 1)
-            pulled = pulled + (wx[0] * u[s, 1] if x == 0 else wx[6] * u[s, 6])
-            pulled1[n, s] = pulled
-            pulled1[n, s, 0:1, :] = pulled1[n, s, 0:1, :] + wyl[x : x + 1, :] * y_lo[8 * s + x : 8 * s + x + 1, :]
-            pulled1[n, s, 127:128, :] = (
-                pulled1[n, s, 127:128, :] + wyh[x : x + 1, :] * y_hi[8 * s + x : 8 * s + x + 1, :]
-            )
-            keep1[n, s] = KEEP * u[s, x]
+        for k in range(16):
+            total = diag[x, tile(k), :]
+            if k == 0:
+                total = total + jnp.where(row == 0, wyl[x : x + 1, :], 0.0)
+            if k == 15:
+                total = total + jnp.where(row == 7, wyh[x : x + 1, :], 0.0)
+            gain[x, tile(k), :] = total if x in (0, 7) else OMEGA * inverse(total)
+
+    def with_halos(pulled, s, k, x):
+        at = 8 * s + x
+        if k == 0:
+            pulled = pulled + jnp.where(row == 0, wyl[pl.ds(x, 1), :] * y_lo[pl.ds(at, 1), :], 0.0)
+        if k == 15:
+            pulled = pulled + jnp.where(row == 7, wyh[pl.ds(x, 1), :] * y_hi[pl.ds(at, 1), :], 0.0)
+        return pulled
 
     def first(x, carry):
-        for s in range(4):
-            pulled = f[s, x] + in_line(wy[x], u[s, x], 0)
-            pulled = pulled + in_line(wz[x], u[s, x], 1)
-            pulled = pulled + wx[x - 1] * u[s, x - 1] + wx[x] * u[s, x + 1]
-            u1[s, x] = KEEP * u[s, x] + gain[x] * pulled
-            low = u1[s, x, 0:1, :] + gain[x, 0:1, :] * wyl[pl.ds(x, 1), :] * y_lo[pl.ds(8 * s + x, 1), :]
-            high = u1[s, x, 127:128, :] + gain[x, 127:128, :] * wyh[pl.ds(x, 1), :] * y_hi[pl.ds(8 * s + x, 1), :]
-            u1[s, x, 0:1, :] = low
-            u1[s, x, 127:128, :] = high
-            edge_lo[pl.ds(8 * s + x, 1), :] = low
-            edge_hi[pl.ds(8 * s + x, 1), :] = high
+        row_of_f(x).wait()
+
+        def emit(s, k, here, pulled):
+            new = KEEP * here + gain[x, tile(k), :] * with_halos(pulled, s, k, x)
+            u1[s, x, tile(k), :] = new
+            if k == 0:
+                edge_lo[pl.ds(8 * s + x, 1), :] = new[0:1]
+            if k == 15:
+                edge_hi[pl.ds(8 * s + x, 1), :] = new[7:8]
+
+        sweep(
+            lambda s, k: u[s, x, tile(k), :],
+            lambda s, k: f[s, x, tile(k), :],
+            lambda k: wy[x, tile(k), :],
+            lambda k: wz[x, tile(k), :],
+            [
+                (lambda k: wx[x - 1, tile(k), :], lambda s, k: u[s, x - 1, tile(k), :]),
+                (lambda k: wx[x, tile(k), :], lambda s, k: u[s, x + 1, tile(k), :]),
+            ],
+            emit,
+        )
         return carry
 
     lax.fori_loop(1, 7, first, 0)
-
-    for s in range(4):
-        pulled2[0, s] = f[s, 0] + wx[0] * u1[s, 1]
-        pulled2[1, s] = f[s, 7] + wx[6] * u1[s, 6]
-        u1[s, 0] = jnp.zeros((128, 256), F32)
-        u1[s, 7] = jnp.zeros((128, 256), F32)
-
-    def second(x, target):
-        slabs = []
-        for s in range(4):
-            pulled = f[s, x] + in_line(wy[x], u1[s, x], 0)
-            pulled = pulled + in_line(wz[x], u1[s, x], 1)
-            pulled = pulled + wx[x - 1] * u1[s, x - 1] + wx[x] * u1[s, x + 1]
-            new = KEEP * u1[s, x] + gain[x] * pulled
-            target[s] = new
-            slabs.append(new)
-        sums[x] = row_sums(slabs)
+    row_of_f(0).wait()
+    row_of_f(7).wait()
+
+    def rim(n, carry):
+        x = 7 * n
+        inside = 1 + 5 * n
+
+        def emit(s, k, here, pulled):
+            pulled1[n, s, tile(k), :] = with_halos(pulled, s, k, x)
+            keep1[n, s, tile(k), :] = KEEP * here
+            pulled2[n, s, tile(k), :] = f[s, x, tile(k), :] + wx[6 * n, tile(k), :] * u1[s, inside, tile(k), :]
+
+        sweep(
+            lambda s, k: u[s, x, tile(k), :],
+            lambda s, k: f[s, x, tile(k), :],
+            lambda k: wy[x, tile(k), :],
+            lambda k: wz[x, tile(k), :],
+            [(lambda k: wx[6 * n, tile(k), :], lambda s, k: u[s, inside, tile(k), :])],
+            emit,
+        )
+        return carry
+
+    lax.fori_loop(0, 2, rim, 0)
+
+    def second(x, sides_at, target):
+        def emit(s, k, here, pulled):
+            new = KEEP * here + gain[x, tile(k), :] * pulled
+            target[s, tile(k), :] = new
+            folded[pl.ds(128 * s + 8 * k, 8), :] = fold(new)
+
+        sweep(
+            lambda s, k: u1[s, x, tile(k), :],
+            lambda s, k: f[s, x, tile(k), :],
+            lambda k: wy[x, tile(k), :],
+            lambda k: wz[x, tile(k), :],
+            sides_at,
+            emit,
+        )
+
+    def below_at(x):
+        return (lambda k: wx[x - 1, tile(k), :], lambda s, k: u1[s, x - 1, tile(k), :])
+
+    def above_at(x):
+        return (lambda k: wx[x, tile(k), :], lambda s, k: u1[s, x + 1, tile(k), :])
 
     def second_middle(x, carry):
-        second(x, middle.at[x - 2])
+        sums[x - 1] = folded_sums(folded[...])
+        second(x, [below_at(x), above_at(x)], middle.at[x - 2])
         pltpu.make_async_copy(middle.at[x - 2], u2_out.at[:, x - 2], sems.at[x - 2]).start()
         return carry
 
+    second(1, [above_at(1)], u2.at[0])
     lax.fori_loop(2, 6, second_middle, 0)
-    second(1, u2.at[0])
-    second(6, u2.at[1])
+    sums[5] = folded_sums(folded[...])
+    second(6, [below_at(6)], u2.at[1])
+    sums[6] = folded_sums(folded[...])
     contact[...] = scatter([cmap[x : x + 1, :] for x in range(1, 7)], [sums[x] for x in range(1, 7)])
     for n in range(4):
         pltpu.make_async_copy(middle.at[n], u2_out.at[:, n], sems.at[n]).wait()
@@ -368,14 +471,17 @@
     ]
     return pl.pallas_call(
         inner_kernel,
-        in_specs=[vmem()] * 11,
+        in_specs=[vmem(), hbm()] + [vmem()] * 9,
         out_specs=[vmem(), hbm()] + [vmem()] * (len(outs) - 2),
         out_shape=outs,
         scratch_shapes=[
             pltpu.VMEM((4, 8, 128, 256), F32),
+            pltpu.VMEM((4, 8, 128, 256), F32),
             pltpu.VMEM((8, 4, 128), F32),
+            pltpu.VMEM((512, 128), F32),
             pltpu.VMEM((4, 4, 128, 256), F32),
             pltpu.SemaphoreType.DMA((4,)),
+            pltpu.SemaphoreType.DMA((8,)),
         ],
         compiler_params=params(16),
         cost_estimate=pl.CostEstimate(flops=100_000_000, bytes_accessed=25_000_000, transcendentals=0),
@@ -384,18 +490,12 @@
 
 
 def outer_kernel(
-    pairs, amplitudes, cmap, admittance, near, far, y_lo, y_hi, x_near, x_far, ends_near, ends_far,
+    pairs, amplitudes, cmap, admittance, rim, y_lo, y_hi, x_near, x_far, ends_near, ends_far,
     wx, wy, wz, gain, wyl, wyh, u2, pulled1, keep1, pulled2, e_lo, e_hi, contact, zeta_in,
-    face_near_out, face_far_out, edge_lo_out, edge_hi_out, u2_out, gain_out, wxf_out, misc_out, zeta_out, mine,
-    ids, face_near, face_far, edge_lo, edge_hi, u2b, gain_b, wxf, misc, c_own, passed, sems, u2_sems, near_sems, edge_sems,
+    face_near_out, face_far_out, edge_lo_out, edge_hi_out, u2_out, gain_out, wxf_out, misc_out, zeta_out, mine, other,
+    ids, face_near, face_far, edge_lo, edge_hi, u2b, gain_b, wxf, misc, folded, sems, u2_sems, edge_sems,
 ):
     copies = []
-    rows_in = [
-        pltpu.make_async_copy(source.at[pl.ds(ROW_C, 128)], c_own.at[n], sems.at[11 + n])
-        for n, source in enumerate((near, far))
-    ]
-    for copy in rows_in:
-        copy.start()
 
     def send(source, target, sem):
         copy = pltpu.make_async_copy(source, target, sem)
@@ -420,24 +520,18 @@
 
     id_rows = []
     values = []
-    for copy in rows_in:
-        copy.wait()
     for n, (side, msg, ends, out, sent) in enumerate(
         zip(sides(), (x_near, x_far), (ends_near, ends_far), (face_near, face_far), (face_near_out, face_far_out))
     ):
         x = 7 * side
         there = msg[ROW_C : ROW_C + 128, :]
-        outside = outer_face(c_own[n], there)
+        outside = outer_face(rim[side], there)
         wxf[n] = outside
         g = OMEGA * inverse(gain[x] + outside)
         gain_b[n] = g
         for s in range(4):
             out[s] = keep1[side, s] + g * (pulled1[side, s] + outside * msg[128 * s : 128 * s + 128, :])
-        if n:
-            send(out, sent, sems.at[4])
-        else:
-            for s in range(4):
-                send(out.at[s], sent.at[pl.ds(128 * s, 128)], near_sems.at[s])
+        send(out, sent, sems.at[4 + n])
         send(gain_b.at[n], gain_out.at[x], sems.at[6 + n])
         spare = jnp.maximum(there, TINY)
         diag = both_sides(line_weight(spare, 0), 0) + both_sides(line_weight(spare, 1), 1) + zeta_t[:, n : n + 1]
@@ -457,16 +551,22 @@
         send(u2b.at[2 * n + 1], u2_out.at[2 * side + 1], u2_sems.at[2 * n + 1])
         id_rows.append(cmap[pl.ds(inside, 1), :])
         values.append(row_sums(slabs))
-        slabs = []
-        for s in range(4):
-            pulled = pulled2[side, s] + in_line(wy[x], out[s], 0)
-            pulled = pulled + in_line(wz[x], out[s], 1)
-            new = KEEP * out[s] + g * pulled
-            u2b[2 * n, s] = new
-            slabs.append(new)
+        def emit(s, k, here, pulled, n=n):
+            new = KEEP * here + gain_b[n, tile(k), :] * pulled
+            u2b[2 * n, s, tile(k), :] = new
+            folded[pl.ds(128 * s + 8 * k, 8), :] = fold(new)
+
+        sweep(
+            lambda s, k, out=out: out[s, tile(k), :],
+            lambda s, k, side=side: pulled2[side, s, tile(k), :],
+            lambda k, x=x: wy[x, tile(k), :],
+            lambda k, x=x: wz[x, tile(k), :],
+            [],
+            emit,
+        )
         send(u2b.at[2 * n], u2_out.at[2 * side], u2_sems.at[2 * n])
         id_rows.append(cmap[pl.ds(x, 1), :])
-        values.append(row_sums(slabs))
+        values.append(folded_sums(folded[...]))
 
     send(wxf, wxf_out, sems.at[8])
 
@@ -508,25 +608,21 @@
         total = total - jnp.where(at & (electrode == pairs[1:2, s : s + 1]), amount, 0.0)
     first_half = lax.axis_index("core") == 0
     mine[...] = jnp.where(first_half, total[0:32], total[32:64])
-    passed[:, 0:128] = jnp.where(first_half, total[32:48], total[0:16])
-    passed[:, 128:256] = jnp.where(first_half, total[48:64], total[16:32])
-    send(passed, face_near_out.at[pl.ds(512, 16)], sems.at[10])
+    other[...] = jnp.where(first_half, total[32:64], total[0:32])
     for copy in copies:
         copy.wait()
 
 
 def outer(pairs, amplitudes, *args):
     outs = [
-        stored(528, 256), stored(4, 128, 256), stored(32, 256), stored(32, 256),
+        stored(4, 128, 256), stored(4, 128, 256), stored(32, 256), stored(32, 256),
         stored(4, 4, 128, 256), stored(8, 128, 256), stored(2, 128, 256), stored(16, 256), stored(128, 128),
-        f32(32, 128),
+        f32(32, 128), f32(32, 128),
     ]
-    specs = [vmem()] * len(args)
-    specs[2] = specs[3] = hbm()
     return pl.pallas_call(
         outer_kernel,
-        in_specs=[vmem()] * 2 + specs,
-        out_specs=[hbm()] * 9 + [vmem()],
+        in_specs=[vmem()] * (2 + len(args)),
+        out_specs=[hbm()] * 9 + [vmem()] * 2,
         out_shape=outs,
         scratch_shapes=[
             pltpu.VMEM((8, 128), jnp.int32),
@@ -538,10 +634,8 @@
             pltpu.VMEM((2, 128, 256), F32),
             pltpu.VMEM((2, 128, 256), F32),
             pltpu.VMEM((16, 256), F32),
-            pltpu.VMEM((2, 128, 256), F32),
-            pltpu.VMEM((16, 256), F32),
-            pltpu.SemaphoreType.DMA((13,)),
-            pltpu.SemaphoreType.DMA((4,)),
+            pltpu.VMEM((512, 128), F32),
+            pltpu.SemaphoreType.DMA((9,)),
             pltpu.SemaphoreType.DMA((4,)),
             pltpu.SemaphoreType.DMA((2,)),
         ],
@@ -551,12 +645,8 @@
     )(pairs, amplitudes, *args)
 
 
-def spread_kernel(mine, got_hbm, out, both, got, got_sem, sems):
-    copy = pltpu.make_async_copy(got_hbm.at[pl.ds(512, 16)], got, got_sem)
-    copy.start()
-    copy.wait()
-    both[0:16, :] = mine[0:16, :] + got[:, 0:128]
-    both[16:32, :] = mine[16:32, :] + got[:, 128:256]
+def spread_kernel(mine, got, out, both, sems):
+    both[...] = mine[...] + got[...]
     copies = [pltpu.make_async_copy(both, out.at[n], sems.at[n]) for n in range(out.shape[0])]
     for copy in copies:
         copy.start()
@@ -567,15 +657,10 @@
 def spread(mine, got, count):
     return pl.pallas_call(
         spread_kernel,
-        in_specs=[vmem(), pl.BlockSpec(memory_space=pl.ANY)],
+        in_specs=[vmem()] * 2,
         out_specs=hbm(),
         out_shape=stored(count, 32, 128),
-        scratch_shapes=[
-            pltpu.VMEM((32, 128), F32),
-            pltpu.VMEM((16, 256), F32),
-            pltpu.SemaphoreType.DMA,
-            pltpu.SemaphoreType.DMA((count,)),
-        ],
+        scratch_shapes=[pltpu.VMEM((32, 128), F32), pltpu.SemaphoreType.DMA((count,))],
         compiler_params=params(2),
         name="spread",
     )(mine, got)
@@ -598,7 +683,7 @@
 def gathered(parts, edge_lo, edge_hi):
     return pl.pallas_call(
         gathered_kernel,
-        in_specs=[hbm()] * 3,
+        in_specs=[pl.BlockSpec(memory_space=pl.ANY)] + [hbm()] * 2,
         out_specs=[vmem()] * 3,
         out_shape=[f32(48, 256), f32(48, 256), f32(16, 256)],
         scratch_shapes=[
@@ -724,7 +809,7 @@
             at = 8 * s + x
             new = base[s, x] + pull[x] * volts_t[:, at : at + 1]
             if x in (0, 7):
-                halo = jnp.where(near_side == x // 7, h_near[128 * s : 128 * s + 128, :], h_far[s])
+                halo = jnp.where(near_side == x // 7, h_near[s], h_far[s])
                 new = new + row_weight[x // 7] * halo
             buf[s, x] = new
             low = weight[x : x + 1, :] * e_lo[16 + at : 17 + at, :]
@@ -781,20 +866,19 @@
     ends_far = far(ends_far)
     ends_near = near(ends_near)
 
-    u, f, wx, wy, wz, diag, zeta_t = weights(u, f, c, in_hbm(cmap), in_hbm(admittance))
+    u, wx, wy, wz, diag, zeta_t, rim = weights(u, c, in_hbm(cmap), in_hbm(admittance))
     u2, u2_inner, gain, wyl, wyh, pulled1, keep1, pulled2, e_lo, e_hi, contact = inner(
         u, f, cmap, own_lo, own_hi, y_lo, y_hi, wx, wy, wz, diag
     )
-    face_near, face_far, edge_lo, edge_hi, u2_outer, gain, wxf, misc, zeta_t, mine = outer(
-        pairs.T, amplitudes.reshape(1, -1), cmap, admittance, in_hbm(row_near), in_hbm(row_far),
-        y_lo, y_hi, x_near, x_far, ends_near, ends_far,
+    face_near, face_far, edge_lo, edge_hi, u2_outer, gain, wxf, misc, zeta_t, mine, other = outer(
+        pairs.T, amplitudes.reshape(1, -1), cmap, admittance, rim, y_lo, y_hi, x_near, x_far, ends_near, ends_far,
         wx, wy, wz, gain, wyl, wyh, u2, pulled1, keep1, pulled2, e_lo, e_hi, contact, zeta_t,
     )
     h_far = far(face_far)
     h_near = near(face_near)
-    parts = spread(mine, h_near, groups)
+    parts = spread(mine, near(other), groups)
     parts = lax.all_to_all(parts, "zx", 0, 0, tiled=True)
-    to_above, to_below, summed = gathered(in_hbm(parts), in_hbm(edge_lo), in_hbm(edge_hi))
+    to_above, to_below, summed = gathered(parts, in_hbm(edge_lo), in_hbm(edge_hi))
     base, pull, weight, row_weight = ready(
         summed, in_hbm(u2_inner), in_hbm(u2_outer), in_hbm(gain), in_hbm(wxf), in_hbm(misc), in_hbm(zeta_t)
     )

time: 80.4 us -> 76 us (0.945)
  Pallas kernels: 30.9 us -> 27.2 us
    pallas_call x5, Pallas kernels: 20.6 us -> 16.9 us  [the longest x1 8.35 us: inner(): pl.pallas_call(inner_kernel, in_specs=[vmem(), hbm()] + [vmem()] * 9, out...]
    ppermute x4 -> x5, waiting for transfers between devices: 2.97 us -> 2.01 us  [near(): return lax.ppermute(a, 'core', [(0, 1), (1, 0)])]
    ppermute x4 -> x5, starting transfers between devices: 6.64 us -> 7.21 us  [near(): return lax.ppermute(a, 'core', [(0, 1), (1, 0)])]
  transfers between devices with their start and end apart: 14 -> 15, of which waited for: 3 -> 4; matrix products, arithmetic and copies ran while one was open for 0% -> 0% of each run, Pallas kernels for 24% -> 23%
where the time goes in v4:
time: 76 us; the launch traced here: 75.7 us
  starting transfers between devices  40.5 us (53%)
  Pallas kernels  27.2 us (36%)
  waiting for transfers between devices  6.96 us (9%)
  between operations  1.04 us (1%)
    ppermute x3, starting transfers between devices, far(): return lax.ppermute(a, TILE, pairs + [(j, i) for i, j in pairs])  13.4 us
    ppermute x6, starting transfers between devices, rotated(): lax.ppermute(a, 'elec', [(i, (i + turn) % elecs) for i in range(elecs)])  9.95 us
    all_to_all x1, starting transfers between devices, per_device(): parts = lax.all_to_all(parts, 'zx', 0, 0, tiled=True)  9.86 us
    pallas_call x1, Pallas kernels, inner(): pl.pallas_call(inner_kernel, in_specs=[vmem(), hbm()] + [vmem()] * 9, out...  8.35 us
    ppermute x5, starting transfers between devices, near(): return lax.ppermute(a, 'core', [(0, 1), (1, 0)])  7.21 us
    all_to_all x1, waiting for transfers between devices, per_device(): parts = lax.all_to_all(parts, 'zx', 0, 0, tiled=True)  4.73 us
    pallas_call x1, Pallas kernels, ready(): pl.pallas_call(ready_kernel, in_specs=[pl.BlockSpec(memory_space=pl.ANY)]...  3.74 us
    pallas_call x1, Pallas kernels, outer(): pl.pallas_call(outer_kernel, in_specs=[vmem()] * (2 + len(args)), out_spe...  3.43 us
  transfers between devices with their start and end apart: 15, of which 4 were waited for; matrix products, arithmetic and copies ran while one was open for 0% of the time, Pallas kernels for 23%

profile of v4, /device:TPU:1, one launch (start us, length us, event | category | flops | bytes accessed | tf_op | source)
XLA Modules:
  0.0 75.7 jit_solution(16024585166483149774)
XLA Ops:
  0.6 2.5 %edges.1 = (f32[184,256]{1,0:T(8,128)S(1)}, f32[184,256]{1,0:T(8,128)S(1)}, f32[776,256]{1,0:T(8,128)S(1)}, f32[776,256]{1,0:T(8,128)S(1)}, f32[128,256]{1,0:T(8,128)}) custom-call(f32[4,8,128,256]{3,2,1,0:T(8,128)} %u_hbm.3, f32[8,128,256]{2,1,0:T(8,128)} %c_hbm.3, f32[4,128,128]{2,1,0:T(8,128)} %imp_hbm.1, s32[8,128]{1,0:T(8,128)} %cmap.5), custom_call_target="tpu_custom_call" | custom-call | tf_op jit(solution)/shard_map/edges/pallas_call | solution.py:231
  3.1 0.0 copy-start.1
  3.1 3.3 %collective-permute-start.2 = (f32[776,256]{1,0:T(8,128)S(1)}, f32[776,256]{1,0:T(8,128)S(1)}, u32[]{:S(2)}, u32[]{:S(2)}) collective-permute-start(f32[776,256]{1,0:T(8,128)S(1)} %get-tuple-element.48), channel_id=1, source_target_pairs={{0,8},{8,0},{1,9},{9,1},{2,10},{10,2},{3,11},{11,3},{4,12},{12,4},... | collective-permute-start | bytes 2383880 | tf_op jit(solution)/shard_map/ppermute | solution.py:853
  6.5 2.8 %collective-permute-start.3 = (f32[776,256]{1,0:T(8,128)S(1)}, f32[776,256]{1,0:T(8,128)S(1)}, u32[]{:S(2)}, u32[]{:S(2)}) collective-permute-start(f32[776,256]{1,0:T(8,128)S(1)} %get-tuple-element.49), channel_id=1, source_target_pairs={{8,16},{24,32},{40,48},{56,64},{72,80},{88,96},{104,112},{120,128}... | collective-permute-start | bytes 2383880 | tf_op jit(solution)/shard_map/ppermute | solution.py:857
  9.3 1.4 %collective-permute-start = (f32[184,256]{1,0:T(8,128)S(1)}, f32[184,256]{1,0:T(8,128)S(1)}, u32[]{:S(2)}, u32[]{:S(2)}) collective-permute-start(f32[184,256]{1,0:T(8,128)S(1)} %get-tuple-element.46.own_hi), channel_id=1, source_target_pairs={{0,1},{1,2},{2,3},{3,0},{4,5},{5,6},{6,7},{7,4},{8,9},{9,10},{10,1... | collective-permute-start | bytes 565256 | tf_op jit(solution)/shard_map/ppermute | solution.py:850
  10.7 1.5 %collective-permute-start.1 = (f32[184,256]{1,0:T(8,128)S(1)}, f32[184,256]{1,0:T(8,128)S(1)}, u32[]{:S(2)}, u32[]{:S(2)}) collective-permute-start(f32[184,256]{1,0:T(8,128)S(1)} %get-tuple-element.47.own_lo), channel_id=1, source_target_pairs={{0,3},{1,0},{2,1},{3,2},{4,7},{5,4},{6,5},{7,6},{8,11},{9,8},{10,9... | collective-permute-start | bytes 565256 | tf_op jit(solution)/shard_map/ppermute | solution.py:850
  12.2 3.0 %weights.1 = (f32[4,8,128,256]{3,2,1,0:T(8,128)S(1)}, f32[7,128,256]{2,1,0:T(8,128)S(1)}, f32[8,128,256]{2,1,0:T(8,128)S(1)}, f32[8,128,256]{2,1,0:T(8,128)S(1)}...) custom-call(f32[4,8,128,256]{3,2,1,0:T(8,128)} %u_hbm.3, f32[8,128,256]{2,1,0:T(8,128)} %c_hbm.3, ...), custom_call_target="tpu_custom_call" | custom-call | flops 20000000 | bytes 6000000 | tf_op jit(solution)/shard_map/weights/pallas_call | solution.py:330
  15.2 0.2 collective-permute-done.y_lo.i0
  15.4 0.0 collective-permute-done.1.y_hi.i1
  15.4 0.1 collective-permute-start.4
  15.5 5.8 %collective-permute-start.5 = (f32[8,256]{1,0:T(8,128)S(1)}, f32[8,256]{1,0:T(8,128)S(1)}, u32[]{:S(2)}, u32[]{:S(2)}) collective-permute-start(f32[8,256]{1,0:T(8,128)S(1)} %get-tuple-element.51), channel_id=1, source_target_pairs={{8,16},{24,32},{40,48},{56,64},{72,80},{88,96},{104,112},{120,128}... | collective-permute-start | bytes 24584 | tf_op jit(solution)/shard_map/ppermute | solution.py:857
  21.3 0.0 copy-done.1
  21.3 0.0 copy-start.2
  21.3 0.0 copy-start.3
  21.3 0.0 copy-start.4
  21.3 8.4 %inner.1 = (f32[2,4,128,256]{3,2,1,0:T(8,128)S(1)}, f32[4,4,128,256]{3,2,1,0:T(8,128)}, f32[8,128,256]{2,1,0:T(8,128)S(1)}, f32[8,256]{1,0:T(8,128)S(1)}, f32[8,...) custom-call(f32[4,8,128,256]{3,2,1,0:T(8,128)S(1)} %get-tuple-elemen, ...), custom_call_target="tpu_custom_call" | custom-call | flops 100000000 | bytes 25000000 | tf_op jit(solution)/shard_map/inner/pallas_call | solution.py:472
  29.7 0.0 collective-permute-done.4.ends_near
  29.7 0.0 collective-permute-done.5.ends_far
  29.7 0.0 collective-permute-done.2.x_near
  29.7 0.0 collective-permute-done.3.x_far
  29.8 0.0 copy-done.2
  29.8 0.0 copy-done.3
  29.8 0.0 copy-done.4
  29.8 0.0 copy-start
  29.8 3.4 %outer.1 = (f32[4,128,256]{2,1,0:T(8,128)}, f32[4,128,256]{2,1,0:T(8,128)}, f32[32,256]{1,0:T(8,128)}, f32[32,256]{1,0:T(8,128)}, f32[4,4,128,256]{3,2,1,0:T(8,1...) custom-call(s32[2,4]{1,0:T(2,128)S(1)} %bitcast.5, ...), custom_call_target="tpu_custom_call" | custom-call | flops 50000000 | bytes 15000000 | tf_op jit(solution)/shard_map/outer/pallas_call | solution.py:622
  33.2 0.1 collective-permute-start.6
  33.3 1.2 %collective-permute-done.6.got = f32[32,128]{1,0:T(8,128)S(1)} collective-permute-done((f32[32,128]{1,0:T(8,128)S(1)}, f32[32,128]{1,0:T(8,128)S(1)}, u32[]{:S(2)}, u32[]{:S(2)}) %collective-permute-start.6) | collective-permute-done | bytes 16416 | tf_op jit(solution)/shard_map/ppermute | solution.py:853
  34.5 0.9 %spread.1 = f32[16,32,128]{2,1,0:T(8,128)} custom-call(f32[32,128]{1,0:T(8,128)S(1)} %get-tuple-element.68.mine, f32[32,128]{1,0:T(8,128)S(1)} %collective-permute-done.6.got), custom_call_target="tpu_custom_call" | custom-call | tf_op jit(solution)/shard_map/spread/pallas_call | solution.py:658
  35.4 9.9 %all-to-all-start = ((f32[16,32,128]{2,1,0:T(8,128)}), f32[16,32,128]{2,1,0:T(8,128)S(1)}, u32[]{:S(2)}, u32[]{:S(2)}) async-start(f32[16,32,128]{2,1,0:T(8,128)} %spread.1), calls=%async_computation | async-start | bytes 524288 | tf_op jit(solution)/shard_map/all_to_all | solution.py:880
  45.2 0.5 collective-permute-start.12
  45.8 4.9 %collective-permute-start.13 = (f32[4,128,256]{2,1,0:T(8,128)}, f32[4,128,256]{2,1,0:T(8,128)S(1)}, u32[]{:S(2)}, u32[]{:S(2)}) collective-permute-start(f32[4,128,256]{2,1,0:T(8,128)} %get-tuple-element.87), channel_id=1, source_target_pairs={{8,16},{24,32},{40,48},{56,64},{72,80},{88,96},{104,112},{120,128}... | collective-permute-start | bytes 1572872 | tf_op jit(solution)/shard_map/ppermute | solution.py:857
  50.6 0.0 copy-done
  50.6 2.7 %collective-permute-start.10 = (f32[128,256]{1,0:T(8,128)S(1)}, f32[128,256]{1,0:T(8,128)S(1)}, u32[]{:S(2)}, u32[]{:S(2)}) collective-permute-start(f32[128,256]{1,0:T(8,128)S(1)} %copy-done), channel_id=1, source_target_pairs={{0,2},{1,3},{2,0},{3,1},{4,6},{5,7},{6,4},{7,5},{8,10},{9,11},{10,... | collective-permute-start | bytes 393224 | tf_op jit(solution)/shard_map/ppermute | solution.py:850
  53.4 4.7 %all-to-all-done.parts_hbm = f32[16,32,128]{2,1,0:T(8,128)S(1)} async-done(((f32[16,32,128]{2,1,0:T(8,128)}), f32[16,32,128]{2,1,0:T(8,128)S(1)}, u32[]{:S(2)}, u32[]{:S(2)}) %all-to-all-start) | async-done | bytes 262176 | tf_op jit(solution)/shard_map/all_to_all | solution.py:880
  58.1 1.3 %gathered.1 = (f32[48,256]{1,0:T(8,128)S(1)}, f32[48,256]{1,0:T(8,128)S(1)}, f32[16,256]{1,0:T(8,128)S(1)}) custom-call(f32[16,32,128]{2,1,0:T(8,128)S(1)} %all-to-all-done.parts_hbm, f32[32,256]{1,0:T(8,128)} %get-tuple-element.70.edge_lo, f32[32,256]{1,0:T(8,128)} %get-tuple-element.71.edge_hi), custom_call_target="tpu_custom_call" | custom-call | tf_op jit(solution)/shard_map/gathered/pallas_call | solution.py:684
  59.4 1.6 %collective-permute-start.7 = (f32[48,256]{1,0:T(8,128)S(1)}, f32[48,256]{1,0:T(8,128)S(1)}, u32[]{:S(2)}, u32[]{:S(2)}) collective-permute-start(f32[48,256]{1,0:T(8,128)S(1)} %get-tuple-element.72), channel_id=1, source_target_pairs={{0,1},{1,2},{2,3},{3,0},{4,5},{5,6},{6,7},{7,4},{8,9},{9,10},{10,1... | collective-permute-start | bytes 147464 | tf_op jit(solution)/shard_map/ppermute | solution.py:850
  60.9 1.5 %collective-permute-start.8 = (f32[48,256]{1,0:T(8,128)S(1)}, f32[48,256]{1,0:T(8,128)S(1)}, u32[]{:S(2)}, u32[]{:S(2)}) collective-permute-start(f32[48,256]{1,0:T(8,128)S(1)} %get-tuple-element.73), channel_id=1, source_target_pairs={{0,3},{1,0},{2,1},{3,2},{4,7},{5,4},{6,5},{7,6},{8,11},{9,8},{10,9... | collective-permute-start | bytes 147464 | tf_op jit(solution)/shard_map/ppermute | solution.py:850
  62.4 0.0 collective-permute-done.10.i3
  62.5 1.3 %collective-permute-start.9 = (f32[16,256]{1,0:T(8,128)S(1)}, f32[16,256]{1,0:T(8,128)S(1)}, u32[]{:S(2)}, u32[]{:S(2)}) collective-permute-start(f32[16,256]{1,0:T(8,128)S(1)} %get-tuple-element.74.after.a2), channel_id=1, source_target_pairs={{0,2},{1,3},{2,0},{3,1},{4,6},{5,7},{6,4},{7,5},{8,10},{9,11},{10,... | collective-permute-start | bytes 49160 | tf_op jit(solution)/shard_map/ppermute | solution.py:850
  63.7 3.7 %ready.1 = (f32[4,8,128,256]{3,2,1,0:T(8,128)S(1)}, f32[8,128,256]{2,1,0:T(8,128)S(1)}, f32[16,256]{1,0:T(8,128)S(1)}, f32[2,128,256]{2,1,0:T(8,128)S(1)}) custom-call(f32[16,256]{1,0:T(8,128)S(1)} %get-tuple-element.74.after.a2, f32[4,4,128,256]{3,2,1,0:T(8,128)} %get-tuple-element.76.inner_hbm, f32[4,4,128,256]{3,2,1,0:T(8,128)} %get-tuple-element.77.outer_hbm, ...), custom_call_target="tpu_custom_call" | custom-call | flops 10000000 | bytes 8000000 | tf_op jit(solution)/shard_map/ready/pallas_call | solution.py:763
  67.5 0.0 collective-permute-done.9.a3
  67.5 0.0 collective-permute-done.7.a0.e_lo
  67.5 0.0 collective-permute-done.8.a1.e_hi
  67.5 0.9 %blocks.1.own = f32[4,8,128]{2,1,0:T(8,128)S(1)} custom-call(f32[48,256]{1,0:T(8,128)S(1)} %collective-permute-done.7.a0.e_lo, f32[48,256]{1,0:T(8,128)S(1)} %collective-permute-done.8.a1.e_hi, f32[16,256]{1,0:T(8,128)S(1)} %get-tuple-element.74.after.a2, f32[16,256]{1,0:T(8,128)S(1)} %collective-permute-done.9.a3, ...), custom_call_target="tpu_custom_call" | custom-call | tf_op jit(solution)/shard_map/blocks/pallas_call | solution.py:716
  68.4 3.2 %collective-permute-start.11 = (f32[4,8,128]{2,1,0:T(8,128)S(1)}, f32[4,8,128]{2,1,0:T(8,128)S(1)}, u32[]{:S(2)}, u32[]{:S(2)}) collective-permute-start(f32[4,8,128]{2,1,0:T(8,128)S(1)} %blocks.1.own), channel_id=1, source_target_pairs={{0,8},{8,0},{1,9},{9,1},{2,10},{10,2},{3,11},{11,3},{4,12},{12,4},... | collective-permute-start | bytes 49160 | tf_op jit(solution)/shard_map/ppermute | solution.py:853
  71.6 0.0 collective-permute-done.12.h_near
  71.6 0.0 collective-permute-done.13.h_far
  71.6 0.8 %collective-permute-done.11.got = f32[4,8,128]{2,1,0:T(8,128)S(1)} collective-permute-done((f32[4,8,128]{2,1,0:T(8,128)S(1)}, f32[4,8,128]{2,1,0:T(8,128)S(1)}, u32[]{:S(2)}, u32[]{:S(2)}) %collective-permute-start.11) | collective-permute-done | bytes 16416 | tf_op jit(solution)/shard_map/ppermute | solution.py:853
  72.4 3.1 %correct.1 = (f32[4,8,128,256]{3,2,1,0:T(8,128)}, f32[4,512]{1,0:T(4,128)}) custom-call(s32[8,128]{1,0:T(8,128)S(1)} %copy-done.1, f32[4,8,128]{2,1,0:T(8,128)S(1)} %blocks.1.own, f32[4,8,128]{2,1,0:T(8,128)S(1)} %collective-permute-done.11.got, f32[4,8,128,256]{3,2,1,0:T(8,128)S(1)} %get-tuple-element.83.base, f32[8,128,256]{2,1,0:T(8,128)S(1)} %get-tuple-element.82.pull, ...), custom_call_target="tpu_custom_call" | custom-call | tf_op jit(solution)/shard_map/correct/pallas_call | solution.py:827
  (1 shorter events, 0.0 us)
Async XLA Ops:
  3.1 18.2 %copy-start.1 = (s32[8,128]{1,0:T(8,128)S(1)}, s32[8,128]{1,0:T(8,128)}, u32[]{:S(2)}) copy-start(s32[8,128]{1,0:T(8,128)} %cmap.5) | copy-start | bytes 12292
  3.1 26.6 %collective-permute-start.2 = (f32[776,256]{1,0:T(8,128)S(1)}, f32[776,256]{1,0:T(8,128)S(1)}, u32[]{:S(2)}, u32[]{:S(2)}) collective-permute-start(f32[776,256]{1,0:T(8,128)S(1)} %get-tuple-element.48), channel_id=1, source_target_pairs={{0,8},{8,0},{1,9},{9,1},{2,10},{10,2},{3,11},{11,3},{4,12},{12,4},... | collective-permute-start | bytes 2383880 | tf_op jit(solution)/shard_map/ppermute | solution.py:853
  6.5 23.3 %collective-permute-start.3 = (f32[776,256]{1,0:T(8,128)S(1)}, f32[776,256]{1,0:T(8,128)S(1)}, u32[]{:S(2)}, u32[]{:S(2)}) collective-permute-start(f32[776,256]{1,0:T(8,128)S(1)} %get-tuple-element.49), channel_id=1, source_target_pairs={{8,16},{24,32},{40,48},{56,64},{72,80},{88,96},{104,112},{120,128}... | collective-permute-start | bytes 2383880 | tf_op jit(solution)/shard_map/ppermute | solution.py:857
  9.3 6.1 %collective-permute-start = (f32[184,256]{1,0:T(8,128)S(1)}, f32[184,256]{1,0:T(8,128)S(1)}, u32[]{:S(2)}, u32[]{:S(2)}) collective-permute-start(f32[184,256]{1,0:T(8,128)S(1)} %get-tuple-element.46.own_hi), channel_id=1, source_target_pairs={{0,1},{1,2},{2,3},{3,0},{4,5},{5,6},{6,7},{7,4},{8,9},{9,10},{10,1... | collective-permute-start | bytes 565256 | tf_op jit(solution)/shard_map/ppermute | solution.py:850
  10.7 4.7 %collective-permute-start.1 = (f32[184,256]{1,0:T(8,128)S(1)}, f32[184,256]{1,0:T(8,128)S(1)}, u32[]{:S(2)}, u32[]{:S(2)}) collective-permute-start(f32[184,256]{1,0:T(8,128)S(1)} %get-tuple-element.47.own_lo), channel_id=1, source_target_pairs={{0,3},{1,0},{2,1},{3,2},{4,7},{5,4},{6,5},{7,6},{8,11},{9,8},{10,9... | collective-permute-start | bytes 565256 | tf_op jit(solution)/shard_map/ppermute | solution.py:850
  15.4 14.3 %collective-permute-start.4 = (f32[8,256]{1,0:T(8,128)S(1)}, f32[8,256]{1,0:T(8,128)S(1)}, u32[]{:S(2)}, u32[]{:S(2)}) collective-permute-start(f32[8,256]{1,0:T(8,128)S(1)} %get-tuple-element.50), channel_id=1, source_target_pairs={{0,8},{8,0},{1,9},{9,1},{2,10},{10,2},{3,11},{11,3},{4,12},{12,4},... | collective-permute-start | bytes 24584 | tf_op jit(solution)/shard_map/ppermute | solution.py:853
  15.5 14.2 %collective-permute-start.5 = (f32[8,256]{1,0:T(8,128)S(1)}, f32[8,256]{1,0:T(8,128)S(1)}, u32[]{:S(2)}, u32[]{:S(2)}) collective-permute-start(f32[8,256]{1,0:T(8,128)S(1)} %get-tuple-element.51), channel_id=1, source_target_pairs={{8,16},{24,32},{40,48},{56,64},{72,80},{88,96},{104,112},{120,128}... | collective-permute-start | bytes 24584 | tf_op jit(solution)/shard_map/ppermute | solution.py:857
  21.3 8.4 %copy-start.2 = (f32[2048]{0:T(1024)S(1)}, f32[2048]{0:T(1024)}, u32[]{:S(2)}) copy-start(f32[2048]{0:T(1024)} %param.12) | copy-start | bytes 24580
  21.3 8.4 %copy-start.3 = (s32[4,2]{0,1:T(2,128)S(1)}, s32[4,2]{0,1:T(2,128)}, u32[]{:S(2)}) copy-start(s32[4,2]{0,1:T(2,128)} %param.14) | copy-start | bytes 100
  21.3 8.4 %copy-start.4 = (f32[4]{0:T(128)S(1)}, f32[4]{0:T(128)}, u32[]{:S(2)}) copy-start(f32[4]{0:T(128)} %param.15) | copy-start | bytes 52
  29.8 20.9 %copy-start = (f32[128,256]{1,0:T(8,128)S(1)}, f32[128,256]{1,0:T(8,128)}, u32[]{:S(2)}) copy-start(f32[128,256]{1,0:T(8,128)} %get-tuple-element.75.i2) | copy-start | bytes 393220
  33.2 1.3 %collective-permute-start.6 = (f32[32,128]{1,0:T(8,128)S(1)}, f32[32,128]{1,0:T(8,128)S(1)}, u32[]{:S(2)}, u32[]{:S(2)}) collective-permute-start(f32[32,128]{1,0:T(8,128)S(1)} %get-tuple-element.69), channel_id=1, source_target_pairs={{0,8},{8,0},{1,9},{9,1},{2,10},{10,2},{3,11},{11,3},{4,12},{12,4},... | collective-permute-start | bytes 49160 | tf_op jit(solution)/shard_map/ppermute | solution.py:853
  35.4 22.7 %all-to-all-start = ((f32[16,32,128]{2,1,0:T(8,128)}), f32[16,32,128]{2,1,0:T(8,128)S(1)}, u32[]{:S(2)}, u32[]{:S(2)}) async-start(f32[16,32,128]{2,1,0:T(8,128)} %spread.1), calls=%async_computation | async-start | bytes 524288 | tf_op jit(solution)/shard_map/all_to_all | solution.py:880
  45.2 26.3 %collective-permute-start.12 = (f32[4,128,256]{2,1,0:T(8,128)}, f32[4,128,256]{2,1,0:T(8,128)S(1)}, u32[]{:S(2)}, u32[]{:S(2)}) collective-permute-start(f32[4,128,256]{2,1,0:T(8,128)} %get-tuple-element.86), channel_id=1, source_target_pairs={{0,8},{8,0},{1,9},{9,1},{2,10},{10,2},{3,11},{11,3},{4,12},{12,4},... | collective-permute-start | bytes 1572872 | tf_op jit(solution)/shard_map/ppermute | solution.py:853
  45.8 25.8 %collective-permute-start.13 = (f32[4,128,256]{2,1,0:T(8,128)}, f32[4,128,256]{2,1,0:T(8,128)S(1)}, u32[]{:S(2)}, u32[]{:S(2)}) collective-permute-start(f32[4,128,256]{2,1,0:T(8,128)} %get-tuple-element.87), channel_id=1, source_target_pairs={{8,16},{24,32},{40,48},{56,64},{72,80},{88,96},{104,112},{120,128}... | collective-permute-start | bytes 1572872 | tf_op jit(solution)/shard_map/ppermute | solution.py:857
  50.6 11.8 %collective-permute-start.10 = (f32[128,256]{1,0:T(8,128)S(1)}, f32[128,256]{1,0:T(8,128)S(1)}, u32[]{:S(2)}, u32[]{:S(2)}) collective-permute-start(f32[128,256]{1,0:T(8,128)S(1)} %copy-done), channel_id=1, source_target_pairs={{0,2},{1,3},{2,0},{3,1},{4,6},{5,7},{6,4},{7,5},{8,10},{9,11},{10,... | collective-permute-start | bytes 393224 | tf_op jit(solution)/shard_map/ppermute | solution.py:850
  59.4 8.1 %collective-permute-start.7 = (f32[48,256]{1,0:T(8,128)S(1)}, f32[48,256]{1,0:T(8,128)S(1)}, u32[]{:S(2)}, u32[]{:S(2)}) collective-permute-start(f32[48,256]{1,0:T(8,128)S(1)} %get-tuple-element.72), channel_id=1, source_target_pairs={{0,1},{1,2},{2,3},{3,0},{4,5},{5,6},{6,7},{7,4},{8,9},{9,10},{10,1... | collective-permute-start | bytes 147464 | tf_op jit(solution)/shard_map/ppermute | solution.py:850
  60.9 6.6 %collective-permute-start.8 = (f32[48,256]{1,0:T(8,128)S(1)}, f32[48,256]{1,0:T(8,128)S(1)}, u32[]{:S(2)}, u32[]{:S(2)}) collective-permute-start(f32[48,256]{1,0:T(8,128)S(1)} %get-tuple-element.73), channel_id=1, source_target_pairs={{0,3},{1,0},{2,1},{3,2},{4,7},{5,4},{6,5},{7,6},{8,11},{9,8},{10,9... | collective-permute-start | bytes 147464 | tf_op jit(solution)/shard_map/ppermute | solution.py:850
  62.5 5.0 %collective-permute-start.9 = (f32[16,256]{1,0:T(8,128)S(1)}, f32[16,256]{1,0:T(8,128)S(1)}, u32[]{:S(2)}, u32[]{:S(2)}) collective-permute-start(f32[16,256]{1,0:T(8,128)S(1)} %get-tuple-element.74.after.a2), channel_id=1, source_target_pairs={{0,2},{1,3},{2,0},{3,1},{4,6},{5,7},{6,4},{7,5},{8,10},{9,11},{10,... | collective-permute-start | bytes 49160 | tf_op jit(solution)/shard_map/ppermute | solution.py:850
  68.4 4.0 %collective-permute-start.11 = (f32[4,8,128]{2,1,0:T(8,128)S(1)}, f32[4,8,128]{2,1,0:T(8,128)S(1)}, u32[]{:S(2)}, u32[]{:S(2)}) collective-permute-start(f32[4,8,128]{2,1,0:T(8,128)S(1)} %blocks.1.own), channel_id=1, source_target_pairs={{0,8},{8,0},{1,9},{9,1},{2,10},{10,2},{3,11},{11,3},{4,12},{12,4},... | collective-permute-start | bytes 49160 | tf_op jit(solution)/shard_map/ppermute | solution.py:853

commit v5 on v4

--- a/solution.py
+++ b/solution.py
@@ -150,19 +150,17 @@
 def scatter(id_rows, values):
     place = iota((64, 128), 0)
     block_of = 4 * ((place // 8) % 4) + 2 * (place // 32) + (place // 4) % 2
-    total = jnp.zeros((192, 128), F32)
+    total = jnp.zeros((128, 128), F32)
     for id_row, value in zip(id_rows, values):
         hit = lax.shift_right_logical(id_row, 7) == block_of
         spread = jnp.where(hit, jnp.concatenate([value] * 16, axis=0), 0.0)
         lane_hit = lax.bitwise_and(id_row, 127) == iota((128, 128), 0)
         onehot = jnp.where(lane_hit, 1.0, 0.0).astype(jnp.bfloat16)
         a = spread.astype(jnp.bfloat16)
-        spread = spread - a.astype(F32)
-        b = spread.astype(jnp.bfloat16)
-        spread = spread - b.astype(F32)
-        parts = jnp.concatenate([a, b, spread.astype(jnp.bfloat16)], axis=0)
+        b = (spread - a.astype(F32)).astype(jnp.bfloat16)
+        parts = jnp.concatenate([a, b], axis=0)
         total = total + lax.dot_general(parts, onehot, NT, preferred_element_type=F32)
-    return total[0:64] + total[64:128] + total[128:192]
+    return total[0:64] + total[64:128]
 
 
 ROW_C = 512
@@ -267,7 +265,8 @@
 
 
 def weights_kernel(
-    u_hbm, c_hbm, cmap_hbm, admittance_hbm, u, wx, wy, wz, diag, zeta_t, rim, c, cmap, admittance, sems, u_sems
+    u_hbm, f, c_hbm, cmap_hbm, admittance_hbm, u, wx, wy, wz, diag, zeta_t, rim, pulled1, keep1,
+    c, cmap, admittance, sems, u_sems,
 ):
     small = [
         pltpu.make_async_copy(cmap_hbm, cmap, sems.at[8]),
@@ -314,22 +313,42 @@
                 total = total + wx[x - 1, tile(k), :]
             wy[x, tile(k), :] = along_y
             wz[x, tile(k), :] = along_z
-            diag[x, tile(k), :] = total
+            diag[x, tile(k), :] = total if x in (0, 7) or k in (0, 15) else OMEGA * inverse(total)
     rim[0] = c[0]
     rim[1] = c[7]
     for copy in later:
         copy.wait()
 
-
-def weights(u, c, cmap, admittance):
+    def rim_row(n, carry):
+        x = 7 * n
+        inside = 1 + 5 * n
+
+        def emit(s, k, here, pulled):
+            pulled1[n, s, tile(k), :] = pulled
+            keep1[n, s, tile(k), :] = KEEP * here
+
+        sweep(
+            lambda s, k: u[s, x, tile(k), :],
+            lambda s, k: f[s, x, tile(k), :],
+            lambda k: wy[x, tile(k), :],
+            lambda k: wz[x, tile(k), :],
+            [(lambda k: wx[6 * n, tile(k), :], lambda s, k: u[s, inside, tile(k), :])],
+            emit,
+        )
+        return carry
+
+    lax.fori_loop(0, 2, rim_row, 0)
+
+
+def weights(u, f, c, cmap, admittance):
     outs = [
         kept(4, 8, 128, 256),
         kept(7, 128, 256), kept(8, 128, 256), kept(8, 128, 256), kept(8, 128, 256), kept(128, 128),
-        kept(2, 128, 256),
+        kept(2, 128, 256), kept(2, 4, 128, 256), kept(2, 4, 128, 256),
     ]
     return pl.pallas_call(
         weights_kernel,
-        in_specs=[hbm()] * 4,
+        in_specs=[hbm(), vmem()] + [hbm()] * 3,
         out_specs=[vmem()] * len(outs),
         out_shape=outs,
         scratch_shapes=[
@@ -342,19 +361,14 @@
         compiler_params=params(4),
         cost_estimate=pl.CostEstimate(flops=20_000_000, bytes_accessed=6_000_000, transcendentals=0),
         name="weights",
-    )(u, c, cmap, admittance)
+    )(u, f, c, cmap, admittance)
 
 
 def inner_kernel(
-    u, f_hbm, cmap, own_lo, own_hi, y_lo, y_hi, wx, wy, wz, diag,
-    u2, u2_out, gain, wyl, wyh, pulled1, keep1, pulled2, edge_lo, edge_hi, contact,
-    f, u1, sums, folded, middle, sems, f_sems,
+    u, f, cmap, own_lo, own_hi, y_lo, y_hi, wx, wy, wz, diag,
+    u2, u2_out, gain, wyl, wyh, pulled2, edge_lo, edge_hi, contact,
+    u1, sums, folded, middle, sems,
 ):
-    def row_of_f(x):
-        return pltpu.make_async_copy(f_hbm.at[:, x], f.at[:, x], f_sems.at[x])
-
-    for x in (1, 2, 3, 4, 5, 6, 0, 7):
-        row_of_f(x).start()
 
     below, above = has_elecs()
     wyl[...] = outer_face(own_lo[32:40, :], below * y_lo[32:40, :])
@@ -367,7 +381,7 @@
                 total = total + jnp.where(row == 0, wyl[x : x + 1, :], 0.0)
             if k == 15:
                 total = total + jnp.where(row == 7, wyh[x : x + 1, :], 0.0)
-            gain[x, tile(k), :] = total if x in (0, 7) else OMEGA * inverse(total)
+            gain[x, tile(k), :] = OMEGA * inverse(total) if 0 < x < 7 and k in (0, 15) else total
 
     def with_halos(pulled, s, k, x):
         at = 8 * s + x
@@ -378,7 +392,6 @@
         return pulled
 
     def first(x, carry):
-        row_of_f(x).wait()
 
         def emit(s, k, here, pulled):
             new = KEEP * here + gain[x, tile(k), :] * with_halos(pulled, s, k, x)
@@ -402,29 +415,12 @@
         return carry
 
     lax.fori_loop(1, 7, first, 0)
-    row_of_f(0).wait()
-    row_of_f(7).wait()
-
-    def rim(n, carry):
-        x = 7 * n
-        inside = 1 + 5 * n
-
-        def emit(s, k, here, pulled):
-            pulled1[n, s, tile(k), :] = with_halos(pulled, s, k, x)
-            keep1[n, s, tile(k), :] = KEEP * here
-            pulled2[n, s, tile(k), :] = f[s, x, tile(k), :] + wx[6 * n, tile(k), :] * u1[s, inside, tile(k), :]
-
-        sweep(
-            lambda s, k: u[s, x, tile(k), :],
-            lambda s, k: f[s, x, tile(k), :],
-            lambda k: wy[x, tile(k), :],
-            lambda k: wz[x, tile(k), :],
-            [(lambda k: wx[6 * n, tile(k), :], lambda s, k: u[s, inside, tile(k), :])],
-            emit,
-        )
-        return carry
-
-    lax.fori_loop(0, 2, rim, 0)
+
+    for n in range(2):
+        for k in range(16):
+            weight = wx[6 * n, tile(k), :]
+            for s in range(4):
+                pulled2[n, s, tile(k), :] = f[s, 7 * n, tile(k), :] + weight * u1[s, 1 + 5 * n, tile(k), :]
 
     def second(x, sides_at, target):
         def emit(s, k, here, pulled):
@@ -466,35 +462,84 @@
 def inner(u, f, cmap, own_lo, own_hi, y_lo, y_hi, wx, wy, wz, diag):
     outs = [
         kept(2, 4, 128, 256), stored(4, 4, 128, 256), kept(8, 128, 256), kept(8, 256), kept(8, 256),
-        kept(2, 4, 128, 256), kept(2, 4, 128, 256), kept(2, 4, 128, 256),
+        kept(2, 4, 128, 256),
         kept(32, 256), kept(32, 256), kept(64, 128),
     ]
     return pl.pallas_call(
         inner_kernel,
-        in_specs=[vmem(), hbm()] + [vmem()] * 9,
+        in_specs=[vmem()] * 11,
         out_specs=[vmem(), hbm()] + [vmem()] * (len(outs) - 2),
         out_shape=outs,
         scratch_shapes=[
-            pltpu.VMEM((4, 8, 128, 256), F32),
             pltpu.VMEM((4, 8, 128, 256), F32),
             pltpu.VMEM((8, 4, 128), F32),
             pltpu.VMEM((512, 128), F32),
             pltpu.VMEM((4, 4, 128, 256), F32),
             pltpu.SemaphoreType.DMA((4,)),
-            pltpu.SemaphoreType.DMA((8,)),
         ],
-        compiler_params=params(16),
+        compiler_params=params(12),
         cost_estimate=pl.CostEstimate(flops=100_000_000, bytes_accessed=25_000_000, transcendentals=0),
         name="inner",
     )(u, f, cmap, own_lo, own_hi, y_lo, y_hi, wx, wy, wz, diag)
 
 
-def outer_kernel(
-    pairs, amplitudes, cmap, admittance, rim, y_lo, y_hi, x_near, x_far, ends_near, ends_far,
-    wx, wy, wz, gain, wyl, wyh, u2, pulled1, keep1, pulled2, e_lo, e_hi, contact, zeta_in,
-    face_near_out, face_far_out, edge_lo_out, edge_hi_out, u2_out, gain_out, wxf_out, misc_out, zeta_out, mine, other,
-    ids, face_near, face_far, edge_lo, edge_hi, u2b, gain_b, wxf, misc, folded, sems, u2_sems, edge_sems,
+def one_side(
+    side, msg, ends, neighbour_ids, cmap, admittance, rim, y_lo, y_hi, wx, wy, wz, gain, wyl, wyh, u2, pulled1, keep1,
+    pulled2, out, g_ref, outside_ref, u2_row, u2_inside, folded, faces_done, inside_done, row_done,
 ):
+    x = 7 * side
+    zeta = gather_rows(jnp.broadcast_to(neighbour_ids, (8, 128)), admittance[...])
+    zeta_t = jnp.transpose(jnp.concatenate([zeta, jnp.zeros((120, 128), F32)], axis=0))
+    row = iota((128, 256), 0)
+    there = msg[ROW_C : ROW_C + 128, :]
+    outside = outer_face(rim[side], there)
+    outside_ref[...] = outside
+    g = OMEGA * inverse(gain[x] + outside)
+    g_ref[...] = g
+    for s in range(4):
+        out[s] = keep1[side, s] + g * (pulled1[side, s] + outside * msg[128 * s : 128 * s + 128, :])
+        at = 8 * s + x
+        low = g[0:1] * wyl[pl.ds(x, 1), :] * y_lo[pl.ds(at, 1), :]
+        high = g[127:128] * wyh[pl.ds(x, 1), :] * y_hi[pl.ds(at, 1), :]
+        out[s, 0:1, :] = out[s, 0:1, :] + low
+        out[s, 127:128, :] = out[s, 127:128, :] + high
+    faces_done()
+    spare = jnp.maximum(there, TINY)
+    diag = both_sides(line_weight(spare, 0), 0) + both_sides(line_weight(spare, 1), 1) + zeta_t[:, 0:1]
+    diag = diag + outside + outer_face(there, msg[ROW_C2 : ROW_C2 + 128, :])
+    diag = diag + jnp.where(row == 0, outer_face(there[0:1], ends[0:1, :]), 0.0)
+    diag = diag + jnp.where(row == 127, outer_face(there[127:128], ends[1:2, :]), 0.0)
+    factor = OMEGA * outside * inverse(jnp.maximum(diag, TINY))
+    beyond = row_sums([factor * out[s] for s in range(4)])
+    inside = 1 + 5 * side
+    factor = gain[inside] * wx[6 * side]
+    slabs = []
+    for s in range(4):
+        new = factor * out[s]
+        u2_inside[s] = u2[side, s] + new
+        slabs.append(new)
+    inside_done()
+    within = row_sums(slabs)
+
+    def emit(s, k, here, pulled):
+        new = KEEP * here + g_ref[tile(k), :] * pulled
+        u2_row[s, tile(k), :] = new
+        folded[pl.ds(128 * s + 8 * k, 8), :] = fold(new)
+
+    sweep(
+        lambda s, k: out[s, tile(k), :],
+        lambda s, k: pulled2[side, s, tile(k), :],
+        lambda k: wy[x, tile(k), :],
+        lambda k: wz[x, tile(k), :],
+        [],
+        emit,
+    )
+    row_done()
+    ids = [neighbour_ids, cmap[pl.ds(inside, 1), :], cmap[pl.ds(x, 1), :]]
+    return ids, [beyond, within, folded_sums(folded[...])]
+
+
+def sender():
     copies = []
 
     def send(source, target, sem):
@@ -502,101 +547,110 @@
         copy.start()
         copies.append(copy)
 
+    return send, copies
+
+
+def near_kernel(
+    cmap, admittance, rim, y_lo, y_hi, msg, ends,
+    wx, wy, wz, gain, wyl, wyh, u2, pulled1, keep1, pulled2, contact_in,
+    face_out, u2_out, face_near, gain_near, outside_near, contact,
+    u2b, folded, sems,
+):
+    send, copies = sender()
+    ids, values = one_side(
+        sides()[0], msg, ends, msg[ROW_MAP : ROW_MAP + 1, 0:128].astype(jnp.int32), cmap, admittance, rim, y_lo, y_hi,
+        wx, wy, wz, gain, wyl, wyh, u2, pulled1, keep1, pulled2, face_near, gain_near, outside_near,
+        u2b.at[0], u2b.at[1], folded,
+        lambda: send(face_near, face_out, sems.at[0]),
+        lambda: send(u2b.at[1], u2_out.at[1], sems.at[1]),
+        lambda: send(u2b.at[0], u2_out.at[0], sems.at[2]),
+    )
+    contact[...] = contact_in[...] + scatter(ids, values)
+    for copy in copies:
+        copy.wait()
+
+
+def near_side(*args):
+    outs = [
+        stored(4, 128, 256), stored(2, 4, 128, 256),
+        kept(4, 128, 256), kept(128, 256), kept(128, 256), kept(64, 128),
+    ]
+    return pl.pallas_call(
+        near_kernel,
+        in_specs=[vmem()] * len(args),
+        out_specs=[hbm()] * 2 + [vmem()] * 4,
+        out_shape=outs,
+        scratch_shapes=[
+            pltpu.VMEM((2, 4, 128, 256), F32),
+            pltpu.VMEM((512, 128), F32),
+            pltpu.SemaphoreType.DMA((3,)),
+        ],
+        compiler_params=params(12),
+        cost_estimate=pl.CostEstimate(flops=25_000_000, bytes_accessed=8_000_000, transcendentals=0),
+        name="near_side",
+    )(*args)
+
+
+def far_kernel(
+    pairs, amplitudes, face_near, gain_near, outside_near, ends_near, e_lo, e_hi, zeta_in,
+    cmap, admittance, rim, y_lo, y_hi, msg, ends,
+    wx, wy, wz, gain, wyl, wyh, u2, pulled1, keep1, pulled2, contact_in,
+    face_out, edge_lo_out, edge_hi_out, u2_out, gain_out, wxf_out, misc_out, zeta_out, mine, other,
+    face_far, edge_lo, edge_hi, u2b, gain_far, outside_far, misc, folded, sems,
+):
+    near, far = sides()
+    send, copies = sender()
     send(gain.at[pl.ds(1, 6)], gain_out.at[pl.ds(1, 6)], sems.at[0])
-    send(zeta_in, zeta_out, sems.at[1])
+    send(gain_near, gain_out.at[7 * near], sems.at[1])
+    send(outside_near, wxf_out.at[0], sems.at[2])
+    send(zeta_in, zeta_out, sems.at[3])
     misc[0:8, :] = wyl[...]
     misc[8:16, :] = wyh[...]
-    send(misc, misc_out, sems.at[3])
-    ids[0:8, :] = jnp.full((8, 128), 2048, jnp.int32)
-    ids[0:1, :] = x_near[ROW_MAP : ROW_MAP + 1, 0:128].astype(jnp.int32)
-    ids[1:2, :] = x_far[ROW_MAP : ROW_MAP + 1, 0:128].astype(jnp.int32)
+    send(misc, misc_out, sems.at[4])
+    id_rows, values = one_side(
+        far, msg, ends, msg[ROW_MAP : ROW_MAP + 1, 0:128].astype(jnp.int32), cmap, admittance, rim, y_lo, y_hi,
+        wx, wy, wz, gain, wyl, wyh, u2, pulled1, keep1, pulled2, face_far, gain_far, outside_far,
+        u2b.at[0], u2b.at[1], folded,
+        lambda: send(face_far, face_out, sems.at[5]),
+        lambda: send(u2b.at[1], u2_out.at[1], sems.at[6]),
+        lambda: send(u2b.at[0], u2_out.at[0], sems.at[7]),
+    )
+    send(gain_far, gain_out.at[7 * far], sems.at[8])
+    send(outside_far, wxf_out.at[1], sems.at[9])
+
     lanes = iota((1, 128), 1)
     low_ids = y_lo[48:49, 0:128].astype(jnp.int32)
     high_ids = pltpu.roll(y_hi[48:49, 0:128], 8, 1).astype(jnp.int32)
-    ids[2:3, :] = jnp.where(lanes < 8, low_ids, jnp.where(lanes < 16, high_ids, 2048))
-    zeta = gather_rows(ids[...], admittance[...])
+    edge_ids = jnp.where(lanes < 8, low_ids, jnp.where(lanes < 16, high_ids, 2048))
+    zeta = gather_rows(jnp.broadcast_to(edge_ids, (8, 128)), admittance[...])
     zeta_t = jnp.transpose(jnp.concatenate([zeta, jnp.zeros((120, 128), F32)], axis=0))
-    row = iota((128, 256), 0)
-
-    id_rows = []
-    values = []
-    for n, (side, msg, ends, out, sent) in enumerate(
-        zip(sides(), (x_near, x_far), (ends_near, ends_far), (face_near, face_far), (face_near_out, face_far_out))
-    ):
-        x = 7 * side
-        there = msg[ROW_C : ROW_C + 128, :]
-        outside = outer_face(rim[side], there)
-        wxf[n] = outside
-        g = OMEGA * inverse(gain[x] + outside)
-        gain_b[n] = g
-        for s in range(4):
-            out[s] = keep1[side, s] + g * (pulled1[side, s] + outside * msg[128 * s : 128 * s + 128, :])
-        send(out, sent, sems.at[4 + n])
-        send(gain_b.at[n], gain_out.at[x], sems.at[6 + n])
-        spare = jnp.maximum(there, TINY)
-        diag = both_sides(line_weight(spare, 0), 0) + both_sides(line_weight(spare, 1), 1) + zeta_t[:, n : n + 1]
-        diag = diag + outside + outer_face(there, msg[ROW_C2 : ROW_C2 + 128, :])
-        diag = diag + jnp.where(row == 0, outer_face(there[0:1], ends[0:1, :]), 0.0)
-        diag = diag + jnp.where(row == 127, outer_face(there[127:128], ends[1:2, :]), 0.0)
-        factor = OMEGA * outside * inverse(jnp.maximum(diag, TINY))
-        id_rows.append(ids[n : n + 1, :])
-        values.append(row_sums([factor * out[s] for s in range(4)]))
-        inside = 1 + 5 * side
-        factor = gain[inside] * wx[6 * side]
-        slabs = []
-        for s in range(4):
-            new = factor * out[s]
-            u2b[2 * n + 1, s] = u2[side, s] + new
-            slabs.append(new)
-        send(u2b.at[2 * n + 1], u2_out.at[2 * side + 1], u2_sems.at[2 * n + 1])
-        id_rows.append(cmap[pl.ds(inside, 1), :])
-        values.append(row_sums(slabs))
-        def emit(s, k, here, pulled, n=n):
-            new = KEEP * here + gain_b[n, tile(k), :] * pulled
-            u2b[2 * n, s, tile(k), :] = new
-            folded[pl.ds(128 * s + 8 * k, 8), :] = fold(new)
-
-        sweep(
-            lambda s, k, out=out: out[s, tile(k), :],
-            lambda s, k, side=side: pulled2[side, s, tile(k), :],
-            lambda k, x=x: wy[x, tile(k), :],
-            lambda k, x=x: wz[x, tile(k), :],
-            [],
-            emit,
-        )
-        send(u2b.at[2 * n], u2_out.at[2 * side], u2_sems.at[2 * n])
-        id_rows.append(cmap[pl.ds(x, 1), :])
-        values.append(folded_sums(folded[...]))
-
-    send(wxf, wxf_out, sems.at[8])
-
     edge_sums = jnp.zeros((4, 128), F32)
-    for n, (msg, own, inside, edge, y, sent) in enumerate(
+    for n, (edge_msg, own, inside, edge, y, sent) in enumerate(
         ((y_lo, wyl, e_lo, edge_lo, 0, edge_lo_out), (y_hi, wyh, e_hi, edge_hi, 127, edge_hi_out))
     ):
         edge[0:32, :] = inside[...]
         for s in range(4):
             for side, out in zip(sides(), (face_near, face_far)):
                 edge[pl.ds(8 * s + 7 * side, 1), :] = out[s, y : y + 1, :]
-        send(edge, sent, edge_sems.at[n])
-        there = msg[32:40, :]
+        send(edge, sent, sems.at[10 + n])
+        there = edge_msg[32:40, :]
         x_rows = iota((8, 256), 0)
         spare = jnp.maximum(there, TINY)
         diag = both_sides(line_weight(spare, 0), 0) + both_sides(line_weight(spare, 1), 1) + own[...]
-        diag = diag + outer_face(there, msg[40:48, :])
-        for side, ends in zip(sides(), (ends_near, ends_far)):
-            diag = diag + jnp.where(x_rows == 7 * side, outer_face(there, ends[n : n + 1, :]), 0.0)
-        diag = diag + zeta_t[8 * n : 8 * n + 8, 2:3]
+        diag = diag + outer_face(there, edge_msg[40:48, :])
+        for side, corner in zip(sides(), (ends_near, ends)):
+            diag = diag + jnp.where(x_rows == 7 * side, outer_face(there, corner[n : n + 1, :]), 0.0)
+        diag = diag + zeta_t[8 * n : 8 * n + 8, 0:1]
         factor = OMEGA * own[...] * inverse(jnp.maximum(diag, TINY))
         lined = []
         for s in range(4):
             line = to_lanes(jnp.sum(factor * edge[8 * s : 8 * s + 8, :], axis=1, keepdims=True))
             lined.append(pltpu.roll(line, 8 * n, 1) if n else line)
         edge_sums = edge_sums + jnp.concatenate(lined, axis=0)
-    id_rows.append(ids[2:3, :])
+    id_rows.append(edge_ids)
     values.append(edge_sums)
 
-    total = (contact[...] + scatter(id_rows, values)) * (1.0 / 256.0)
+    total = (contact_in[...] + scatter(id_rows, values)) * (1.0 / 256.0)
     place = iota((64, 128), 0)
     electrode = (4 * ((place // 8) % 4) + 2 * (place // 32) + (place // 4) % 2) * 128 + iota((64, 128), 1)
     adds = jnp.logical_and(lax.axis_index("zx") == 0, lax.axis_index("elec") == 0)
@@ -613,45 +667,41 @@
         copy.wait()
 
 
-def outer(pairs, amplitudes, *args):
+def far_side(*args):
     outs = [
-        stored(4, 128, 256), stored(4, 128, 256), stored(32, 256), stored(32, 256),
-        stored(4, 4, 128, 256), stored(8, 128, 256), stored(2, 128, 256), stored(16, 256), stored(128, 128),
+        stored(4, 128, 256), stored(32, 256), stored(32, 256),
+        stored(2, 4, 128, 256), stored(8, 128, 256), stored(2, 128, 256), stored(16, 256), stored(128, 128),
         f32(32, 128), f32(32, 128),
     ]
     return pl.pallas_call(
-        outer_kernel,
-        in_specs=[vmem()] * (2 + len(args)),
-        out_specs=[hbm()] * 9 + [vmem()] * 2,
+        far_kernel,
+        in_specs=[vmem()] * len(args),
+        out_specs=[hbm()] * 8 + [vmem()] * 2,
         out_shape=outs,
         scratch_shapes=[
-            pltpu.VMEM((8, 128), jnp.int32),
-            pltpu.VMEM((4, 128, 256), F32),
             pltpu.VMEM((4, 128, 256), F32),
             pltpu.VMEM((32, 256), F32),
             pltpu.VMEM((32, 256), F32),
-            pltpu.VMEM((4, 4, 128, 256), F32),
-            pltpu.VMEM((2, 128, 256), F32),
-            pltpu.VMEM((2, 128, 256), F32),
+            pltpu.VMEM((2, 4, 128, 256), F32),
+            pltpu.VMEM((128, 256), F32),
+            pltpu.VMEM((128, 256), F32),
             pltpu.VMEM((16, 256), F32),
             pltpu.VMEM((512, 128), F32),
-            pltpu.SemaphoreType.DMA((9,)),
-            pltpu.SemaphoreType.DMA((4,)),
-            pltpu.SemaphoreType.DMA((2,)),
+            pltpu.SemaphoreType.DMA((12,)),
         ],
-        compiler_params=params(32),
-        cost_estimate=pl.CostEstimate(flops=50_000_000, bytes_accessed=15_000_000, transcendentals=0),
-        name="outer",
-    )(pairs, amplitudes, *args)
-
-
-def spread_kernel(mine, got, out, both, sems):
-    both[...] = mine[...] + got[...]
-    copies = [pltpu.make_async_copy(both, out.at[n], sems.at[n]) for n in range(out.shape[0])]
-    for copy in copies:
-        copy.start()
-    for copy in copies:
-        copy.wait()
+        compiler_params=params(12),
+        cost_estimate=pl.CostEstimate(flops=25_000_000, bytes_accessed=8_000_000, transcendentals=0),
+        name="far_side",
+    )(*args)
+
+
+def spread_kernel(mine, got, out, copies, sem):
+    both = mine[...] + got[...]
+    for n in range(out.shape[0]):
+        copies[n] = both
+    copy = pltpu.make_async_copy(copies, out, sem)
+    copy.start()
+    copy.wait()
 
 
 def spread(mine, got, count):
@@ -660,14 +710,14 @@
         in_specs=[vmem()] * 2,
         out_specs=hbm(),
         out_shape=stored(count, 32, 128),
-        scratch_shapes=[pltpu.VMEM((32, 128), F32), pltpu.SemaphoreType.DMA((count,))],
+        scratch_shapes=[pltpu.VMEM((count, 32, 128), F32), pltpu.SemaphoreType.DMA],
         compiler_params=params(2),
         name="spread",
     )(mine, got)
 
 
 def gathered_kernel(parts_hbm, edge_lo, edge_hi, to_above, to_below, out, parts, sems, edge_sems):
-    copies = [pltpu.make_async_copy(parts_hbm.at[n], parts.at[n], sems.at[n]) for n in range(parts.shape[0])]
+    copies = [pltpu.make_async_copy(parts_hbm, parts, sems.at[0])]
     for n, (source, target) in enumerate(((edge_hi, to_above), (edge_lo, to_below))):
         copies.append(pltpu.make_async_copy(source, target.at[pl.ds(16, 32)], edge_sems.at[n]))
     for copy in copies:
@@ -688,7 +738,7 @@
         out_shape=[f32(48, 256), f32(48, 256), f32(16, 256)],
         scratch_shapes=[
             pltpu.VMEM(parts.shape, F32),
-            pltpu.SemaphoreType.DMA((parts.shape[0],)),
+            pltpu.SemaphoreType.DMA((1,)),
             pltpu.SemaphoreType.DMA((2,)),
         ],
         compiler_params=params(4),
@@ -725,13 +775,16 @@
 
 
 def ready_kernel(
-    after, inner_hbm, outer_hbm, gain_hbm, wxf_hbm, misc_hbm, zeta_hbm, base, pull, sides_out, rows_out,
+    after, inner_hbm, near_hbm, far_hbm, gain_hbm, wxf_hbm, misc_hbm, zeta_hbm, base, pull, sides_out, rows_out,
     gain, wxf, misc, zeta_t, sems, small_sems,
 ):
     order = (2, 3, 4, 5, 1, 6, 0, 7)
-    rows = {x: inner_hbm.at[:, x - 2] for x in range(2, 6)}
-    rows.update({x: outer_hbm.at[n] for n, x in enumerate((0, 1, 7, 6))})
-    copies = {x: pltpu.make_async_copy(rows[x], base.at[:, x], sems.at[x]) for x in order}
+    middle = [pltpu.make_async_copy(inner_hbm, base.at[:, pl.ds(2, 4)], sems.at[0])]
+    rest = []
+    for n, (side, source) in enumerate(zip(sides(), (near_hbm, far_hbm))):
+        for inside in range(2):
+            x = 7 * side + inside * (1 - 2 * side)
+            rest.append(pltpu.make_async_copy(source.at[inside], base.at[:, x], sems.at[1 + 2 * n + inside]))
     small = [
         pltpu.make_async_copy(source, target, small_sems.at[n])
         for n, (source, target) in enumerate(
@@ -740,8 +793,8 @@
     ]
     for copy in small:
         copy.start()
-    for x in order:
-        copies[x].start()
+    for copy in middle + rest:
+        copy.start()
     for copy in small:
         copy.wait()
     for x in order:
@@ -750,7 +803,8 @@
         pull[x] = part
         sides_out[x : x + 1, :] = (1.0 - part[0:1]) * g[0:1] * misc[x : x + 1, :]
         sides_out[8 + x : 9 + x, :] = (1.0 - part[127:128]) * g[127:128] * misc[8 + x : 9 + x, :]
-        copies[x].wait()
+        for copy in {2: middle, 1: rest}.get(x, ()):
+            copy.wait()
         if x in (0, 7):
             n = jnp.where(sides()[0] == x // 7, 0, 1)
             rows_out[x // 7] = (1.0 - part) * g * wxf[n]
@@ -762,7 +816,7 @@
 def ready(*args):
     return pl.pallas_call(
         ready_kernel,
-        in_specs=[pl.BlockSpec(memory_space=pl.ANY)] + [hbm()] * 6,
+        in_specs=[pl.BlockSpec(memory_space=pl.ANY)] + [hbm()] * 7,
         out_specs=[vmem()] * 4,
         out_shape=[kept(4, 8, 128, 256), kept(8, 128, 256), kept(16, 256), kept(2, 128, 256)],
         scratch_shapes=[
@@ -844,7 +898,7 @@
     groups = lax.axis_size("zx")
     elecs = lax.axis_size("elec")
     admittance = admittance.reshape(16, 128)
-    u, f, c, impedance = in_hbm(u), in_hbm(f), in_hbm(c), in_hbm(impedance)
+    u_hbm, c, impedance = in_hbm(u), in_hbm(c), in_hbm(impedance)
 
     def rotated(a, turn):
         return lax.ppermute(a, "elec", [(i, (i + turn) % elecs) for i in range(elecs)])
@@ -856,7 +910,7 @@
         pairs = [(i, i + 1) for i in range(1, tiles - 1, 2)]
         return lax.ppermute(a, TILE, pairs + [(j, i) for i, j in pairs])
 
-    own_lo, own_hi, row_near, row_far, side = edges(u, c, impedance, in_hbm(cmap))
+    own_lo, own_hi, row_near, row_far, side = edges(u_hbm, c, impedance, in_hbm(cmap))
     y_lo = rotated(own_hi, 1)
     y_hi = rotated(own_lo, elecs - 1)
     x_far = far(row_far)
@@ -866,13 +920,17 @@
     ends_far = far(ends_far)
     ends_near = near(ends_near)
 
-    u, wx, wy, wz, diag, zeta_t, rim = weights(u, c, in_hbm(cmap), in_hbm(admittance))
-    u2, u2_inner, gain, wyl, wyh, pulled1, keep1, pulled2, e_lo, e_hi, contact = inner(
+    u, wx, wy, wz, diag, zeta_t, rim, pulled1, keep1 = weights(u_hbm, f, c, in_hbm(cmap), in_hbm(admittance))
+    u2, u2_inner, gain, wyl, wyh, pulled2, e_lo, e_hi, contact = inner(
         u, f, cmap, own_lo, own_hi, y_lo, y_hi, wx, wy, wz, diag
     )
-    face_near, face_far, edge_lo, edge_hi, u2_outer, gain, wxf, misc, zeta_t, mine, other = outer(
-        pairs.T, amplitudes.reshape(1, -1), cmap, admittance, rim, y_lo, y_hi, x_near, x_far, ends_near, ends_far,
-        wx, wy, wz, gain, wyl, wyh, u2, pulled1, keep1, pulled2, e_lo, e_hi, contact, zeta_t,
+    shared = (wx, wy, wz, gain, wyl, wyh, u2, pulled1, keep1, pulled2)
+    face_near, u2_near, own_near, gain_near, outside_near, contact = near_side(
+        cmap, admittance, rim, y_lo, y_hi, x_near, ends_near, *shared, contact
+    )
+    face_far, edge_lo, edge_hi, u2_far, gain, wxf, misc, zeta_t, mine, other = far_side(
+        pairs.T, amplitudes.reshape(1, -1), own_near, gain_near, outside_near, ends_near, e_lo, e_hi, zeta_t,
+        cmap, admittance, rim, y_lo, y_hi, x_far, ends_far, *shared, contact,
     )
     h_far = far(face_far)
     h_near = near(face_near)
@@ -880,7 +938,7 @@
     parts = lax.all_to_all(parts, "zx", 0, 0, tiled=True)
     to_above, to_below, summed = gathered(parts, in_hbm(edge_lo), in_hbm(edge_hi))
     base, pull, weight, row_weight = ready(
-        summed, in_hbm(u2_inner), in_hbm(u2_outer), in_hbm(gain), in_hbm(wxf), in_hbm(misc), in_hbm(zeta_t)
+        summed, in_hbm(u2_inner), in_hbm(u2_near), in_hbm(u2_far), in_hbm(gain), in_hbm(wxf), in_hbm(misc), in_hbm(zeta_t)
     )
     e_lo = rotated(to_above, 1)
     e_hi = rotated(to_below, elecs - 1)

time: 76 us -> 74.2 us (0.976)
  Pallas kernels: 27.2 us -> 25.8 us
    pallas_call x3 -> x4, Pallas kernels: 14.8 us -> 14.5 us  [the longest x1 6.55 us: inner(): pl.pallas_call(inner_kernel, in_specs=[vmem()] * 11, out_specs=[vmem(), h...]
  transfers between devices with their start and end apart: 15 -> 15, of which waited for: 4 -> 3; matrix products, arithmetic and copies ran while one was open for 0% -> 0% of each run, Pallas kernels for 23% -> 23%
where the time goes in v5:
time: 74.2 us; the launch traced here: 73.9 us
  starting transfers between devices  40.3 us (54%)
  Pallas kernels  25.8 us (35%)
  waiting for transfers between devices  6.67 us (9%)
  between operations  1.09 us (1%)
    ppermute x3, starting transfers between devices, far(): return lax.ppermute(a, TILE, pairs + [(j, i) for i, j in pairs])  13.2 us
    ppermute x6, starting transfers between devices, rotated(): lax.ppermute(a, 'elec', [(i, (i + turn) % elecs) for i in range(elecs)])  9.95 us
    all_to_all x1, starting transfers between devices, per_device(): parts = lax.all_to_all(parts, 'zx', 0, 0, tiled=True)  9.86 us
    ppermute x5, starting transfers between devices, near(): return lax.ppermute(a, 'core', [(0, 1), (1, 0)])  7.29 us
    pallas_call x1, Pallas kernels, inner(): pl.pallas_call(inner_kernel, in_specs=[vmem()] * 11, out_specs=[vmem(), h...  6.55 us
    all_to_all x1, waiting for transfers between devices, per_device(): parts = lax.all_to_all(parts, 'zx', 0, 0, tiled=True)  4.64 us
    pallas_call x1, Pallas kernels, weights(): pl.pallas_call(weights_kernel, in_specs=[hbm(), vmem()] + [hbm()] * 3, ou...  3.88 us
    pallas_call x1, Pallas kernels, correct(): pl.pallas_call(correct_kernel, in_specs=[vmem()] * 11, out_specs=[hbm(),...  3.09 us
  transfers between devices with their start and end apart: 15, of which 3 were waited for; matrix products, arithmetic and copies ran while one was open for 0% of the time, Pallas kernels for 23%

profile of v5, /device:TPU:1, one launch (start us, length us, event | category | flops | bytes accessed | tf_op | source)
XLA Modules:
  0.0 73.9 jit_solution(5783387510665565903)
XLA Ops:
  0.6 0.0 copy-start
  0.6 2.6 %edges.1 = (f32[184,256]{1,0:T(8,128)S(1)}, f32[184,256]{1,0:T(8,128)S(1)}, f32[776,256]{1,0:T(8,128)S(1)}, f32[776,256]{1,0:T(8,128)S(1)}, f32[128,256]{1,0:T(8,128)}) custom-call(f32[4,8,128,256]{3,2,1,0:T(8,128)} %u_hbm.3, f32[8,128,256]{2,1,0:T(8,128)} %c_hbm.3, f32[4,128,128]{2,1,0:T(8,128)} %imp_hbm.1, s32[8,128]{1,0:T(8,128)} %cmap.7), custom_call_target="tpu_custom_call" | custom-call | tf_op jit(solution)/shard_map/edges/pallas_call | solution.py:229
  3.3 3.3 %collective-permute-start.2 = (f32[776,256]{1,0:T(8,128)S(1)}, f32[776,256]{1,0:T(8,128)S(1)}, u32[]{:S(2)}, u32[]{:S(2)}) collective-permute-start(f32[776,256]{1,0:T(8,128)S(1)} %get-tuple-element.53), channel_id=1, source_target_pairs={{0,8},{8,0},{1,9},{9,1},{2,10},{10,2},{3,11},{11,3},{4,12},{12,4},... | collective-permute-start | bytes 2383880 | tf_op jit(solution)/shard_map/ppermute | solution.py:907
  6.6 2.8 %collective-permute-start.4 = (f32[776,256]{1,0:T(8,128)S(1)}, f32[776,256]{1,0:T(8,128)S(1)}, u32[]{:S(2)}, u32[]{:S(2)}) collective-permute-start(f32[776,256]{1,0:T(8,128)S(1)} %get-tuple-element.74), channel_id=1, source_target_pairs={{8,16},{24,32},{40,48},{56,64},{72,80},{88,96},{104,112},{120,128}... | collective-permute-start | bytes 2383880 | tf_op jit(solution)/shard_map/ppermute | solution.py:911
  9.4 1.4 %collective-permute-start = (f32[184,256]{1,0:T(8,128)S(1)}, f32[184,256]{1,0:T(8,128)S(1)}, u32[]{:S(2)}, u32[]{:S(2)}) collective-permute-start(f32[184,256]{1,0:T(8,128)S(1)} %get-tuple-element.51.own_hi), channel_id=1, source_target_pairs={{0,1},{1,2},{2,3},{3,0},{4,5},{5,6},{6,7},{7,4},{8,9},{9,10},{10,1... | collective-permute-start | bytes 565256 | tf_op jit(solution)/shard_map/ppermute | solution.py:904
  10.8 1.5 %collective-permute-start.1 = (f32[184,256]{1,0:T(8,128)S(1)}, f32[184,256]{1,0:T(8,128)S(1)}, u32[]{:S(2)}, u32[]{:S(2)}) collective-permute-start(f32[184,256]{1,0:T(8,128)S(1)} %get-tuple-element.52.own_lo), channel_id=1, source_target_pairs={{0,3},{1,0},{2,1},{3,2},{4,7},{5,4},{6,5},{7,6},{8,11},{9,8},{10,9... | collective-permute-start | bytes 565256 | tf_op jit(solution)/shard_map/ppermute | solution.py:904
  12.3 0.0 copy-done
  12.3 0.0 copy-start.1
  12.3 3.9 %weights.1 = (f32[4,8,128,256]{3,2,1,0:T(8,128)S(1)}, f32[7,128,256]{2,1,0:T(8,128)S(1)}, f32[8,128,256]{2,1,0:T(8,128)S(1)}, f32[8,128,256]{2,1,0:T(8,128)S(1)}...) custom-call(f32[4,8,128,256]{3,2,1,0:T(8,128)} %u_hbm.3, ...), custom_call_target="tpu_custom_call" | custom-call | flops 20000000 | bytes 6000000 | tf_op jit(solution)/shard_map/weights/pallas_call | solution.py:349
  16.2 0.0 collective-permute-done.y_lo.i0
  16.2 0.0 collective-permute-done.1.y_hi.i1
  16.3 0.1 collective-permute-start.3
  16.4 5.0 %collective-permute-start.5 = (f32[8,256]{1,0:T(8,128)S(1)}, f32[8,256]{1,0:T(8,128)S(1)}, u32[]{:S(2)}, u32[]{:S(2)}) collective-permute-start(f32[8,256]{1,0:T(8,128)S(1)} %get-tuple-element.75), channel_id=1, source_target_pairs={{8,16},{24,32},{40,48},{56,64},{72,80},{88,96},{104,112},{120,128}... | collective-permute-start | bytes 24584 | tf_op jit(solution)/shard_map/ppermute | solution.py:911
  21.4 0.0 copy-done.1
  21.4 0.0 copy-start.3
  21.5 6.6 %inner.1 = (f32[2,4,128,256]{3,2,1,0:T(8,128)S(1)}, f32[4,4,128,256]{3,2,1,0:T(8,128)}, f32[8,128,256]{2,1,0:T(8,128)S(1)}, f32[8,256]{1,0:T(8,128)S(1)}, f32[8,...) custom-call(f32[4,8,128,256]{3,2,1,0:T(8,128)S(1)} %get-tuple-elemen, ...), custom_call_target="tpu_custom_call" | custom-call | flops 100000000 | bytes 25000000 | tf_op jit(solution)/shard_map/inner/pallas_call | solution.py:468
  28.0 0.0 collective-permute-done.3.ends.ends_near
  28.0 0.0 collective-permute-done.2.msg
  28.0 0.0 copy-done.3
  28.1 0.0 copy-start.4
  28.1 0.0 copy-start.5
  28.1 1.9 %near_side.1 = (f32[4,128,256]{2,1,0:T(8,128)}, f32[2,4,128,256]{3,2,1,0:T(8,128)}, f32[4,128,256]{2,1,0:T(8,128)S(1)}, f32[128,256]{1,0:T(8,128)S(1)}, f32[128,256]{1,0:T(8,128)S(1)}, /*index=5*/f32[64,128]{1,0:T(8,128)S(1)}) custom-call(s32[8,128]{1,0:T(8,128)S(1)} %copy-done.1, f32[16,128]{1,0:T(8,128)S(1)} %bitcast.4, ...), custom_call_target="tpu_custom_call" | custom-call | flops 25000000 | bytes 8000000 | tf_op jit(solution)/shard_map/near_side/pallas_call | solution.py:578
  30.0 0.0 collective-permute-done.5.ends
  30.0 0.0 collective-permute-done.4.msg
  30.0 0.0 copy-done.4
  30.0 0.0 copy-done.5
  30.0 0.0 copy-start.6
  30.1 0.0 copy-start.2
  30.1 2.2 %far_side.1 = (f32[4,128,256]{2,1,0:T(8,128)}, f32[32,256]{1,0:T(8,128)}, f32[32,256]{1,0:T(8,128)}, f32[2,4,128,256]{3,2,1,0:T(8,128)}, f32[8,128,256]{2,1,0:T(...) custom-call(s32[2,4]{1,0:T(2,128)S(1)} %bitcast.6, ...), custom_call_target="tpu_custom_call" | custom-call | flops 25000000 | bytes 8000000 | tf_op jit(solution)/shard_map/far_side/pallas_call | solution.py:676
  32.2 0.1 collective-permute-start.6
  32.3 1.2 %collective-permute-done.6.got = f32[32,128]{1,0:T(8,128)S(1)} collective-permute-done((f32[32,128]{1,0:T(8,128)S(1)}, f32[32,128]{1,0:T(8,128)S(1)}, u32[]{:S(2)}, u32[]{:S(2)}) %collective-permute-start.6) | collective-permute-done | bytes 16416 | tf_op jit(solution)/shard_map/ppermute | solution.py:907
  33.5 0.8 %spread.1 = f32[16,32,128]{2,1,0:T(8,128)} custom-call(f32[32,128]{1,0:T(8,128)S(1)} %get-tuple-element.77.mine, f32[32,128]{1,0:T(8,128)S(1)} %collective-permute-done.6.got), custom_call_target="tpu_custom_call" | custom-call | tf_op jit(solution)/shard_map/spread/pallas_call | solution.py:708
  34.3 9.9 %all-to-all-start = ((f32[16,32,128]{2,1,0:T(8,128)}), f32[16,32,128]{2,1,0:T(8,128)S(1)}, u32[]{:S(2)}, u32[]{:S(2)}) async-start(f32[16,32,128]{2,1,0:T(8,128)} %spread.1), calls=%async_computation | async-start | bytes 524288 | tf_op jit(solution)/shard_map/all_to_all | solution.py:938
  44.1 5.4 %collective-permute-start.13 = (f32[4,128,256]{2,1,0:T(8,128)}, f32[4,128,256]{2,1,0:T(8,128)S(1)}, u32[]{:S(2)}, u32[]{:S(2)}) collective-permute-start(f32[4,128,256]{2,1,0:T(8,128)} %get-tuple-element.97), channel_id=1, source_target_pairs={{8,16},{24,32},{40,48},{56,64},{72,80},{88,96},{104,112},{120,128}... | collective-permute-start | bytes 1572872 | tf_op jit(solution)/shard_map/ppermute | solution.py:911
  49.5 0.0 copy-done.6
  49.5 0.1 collective-permute-start.12
  49.6 0.0 copy-done.2
  49.6 2.7 %collective-permute-start.10 = (f32[128,256]{1,0:T(8,128)S(1)}, f32[128,256]{1,0:T(8,128)S(1)}, u32[]{:S(2)}, u32[]{:S(2)}) collective-permute-start(f32[128,256]{1,0:T(8,128)S(1)} %copy-done.2), channel_id=1, source_target_pairs={{0,2},{1,3},{2,0},{3,1},{4,6},{5,7},{6,4},{7,5},{8,10},{9,11},{10,... | collective-permute-start | bytes 393224 | tf_op jit(solution)/shard_map/ppermute | solution.py:904
  52.4 4.6 %all-to-all-done.parts_hbm = f32[16,32,128]{2,1,0:T(8,128)S(1)} async-done(((f32[16,32,128]{2,1,0:T(8,128)}), f32[16,32,128]{2,1,0:T(8,128)S(1)}, u32[]{:S(2)}, u32[]{:S(2)}) %all-to-all-start) | async-done | bytes 262176 | tf_op jit(solution)/shard_map/all_to_all | solution.py:938
  57.0 0.8 %gathered.1 = (f32[48,256]{1,0:T(8,128)S(1)}, f32[48,256]{1,0:T(8,128)S(1)}, f32[16,256]{1,0:T(8,128)S(1)}) custom-call(f32[16,32,128]{2,1,0:T(8,128)S(1)} %all-to-all-done.parts_hbm, f32[32,256]{1,0:T(8,128)} %get-tuple-element.79.edge_lo, f32[32,256]{1,0:T(8,128)} %get-tuple-element.80.edge_hi), custom_call_target="tpu_custom_call" | custom-call | tf_op jit(solution)/shard_map/gathered/pallas_call | solution.py:734
  57.8 1.6 %collective-permute-start.7 = (f32[48,256]{1,0:T(8,128)S(1)}, f32[48,256]{1,0:T(8,128)S(1)}, u32[]{:S(2)}, u32[]{:S(2)}) collective-permute-start(f32[48,256]{1,0:T(8,128)S(1)} %get-tuple-element.81), channel_id=1, source_target_pairs={{0,1},{1,2},{2,3},{3,0},{4,5},{5,6},{6,7},{7,4},{8,9},{9,10},{10,1... | collective-permute-start | bytes 147464 | tf_op jit(solution)/shard_map/ppermute | solution.py:904
  59.4 1.5 %collective-permute-start.8 = (f32[48,256]{1,0:T(8,128)S(1)}, f32[48,256]{1,0:T(8,128)S(1)}, u32[]{:S(2)}, u32[]{:S(2)}) collective-permute-start(f32[48,256]{1,0:T(8,128)S(1)} %get-tuple-element.82), channel_id=1, source_target_pairs={{0,3},{1,0},{2,1},{3,2},{4,7},{5,4},{6,5},{7,6},{8,11},{9,8},{10,9... | collective-permute-start | bytes 147464 | tf_op jit(solution)/shard_map/ppermute | solution.py:904
  60.9 0.0 collective-permute-done.10.i3
  60.9 1.3 %collective-permute-start.9 = (f32[16,256]{1,0:T(8,128)S(1)}, f32[16,256]{1,0:T(8,128)S(1)}, u32[]{:S(2)}, u32[]{:S(2)}) collective-permute-start(f32[16,256]{1,0:T(8,128)S(1)} %get-tuple-element.83.after.a2), channel_id=1, source_target_pairs={{0,2},{1,3},{2,0},{3,1},{4,6},{5,7},{6,4},{7,5},{8,10},{9,11},{10,... | collective-permute-start | bytes 49160 | tf_op jit(solution)/shard_map/ppermute | solution.py:904
  62.2 3.0 %ready.1 = (f32[4,8,128,256]{3,2,1,0:T(8,128)S(1)}, f32[8,128,256]{2,1,0:T(8,128)S(1)}, f32[16,256]{1,0:T(8,128)S(1)}, f32[2,128,256]{2,1,0:T(8,128)S(1)}) custom-call(f32[16,256]{1,0:T(8,128)S(1)} %get-tuple-element.83.after.a2, f32[4,4,128,256]{3,2,1,0:T(8,128)} %get-tuple-element.85.inner_hbm, f32[2,4,128,256]{3,2,1,0:T(8,128)} %get-tuple-element.86.near_hbm, ...), custom_call_target="tpu_custom_call" | custom-call | flops 10000000 | bytes 8000000 | tf_op jit(solution)/shard_map/ready/pallas_call | solution.py:817
  65.2 0.0 collective-permute-done.9.a3
  65.2 0.0 collective-permute-done.7.a0.e_lo
  65.2 0.0 collective-permute-done.8.a1.e_hi
  65.2 0.9 %blocks.1.own = f32[4,8,128]{2,1,0:T(8,128)S(1)} custom-call(f32[48,256]{1,0:T(8,128)S(1)} %collective-permute-done.7.a0.e_lo, f32[48,256]{1,0:T(8,128)S(1)} %collective-permute-done.8.a1.e_hi, f32[16,256]{1,0:T(8,128)S(1)} %get-tuple-element.83.after.a2, f32[16,256]{1,0:T(8,128)S(1)} %collective-permute-done.9.a3, ...), custom_call_target="tpu_custom_call" | custom-call | tf_op jit(solution)/shard_map/blocks/pallas_call | solution.py:766
  66.1 3.7 %collective-permute-start.11 = (f32[4,8,128]{2,1,0:T(8,128)S(1)}, f32[4,8,128]{2,1,0:T(8,128)S(1)}, u32[]{:S(2)}, u32[]{:S(2)}) collective-permute-start(f32[4,8,128]{2,1,0:T(8,128)S(1)} %blocks.1.own), channel_id=1, source_target_pairs={{0,8},{8,0},{1,9},{9,1},{2,10},{10,2},{3,11},{11,3},{4,12},{12,4},... | collective-permute-start | bytes 49160 | tf_op jit(solution)/shard_map/ppermute | solution.py:907
  69.8 0.0 collective-permute-done.13.h_far
  69.8 0.0 collective-permute-done.12.h_near
  69.8 0.8 %collective-permute-done.11.got = f32[4,8,128]{2,1,0:T(8,128)S(1)} collective-permute-done((f32[4,8,128]{2,1,0:T(8,128)S(1)}, f32[4,8,128]{2,1,0:T(8,128)S(1)}, u32[]{:S(2)}, u32[]{:S(2)}) %collective-permute-start.11) | collective-permute-done | bytes 16416 | tf_op jit(solution)/shard_map/ppermute | solution.py:907
  70.7 3.1 %correct.1 = (f32[4,8,128,256]{3,2,1,0:T(8,128)}, f32[4,512]{1,0:T(4,128)}) custom-call(s32[8,128]{1,0:T(8,128)S(1)} %copy-done.1, f32[4,8,128]{2,1,0:T(8,128)S(1)} %blocks.1.own, f32[4,8,128]{2,1,0:T(8,128)S(1)} %collective-permute-done.11.got, f32[4,8,128,256]{3,2,1,0:T(8,128)S(1)} %get-tuple-element.93.base, f32[8,128,256]{2,1,0:T(8,128)S(1)} %get-tuple-element.92.pull, ...), custom_call_target="tpu_custom_call" | custom-call | tf_op jit(solution)/shard_map/correct/pallas_call | solution.py:881
  (1 shorter events, 0.0 us)
Async XLA Ops:
  0.6 11.7 %copy-start = (f32[4,8,128,256]{3,2,1,0:T(8,128)S(1)}, f32[4,8,128,256]{3,2,1,0:T(8,128)}, u32[]{:S(2)}) copy-start(f32[4,8,128,256]{3,2,1,0:T(8,128)} %f.3) | copy-start | bytes 12582916
  3.3 24.7 %collective-permute-start.2 = (f32[776,256]{1,0:T(8,128)S(1)}, f32[776,256]{1,0:T(8,128)S(1)}, u32[]{:S(2)}, u32[]{:S(2)}) collective-permute-start(f32[776,256]{1,0:T(8,128)S(1)} %get-tuple-element.53), channel_id=1, source_target_pairs={{0,8},{8,0},{1,9},{9,1},{2,10},{10,2},{3,11},{11,3},{4,12},{12,4},... | collective-permute-start | bytes 2383880 | tf_op jit(solution)/shard_map/ppermute | solution.py:907
  6.6 23.4 %collective-permute-start.4 = (f32[776,256]{1,0:T(8,128)S(1)}, f32[776,256]{1,0:T(8,128)S(1)}, u32[]{:S(2)}, u32[]{:S(2)}) collective-permute-start(f32[776,256]{1,0:T(8,128)S(1)} %get-tuple-element.74), channel_id=1, source_target_pairs={{8,16},{24,32},{40,48},{56,64},{72,80},{88,96},{104,112},{120,128}... | collective-permute-start | bytes 2383880 | tf_op jit(solution)/shard_map/ppermute | solution.py:911
  9.4 6.8 %collective-permute-start = (f32[184,256]{1,0:T(8,128)S(1)}, f32[184,256]{1,0:T(8,128)S(1)}, u32[]{:S(2)}, u32[]{:S(2)}) collective-permute-start(f32[184,256]{1,0:T(8,128)S(1)} %get-tuple-element.51.own_hi), channel_id=1, source_target_pairs={{0,1},{1,2},{2,3},{3,0},{4,5},{5,6},{6,7},{7,4},{8,9},{9,10},{10,1... | collective-permute-start | bytes 565256 | tf_op jit(solution)/shard_map/ppermute | solution.py:904
  10.8 5.4 %collective-permute-start.1 = (f32[184,256]{1,0:T(8,128)S(1)}, f32[184,256]{1,0:T(8,128)S(1)}, u32[]{:S(2)}, u32[]{:S(2)}) collective-permute-start(f32[184,256]{1,0:T(8,128)S(1)} %get-tuple-element.52.own_lo), channel_id=1, source_target_pairs={{0,3},{1,0},{2,1},{3,2},{4,7},{5,4},{6,5},{7,6},{8,11},{9,8},{10,9... | collective-permute-start | bytes 565256 | tf_op jit(solution)/shard_map/ppermute | solution.py:904
  12.3 9.1 %copy-start.1 = (s32[8,128]{1,0:T(8,128)S(1)}, s32[8,128]{1,0:T(8,128)}, u32[]{:S(2)}) copy-start(s32[8,128]{1,0:T(8,128)} %cmap.7) | copy-start | bytes 12292
  16.3 11.7 %collective-permute-start.3 = (f32[8,256]{1,0:T(8,128)S(1)}, f32[8,256]{1,0:T(8,128)S(1)}, u32[]{:S(2)}, u32[]{:S(2)}) collective-permute-start(f32[8,256]{1,0:T(8,128)S(1)} %get-tuple-element.54), channel_id=1, source_target_pairs={{0,8},{8,0},{1,9},{9,1},{2,10},{10,2},{3,11},{11,3},{4,12},{12,4},... | collective-permute-start | bytes 24584 | tf_op jit(solution)/shard_map/ppermute | solution.py:907
  16.4 13.6 %collective-permute-start.5 = (f32[8,256]{1,0:T(8,128)S(1)}, f32[8,256]{1,0:T(8,128)S(1)}, u32[]{:S(2)}, u32[]{:S(2)}) collective-permute-start(f32[8,256]{1,0:T(8,128)S(1)} %get-tuple-element.75), channel_id=1, source_target_pairs={{8,16},{24,32},{40,48},{56,64},{72,80},{88,96},{104,112},{120,128}... | collective-permute-start | bytes 24584 | tf_op jit(solution)/shard_map/ppermute | solution.py:911
  21.4 6.6 %copy-start.3 = (f32[2048]{0:T(1024)S(1)}, f32[2048]{0:T(1024)}, u32[]{:S(2)}) copy-start(f32[2048]{0:T(1024)} %param.12) | copy-start | bytes 24580
  28.1 2.0 %copy-start.4 = (s32[4,2]{0,1:T(2,128)S(1)}, s32[4,2]{0,1:T(2,128)}, u32[]{:S(2)}) copy-start(s32[4,2]{0,1:T(2,128)} %param.14) | copy-start | bytes 100
  28.1 2.0 %copy-start.5 = (f32[4]{0:T(128)S(1)}, f32[4]{0:T(128)}, u32[]{:S(2)}) copy-start(f32[4]{0:T(128)} %param.15) | copy-start | bytes 52
  30.0 19.5 %copy-start.6 = (f32[4,128,256]{2,1,0:T(8,128)S(1)}, f32[4,128,256]{2,1,0:T(8,128)}, u32[]{:S(2)}) copy-start(f32[4,128,256]{2,1,0:T(8,128)} %get-tuple-element.96) | copy-start | bytes 1572868
  30.1 19.6 %copy-start.2 = (f32[128,256]{1,0:T(8,128)S(1)}, f32[128,256]{1,0:T(8,128)}, u32[]{:S(2)}) copy-start(f32[128,256]{1,0:T(8,128)} %get-tuple-element.84.i2) | copy-start | bytes 393220
  32.2 1.3 %collective-permute-start.6 = (f32[32,128]{1,0:T(8,128)S(1)}, f32[32,128]{1,0:T(8,128)S(1)}, u32[]{:S(2)}, u32[]{:S(2)}) collective-permute-start(f32[32,128]{1,0:T(8,128)S(1)} %get-tuple-element.78), channel_id=1, source_target_pairs={{0,8},{8,0},{1,9},{9,1},{2,10},{10,2},{3,11},{11,3},{4,12},{12,4},... | collective-permute-start | bytes 49160 | tf_op jit(solution)/shard_map/ppermute | solution.py:907
  34.3 22.7 %all-to-all-start = ((f32[16,32,128]{2,1,0:T(8,128)}), f32[16,32,128]{2,1,0:T(8,128)S(1)}, u32[]{:S(2)}, u32[]{:S(2)}) async-start(f32[16,32,128]{2,1,0:T(8,128)} %spread.1), calls=%async_computation | async-start | bytes 524288 | tf_op jit(solution)/shard_map/all_to_all | solution.py:938
  44.1 25.7 %collective-permute-start.13 = (f32[4,128,256]{2,1,0:T(8,128)}, f32[4,128,256]{2,1,0:T(8,128)S(1)}, u32[]{:S(2)}, u32[]{:S(2)}) collective-permute-start(f32[4,128,256]{2,1,0:T(8,128)} %get-tuple-element.97), channel_id=1, source_target_pairs={{8,16},{24,32},{40,48},{56,64},{72,80},{88,96},{104,112},{120,128}... | collective-permute-start | bytes 1572872 | tf_op jit(solution)/shard_map/ppermute | solution.py:911
  49.5 20.3 %collective-permute-start.12 = (f32[4,128,256]{2,1,0:T(8,128)S(1)}, f32[4,128,256]{2,1,0:T(8,128)S(1)}, u32[]{:S(2)}, u32[]{:S(2)}) collective-permute-start(f32[4,128,256]{2,1,0:T(8,128)S(1)} %copy-done.6), channel_id=1, source_target_pairs={{0,8},{8,0},{1,9},{9,1},{2,10},{10,2},{3,11},{11,3},{4,12},{12,4},... | collective-permute-start | bytes 1572872 | tf_op jit(solution)/shard_map/ppermute | solution.py:907
  49.6 11.3 %collective-permute-start.10 = (f32[128,256]{1,0:T(8,128)S(1)}, f32[128,256]{1,0:T(8,128)S(1)}, u32[]{:S(2)}, u32[]{:S(2)}) collective-permute-start(f32[128,256]{1,0:T(8,128)S(1)} %copy-done.2), channel_id=1, source_target_pairs={{0,2},{1,3},{2,0},{3,1},{4,6},{5,7},{6,4},{7,5},{8,10},{9,11},{10,... | collective-permute-start | bytes 393224 | tf_op jit(solution)/shard_map/ppermute | solution.py:904
  57.8 7.4 %collective-permute-start.7 = (f32[48,256]{1,0:T(8,128)S(1)}, f32[48,256]{1,0:T(8,128)S(1)}, u32[]{:S(2)}, u32[]{:S(2)}) collective-permute-start(f32[48,256]{1,0:T(8,128)S(1)} %get-tuple-element.81), channel_id=1, source_target_pairs={{0,1},{1,2},{2,3},{3,0},{4,5},{5,6},{6,7},{7,4},{8,9},{9,10},{10,1... | collective-permute-start | bytes 147464 | tf_op jit(solution)/shard_map/ppermute | solution.py:904
  59.4 5.8 %collective-permute-start.8 = (f32[48,256]{1,0:T(8,128)S(1)}, f32[48,256]{1,0:T(8,128)S(1)}, u32[]{:S(2)}, u32[]{:S(2)}) collective-permute-start(f32[48,256]{1,0:T(8,128)S(1)} %get-tuple-element.82), channel_id=1, source_target_pairs={{0,3},{1,0},{2,1},{3,2},{4,7},{5,4},{6,5},{7,6},{8,11},{9,8},{10,9... | collective-permute-start | bytes 147464 | tf_op jit(solution)/shard_map/ppermute | solution.py:904
  60.9 4.3 %collective-permute-start.9 = (f32[16,256]{1,0:T(8,128)S(1)}, f32[16,256]{1,0:T(8,128)S(1)}, u32[]{:S(2)}, u32[]{:S(2)}) collective-permute-start(f32[16,256]{1,0:T(8,128)S(1)} %get-tuple-element.83.after.a2), channel_id=1, source_target_pairs={{0,2},{1,3},{2,0},{3,1},{4,6},{5,7},{6,4},{7,5},{8,10},{9,11},{10,... | collective-permute-start | bytes 49160 | tf_op jit(solution)/shard_map/ppermute | solution.py:904
  66.1 4.5 %collective-permute-start.11 = (f32[4,8,128]{2,1,0:T(8,128)S(1)}, f32[4,8,128]{2,1,0:T(8,128)S(1)}, u32[]{:S(2)}, u32[]{:S(2)}) collective-permute-start(f32[4,8,128]{2,1,0:T(8,128)S(1)} %blocks.1.own), channel_id=1, source_target_pairs={{0,8},{8,0},{1,9},{9,1},{2,10},{10,2},{3,11},{11,3},{4,12},{12,4},... | collective-permute-start | bytes 49160 | tf_op jit(solution)/shard_map/ppermute | solution.py:907

commit v6 on v5

--- a/solution.py
+++ b/solution.py
@@ -10,7 +10,6 @@
 KEEP = 1.0 - OMEGA
 TINY = 1e-30
 F32 = jnp.float32
-EXACT = lax.Precision.HIGHEST
 MIB = 1024 * 1024
 TILE = ("zx", "core")
 
@@ -752,13 +751,25 @@
     for e in range(4):
         charges[e] = total[8 * (e % 2) : 8 * (e % 2) + 8, 128 * (e // 2) : 128 * (e // 2) + 128]
     upper = iota((8, 128), 0) < 4
+
+    def split(a):
+        head = a.astype(jnp.bfloat16)
+        return head, (a - head.astype(F32)).astype(jnp.bfloat16)
+
+    def product(charge, block):
+        head, rest = split(charge)
+        block_head, block_rest = split(block)
+        total = lax.dot_general(head, block_head, NT, preferred_element_type=F32)
+        total = total + lax.dot_general(rest, block_head, NT, preferred_element_type=F32)
+        return total + lax.dot_general(head, block_rest, NT, preferred_element_type=F32)
+
     for turn, blocks in ((3, i0), (1, i1), (0, i2), (2, i3)):
         e = lax.rem(elec + turn, 4)
         charge = charges[e]
         start = blocks.shape[0] - 128
         both = blocks[start : start + 128, :]
-        first = lax.dot_general(charge, both[:, 0:128], NT, precision=EXACT, preferred_element_type=F32)
-        second = lax.dot_general(charge, both[:, 128:256], NT, precision=EXACT, preferred_element_type=F32)
+        first = product(charge, both[:, 0:128])
+        second = product(charge, both[:, 128:256])
         out[e] = jnp.where(upper, first, second)
 
 
@@ -833,8 +844,40 @@
     )(*args)
 
 
+def look_up(ids, half, volts):
+    block = lax.shift_right_logical(ids, 7)
+    lane = lax.bitwise_and(ids, 127)
+    touched = []
+    for s in range(4):
+        found = jnp.zeros((8, 128), F32)
+        for e in range(4):
+            for j in range(2):
+                row = jnp.broadcast_to(volts[e, 4 * j + s : 4 * j + s + 1, :], (8, 128))
+                there = jnp.take_along_axis(row, lane, axis=1)
+                found = jnp.where(block == 4 * e + 2 * half + j, there, found)
+        touched.append(found)
+    return touched
+
+
+def own_half_kernel(cmap, own, out):
+    found = look_up(cmap[...], lax.axis_index("core"), own)
+    for s in range(4):
+        out[8 * s : 8 * s + 8, :] = found[s]
+
+
+def own_half(cmap, own):
+    return pl.pallas_call(
+        own_half_kernel,
+        in_specs=[vmem()] * 2,
+        out_specs=vmem(),
+        out_shape=f32(32, 128),
+        compiler_params=params(2),
+        name="own_half",
+    )(cmap, own)
+
+
 def correct_kernel(
-    cmap, own, got, base, pull, weight, row_weight, e_lo, e_hi, h_near, h_far, out_hbm, volts, table, buf, sems
+    cmap, half, own, got, base, pull, weight, row_weight, e_lo, e_hi, h_near, h_far, out_hbm, volts, table, buf, sems
 ):
     core = lax.axis_index("core")
     elec = lax.axis_index("elec")
@@ -843,17 +886,8 @@
     for h in range(2):
         for j in range(2):
             volts[:, 128 * (2 * h + j) : 128 * (2 * h + j) + 128] = table[h, elec, 4 * j : 4 * j + 4, :]
-    ids = cmap[...]
-    block = lax.shift_right_logical(ids, 7)
-    lane = lax.bitwise_and(ids, 127)
-    touched = []
-    for s in range(4):
-        found = jnp.zeros((8, 128), F32)
-        for b in range(16):
-            e, h, j = b // 4, (b // 2) % 2, b % 2
-            row = jnp.broadcast_to(table[h, e, 4 * j + s : 4 * j + s + 1, :], (8, 128))
-            found = jnp.where(block == b, jnp.take_along_axis(row, lane, axis=1), found)
-        touched.append(found)
+    found = look_up(cmap[...], 1 - core, got)
+    touched = [found[s] + half[8 * s : 8 * s + 8, :] for s in range(4)]
     stacked = jnp.concatenate(touched + [jnp.zeros((96, 128), F32)], axis=0)
     volts_t = jnp.transpose(stacked)
     copies = []
@@ -880,7 +914,7 @@
 def correct(*args):
     return pl.pallas_call(
         correct_kernel,
-        in_specs=[vmem()] * 11,
+        in_specs=[vmem()] * 12,
         out_specs=[hbm(), vmem()],
         out_shape=[f32(4, 8, 128, 256), f32(4, 512)],
         scratch_shapes=[
@@ -944,7 +978,7 @@
     e_hi = rotated(to_below, elecs - 1)
     own = blocks((e_lo, e_hi, summed, rotated(summed, 2)), (y_lo, y_hi, side, opposite), pull)
     got = near(own)
-    out, volts = correct(cmap, own, got, base, pull, weight, row_weight, e_lo, e_hi, h_near, h_far)
+    out, volts = correct(cmap, own_half(cmap, own), own, got, base, pull, weight, row_weight, e_lo, e_hi, h_near, h_far)
     return out, volts
 
 

time: 74.2 us -> 73.8 us (level)
    pallas_call x1 -> x2, Pallas kernels: 3.09 us -> 3.18 us  [the longest x1 3.08 us: correct(): pl.pallas_call(correct_kernel, in_specs=[vmem()] * 12, out_specs=[hbm(),...]
where the time goes in v6:
time: 73.8 us; the launch traced here: 73.5 us
  starting transfers between devices  40.4 us (55%)
  Pallas kernels  25.5 us (35%)
  waiting for transfers between devices  6.55 us (9%)
  between operations  1.11 us (2%)
    ppermute x3, starting transfers between devices, far(): return lax.ppermute(a, TILE, pairs + [(j, i) for i, j in pairs])  13.2 us
    ppermute x6, starting transfers between devices, rotated(): lax.ppermute(a, 'elec', [(i, (i + turn) % elecs) for i in range(elecs)])  9.95 us
    all_to_all x1, starting transfers between devices, per_device(): parts = lax.all_to_all(parts, 'zx', 0, 0, tiled=True)  9.86 us
    ppermute x5, starting transfers between devices, near(): return lax.ppermute(a, 'core', [(0, 1), (1, 0)])  7.29 us
    pallas_call x1, Pallas kernels, inner(): pl.pallas_call(inner_kernel, in_specs=[vmem()] * 11, out_specs=[vmem(), h...  6.56 us
    all_to_all x1, waiting for transfers between devices, per_device(): parts = lax.all_to_all(parts, 'zx', 0, 0, tiled=True)  4.64 us
    pallas_call x1, Pallas kernels, weights(): pl.pallas_call(weights_kernel, in_specs=[hbm(), vmem()] + [hbm()] * 3, ou...  3.87 us
    pallas_call x1, Pallas kernels, correct(): pl.pallas_call(correct_kernel, in_specs=[vmem()] * 12, out_specs=[hbm(),...  3.08 us
  transfers between devices with their start and end apart: 15, of which 3 were waited for; matrix products, arithmetic and copies ran while one was open for 0% of the time, Pallas kernels for 23%

profile of v6, /device:TPU:1, one launch (start us, length us, event | category | flops | bytes accessed | tf_op | source)
XLA Modules:
  0.0 73.5 jit_solution(10508713211385843908)
XLA Ops:
  0.6 0.0 copy-start
  0.6 2.6 %edges.1 = (f32[184,256]{1,0:T(8,128)S(1)}, f32[184,256]{1,0:T(8,128)S(1)}, f32[776,256]{1,0:T(8,128)S(1)}, f32[776,256]{1,0:T(8,128)S(1)}, f32[128,256]{1,0:T(8,128)}) custom-call(f32[4,8,128,256]{3,2,1,0:T(8,128)} %u_hbm.3, f32[8,128,256]{2,1,0:T(8,128)} %c_hbm.3, f32[4,128,128]{2,1,0:T(8,128)} %imp_hbm.1, s32[8,128]{1,0:T(8,128)} %cmap.9), custom_call_target="tpu_custom_call" | custom-call | tf_op jit(solution)/shard_map/edges/pallas_call | solution.py:228
  3.3 3.3 %collective-permute-start.2 = (f32[776,256]{1,0:T(8,128)S(1)}, f32[776,256]{1,0:T(8,128)S(1)}, u32[]{:S(2)}, u32[]{:S(2)}) collective-permute-start(f32[776,256]{1,0:T(8,128)S(1)} %get-tuple-element.53), channel_id=1, source_target_pairs={{0,8},{8,0},{1,9},{9,1},{2,10},{10,2},{3,11},{11,3},{4,12},{12,4},... | collective-permute-start | bytes 2383880 | tf_op jit(solution)/shard_map/ppermute | solution.py:941
  6.6 2.8 %collective-permute-start.4 = (f32[776,256]{1,0:T(8,128)S(1)}, f32[776,256]{1,0:T(8,128)S(1)}, u32[]{:S(2)}, u32[]{:S(2)}) collective-permute-start(f32[776,256]{1,0:T(8,128)S(1)} %get-tuple-element.74), channel_id=1, source_target_pairs={{8,16},{24,32},{40,48},{56,64},{72,80},{88,96},{104,112},{120,128}... | collective-permute-start | bytes 2383880 | tf_op jit(solution)/shard_map/ppermute | solution.py:945
  9.4 1.4 %collective-permute-start = (f32[184,256]{1,0:T(8,128)S(1)}, f32[184,256]{1,0:T(8,128)S(1)}, u32[]{:S(2)}, u32[]{:S(2)}) collective-permute-start(f32[184,256]{1,0:T(8,128)S(1)} %get-tuple-element.51.own_hi), channel_id=1, source_target_pairs={{0,1},{1,2},{2,3},{3,0},{4,5},{5,6},{6,7},{7,4},{8,9},{9,10},{10,1... | collective-permute-start | bytes 565256 | tf_op jit(solution)/shard_map/ppermute | solution.py:938
  10.8 1.5 %collective-permute-start.1 = (f32[184,256]{1,0:T(8,128)S(1)}, f32[184,256]{1,0:T(8,128)S(1)}, u32[]{:S(2)}, u32[]{:S(2)}) collective-permute-start(f32[184,256]{1,0:T(8,128)S(1)} %get-tuple-element.52.own_lo), channel_id=1, source_target_pairs={{0,3},{1,0},{2,1},{3,2},{4,7},{5,4},{6,5},{7,6},{8,11},{9,8},{10,9... | collective-permute-start | bytes 565256 | tf_op jit(solution)/shard_map/ppermute | solution.py:938
  12.3 0.0 copy-done
  12.3 0.0 copy-start.1
  12.3 3.9 %weights.1 = (f32[4,8,128,256]{3,2,1,0:T(8,128)S(1)}, f32[7,128,256]{2,1,0:T(8,128)S(1)}, f32[8,128,256]{2,1,0:T(8,128)S(1)}, f32[8,128,256]{2,1,0:T(8,128)S(1)}...) custom-call(f32[4,8,128,256]{3,2,1,0:T(8,128)} %u_hbm.3, ...), custom_call_target="tpu_custom_call" | custom-call | flops 20000000 | bytes 6000000 | tf_op jit(solution)/shard_map/weights/pallas_call | solution.py:348
  16.2 0.0 collective-permute-done.y_lo.i0
  16.2 0.0 collective-permute-done.1.y_hi.i1
  16.3 0.1 collective-permute-start.3
  16.4 5.1 %collective-permute-start.5 = (f32[8,256]{1,0:T(8,128)S(1)}, f32[8,256]{1,0:T(8,128)S(1)}, u32[]{:S(2)}, u32[]{:S(2)}) collective-permute-start(f32[8,256]{1,0:T(8,128)S(1)} %get-tuple-element.75), channel_id=1, source_target_pairs={{8,16},{24,32},{40,48},{56,64},{72,80},{88,96},{104,112},{120,128}... | collective-permute-start | bytes 24584 | tf_op jit(solution)/shard_map/ppermute | solution.py:945
  21.4 0.0 copy-done.1
  21.4 0.0 copy-start.3
  21.5 6.6 %inner.1 = (f32[2,4,128,256]{3,2,1,0:T(8,128)S(1)}, f32[4,4,128,256]{3,2,1,0:T(8,128)}, f32[8,128,256]{2,1,0:T(8,128)S(1)}, f32[8,256]{1,0:T(8,128)S(1)}, f32[8,...) custom-call(f32[4,8,128,256]{3,2,1,0:T(8,128)S(1)} %get-tuple-elemen, ...), custom_call_target="tpu_custom_call" | custom-call | flops 100000000 | bytes 25000000 | tf_op jit(solution)/shard_map/inner/pallas_call | solution.py:467
  28.0 0.0 collective-permute-done.3.ends.ends_near
  28.0 0.0 collective-permute-done.2.msg
  28.1 0.0 copy-done.3
  28.1 0.0 copy-start.4
  28.1 0.0 copy-start.5
  28.1 1.9 %near_side.1 = (f32[4,128,256]{2,1,0:T(8,128)}, f32[2,4,128,256]{3,2,1,0:T(8,128)}, f32[4,128,256]{2,1,0:T(8,128)S(1)}, f32[128,256]{1,0:T(8,128)S(1)}, f32[128,256]{1,0:T(8,128)S(1)}, /*index=5*/f32[64,128]{1,0:T(8,128)S(1)}) custom-call(s32[8,128]{1,0:T(8,128)S(1)} %copy-done.1, f32[16,128]{1,0:T(8,128)S(1)} %bitcast.4, ...), custom_call_target="tpu_custom_call" | custom-call | flops 25000000 | bytes 8000000 | tf_op jit(solution)/shard_map/near_side/pallas_call | solution.py:577
  30.0 0.0 collective-permute-done.5.ends
  30.0 0.0 collective-permute-done.4.msg
  30.0 0.0 copy-done.4
  30.1 0.0 copy-done.5
  30.1 0.0 copy-start.6
  30.1 0.0 copy-start.2
  30.1 2.2 %far_side.1 = (f32[4,128,256]{2,1,0:T(8,128)}, f32[32,256]{1,0:T(8,128)}, f32[32,256]{1,0:T(8,128)}, f32[2,4,128,256]{3,2,1,0:T(8,128)}, f32[8,128,256]{2,1,0:T(...) custom-call(s32[2,4]{1,0:T(2,128)S(1)} %bitcast.6, ...), custom_call_target="tpu_custom_call" | custom-call | flops 25000000 | bytes 8000000 | tf_op jit(solution)/shard_map/far_side/pallas_call | solution.py:675
  32.3 0.1 collective-permute-start.6
  32.4 1.2 %collective-permute-done.6.got = f32[32,128]{1,0:T(8,128)S(1)} collective-permute-done((f32[32,128]{1,0:T(8,128)S(1)}, f32[32,128]{1,0:T(8,128)S(1)}, u32[]{:S(2)}, u32[]{:S(2)}) %collective-permute-start.6) | collective-permute-done | bytes 16416 | tf_op jit(solution)/shard_map/ppermute | solution.py:941
  33.5 0.8 %spread.1 = f32[16,32,128]{2,1,0:T(8,128)} custom-call(f32[32,128]{1,0:T(8,128)S(1)} %get-tuple-element.77.mine, f32[32,128]{1,0:T(8,128)S(1)} %collective-permute-done.6.got), custom_call_target="tpu_custom_call" | custom-call | tf_op jit(solution)/shard_map/spread/pallas_call | solution.py:707
  34.3 9.9 %all-to-all-start = ((f32[16,32,128]{2,1,0:T(8,128)}), f32[16,32,128]{2,1,0:T(8,128)S(1)}, u32[]{:S(2)}, u32[]{:S(2)}) async-start(f32[16,32,128]{2,1,0:T(8,128)} %spread.1), calls=%async_computation | async-start | bytes 524288 | tf_op jit(solution)/shard_map/all_to_all | solution.py:972
  44.2 5.4 %collective-permute-start.13 = (f32[4,128,256]{2,1,0:T(8,128)}, f32[4,128,256]{2,1,0:T(8,128)S(1)}, u32[]{:S(2)}, u32[]{:S(2)}) collective-permute-start(f32[4,128,256]{2,1,0:T(8,128)} %get-tuple-element.97), channel_id=1, source_target_pairs={{8,16},{24,32},{40,48},{56,64},{72,80},{88,96},{104,112},{120,128}... | collective-permute-start | bytes 1572872 | tf_op jit(solution)/shard_map/ppermute | solution.py:945
  49.6 0.0 copy-done.6
  49.6 0.1 collective-permute-start.12
  49.7 0.0 copy-done.2
  49.7 2.7 %collective-permute-start.10 = (f32[128,256]{1,0:T(8,128)S(1)}, f32[128,256]{1,0:T(8,128)S(1)}, u32[]{:S(2)}, u32[]{:S(2)}) collective-permute-start(f32[128,256]{1,0:T(8,128)S(1)} %copy-done.2), channel_id=1, source_target_pairs={{0,2},{1,3},{2,0},{3,1},{4,6},{5,7},{6,4},{7,5},{8,10},{9,11},{10,... | collective-permute-start | bytes 393224 | tf_op jit(solution)/shard_map/ppermute | solution.py:938
  52.4 4.6 %all-to-all-done.parts_hbm = f32[16,32,128]{2,1,0:T(8,128)S(1)} async-done(((f32[16,32,128]{2,1,0:T(8,128)}), f32[16,32,128]{2,1,0:T(8,128)S(1)}, u32[]{:S(2)}, u32[]{:S(2)}) %all-to-all-start) | async-done | bytes 262176 | tf_op jit(solution)/shard_map/all_to_all | solution.py:972
  57.0 0.8 %gathered.1 = (f32[48,256]{1,0:T(8,128)S(1)}, f32[48,256]{1,0:T(8,128)S(1)}, f32[16,256]{1,0:T(8,128)S(1)}) custom-call(f32[16,32,128]{2,1,0:T(8,128)S(1)} %all-to-all-done.parts_hbm, f32[32,256]{1,0:T(8,128)} %get-tuple-element.79.edge_lo, f32[32,256]{1,0:T(8,128)} %get-tuple-element.80.edge_hi), custom_call_target="tpu_custom_call" | custom-call | tf_op jit(solution)/shard_map/gathered/pallas_call | solution.py:733
  57.9 1.6 %collective-permute-start.7 = (f32[48,256]{1,0:T(8,128)S(1)}, f32[48,256]{1,0:T(8,128)S(1)}, u32[]{:S(2)}, u32[]{:S(2)}) collective-permute-start(f32[48,256]{1,0:T(8,128)S(1)} %get-tuple-element.81), channel_id=1, source_target_pairs={{0,1},{1,2},{2,3},{3,0},{4,5},{5,6},{6,7},{7,4},{8,9},{9,10},{10,1... | collective-permute-start | bytes 147464 | tf_op jit(solution)/shard_map/ppermute | solution.py:938
  59.4 1.5 %collective-permute-start.8 = (f32[48,256]{1,0:T(8,128)S(1)}, f32[48,256]{1,0:T(8,128)S(1)}, u32[]{:S(2)}, u32[]{:S(2)}) collective-permute-start(f32[48,256]{1,0:T(8,128)S(1)} %get-tuple-element.82), channel_id=1, source_target_pairs={{0,3},{1,0},{2,1},{3,2},{4,7},{5,4},{6,5},{7,6},{8,11},{9,8},{10,9... | collective-permute-start | bytes 147464 | tf_op jit(solution)/shard_map/ppermute | solution.py:938
  61.0 0.0 collective-permute-done.10.i3
  61.0 1.3 %collective-permute-start.9 = (f32[16,256]{1,0:T(8,128)S(1)}, f32[16,256]{1,0:T(8,128)S(1)}, u32[]{:S(2)}, u32[]{:S(2)}) collective-permute-start(f32[16,256]{1,0:T(8,128)S(1)} %get-tuple-element.83.after.a2), channel_id=1, source_target_pairs={{0,2},{1,3},{2,0},{3,1},{4,6},{5,7},{6,4},{7,5},{8,10},{9,11},{10,... | collective-permute-start | bytes 49160 | tf_op jit(solution)/shard_map/ppermute | solution.py:938
  62.2 3.0 %ready.1 = (f32[4,8,128,256]{3,2,1,0:T(8,128)S(1)}, f32[8,128,256]{2,1,0:T(8,128)S(1)}, f32[16,256]{1,0:T(8,128)S(1)}, f32[2,128,256]{2,1,0:T(8,128)S(1)}) custom-call(f32[16,256]{1,0:T(8,128)S(1)} %get-tuple-element.83.after.a2, f32[4,4,128,256]{3,2,1,0:T(8,128)} %get-tuple-element.85.inner_hbm, f32[2,4,128,256]{3,2,1,0:T(8,128)} %get-tuple-element.86.near_hbm, ...), custom_call_target="tpu_custom_call" | custom-call | flops 10000000 | bytes 8000000 | tf_op jit(solution)/shard_map/ready/pallas_call | solution.py:828
  65.2 0.0 collective-permute-done.9.a3
  65.2 0.0 collective-permute-done.7.a0.e_lo
  65.2 0.0 collective-permute-done.8.a1.e_hi
  65.3 0.5 blocks.1.own
  65.8 3.7 %collective-permute-start.11 = (f32[4,8,128]{2,1,0:T(8,128)S(1)}, f32[4,8,128]{2,1,0:T(8,128)S(1)}, u32[]{:S(2)}, u32[]{:S(2)}) collective-permute-start(f32[4,8,128]{2,1,0:T(8,128)S(1)} %blocks.1.own), channel_id=1, source_target_pairs={{0,8},{8,0},{1,9},{9,1},{2,10},{10,2},{3,11},{11,3},{4,12},{12,4},... | collective-permute-start | bytes 49160 | tf_op jit(solution)/shard_map/ppermute | solution.py:941
  69.4 0.1 own_half.1.half
  69.5 0.0 collective-permute-done.13.h_far
  69.6 0.0 collective-permute-done.12.h_near
  69.6 0.7 collective-permute-done.11.got
  70.3 3.1 %correct.1 = (f32[4,8,128,256]{3,2,1,0:T(8,128)}, f32[4,512]{1,0:T(4,128)}) custom-call(s32[8,128]{1,0:T(8,128)S(1)} %copy-done.1, f32[32,128]{1,0:T(8,128)S(1)} %own_half.1.half, f32[4,8,128]{2,1,0:T(8,128)S(1)} %blocks.1.own, f32[4,8,128]{2,1,0:T(8,128)S(1)} %collective-permute-done.11.got, f32[4,8,128,256]{3,2,1,0:T(8,128)S(1)} %get-tuple-element.93.base, ...), custom_call_target="tpu_custom_call" | custom-call | tf_op jit(solution)/shard_map/correct/pallas_call | solution.py:915
  (1 shorter events, 0.0 us)
Async XLA Ops:
  0.6 11.7 %copy-start = (f32[4,8,128,256]{3,2,1,0:T(8,128)S(1)}, f32[4,8,128,256]{3,2,1,0:T(8,128)}, u32[]{:S(2)}) copy-start(f32[4,8,128,256]{3,2,1,0:T(8,128)} %f.3) | copy-start | bytes 12582916
  3.3 24.8 %collective-permute-start.2 = (f32[776,256]{1,0:T(8,128)S(1)}, f32[776,256]{1,0:T(8,128)S(1)}, u32[]{:S(2)}, u32[]{:S(2)}) collective-permute-start(f32[776,256]{1,0:T(8,128)S(1)} %get-tuple-element.53), channel_id=1, source_target_pairs={{0,8},{8,0},{1,9},{9,1},{2,10},{10,2},{3,11},{11,3},{4,12},{12,4},... | collective-permute-start | bytes 2383880 | tf_op jit(solution)/shard_map/ppermute | solution.py:941
  6.6 23.4 %collective-permute-start.4 = (f32[776,256]{1,0:T(8,128)S(1)}, f32[776,256]{1,0:T(8,128)S(1)}, u32[]{:S(2)}, u32[]{:S(2)}) collective-permute-start(f32[776,256]{1,0:T(8,128)S(1)} %get-tuple-element.74), channel_id=1, source_target_pairs={{8,16},{24,32},{40,48},{56,64},{72,80},{88,96},{104,112},{120,128}... | collective-permute-start | bytes 2383880 | tf_op jit(solution)/shard_map/ppermute | solution.py:945
  9.4 6.8 %collective-permute-start = (f32[184,256]{1,0:T(8,128)S(1)}, f32[184,256]{1,0:T(8,128)S(1)}, u32[]{:S(2)}, u32[]{:S(2)}) collective-permute-start(f32[184,256]{1,0:T(8,128)S(1)} %get-tuple-element.51.own_hi), channel_id=1, source_target_pairs={{0,1},{1,2},{2,3},{3,0},{4,5},{5,6},{6,7},{7,4},{8,9},{9,10},{10,1... | collective-permute-start | bytes 565256 | tf_op jit(solution)/shard_map/ppermute | solution.py:938
  10.8 5.4 %collective-permute-start.1 = (f32[184,256]{1,0:T(8,128)S(1)}, f32[184,256]{1,0:T(8,128)S(1)}, u32[]{:S(2)}, u32[]{:S(2)}) collective-permute-start(f32[184,256]{1,0:T(8,128)S(1)} %get-tuple-element.52.own_lo), channel_id=1, source_target_pairs={{0,3},{1,0},{2,1},{3,2},{4,7},{5,4},{6,5},{7,6},{8,11},{9,8},{10,9... | collective-permute-start | bytes 565256 | tf_op jit(solution)/shard_map/ppermute | solution.py:938
  12.3 9.1 %copy-start.1 = (s32[8,128]{1,0:T(8,128)S(1)}, s32[8,128]{1,0:T(8,128)}, u32[]{:S(2)}) copy-start(s32[8,128]{1,0:T(8,128)} %cmap.9) | copy-start | bytes 12292
  16.3 11.8 %collective-permute-start.3 = (f32[8,256]{1,0:T(8,128)S(1)}, f32[8,256]{1,0:T(8,128)S(1)}, u32[]{:S(2)}, u32[]{:S(2)}) collective-permute-start(f32[8,256]{1,0:T(8,128)S(1)} %get-tuple-element.54), channel_id=1, source_target_pairs={{0,8},{8,0},{1,9},{9,1},{2,10},{10,2},{3,11},{11,3},{4,12},{12,4},... | collective-permute-start | bytes 24584 | tf_op jit(solution)/shard_map/ppermute | solution.py:941
  16.4 13.7 %collective-permute-start.5 = (f32[8,256]{1,0:T(8,128)S(1)}, f32[8,256]{1,0:T(8,128)S(1)}, u32[]{:S(2)}, u32[]{:S(2)}) collective-permute-start(f32[8,256]{1,0:T(8,128)S(1)} %get-tuple-element.75), channel_id=1, source_target_pairs={{8,16},{24,32},{40,48},{56,64},{72,80},{88,96},{104,112},{120,128}... | collective-permute-start | bytes 24584 | tf_op jit(solution)/shard_map/ppermute | solution.py:945
  21.4 6.6 %copy-start.3 = (f32[2048]{0:T(1024)S(1)}, f32[2048]{0:T(1024)}, u32[]{:S(2)}) copy-start(f32[2048]{0:T(1024)} %param.12) | copy-start | bytes 24580
  28.1 2.0 %copy-start.4 = (s32[4,2]{0,1:T(2,128)S(1)}, s32[4,2]{0,1:T(2,128)}, u32[]{:S(2)}) copy-start(s32[4,2]{0,1:T(2,128)} %param.14) | copy-start | bytes 100
  28.1 2.0 %copy-start.5 = (f32[4]{0:T(128)S(1)}, f32[4]{0:T(128)}, u32[]{:S(2)}) copy-start(f32[4]{0:T(128)} %param.15) | copy-start | bytes 52
  30.1 19.5 %copy-start.6 = (f32[4,128,256]{2,1,0:T(8,128)S(1)}, f32[4,128,256]{2,1,0:T(8,128)}, u32[]{:S(2)}) copy-start(f32[4,128,256]{2,1,0:T(8,128)} %get-tuple-element.96) | copy-start | bytes 1572868
  30.1 19.6 %copy-start.2 = (f32[128,256]{1,0:T(8,128)S(1)}, f32[128,256]{1,0:T(8,128)}, u32[]{:S(2)}) copy-start(f32[128,256]{1,0:T(8,128)} %get-tuple-element.84.i2) | copy-start | bytes 393220
  32.3 1.3 %collective-permute-start.6 = (f32[32,128]{1,0:T(8,128)S(1)}, f32[32,128]{1,0:T(8,128)S(1)}, u32[]{:S(2)}, u32[]{:S(2)}) collective-permute-start(f32[32,128]{1,0:T(8,128)S(1)} %get-tuple-element.78), channel_id=1, source_target_pairs={{0,8},{8,0},{1,9},{9,1},{2,10},{10,2},{3,11},{11,3},{4,12},{12,4},... | collective-permute-start | bytes 49160 | tf_op jit(solution)/shard_map/ppermute | solution.py:941
  34.3 22.7 %all-to-all-start = ((f32[16,32,128]{2,1,0:T(8,128)}), f32[16,32,128]{2,1,0:T(8,128)S(1)}, u32[]{:S(2)}, u32[]{:S(2)}) async-start(f32[16,32,128]{2,1,0:T(8,128)} %spread.1), calls=%async_computation | async-start | bytes 524288 | tf_op jit(solution)/shard_map/all_to_all | solution.py:972
  44.2 25.4 %collective-permute-start.13 = (f32[4,128,256]{2,1,0:T(8,128)}, f32[4,128,256]{2,1,0:T(8,128)S(1)}, u32[]{:S(2)}, u32[]{:S(2)}) collective-permute-start(f32[4,128,256]{2,1,0:T(8,128)} %get-tuple-element.97), channel_id=1, source_target_pairs={{8,16},{24,32},{40,48},{56,64},{72,80},{88,96},{104,112},{120,128}... | collective-permute-start | bytes 1572872 | tf_op jit(solution)/shard_map/ppermute | solution.py:945
  49.6 20.0 %collective-permute-start.12 = (f32[4,128,256]{2,1,0:T(8,128)S(1)}, f32[4,128,256]{2,1,0:T(8,128)S(1)}, u32[]{:S(2)}, u32[]{:S(2)}) collective-permute-start(f32[4,128,256]{2,1,0:T(8,128)S(1)} %copy-done.6), channel_id=1, source_target_pairs={{0,8},{8,0},{1,9},{9,1},{2,10},{10,2},{3,11},{11,3},{4,12},{12,4},... | collective-permute-start | bytes 1572872 | tf_op jit(solution)/shard_map/ppermute | solution.py:941
  49.7 11.3 %collective-permute-start.10 = (f32[128,256]{1,0:T(8,128)S(1)}, f32[128,256]{1,0:T(8,128)S(1)}, u32[]{:S(2)}, u32[]{:S(2)}) collective-permute-start(f32[128,256]{1,0:T(8,128)S(1)} %copy-done.2), channel_id=1, source_target_pairs={{0,2},{1,3},{2,0},{3,1},{4,6},{5,7},{6,4},{7,5},{8,10},{9,11},{10,... | collective-permute-start | bytes 393224 | tf_op jit(solution)/shard_map/ppermute | solution.py:938
  57.9 7.4 %collective-permute-start.7 = (f32[48,256]{1,0:T(8,128)S(1)}, f32[48,256]{1,0:T(8,128)S(1)}, u32[]{:S(2)}, u32[]{:S(2)}) collective-permute-start(f32[48,256]{1,0:T(8,128)S(1)} %get-tuple-element.81), channel_id=1, source_target_pairs={{0,1},{1,2},{2,3},{3,0},{4,5},{5,6},{6,7},{7,4},{8,9},{9,10},{10,1... | collective-permute-start | bytes 147464 | tf_op jit(solution)/shard_map/ppermute | solution.py:938
  59.4 5.8 %collective-permute-start.8 = (f32[48,256]{1,0:T(8,128)S(1)}, f32[48,256]{1,0:T(8,128)S(1)}, u32[]{:S(2)}, u32[]{:S(2)}) collective-permute-start(f32[48,256]{1,0:T(8,128)S(1)} %get-tuple-element.82), channel_id=1, source_target_pairs={{0,3},{1,0},{2,1},{3,2},{4,7},{5,4},{6,5},{7,6},{8,11},{9,8},{10,9... | collective-permute-start | bytes 147464 | tf_op jit(solution)/shard_map/ppermute | solution.py:938
  61.0 4.3 %collective-permute-start.9 = (f32[16,256]{1,0:T(8,128)S(1)}, f32[16,256]{1,0:T(8,128)S(1)}, u32[]{:S(2)}, u32[]{:S(2)}) collective-permute-start(f32[16,256]{1,0:T(8,128)S(1)} %get-tuple-element.83.after.a2), channel_id=1, source_target_pairs={{0,2},{1,3},{2,0},{3,1},{4,6},{5,7},{6,4},{7,5},{8,10},{9,11},{10,... | collective-permute-start | bytes 49160 | tf_op jit(solution)/shard_map/ppermute | solution.py:938
  65.8 4.5 %collective-permute-start.11 = (f32[4,8,128]{2,1,0:T(8,128)S(1)}, f32[4,8,128]{2,1,0:T(8,128)S(1)}, u32[]{:S(2)}, u32[]{:S(2)}) collective-permute-start(f32[4,8,128]{2,1,0:T(8,128)S(1)} %blocks.1.own), channel_id=1, source_target_pairs={{0,8},{8,0},{1,9},{9,1},{2,10},{10,2},{3,11},{11,3},{4,12},{12,4},... | collective-permute-start | bytes 49160 | tf_op jit(solution)/shard_map/ppermute | solution.py:941

commit v7 on v6

--- a/solution.py
+++ b/solution.py
@@ -495,6 +495,12 @@
     outside_ref[...] = outside
     g = OMEGA * inverse(gain[x] + outside)
     g_ref[...] = g
+    spare = jnp.maximum(there, TINY)
+    diag = both_sides(line_weight(spare, 0), 0) + both_sides(line_weight(spare, 1), 1) + zeta_t[:, 0:1]
+    diag = diag + outside + outer_face(there, msg[ROW_C2 : ROW_C2 + 128, :])
+    diag = diag + jnp.where(row == 0, outer_face(there[0:1], ends[0:1, :]), 0.0)
+    diag = diag + jnp.where(row == 127, outer_face(there[127:128], ends[1:2, :]), 0.0)
+    factor = OMEGA * outside * inverse(jnp.maximum(diag, TINY))
     for s in range(4):
         out[s] = keep1[side, s] + g * (pulled1[side, s] + outside * msg[128 * s : 128 * s + 128, :])
         at = 8 * s + x
@@ -503,12 +509,6 @@
         out[s, 0:1, :] = out[s, 0:1, :] + low
         out[s, 127:128, :] = out[s, 127:128, :] + high
     faces_done()
-    spare = jnp.maximum(there, TINY)
-    diag = both_sides(line_weight(spare, 0), 0) + both_sides(line_weight(spare, 1), 1) + zeta_t[:, 0:1]
-    diag = diag + outside + outer_face(there, msg[ROW_C2 : ROW_C2 + 128, :])
-    diag = diag + jnp.where(row == 0, outer_face(there[0:1], ends[0:1, :]), 0.0)
-    diag = diag + jnp.where(row == 127, outer_face(there[127:128], ends[1:2, :]), 0.0)
-    factor = OMEGA * outside * inverse(jnp.maximum(diag, TINY))
     beyond = row_sums([factor * out[s] for s in range(4)])
     inside = 1 + 5 * side
     factor = gain[inside] * wx[6 * side]
@@ -599,6 +599,23 @@
 ):
     near, far = sides()
     send, copies = sender()
+    lanes = iota((1, 128), 1)
+    low_ids = y_lo[48:49, 0:128].astype(jnp.int32)
+    high_ids = pltpu.roll(y_hi[48:49, 0:128], 8, 1).astype(jnp.int32)
+    edge_ids = jnp.where(lanes < 8, low_ids, jnp.where(lanes < 16, high_ids, 2048))
+    zeta = gather_rows(jnp.broadcast_to(edge_ids, (8, 128)), admittance[...])
+    zeta_t = jnp.transpose(jnp.concatenate([zeta, jnp.zeros((120, 128), F32)], axis=0))
+    edge_factors = []
+    for n, (edge_msg, own) in enumerate(((y_lo, wyl), (y_hi, wyh))):
+        there = edge_msg[32:40, :]
+        x_rows = iota((8, 256), 0)
+        spare = jnp.maximum(there, TINY)
+        diag = both_sides(line_weight(spare, 0), 0) + both_sides(line_weight(spare, 1), 1) + own[...]
+        diag = diag + outer_face(there, edge_msg[40:48, :])
+        for side, corner in zip(sides(), (ends_near, ends)):
+            diag = diag + jnp.where(x_rows == 7 * side, outer_face(there, corner[n : n + 1, :]), 0.0)
+        diag = diag + zeta_t[8 * n : 8 * n + 8, 0:1]
+        edge_factors.append(OMEGA * own[...] * inverse(jnp.maximum(diag, TINY)))
     send(gain.at[pl.ds(1, 6)], gain_out.at[pl.ds(1, 6)], sems.at[0])
     send(gain_near, gain_out.at[7 * near], sems.at[1])
     send(outside_near, wxf_out.at[0], sems.at[2])
@@ -617,33 +634,18 @@
     send(gain_far, gain_out.at[7 * far], sems.at[8])
     send(outside_far, wxf_out.at[1], sems.at[9])
 
-    lanes = iota((1, 128), 1)
-    low_ids = y_lo[48:49, 0:128].astype(jnp.int32)
-    high_ids = pltpu.roll(y_hi[48:49, 0:128], 8, 1).astype(jnp.int32)
-    edge_ids = jnp.where(lanes < 8, low_ids, jnp.where(lanes < 16, high_ids, 2048))
-    zeta = gather_rows(jnp.broadcast_to(edge_ids, (8, 128)), admittance[...])
-    zeta_t = jnp.transpose(jnp.concatenate([zeta, jnp.zeros((120, 128), F32)], axis=0))
     edge_sums = jnp.zeros((4, 128), F32)
-    for n, (edge_msg, own, inside, edge, y, sent) in enumerate(
-        ((y_lo, wyl, e_lo, edge_lo, 0, edge_lo_out), (y_hi, wyh, e_hi, edge_hi, 127, edge_hi_out))
+    for n, (inside, edge, y, sent) in enumerate(
+        ((e_lo, edge_lo, 0, edge_lo_out), (e_hi, edge_hi, 127, edge_hi_out))
     ):
         edge[0:32, :] = inside[...]
         for s in range(4):
             for side, out in zip(sides(), (face_near, face_far)):
                 edge[pl.ds(8 * s + 7 * side, 1), :] = out[s, y : y + 1, :]
         send(edge, sent, sems.at[10 + n])
-        there = edge_msg[32:40, :]
-        x_rows = iota((8, 256), 0)
-        spare = jnp.maximum(there, TINY)
-        diag = both_sides(line_weight(spare, 0), 0) + both_sides(line_weight(spare, 1), 1) + own[...]
-        diag = diag + outer_face(there, edge_msg[40:48, :])
-        for side, corner in zip(sides(), (ends_near, ends)):
-            diag = diag + jnp.where(x_rows == 7 * side, outer_face(there, corner[n : n + 1, :]), 0.0)
-        diag = diag + zeta_t[8 * n : 8 * n + 8, 0:1]
-        factor = OMEGA * own[...] * inverse(jnp.maximum(diag, TINY))
         lined = []
         for s in range(4):
-            line = to_lanes(jnp.sum(factor * edge[8 * s : 8 * s + 8, :], axis=1, keepdims=True))
+            line = to_lanes(jnp.sum(edge_factors[n] * edge[8 * s : 8 * s + 8, :], axis=1, keepdims=True))
             lined.append(pltpu.roll(line, 8 * n, 1) if n else line)
         edge_sums = edge_sums + jnp.concatenate(lined, axis=0)
     id_rows.append(edge_ids)

time: 73.8 us -> 73.8 us (level)
  no operation moved by 1% of the time
where the time goes in v7:
time: 73.8 us; the launch traced here: 73.5 us
  starting transfers between devices  40.4 us (55%)
  Pallas kernels  25.6 us (35%)
  waiting for transfers between devices  6.37 us (9%)
  between operations  1.11 us (2%)
    ppermute x3, starting transfers between devices, far(): return lax.ppermute(a, TILE, pairs + [(j, i) for i, j in pairs])  13.2 us
    ppermute x6, starting transfers between devices, rotated(): lax.ppermute(a, 'elec', [(i, (i + turn) % elecs) for i in range(elecs)])  9.95 us
    all_to_all x1, starting transfers between devices, per_device(): parts = lax.all_to_all(parts, 'zx', 0, 0, tiled=True)  9.86 us
    ppermute x5, starting transfers between devices, near(): return lax.ppermute(a, 'core', [(0, 1), (1, 0)])  7.29 us
    pallas_call x1, Pallas kernels, inner(): pl.pallas_call(inner_kernel, in_specs=[vmem()] * 11, out_specs=[vmem(), h...  6.56 us
    all_to_all x1, waiting for transfers between devices, per_device(): parts = lax.all_to_all(parts, 'zx', 0, 0, tiled=True)  4.45 us
    pallas_call x1, Pallas kernels, weights(): pl.pallas_call(weights_kernel, in_specs=[hbm(), vmem()] + [hbm()] * 3, ou...  3.87 us
    pallas_call x1, Pallas kernels, correct(): pl.pallas_call(correct_kernel, in_specs=[vmem()] * 12, out_specs=[hbm(),...  3.08 us
  transfers between devices with their start and end apart: 15, of which 3 were waited for; matrix products, arithmetic and copies ran while one was open for 0% of the time, Pallas kernels for 23%

profile of v7, /device:TPU:1, one launch (start us, length us, event | category | flops | bytes accessed | tf_op | source)
XLA Modules:
  0.0 73.5 jit_solution(11438162778107037314)
XLA Ops:
  0.6 0.0 copy-start
  0.6 2.6 %edges.1 = (f32[184,256]{1,0:T(8,128)S(1)}, f32[184,256]{1,0:T(8,128)S(1)}, f32[776,256]{1,0:T(8,128)S(1)}, f32[776,256]{1,0:T(8,128)S(1)}, f32[128,256]{1,0:T(8,128)}) custom-call(f32[4,8,128,256]{3,2,1,0:T(8,128)} %u_hbm.3, f32[8,128,256]{2,1,0:T(8,128)} %c_hbm.3, f32[4,128,128]{2,1,0:T(8,128)} %imp_hbm.1, s32[8,128]{1,0:T(8,128)} %cmap.9), custom_call_target="tpu_custom_call" | custom-call | tf_op jit(solution)/shard_map/edges/pallas_call | solution.py:228
  3.3 3.3 %collective-permute-start.2 = (f32[776,256]{1,0:T(8,128)S(1)}, f32[776,256]{1,0:T(8,128)S(1)}, u32[]{:S(2)}, u32[]{:S(2)}) collective-permute-start(f32[776,256]{1,0:T(8,128)S(1)} %get-tuple-element.53), channel_id=1, source_target_pairs={{0,8},{8,0},{1,9},{9,1},{2,10},{10,2},{3,11},{11,3},{4,12},{12,4},... | collective-permute-start | bytes 2383880 | tf_op jit(solution)/shard_map/ppermute | solution.py:943
  6.6 2.8 %collective-permute-start.4 = (f32[776,256]{1,0:T(8,128)S(1)}, f32[776,256]{1,0:T(8,128)S(1)}, u32[]{:S(2)}, u32[]{:S(2)}) collective-permute-start(f32[776,256]{1,0:T(8,128)S(1)} %get-tuple-element.74), channel_id=1, source_target_pairs={{8,16},{24,32},{40,48},{56,64},{72,80},{88,96},{104,112},{120,128}... | collective-permute-start | bytes 2383880 | tf_op jit(solution)/shard_map/ppermute | solution.py:947
  9.4 1.4 %collective-permute-start = (f32[184,256]{1,0:T(8,128)S(1)}, f32[184,256]{1,0:T(8,128)S(1)}, u32[]{:S(2)}, u32[]{:S(2)}) collective-permute-start(f32[184,256]{1,0:T(8,128)S(1)} %get-tuple-element.51.own_hi), channel_id=1, source_target_pairs={{0,1},{1,2},{2,3},{3,0},{4,5},{5,6},{6,7},{7,4},{8,9},{9,10},{10,1... | collective-permute-start | bytes 565256 | tf_op jit(solution)/shard_map/ppermute | solution.py:940
  10.8 1.5 %collective-permute-start.1 = (f32[184,256]{1,0:T(8,128)S(1)}, f32[184,256]{1,0:T(8,128)S(1)}, u32[]{:S(2)}, u32[]{:S(2)}) collective-permute-start(f32[184,256]{1,0:T(8,128)S(1)} %get-tuple-element.52.own_lo), channel_id=1, source_target_pairs={{0,3},{1,0},{2,1},{3,2},{4,7},{5,4},{6,5},{7,6},{8,11},{9,8},{10,9... | collective-permute-start | bytes 565256 | tf_op jit(solution)/shard_map/ppermute | solution.py:940
  12.3 0.0 copy-done
  12.3 0.0 copy-start.1
  12.3 3.9 %weights.1 = (f32[4,8,128,256]{3,2,1,0:T(8,128)S(1)}, f32[7,128,256]{2,1,0:T(8,128)S(1)}, f32[8,128,256]{2,1,0:T(8,128)S(1)}, f32[8,128,256]{2,1,0:T(8,128)S(1)}...) custom-call(f32[4,8,128,256]{3,2,1,0:T(8,128)} %u_hbm.3, ...), custom_call_target="tpu_custom_call" | custom-call | flops 20000000 | bytes 6000000 | tf_op jit(solution)/shard_map/weights/pallas_call | solution.py:348
  16.2 0.0 collective-permute-done.y_lo.i0
  16.2 0.0 collective-permute-done.1.y_hi.i1
  16.3 0.1 collective-permute-start.3
  16.4 5.1 %collective-permute-start.5 = (f32[8,256]{1,0:T(8,128)S(1)}, f32[8,256]{1,0:T(8,128)S(1)}, u32[]{:S(2)}, u32[]{:S(2)}) collective-permute-start(f32[8,256]{1,0:T(8,128)S(1)} %get-tuple-element.75), channel_id=1, source_target_pairs={{8,16},{24,32},{40,48},{56,64},{72,80},{88,96},{104,112},{120,128}... | collective-permute-start | bytes 24584 | tf_op jit(solution)/shard_map/ppermute | solution.py:947
  21.4 0.0 copy-done.1
  21.4 0.0 copy-start.3
  21.5 6.6 %inner.1 = (f32[2,4,128,256]{3,2,1,0:T(8,128)S(1)}, f32[4,4,128,256]{3,2,1,0:T(8,128)}, f32[8,128,256]{2,1,0:T(8,128)S(1)}, f32[8,256]{1,0:T(8,128)S(1)}, f32[8,...) custom-call(f32[4,8,128,256]{3,2,1,0:T(8,128)S(1)} %get-tuple-elemen, ...), custom_call_target="tpu_custom_call" | custom-call | flops 100000000 | bytes 25000000 | tf_op jit(solution)/shard_map/inner/pallas_call | solution.py:467
  28.0 0.0 collective-permute-done.3.ends.ends_near
  28.0 0.0 collective-permute-done.2.msg
  28.1 0.0 copy-done.3
  28.1 0.0 copy-start.4
  28.1 0.0 copy-start.5
  28.1 1.9 %near_side.1 = (f32[4,128,256]{2,1,0:T(8,128)}, f32[2,4,128,256]{3,2,1,0:T(8,128)}, f32[4,128,256]{2,1,0:T(8,128)S(1)}, f32[128,256]{1,0:T(8,128)S(1)}, f32[128,256]{1,0:T(8,128)S(1)}, /*index=5*/f32[64,128]{1,0:T(8,128)S(1)}) custom-call(s32[8,128]{1,0:T(8,128)S(1)} %copy-done.1, f32[16,128]{1,0:T(8,128)S(1)} %bitcast.4, ...), custom_call_target="tpu_custom_call" | custom-call | flops 25000000 | bytes 8000000 | tf_op jit(solution)/shard_map/near_side/pallas_call | solution.py:577
  30.0 0.0 collective-permute-done.5.ends
  30.0 0.0 collective-permute-done.4.msg
  30.0 0.0 copy-done.4
  30.1 0.0 copy-done.5
  30.1 0.0 copy-start.6
  30.1 0.0 copy-start.2
  30.1 2.3 %far_side.1 = (f32[4,128,256]{2,1,0:T(8,128)}, f32[32,256]{1,0:T(8,128)}, f32[32,256]{1,0:T(8,128)}, f32[2,4,128,256]{3,2,1,0:T(8,128)}, f32[8,128,256]{2,1,0:T(...) custom-call(s32[2,4]{1,0:T(2,128)S(1)} %bitcast.6, ...), custom_call_target="tpu_custom_call" | custom-call | flops 25000000 | bytes 8000000 | tf_op jit(solution)/shard_map/far_side/pallas_call | solution.py:677
  32.4 0.1 collective-permute-start.6
  32.5 1.2 %collective-permute-done.6.got = f32[32,128]{1,0:T(8,128)S(1)} collective-permute-done((f32[32,128]{1,0:T(8,128)S(1)}, f32[32,128]{1,0:T(8,128)S(1)}, u32[]{:S(2)}, u32[]{:S(2)}) %collective-permute-start.6) | collective-permute-done | bytes 16416 | tf_op jit(solution)/shard_map/ppermute | solution.py:943
  33.7 0.8 %spread.1 = f32[16,32,128]{2,1,0:T(8,128)} custom-call(f32[32,128]{1,0:T(8,128)S(1)} %get-tuple-element.77.mine, f32[32,128]{1,0:T(8,128)S(1)} %collective-permute-done.6.got), custom_call_target="tpu_custom_call" | custom-call | tf_op jit(solution)/shard_map/spread/pallas_call | solution.py:709
  34.4 9.9 %all-to-all-start = ((f32[16,32,128]{2,1,0:T(8,128)}), f32[16,32,128]{2,1,0:T(8,128)S(1)}, u32[]{:S(2)}, u32[]{:S(2)}) async-start(f32[16,32,128]{2,1,0:T(8,128)} %spread.1), calls=%async_computation | async-start | bytes 524288 | tf_op jit(solution)/shard_map/all_to_all | solution.py:974
  44.3 5.4 %collective-permute-start.13 = (f32[4,128,256]{2,1,0:T(8,128)}, f32[4,128,256]{2,1,0:T(8,128)S(1)}, u32[]{:S(2)}, u32[]{:S(2)}) collective-permute-start(f32[4,128,256]{2,1,0:T(8,128)} %get-tuple-element.97), channel_id=1, source_target_pairs={{8,16},{24,32},{40,48},{56,64},{72,80},{88,96},{104,112},{120,128}... | collective-permute-start | bytes 1572872 | tf_op jit(solution)/shard_map/ppermute | solution.py:947
  49.7 0.0 copy-done.6
  49.7 0.1 collective-permute-start.12
  49.8 0.0 copy-done.2
  49.8 2.9 %collective-permute-start.10 = (f32[128,256]{1,0:T(8,128)S(1)}, f32[128,256]{1,0:T(8,128)S(1)}, u32[]{:S(2)}, u32[]{:S(2)}) collective-permute-start(f32[128,256]{1,0:T(8,128)S(1)} %copy-done.2), channel_id=1, source_target_pairs={{0,2},{1,3},{2,0},{3,1},{4,6},{5,7},{6,4},{7,5},{8,10},{9,11},{10,... | collective-permute-start | bytes 393224 | tf_op jit(solution)/shard_map/ppermute | solution.py:940
  52.7 4.5 %all-to-all-done.parts_hbm = f32[16,32,128]{2,1,0:T(8,128)S(1)} async-done(((f32[16,32,128]{2,1,0:T(8,128)}), f32[16,32,128]{2,1,0:T(8,128)S(1)}, u32[]{:S(2)}, u32[]{:S(2)}) %all-to-all-start) | async-done | bytes 262176 | tf_op jit(solution)/shard_map/all_to_all | solution.py:974
  57.2 0.8 %gathered.1 = (f32[48,256]{1,0:T(8,128)S(1)}, f32[48,256]{1,0:T(8,128)S(1)}, f32[16,256]{1,0:T(8,128)S(1)}) custom-call(f32[16,32,128]{2,1,0:T(8,128)S(1)} %all-to-all-done.parts_hbm, f32[32,256]{1,0:T(8,128)} %get-tuple-element.79.edge_lo, f32[32,256]{1,0:T(8,128)} %get-tuple-element.80.edge_hi), custom_call_target="tpu_custom_call" | custom-call | tf_op jit(solution)/shard_map/gathered/pallas_call | solution.py:735
  58.0 1.4 %collective-permute-start.7 = (f32[48,256]{1,0:T(8,128)S(1)}, f32[48,256]{1,0:T(8,128)S(1)}, u32[]{:S(2)}, u32[]{:S(2)}) collective-permute-start(f32[48,256]{1,0:T(8,128)S(1)} %get-tuple-element.81), channel_id=1, source_target_pairs={{0,1},{1,2},{2,3},{3,0},{4,5},{5,6},{6,7},{7,4},{8,9},{9,10},{10,1... | collective-permute-start | bytes 147464 | tf_op jit(solution)/shard_map/ppermute | solution.py:940
  59.4 1.5 %collective-permute-start.8 = (f32[48,256]{1,0:T(8,128)S(1)}, f32[48,256]{1,0:T(8,128)S(1)}, u32[]{:S(2)}, u32[]{:S(2)}) collective-permute-start(f32[48,256]{1,0:T(8,128)S(1)} %get-tuple-element.82), channel_id=1, source_target_pairs={{0,3},{1,0},{2,1},{3,2},{4,7},{5,4},{6,5},{7,6},{8,11},{9,8},{10,9... | collective-permute-start | bytes 147464 | tf_op jit(solution)/shard_map/ppermute | solution.py:940
  60.9 0.0 collective-permute-done.10.i3
  60.9 1.3 %collective-permute-start.9 = (f32[16,256]{1,0:T(8,128)S(1)}, f32[16,256]{1,0:T(8,128)S(1)}, u32[]{:S(2)}, u32[]{:S(2)}) collective-permute-start(f32[16,256]{1,0:T(8,128)S(1)} %get-tuple-element.83.after.a2), channel_id=1, source_target_pairs={{0,2},{1,3},{2,0},{3,1},{4,6},{5,7},{6,4},{7,5},{8,10},{9,11},{10,... | collective-permute-start | bytes 49160 | tf_op jit(solution)/shard_map/ppermute | solution.py:940
  62.2 3.0 %ready.1 = (f32[4,8,128,256]{3,2,1,0:T(8,128)S(1)}, f32[8,128,256]{2,1,0:T(8,128)S(1)}, f32[16,256]{1,0:T(8,128)S(1)}, f32[2,128,256]{2,1,0:T(8,128)S(1)}) custom-call(f32[16,256]{1,0:T(8,128)S(1)} %get-tuple-element.83.after.a2, f32[4,4,128,256]{3,2,1,0:T(8,128)} %get-tuple-element.85.inner_hbm, f32[2,4,128,256]{3,2,1,0:T(8,128)} %get-tuple-element.86.near_hbm, ...), custom_call_target="tpu_custom_call" | custom-call | flops 10000000 | bytes 8000000 | tf_op jit(solution)/shard_map/ready/pallas_call | solution.py:830
  65.2 0.0 collective-permute-done.9.a3
  65.2 0.0 collective-permute-done.7.a0.e_lo
  65.2 0.0 collective-permute-done.8.a1.e_hi
  65.2 0.5 blocks.1.own
  65.7 3.7 %collective-permute-start.11 = (f32[4,8,128]{2,1,0:T(8,128)S(1)}, f32[4,8,128]{2,1,0:T(8,128)S(1)}, u32[]{:S(2)}, u32[]{:S(2)}) collective-permute-start(f32[4,8,128]{2,1,0:T(8,128)S(1)} %blocks.1.own), channel_id=1, source_target_pairs={{0,8},{8,0},{1,9},{9,1},{2,10},{10,2},{3,11},{11,3},{4,12},{12,4},... | collective-permute-start | bytes 49160 | tf_op jit(solution)/shard_map/ppermute | solution.py:943
  69.4 0.1 own_half.1.half
  69.5 0.0 collective-permute-done.13.h_far
  69.5 0.0 collective-permute-done.12.h_near
  69.5 0.7 collective-permute-done.11.got
  70.2 3.1 %correct.1 = (f32[4,8,128,256]{3,2,1,0:T(8,128)}, f32[4,512]{1,0:T(4,128)}) custom-call(s32[8,128]{1,0:T(8,128)S(1)} %copy-done.1, f32[32,128]{1,0:T(8,128)S(1)} %own_half.1.half, f32[4,8,128]{2,1,0:T(8,128)S(1)} %blocks.1.own, f32[4,8,128]{2,1,0:T(8,128)S(1)} %collective-permute-done.11.got, f32[4,8,128,256]{3,2,1,0:T(8,128)S(1)} %get-tuple-element.93.base, ...), custom_call_target="tpu_custom_call" | custom-call | tf_op jit(solution)/shard_map/correct/pallas_call | solution.py:917
  (1 shorter events, 0.0 us)
Async XLA Ops:
  0.6 11.7 %copy-start = (f32[4,8,128,256]{3,2,1,0:T(8,128)S(1)}, f32[4,8,128,256]{3,2,1,0:T(8,128)}, u32[]{:S(2)}) copy-start(f32[4,8,128,256]{3,2,1,0:T(8,128)} %f.3) | copy-start | bytes 12582916
  3.3 24.8 %collective-permute-start.2 = (f32[776,256]{1,0:T(8,128)S(1)}, f32[776,256]{1,0:T(8,128)S(1)}, u32[]{:S(2)}, u32[]{:S(2)}) collective-permute-start(f32[776,256]{1,0:T(8,128)S(1)} %get-tuple-element.53), channel_id=1, source_target_pairs={{0,8},{8,0},{1,9},{9,1},{2,10},{10,2},{3,11},{11,3},{4,12},{12,4},... | collective-permute-start | bytes 2383880 | tf_op jit(solution)/shard_map/ppermute | solution.py:943
  6.6 23.4 %collective-permute-start.4 = (f32[776,256]{1,0:T(8,128)S(1)}, f32[776,256]{1,0:T(8,128)S(1)}, u32[]{:S(2)}, u32[]{:S(2)}) collective-permute-start(f32[776,256]{1,0:T(8,128)S(1)} %get-tuple-element.74), channel_id=1, source_target_pairs={{8,16},{24,32},{40,48},{56,64},{72,80},{88,96},{104,112},{120,128}... | collective-permute-start | bytes 2383880 | tf_op jit(solution)/shard_map/ppermute | solution.py:947
  9.4 6.8 %collective-permute-start = (f32[184,256]{1,0:T(8,128)S(1)}, f32[184,256]{1,0:T(8,128)S(1)}, u32[]{:S(2)}, u32[]{:S(2)}) collective-permute-start(f32[184,256]{1,0:T(8,128)S(1)} %get-tuple-element.51.own_hi), channel_id=1, source_target_pairs={{0,1},{1,2},{2,3},{3,0},{4,5},{5,6},{6,7},{7,4},{8,9},{9,10},{10,1... | collective-permute-start | bytes 565256 | tf_op jit(solution)/shard_map/ppermute | solution.py:940
  10.8 5.4 %collective-permute-start.1 = (f32[184,256]{1,0:T(8,128)S(1)}, f32[184,256]{1,0:T(8,128)S(1)}, u32[]{:S(2)}, u32[]{:S(2)}) collective-permute-start(f32[184,256]{1,0:T(8,128)S(1)} %get-tuple-element.52.own_lo), channel_id=1, source_target_pairs={{0,3},{1,0},{2,1},{3,2},{4,7},{5,4},{6,5},{7,6},{8,11},{9,8},{10,9... | collective-permute-start | bytes 565256 | tf_op jit(solution)/shard_map/ppermute | solution.py:940
  12.3 9.1 %copy-start.1 = (s32[8,128]{1,0:T(8,128)S(1)}, s32[8,128]{1,0:T(8,128)}, u32[]{:S(2)}) copy-start(s32[8,128]{1,0:T(8,128)} %cmap.9) | copy-start | bytes 12292
  16.3 11.8 %collective-permute-start.3 = (f32[8,256]{1,0:T(8,128)S(1)}, f32[8,256]{1,0:T(8,128)S(1)}, u32[]{:S(2)}, u32[]{:S(2)}) collective-permute-start(f32[8,256]{1,0:T(8,128)S(1)} %get-tuple-element.54), channel_id=1, source_target_pairs={{0,8},{8,0},{1,9},{9,1},{2,10},{10,2},{3,11},{11,3},{4,12},{12,4},... | collective-permute-start | bytes 24584 | tf_op jit(solution)/shard_map/ppermute | solution.py:943
  16.4 13.7 %collective-permute-start.5 = (f32[8,256]{1,0:T(8,128)S(1)}, f32[8,256]{1,0:T(8,128)S(1)}, u32[]{:S(2)}, u32[]{:S(2)}) collective-permute-start(f32[8,256]{1,0:T(8,128)S(1)} %get-tuple-element.75), channel_id=1, source_target_pairs={{8,16},{24,32},{40,48},{56,64},{72,80},{88,96},{104,112},{120,128}... | collective-permute-start | bytes 24584 | tf_op jit(solution)/shard_map/ppermute | solution.py:947
  21.4 6.6 %copy-start.3 = (f32[2048]{0:T(1024)S(1)}, f32[2048]{0:T(1024)}, u32[]{:S(2)}) copy-start(f32[2048]{0:T(1024)} %param.12) | copy-start | bytes 24580
  28.1 2.0 %copy-start.4 = (s32[4,2]{0,1:T(2,128)S(1)}, s32[4,2]{0,1:T(2,128)}, u32[]{:S(2)}) copy-start(s32[4,2]{0,1:T(2,128)} %param.14) | copy-start | bytes 100
  28.1 2.0 %copy-start.5 = (f32[4]{0:T(128)S(1)}, f32[4]{0:T(128)}, u32[]{:S(2)}) copy-start(f32[4]{0:T(128)} %param.15) | copy-start | bytes 52
  30.1 19.6 %copy-start.6 = (f32[4,128,256]{2,1,0:T(8,128)S(1)}, f32[4,128,256]{2,1,0:T(8,128)}, u32[]{:S(2)}) copy-start(f32[4,128,256]{2,1,0:T(8,128)} %get-tuple-element.96) | copy-start | bytes 1572868
  30.1 19.7 %copy-start.2 = (f32[128,256]{1,0:T(8,128)S(1)}, f32[128,256]{1,0:T(8,128)}, u32[]{:S(2)}) copy-start(f32[128,256]{1,0:T(8,128)} %get-tuple-element.84.i2) | copy-start | bytes 393220
  32.4 1.3 %collective-permute-start.6 = (f32[32,128]{1,0:T(8,128)S(1)}, f32[32,128]{1,0:T(8,128)S(1)}, u32[]{:S(2)}, u32[]{:S(2)}) collective-permute-start(f32[32,128]{1,0:T(8,128)S(1)} %get-tuple-element.78), channel_id=1, source_target_pairs={{0,8},{8,0},{1,9},{9,1},{2,10},{10,2},{3,11},{11,3},{4,12},{12,4},... | collective-permute-start | bytes 49160 | tf_op jit(solution)/shard_map/ppermute | solution.py:943
  34.4 22.7 %all-to-all-start = ((f32[16,32,128]{2,1,0:T(8,128)}), f32[16,32,128]{2,1,0:T(8,128)S(1)}, u32[]{:S(2)}, u32[]{:S(2)}) async-start(f32[16,32,128]{2,1,0:T(8,128)} %spread.1), calls=%async_computation | async-start | bytes 524288 | tf_op jit(solution)/shard_map/all_to_all | solution.py:974
  44.3 25.2 %collective-permute-start.13 = (f32[4,128,256]{2,1,0:T(8,128)}, f32[4,128,256]{2,1,0:T(8,128)S(1)}, u32[]{:S(2)}, u32[]{:S(2)}) collective-permute-start(f32[4,128,256]{2,1,0:T(8,128)} %get-tuple-element.97), channel_id=1, source_target_pairs={{8,16},{24,32},{40,48},{56,64},{72,80},{88,96},{104,112},{120,128}... | collective-permute-start | bytes 1572872 | tf_op jit(solution)/shard_map/ppermute | solution.py:947
  49.7 19.8 %collective-permute-start.12 = (f32[4,128,256]{2,1,0:T(8,128)S(1)}, f32[4,128,256]{2,1,0:T(8,128)S(1)}, u32[]{:S(2)}, u32[]{:S(2)}) collective-permute-start(f32[4,128,256]{2,1,0:T(8,128)S(1)} %copy-done.6), channel_id=1, source_target_pairs={{0,8},{8,0},{1,9},{9,1},{2,10},{10,2},{3,11},{11,3},{4,12},{12,4},... | collective-permute-start | bytes 1572872 | tf_op jit(solution)/shard_map/ppermute | solution.py:943
  49.8 11.1 %collective-permute-start.10 = (f32[128,256]{1,0:T(8,128)S(1)}, f32[128,256]{1,0:T(8,128)S(1)}, u32[]{:S(2)}, u32[]{:S(2)}) collective-permute-start(f32[128,256]{1,0:T(8,128)S(1)} %copy-done.2), channel_id=1, source_target_pairs={{0,2},{1,3},{2,0},{3,1},{4,6},{5,7},{6,4},{7,5},{8,10},{9,11},{10,... | collective-permute-start | bytes 393224 | tf_op jit(solution)/shard_map/ppermute | solution.py:940
  58.0 7.2 %collective-permute-start.7 = (f32[48,256]{1,0:T(8,128)S(1)}, f32[48,256]{1,0:T(8,128)S(1)}, u32[]{:S(2)}, u32[]{:S(2)}) collective-permute-start(f32[48,256]{1,0:T(8,128)S(1)} %get-tuple-element.81), channel_id=1, source_target_pairs={{0,1},{1,2},{2,3},{3,0},{4,5},{5,6},{6,7},{7,4},{8,9},{9,10},{10,1... | collective-permute-start | bytes 147464 | tf_op jit(solution)/shard_map/ppermute | solution.py:940
  59.4 5.8 %collective-permute-start.8 = (f32[48,256]{1,0:T(8,128)S(1)}, f32[48,256]{1,0:T(8,128)S(1)}, u32[]{:S(2)}, u32[]{:S(2)}) collective-permute-start(f32[48,256]{1,0:T(8,128)S(1)} %get-tuple-element.82), channel_id=1, source_target_pairs={{0,3},{1,0},{2,1},{3,2},{4,7},{5,4},{6,5},{7,6},{8,11},{9,8},{10,9... | collective-permute-start | bytes 147464 | tf_op jit(solution)/shard_map/ppermute | solution.py:940
  60.9 4.3 %collective-permute-start.9 = (f32[16,256]{1,0:T(8,128)S(1)}, f32[16,256]{1,0:T(8,128)S(1)}, u32[]{:S(2)}, u32[]{:S(2)}) collective-permute-start(f32[16,256]{1,0:T(8,128)S(1)} %get-tuple-element.83.after.a2), channel_id=1, source_target_pairs={{0,2},{1,3},{2,0},{3,1},{4,6},{5,7},{6,4},{7,5},{8,10},{9,11},{10,... | collective-permute-start | bytes 49160 | tf_op jit(solution)/shard_map/ppermute | solution.py:940
  65.7 4.5 %collective-permute-start.11 = (f32[4,8,128]{2,1,0:T(8,128)S(1)}, f32[4,8,128]{2,1,0:T(8,128)S(1)}, u32[]{:S(2)}, u32[]{:S(2)}) collective-permute-start(f32[4,8,128]{2,1,0:T(8,128)S(1)} %blocks.1.own), channel_id=1, source_target_pairs={{0,8},{8,0},{1,9},{9,1},{2,10},{10,2},{3,11},{11,3},{4,12},{12,4},... | collective-permute-start | bytes 49160 | tf_op jit(solution)/shard_map/ppermute | solution.py:943
